TPU v7x, 512 devices: a whole 4x8x8 slice. The times are simulated.
512 devices in a mesh: dom: 128 (over x, y, z_lo), edge: 4 (over z_hi, core).
Axes of the slice: x: 4, y: 8, z: 8 (z_hi: 2, z_lo: 4; z = z_hi * 4 + z_lo), core: 2. Of those that a mesh axis runs over, the one named last changes fastest.
Arguments:
- entity: float32 [65536, 400], P('dom'), may hold values from -1.5 to 1.5
- state: float32 [65536], P('dom'), may hold values from 0.01 to 0.5
- relation: float32 [2112, 400], P('edge'), may hold values from 0.5 to 1.5
- edge_head: int32 [2, 128, 4, 512], P(None, 'dom', 'edge'), may hold values from 0 to 511
- edge_rel: int32 [2, 128, 4, 512], P(None, 'dom', 'edge'), may hold values from 0 to 2111
- edge_tail: int32 [2, 128, 4, 512], P(None, 'dom', 'edge'), may hold values from 0 to 511
- negatives: int32 [2, 128, 4, 320], P(None, 'dom', 'edge'), may hold values from 0 to 511
- counts: int32 [2, 128, 4], P(None, 'dom', 'edge'), may hold values from 1 to 512, 1536 in all within a row
- matching: int32 [2, 128], replicated, may hold values from 0 to 127, each once within a row
Outputs:
- updated: float32 [65536, 400], P('dom')
- accum: float32 [65536], P('dom')
Inputs may be any that keep to these rules, and one draw needn't show every extreme that they name: `matching`: each row is a permutation of the partitions. The 4 counts of one bucket and partition sum to 1536; the largest is exactly 512.
All inputs are finite; a program needn't handle non-finite values. No bound on the sum of `counts` on one device may be relied on, other than what follows from the above.
Results may differ from a plain program's by a relative error of at most 0.0003.
Values sent between devices are 32-bit elements; how exact they have to be, the bound alone decides.
No kernel may reach another device: no remote copies, remote signals or barrier semaphores. Data moves between devices by JAX's collectives and lax.ppermute only.
A program may use at most 64 MiB of HBM per device.

v0:
```python
import jax
import jax.numpy as jnp
from jax import lax
from jax.sharding import PartitionSpec as P

learn_rate = 0.1
highest_prec = lax.Precision.HIGHEST


def edge_terms(heads, rel_rows, tails, negs, live_mask):
    left_side = heads * rel_rows
    pos_score = jnp.sum(left_side * tails, axis=1)
    neg_scores = jnp.dot(left_side, negs.T, precision=highest_prec)
    row_top = jnp.maximum(pos_score, jnp.max(neg_scores, axis=1))
    weight_pos = jnp.exp(pos_score - row_top)
    weight_neg = jnp.exp(neg_scores - row_top[:, None])
    partition_sum = weight_pos + jnp.sum(weight_neg, axis=1)
    grad_pos = jnp.where(live_mask, weight_pos / partition_sum - 1.0, 0.0)
    grad_neg = jnp.where(live_mask[:, None], weight_neg / partition_sum[:, None], 0.0)
    grad_left = grad_pos[:, None] * tails + jnp.dot(grad_neg, negs, precision=highest_prec)
    return (
        grad_left * rel_rows,
        grad_pos[:, None] * left_side,
        jnp.dot(grad_neg.T, left_side, precision=highest_prec),
    )


def shards(entity, state, relation, edge_head, edge_rel, edge_tail, negatives, counts, matching):
    dom_count = lax.axis_size("dom")
    block_rows, feat_width = entity.shape
    relations = lax.all_gather(relation, "edge", axis=0, tiled=True)
    spread = lax.all_to_all(
        entity.reshape(dom_count, block_rows // dom_count, feat_width),
        "dom",
        split_axis=0,
        concat_axis=0,
        tiled=True,
    )
    outgoing = jnp.take(spread, matching, axis=0)
    partners = lax.all_to_all(outgoing, "dom", split_axis=1, concat_axis=1, tiled=True).reshape(
        2, block_rows, feat_width
    )
    slot_index = jnp.arange(edge_head.shape[-1], dtype=jnp.int32)
    head_grad = jnp.zeros((block_rows, feat_width), jnp.float32)
    tail_list = []
    for bucket in range(2):
        head_idx = edge_head[bucket, 0, 0]
        tail_idx = edge_tail[bucket, 0, 0]
        neg_idx = negatives[bucket, 0, 0]
        live_mask = slot_index < counts[bucket, 0, 0]
        partner_block = partners[bucket]
        grad_heads, grad_tails, grad_negs = edge_terms(
            entity[head_idx],
            relations[edge_rel[bucket, 0, 0]],
            partner_block[tail_idx],
            partner_block[neg_idx],
            live_mask,
        )
        head_grad = head_grad.at[head_idx].add(grad_heads)
        tail_grad = (
            jnp.zeros((block_rows, feat_width), jnp.float32)
            .at[tail_idx]
            .add(grad_tails)
            .at[neg_idx]
            .add(grad_negs)
        )
        tail_list.append(tail_grad)
    tail_stack = jnp.stack(tail_list)
    dom_ids = jnp.arange(dom_count, dtype=jnp.int32)
    inverse = (
        jnp.zeros((2, dom_count), jnp.int32)
        .at[jnp.arange(2, dtype=jnp.int32)[:, None], matching]
        .set(jnp.broadcast_to(dom_ids[None, :], (2, dom_count)))
    )
    back = lax.all_to_all(
        tail_stack.reshape(2, dom_count, block_rows // dom_count, feat_width),
        "dom",
        split_axis=1,
        concat_axis=1,
        tiled=True,
    )
    owed = jnp.take(back[0], inverse[0], axis=0) + jnp.take(back[1], inverse[1], axis=0)
    returned = lax.all_to_all(owed, "dom", split_axis=0, concat_axis=0, tiled=True).reshape(
        block_rows, feat_width
    )
    gradient = lax.psum(head_grad + returned, "edge")
    accum = state + jnp.mean(gradient * gradient, axis=1)
    updated = entity - learn_rate * gradient / jnp.sqrt(accum)[:, None]
    return (updated, accum)


def solution(mesh):
    return jax.shard_map(
        shards,
        mesh=mesh,
        in_specs=(
            P("dom", None),
            P("dom"),
            P("edge", None),
            P(None, "dom", "edge", None),
            P(None, "dom", "edge", None),
            P(None, "dom", "edge", None),
            P(None, "dom", "edge", None),
            P(None, "dom", "edge"),
            P(),
        ),
        out_specs=(P("dom", None), P("dom")),
        check_vma=False,
    )
```

profile of v0, /device:TPU:1, one launch (start us, length us, event | category | flops | bytes accessed | tf_op | source)
XLA Modules:
  0.0 439.4 jit_solution(5321631579421497999)
XLA Ops:
  10.0 17.8 %all-to-all-start = ((f32[128,4,400]{2,1,0:T(4,128)}), f32[128,4,400]{2,1,0:T(4,128)S(1)}, u32[]{:S(2)}, u32[]{:S(2)}) async-start(f32[128,4,400]{2,1,0:T(4,128)} %reshape.315), calls=%async_computation | async-start | bytes 2097152 | tf_op jit(solution)/shard_map/all_to_all | solution.py:32
  28.7 26.1 %all-to-all-done = f32[128,4,400]{2,1,0:T(4,128)S(1)} async-done(((f32[128,4,400]{2,1,0:T(4,128)}), f32[128,4,400]{2,1,0:T(4,128)S(1)}, u32[]{:S(2)}, u32[]{:S(2)}) %all-to-all-start) | async-done | bytes 819232 | tf_op jit(solution)/shard_map/all_to_all | solution.py:32
  54.8 3.0 gather_fusion.2
  57.8 2.9 copy_select_fusion
  60.7 36.5 %all-to-all-start.1 = ((f32[2,128,4,400]{3,2,0,1:T(4,128)}), f32[2,128,4,400]{3,2,0,1:T(4,128)S(1)}, u32[]{:S(2)}, u32[]{:S(2)}) async-start(f32[2,128,4,400]{3,2,0,1:T(4,128)} %copy_select_fusion), calls=%async_computation.1 | async-start | bytes 4194304 | tf_op jit(solution)/shard_map/all_to_all | solution.py:40
  97.2 2.3 gather_fusion.5
  99.6 2.4 copy.58
  102.1 2.3 gather_fusion
  104.4 2.4 copy.49
  108.9 37.5 %all-to-all-done.1 = f32[2,128,4,400]{3,2,0,1:T(4,128)S(1)} async-done(((f32[2,128,4,400]{3,2,0,1:T(4,128)}), f32[2,128,4,400]{3,2,0,1:T(4,128)S(1)}, u32[]{:S(2)}, u32[]{:S(2)}) %all-to-all-start.1) | async-done | bytes 1638432 | tf_op jit(solution)/shard_map/all_to_all | solution.py:40
  149.7 2.2 gather_fusion.4
  156.4 2.2 gather_fusion.8
  161.4 5.3 %copy.48 = f32[4,528,400]{2,1,0:T(8,128)} copy(f32[4,528,400]{1,2,0:T(8,128)} %all-gather.3.cloned.1.call-done) | data formatting | bytes 6758400 | tf_op jit(solution)/shard_map/all_gather | solution.py:31
  166.7 4.2 gather_fusion.6
  170.9 4.3 gather_fusion.1
  185.1 4.7 %scatter_custom_fusion = f32[512,400]{1,0:T(8,128)S(1)} fusion(s32[512]{0:T(512)S(1)} %bitcast.73, f32[512,400]{1,0:T(8,128)} %copy.55, f32[]{:T(128)} %constant.19.clone.1), kind=kCustom, calls=%fused_computation.39 | custom fusion | flops 204800 | bytes 819712 | tf_op jit(solution)/shard_map/scatter-add | solution.py:63
  189.8 3.4 scatter_fusion
  200.2 4.5 %scatter_custom_fusion.2 = f32[512,400]{1,0:T(8,128)S(1)} fusion(s32[512]{0:T(512)S(1)} %bitcast.71, f32[512,400]{1,0:T(8,128)} %copy.61, f32[]{:T(128)} %constant.19.clone.1), kind=kCustom, calls=%fused_computation.37 | custom fusion | flops 204800 | bytes 819712 | tf_op jit(solution)/shard_map/scatter-add | solution.py:63
  204.7 3.3 fusion.9
  207.9 3.6 scatter_fusion.1
  216.8 11.7 %all-to-all-start.2 = ((f32[2,128,4,400]{3,2,0,1:T(4,128)}), f32[2,128,4,400]{3,2,0,1:T(4,128)S(1)}, u32[]{:S(2)}, u32[]{:S(2)}) async-start(f32[2,128,4,400]{3,2,0,1:T(4,128)} %copy.63), calls=%async_computation.2 | async-start | bytes 4194304 | tf_op jit(solution)/shard_map/all_to_all | solution.py:75
  228.5 11.4 %scatter_fusion.2 = s32[2,128]{1,0:T(2,128)S(1)} fusion(s32[2,128]{1,0:T(2,128)S(1)} %lt.133, s32[256]{0:T(256)S(1)} %fusion.14, s32[256]{0:T(256)S(1)} %iota_bitcast_fusion), kind=kCustom, calls=%fused_computation.15 | custom fusion | bytes 5120 | tf_op jit(solution)/shard_map/scatter | solution.py:73
  240.0 37.4 %all-to-all-done.2 = f32[2,128,4,400]{3,2,0,1:T(4,128)S(1)} async-done(((f32[2,128,4,400]{3,2,0,1:T(4,128)}), f32[2,128,4,400]{3,2,0,1:T(4,128)S(1)}, u32[]{:S(2)}, u32[]{:S(2)}) %all-to-all-start.2) | async-done | bytes 1638432 | tf_op jit(solution)/shard_map/all_to_all | solution.py:75
  279.1 2.4 gather_fusion.9
  281.5 2.4 gather_fusion.10
  285.5 10.9 %all-to-all-start.3 = ((f32[128,4,400]{2,1,0:T(4,128)}), f32[128,4,400]{2,1,0:T(4,128)}, u32[]{:S(2)}, u32[]{:S(2)}) async-start(f32[128,4,400]{2,1,0:T(4,128)} %select_add_fusion), calls=%async_computation.3 | async-start | bytes 2097152 | tf_op jit(solution)/shard_map/all_to_all | solution.py:83
  296.7 3.8 fusion.1
  302.0 3.4 fusion
  306.8 15.3 %all-to-all-done.3 = f32[128,4,400]{2,1,0:T(4,128)} async-done(((f32[128,4,400]{2,1,0:T(4,128)}), f32[128,4,400]{2,1,0:T(4,128)}, u32[]{:S(2)}, u32[]{:S(2)}) %all-to-all-start.3) | async-done | bytes 819232 | tf_op jit(solution)/shard_map/all_to_all | solution.py:83
  323.7 4.0 scatter_fusion.3
  327.7 4.7 %scatter_fusion.4 = f32[512,400]{1,0:T(8,128)S(1)} fusion(f32[512,400]{1,0:T(8,128)S(1)} %scatter_fusion.3, s32[512]{0:T(512)S(1)} %bitcast.67, f32[512,400]{1,0:T(8,128)} %copy.71), kind=kCustom, calls=%fused_computation.17 | custom fusion | flops 204800 | bytes 2459648 | tf_op jit(solution)/shard_map/scatter-add | solution.py:59
  333.4 94.1 %all-reduce.2.cloned.1.call-done = f32[512,400]{1,0:T(8,128)} async-done(((f32[512,400]{1,0:T(8,128)}), f32[512,400]{1,0:T(8,128)}) %all-reduce.2.cloned.1.call-update) | async-done | bytes 819216 | tf_op jit(solution)/shard_map/psum | solution.py:86
  (99 shorter events, 51.9 us)
Async XLA Ops:
  8.6 19.9 %copy-start.12 = (s32[2,128]{1,0:T(2,128)S(1)}, s32[2,128]{1,0:T(2,128)}, u32[]{:S(2)}) copy-start(s32[2,128]{1,0:T(2,128)} %param.19) | copy-start | bytes 3076
  10.0 44.8 %all-to-all-start = ((f32[128,4,400]{2,1,0:T(4,128)}), f32[128,4,400]{2,1,0:T(4,128)S(1)}, u32[]{:S(2)}, u32[]{:S(2)}) async-start(f32[128,4,400]{2,1,0:T(4,128)} %reshape.315), calls=%async_computation | async-start | bytes 2097152 | tf_op jit(solution)/shard_map/all_to_all | solution.py:32
  27.8 133.6 %all-gather.3.cloned.1.call-start = ((), (), s32[]{:S(2)}) async-start(), calls=%async_computation.5 | async-start | bytes 5120000 | tf_op jit(solution)/shard_map/all_gather | solution.py:31
  60.7 36.5 %copy-start.9 = (s32[2,1,1,512]{3,2,1,0:T(1,128)S(1)}, s32[2,1,1,512]{3,2,1,0:T(1,128)}, u32[]{:S(2)}) copy-start(s32[2,1,1,512]{3,2,1,0:T(1,128)} %param.14) | copy-start | bytes 12292
  60.7 85.7 %all-to-all-start.1 = ((f32[2,128,4,400]{3,2,0,1:T(4,128)}), f32[2,128,4,400]{3,2,0,1:T(4,128)S(1)}, u32[]{:S(2)}, u32[]{:S(2)}) async-start(f32[2,128,4,400]{3,2,0,1:T(4,128)} %copy_select_fusion), calls=%async_computation.1 | async-start | bytes 4194304 | tf_op jit(solution)/shard_map/all_to_all | solution.py:40
  102.0 4.8 %copy-start.14 = (s32[2,1,1]{0,2,1:T(1,128)S(1)}, s32[2,1,1]{0,2,1:T(1,128)}, u32[]{:S(2)}) copy-start(s32[2,1,1]{0,2,1:T(1,128)} %param.18) | copy-start | bytes 28
  102.0 6.7 %copy-start.10 = (s32[2,1,1,512]{3,2,1,0:T(1,128)S(1)}, s32[2,1,1,512]{3,2,1,0:T(1,128)}, u32[]{:S(2)}) copy-start(s32[2,1,1,512]{3,2,1,0:T(1,128)} %param.15) | copy-start | bytes 12292
  102.0 6.8 %copy-start.11 = (s32[2,1,1,512]{3,2,1,0:T(1,128)S(1)}, s32[2,1,1,512]{3,2,1,0:T(1,128)}, u32[]{:S(2)}) copy-start(s32[2,1,1,512]{3,2,1,0:T(1,128)} %param.16) | copy-start | bytes 12292
  102.0 6.8 %copy-start.13 = (s32[2,1,1,320]{3,2,1,0:T(1,128)S(1)}, s32[2,1,1,320]{3,2,1,0:T(1,128)}, u32[]{:S(2)}) copy-start(s32[2,1,1,320]{3,2,1,0:T(1,128)} %param.17) | copy-start | bytes 7684
  176.4 1.2 copy-start.2
  177.6 1.7 copy-start.7
  180.6 2.3 copy-start.5
  194.5 2.0 copy-start.8
  197.8 0.9 copy-start.6
  211.6 1.4 copy-start.1
  216.8 60.6 %all-to-all-start.2 = ((f32[2,128,4,400]{3,2,0,1:T(4,128)}), f32[2,128,4,400]{3,2,0,1:T(4,128)S(1)}, u32[]{:S(2)}, u32[]{:S(2)}) async-start(f32[2,128,4,400]{3,2,0,1:T(4,128)} %copy.63), calls=%async_computation.2 | async-start | bytes 4194304 | tf_op jit(solution)/shard_map/all_to_all | solution.py:75
  285.5 11.2 %copy-start.3 = (f32[512,400]{0,1:T(8,128)S(1)}, f32[512,400]{0,1:T(8,128)}, u32[]{:S(2)}) copy-start(f32[512,400]{0,1:T(8,128)} %copy.54) | copy-start | bytes 2457604
  285.5 11.2 %copy-start.4 = (f32[512,400]{0,1:T(8,128)S(1)}, f32[512,400]{0,1:T(8,128)}, u32[]{:S(2)}) copy-start(f32[512,400]{0,1:T(8,128)} %copy.50) | copy-start | bytes 2457604
  285.5 36.6 %all-to-all-start.3 = ((f32[128,4,400]{2,1,0:T(4,128)}), f32[128,4,400]{2,1,0:T(4,128)}, u32[]{:S(2)}, u32[]{:S(2)}) async-start(f32[128,4,400]{2,1,0:T(4,128)} %select_add_fusion), calls=%async_computation.3 | async-start | bytes 2097152 | tf_op jit(solution)/shard_map/all_to_all | solution.py:83
  296.4 131.1 %all-reduce.2.cloned.1.call-start = ((), (), s32[]{:S(2)}) async-start(), calls=%async_computation.4 | async-start | bytes 2097152 | tf_op jit(solution)/shard_map/psum | solution.py:86
  332.4 1.0 copy-start
  332.4 96.5 %copy-start.15 = (f32[512]{0:T(512)S(1)}, f32[512]{0:T(512)}, u32[]{:S(2)}) copy-start(f32[512]{0:T(512)} %param.12) | copy-start | bytes 6148
Sparse Core Ops, SparseCore 0:
  30.7 72.2 all-gather.2
  333.6 93.8 all-reduce.1
where the time goes:
time: 446 us; the launch traced here: 439 us
  waiting for transfers between devices  211 us (47%)
  local copies, waits for them, and re-layouts  79.6 us (18%)
  starting transfers between devices  77.2 us (17%)
  other arithmetic  41.3 us (9%)
  matrix products  15.2 us (3%)
  between operations  15 us (3%)
    psum x1, waiting for transfers between devices, shards(): gradient = lax.psum(head_grad + returned, 'edge')  94.1 us
    all_to_all x1, waiting for transfers between devices, shards(): lax.all_to_all(outgoing, 'dom', split_axis=1, concat_axis=1, tiled=True)  37.5 us
    all_to_all x1, waiting for transfers between devices, shards(): lax.all_to_all(tail_stack.reshape(2, dom_count, block_rows // dom_count,...  37.4 us
    all_to_all x1, starting transfers between devices, shards(): lax.all_to_all(outgoing, 'dom', split_axis=1, concat_axis=1, tiled=True)  36.5 us
    all_to_all x1, waiting for transfers between devices, shards(): lax.all_to_all(entity.reshape(dom_count, block_rows // dom_count, feat_wi...  26.1 us
    all_to_all x1, starting transfers between devices, shards(): lax.all_to_all(entity.reshape(dom_count, block_rows // dom_count, feat_wi...  17.8 us
    scatter-add x4, other arithmetic, shards(): tail_grad = jnp.zeros((block_rows, feat_width), jnp.float32).at[tail_idx]...  16.2 us
    all_to_all x1, waiting for transfers between devices, shards(): lax.all_to_all(owed, 'dom', split_axis=0, concat_axis=0, tiled=True)  15.3 us
  transfers between devices with their start and end apart: 6, of which 5 were waited for; matrix products, arithmetic and copies ran while one was open for 12% of the time, Pallas kernels for 0%

commit v1 on v0

v1 whole, which is shorter than its diff:
```python
import functools

import jax
import jax.numpy as jnp
from jax import lax
from jax.experimental import pallas as pl
from jax.experimental.pallas import tpu as pltpu
from jax.sharding import PartitionSpec as P


LEARN_RATE = 0.1
D = 400
ROWS = 512
HALF = 256
SLOTS = 512
REL_DEV = 528
PIECES = 4
PIECE = 144
PIECE_STEP = 144
PIECE_LAST = REL_DEV - PIECE
TABLE = 2 * REL_DEV + 2 * PIECES * PIECE
LIST = 16
LEG1 = 896
LEG2 = 1664
TAIL0 = 1536
F32 = jnp.float32
BF16 = jnp.bfloat16
VMEM_LIMIT = 40 * 1024 * 1024


def split2(x):
    hi = x.astype(BF16)
    return hi, (x - hi.astype(F32)).astype(BF16)


def split3(x):
    hi = x.astype(BF16)
    rest = x - hi.astype(F32)
    mid = rest.astype(BF16)
    return hi, mid, (rest - mid.astype(F32)).astype(BF16)


def dot_nn(a, b):
    return lax.dot_general(a, b, (((1,), (0,)), ((), ())), preferred_element_type=F32)


def dot_nt(a, b):
    return lax.dot_general(a, b, (((1,), (1,)), ((), ())), preferred_element_type=F32)


def iota(shape, dim):
    return lax.broadcasted_iota(jnp.int32, shape, dim)


def place():
    edge = lax.axis_index("edge")
    return edge // 2, lax.rem(edge, 2)


def onehot_cols(lists, first, count, columns):
    blocks = [(lists[:, first + j : first + j + 1] == columns) for j in range(count)]
    return jnp.concatenate([jnp.where(b, 1.0, 0.0) for b in blocks], axis=0).astype(BF16)


def pack_kernel(entity_ref, head_ref, rel_ref, tail_ref, neg_ref, count_ref, out_ref, lists_ref, rows_ref):
    zh, core = place()
    rows_ref[...] = jnp.full((128, 128), -1.0, F32)
    lane = iota((1, 128), 1)
    for bucket in range(2):
        at = bucket * LIST
        live = count_ref[bucket, 0, 0]
        for j in range(4):
            span = pl.ds(128 * j, 128)
            head = jnp.where(lane + 128 * j < live, head_ref[bucket, 0, 0:1, span], -1)
            rows_ref[at + j : at + j + 1, :] = head.astype(F32)
            rows_ref[at + 4 + j : at + 5 + j, :] = rel_ref[bucket, 0, 0:1, span].astype(F32)
            rows_ref[at + 8 + j : at + 9 + j, :] = tail_ref[bucket, 0, 0:1, span].astype(F32)
        rows_ref[at + 12 : at + 13, :] = neg_ref[bucket, 0, 0:1, 0:128].astype(F32)
        rows_ref[at + 13 : at + 14, :] = neg_ref[bucket, 0, 0:1, 128:256].astype(F32)
        rows_ref[at + 14 : at + 15, 0:64] = neg_ref[bucket, 0, 0:1, 256:320].astype(F32)
    one, two = rows_ref[0:LIST, :], rows_ref[LIST : 2 * LIST, :]
    keep = jnp.where(zh == 0, one, two)
    give = jnp.where(zh == 0, two, one)
    both = jnp.concatenate([keep, give, rows_ref[2 * LIST :, :]], axis=0).T
    lists_ref[...] = both
    start = pl.multiple_of(core * HALF, HALF)
    out_ref[...] = jnp.concatenate(
        [entity_ref[pl.ds(start, 128), :], entity_ref[pl.ds(start + 128, 128), :], both[:, 0 : LEG1 - 2 * D]], axis=1
    )


def route_kernel(x_ref, matching_ref, out_ref):
    zh, _ = place()
    x = x_ref[...]
    parts = split3(x)
    rows = iota((128, 128), 0)
    marks = [jnp.where(matching_ref[b : b + 1, :] == rows, 1.0, 0.0) for b in range(2)]
    back_keep = jnp.where(zh == 0, marks[0], marks[1])
    back_give = jnp.where(zh == 0, marks[1], marks[0])
    fore = back_keep.T.astype(BF16)
    back_keep, back_give = back_keep.astype(BF16), back_give.astype(BF16)
    partner = sum(dot_nn(fore, p) for p in reversed(parts))
    source = sum(dot_nn(back_keep, p) for p in reversed(parts))
    given = sum(dot_nn(back_give, p[:, 768:LEG1]) for p in reversed(parts))
    out_ref[...] = jnp.concatenate(
        [partner[:, 0 : 2 * D], source[:, 0 : 2 * D + LIST], given[:, 48:64], jnp.zeros((128, LEG2 - 4 * D - 2 * LIST), F32)],
        axis=1,
    )


def table_row(rel, zh, core, spot):
    owner = (rel >= REL_DEV).astype(jnp.int32) + (rel >= 2 * REL_DEV).astype(jnp.int32)
    owner = owner + (rel >= 3 * REL_DEV).astype(jnp.int32)
    off = rel - REL_DEV * owner
    owner_zh = (owner >= 2).astype(jnp.int32)
    other_core = (owner - 2 * owner_zh) != core
    piece = (off >= PIECE_STEP).astype(jnp.int32) + (off >= 2 * PIECE_STEP).astype(jnp.int32)
    piece = piece + (off >= 3 * PIECE_STEP).astype(jnp.int32)
    start = jnp.minimum(PIECE_STEP * piece, PIECE_LAST)
    slot = spot - piece
    slot = jnp.where(slot < 0, slot + PIECES, slot)
    near = jnp.where(other_core, REL_DEV, 0) + off
    far = 2 * REL_DEV + jnp.where(other_core, PIECES * PIECE, 0) + slot * PIECE + off - start
    return jnp.where(owner_zh == zh, near, far)


def spot_of_device():
    return lax.axis_index("dom") // 32


def left_kernel(
    entity_ref, mine_ref, theirs_ref, near_ref, near2_ref, far_ref, far2_ref, rel_out, left_hi, left_lo, table_hi, table_lo
):
    zh, core = place()
    spot = spot_of_device()
    at = 0
    for ref in (near_ref, near2_ref, far_ref, far2_ref):
        count = ref.shape[0]
        hi, lo = split2(ref[...])
        table_hi[at : at + count, :] = hi
        table_lo[at : at + count, :] = lo
        at += count
    entity_hi, entity_lo = split2(entity_ref[...])
    own = iota((128, ROWS), 1).astype(F32)
    table_at = iota((128, TABLE), 1)
    for k in range(2):
        lists = (mine_ref[:, 0:LIST], theirs_ref[:, LIST : 2 * LIST])[k]
        heads = onehot_cols(lists, 0, 4, own)
        head_rows = dot_nn(heads, entity_hi) + dot_nn(heads, entity_lo)
        rel_at = table_row(lists[:, 4:8].astype(jnp.int32), zh, core, spot)
        rels = onehot_cols(rel_at, 0, 4, table_at)
        rel_rows = dot_nn(rels, table_hi[...]) + dot_nn(rels, table_lo[...])
        hi, lo = split2(head_rows * rel_rows)
        span = pl.ds(k * SLOTS, SLOTS)
        rel_out[span, :] = rel_rows
        left_hi[span, :] = hi
        left_lo[span, :] = lo


def fill_block(hi_ref, lo_ref, mine_ref, theirs_ref, first):
    for k, (ref, lane) in enumerate(((mine_ref, 0), (mine_ref, D), (theirs_ref, 0), (theirs_ref, D))):
        hi, lo = split2(ref[:, first + lane : first + lane + D])
        hi_ref[128 * k : 128 * (k + 1), :] = hi
        lo_ref[128 * k : 128 * (k + 1), :] = lo


def lists_rows(lists):
    return jnp.concatenate([lists, jnp.zeros((128, 128 - LIST), F32)], axis=1).T


def head_kernel(mine_ref, theirs_ref, lists_mine, lists_theirs, rel_ref, left_hi, left_lo, grad_ref, block_hi, block_lo):
    _, core = place()
    fill_block(block_hi, block_lo, mine_ref, theirs_ref, 0)
    numbers = jnp.bitwise_xor(iota((128, ROWS), 1), core * HALF).astype(F32)
    heads_at = iota((ROWS, 128), 0).astype(F32)
    total = None
    for k in range(2):
        lists = (lists_mine[:, 0:LIST], lists_theirs[:, LIST : 2 * LIST])[k]
        span = pl.ds(k * SLOTS, SLOTS)
        hi, lo = left_hi[span, :], left_lo[span, :]
        b_hi, b_lo = block_hi[...], block_lo[...]
        scores = dot_nt(hi, b_lo) + dot_nt(lo, b_hi) + dot_nt(hi, b_hi)
        tails = jnp.concatenate(
            [jnp.where(lists[:, 8 + j : 9 + j] == numbers, 1.0, 0.0) for j in range(4)], axis=0
        )
        drawn = sum(jnp.where(lists[:, 12 + j : 13 + j] == numbers, 1.0, 0.0) for j in range(3))
        times = jnp.sum(drawn, axis=0, keepdims=True) + tails
        scores = jnp.where(times > 0.0, scores, -3.0e38)
        weights = times * jnp.exp(scores - jnp.max(scores, axis=1, keepdims=True))
        weights = weights / jnp.sum(weights, axis=1, keepdims=True) - tails
        w_hi, w_lo = split2(weights)
        grad_left = dot_nn(w_hi, b_lo) + dot_nn(w_lo, b_hi) + dot_nn(w_hi, b_hi)
        g_hi, g_lo = split2(grad_left * rel_ref[span, :])
        rows = lists_rows(lists)
        marks = jnp.concatenate(
            [jnp.where(rows[j : j + 1, :] == heads_at, 1.0, 0.0) for j in range(4)], axis=1
        ).astype(BF16)
        part = dot_nn(marks, g_lo) + dot_nn(marks, g_hi)
        total = part if total is None else total + part
    grad_ref[...] = total


def tail_kernel(
    mine_ref, theirs_ref, given_ref, entity_ref, table_hi, table_lo, head_grad, keep_ref, send_ref, block_hi, block_lo, sum_ref
):
    zh, core = place()
    spot = spot_of_device()
    fill_block(block_hi, block_lo, mine_ref, theirs_ref, 2 * D)
    e_hi, e_lo = split2(entity_ref[...])
    numbers = jnp.bitwise_xor(iota((128, ROWS), 1), core * HALF).astype(F32)
    rows_at = iota((ROWS, 128), 0).astype(F32)
    table_at = iota((128, TABLE), 1)
    total = head_grad[...]
    for k in range(2):
        if k == 0:
            lists = mine_ref[:, 4 * D : 4 * D + LIST]
        else:
            lists = given_ref[:, 4 * D + LIST - TAIL0 : 4 * D + 2 * LIST - TAIL0]
        heads = onehot_cols(lists, 0, 4, numbers)
        head_rows = dot_nn(heads, block_hi[...]) + dot_nn(heads, block_lo[...])
        rel_at = table_row(lists[:, 4:8].astype(jnp.int32), zh, core, spot)
        rels = onehot_cols(rel_at, 0, 4, table_at)
        rel_rows = dot_nn(rels, table_hi[...]) + dot_nn(rels, table_lo[...])
        l_hi, l_lo = split2(head_rows * rel_rows)
        scores = dot_nt(e_lo, l_hi) + dot_nt(e_hi, l_lo) + dot_nt(e_hi, l_hi)
        rows = lists_rows(lists)
        tails = jnp.concatenate(
            [jnp.where(rows[8 + j : 9 + j, :] == rows_at, 1.0, 0.0) for j in range(4)], axis=1
        )
        drawn = sum(jnp.where(rows[12 + j : 13 + j, :] == rows_at, 1.0, 0.0) for j in range(3))
        times = jnp.sum(drawn, axis=1, keepdims=True) + tails
        scores = jnp.where(times > 0.0, scores, -3.0e38)
        weights = times * jnp.exp(scores - jnp.max(scores, axis=0, keepdims=True))
        weights = weights / jnp.sum(weights, axis=0, keepdims=True) - tails
        w_hi, w_lo = split2(weights)
        total = total + (dot_nn(w_lo, l_hi) + dot_nn(w_hi, l_lo) + dot_nn(w_hi, l_hi))
    sum_ref[...] = total
    keep_ref[...] = sum_ref[pl.ds(pl.multiple_of(core * HALF, HALF), HALF), :]
    send_ref[...] = sum_ref[pl.ds(pl.multiple_of((1 - core) * HALF, HALF), HALF), :]


def update_kernel(mine_ref, theirs_ref, entity_ref, state_ref, updated_ref, accum_ref):
    _, core = place()
    lane = iota((128, 128), 1)
    state = jnp.concatenate([state_ref[...], jnp.zeros((124, 128), F32)], axis=0).T
    accums = jnp.zeros((128, 128), F32)
    for j in range(4):
        a = mine_ref[128 * (j % 2) : 128 * (j % 2) + 128, :]
        b = theirs_ref[128 * (j % 2) : 128 * (j % 2) + 128, :]
        gradient = jnp.where(core == j // 2, a, b)
        accum = state[:, j : j + 1] + jnp.sum(gradient * gradient, axis=1, keepdims=True) / float(D)
        accums = jnp.where(lane == j, accum, accums)
        span = slice(128 * j, 128 * j + 128)
        updated_ref[span, :] = entity_ref[span, :] - LEARN_RATE * gradient / jnp.sqrt(accum)
    accum_ref[...] = accums.T[0:4, :]


def call(kernel, out_shape, args, scratch=(), cost=None, smem=()):
    out_shape = jax.tree.map(lambda s: jax.ShapeDtypeStruct(*s), out_shape, is_leaf=lambda s: isinstance(s, tuple))
    specs = [
        pl.BlockSpec(memory_space=pltpu.SMEM if i in smem else pltpu.VMEM) for i in range(len(args))
    ]
    return pl.pallas_call(
        kernel,
        out_shape=out_shape,
        in_specs=specs,
        out_specs=jax.tree.map(lambda _: pl.BlockSpec(memory_space=pltpu.VMEM), out_shape),
        scratch_shapes=list(scratch),
        compiler_params=pltpu.CompilerParams(vmem_limit_bytes=VMEM_LIMIT),
        cost_estimate=cost,
        name=kernel.__name__,
    )(*args)


def flops(us):
    return pl.CostEstimate(flops=int(us * 1.0e9), bytes_accessed=4_000_000, transcendentals=0)


def shards(entity, state, relation, edge_head, edge_rel, edge_tail, negatives, counts, matching):
    edge = lax.axis_index("edge")
    doms = lax.axis_size("dom")
    spot = spot_of_device()
    swap_core = functools.partial(lax.ppermute, axis_name="edge", perm=[(0, 1), (1, 0), (2, 3), (3, 2)])
    swap_zh = functools.partial(lax.ppermute, axis_name="edge", perm=[(0, 2), (2, 0), (1, 3), (3, 1)])

    payload, lists = call(
        pack_kernel,
        [((128, LEG1), F32), ((128, 128), F32)],
        (entity, edge_head, edge_rel, edge_tail, negatives, counts),
        scratch=[pltpu.VMEM((128, 128), F32)],
        smem=(5,),
    )
    spread = lax.all_to_all(payload, "dom", split_axis=0, concat_axis=0, tiled=True)
    lists_other = swap_zh(lists)

    start = jnp.minimum(PIECE_STEP * spot, PIECE_LAST)
    piece = swap_zh(lax.dynamic_slice_in_dim(relation, start, PIECE, axis=0))
    far = [piece]
    for shift in range(1, PIECES):
        far.append(lax.ppermute(piece, "dom", perm=[(d, (d + 32 * shift) % doms) for d in range(doms)]))
    far = jnp.concatenate(far, axis=0)
    near2 = swap_core(relation)
    far2 = swap_core(far)

    routed = call(route_kernel, ((128, LEG2), F32), (spread, matching))
    fetched = lax.all_to_all(routed, "dom", split_axis=0, concat_axis=0, tiled=True)
    rel_rows, left_hi, left_lo, table_hi, table_lo = call(
        left_kernel,
        [
            ((2 * SLOTS, D), F32),
            ((2 * SLOTS, D), BF16),
            ((2 * SLOTS, D), BF16),
            ((TABLE, D), BF16),
            ((TABLE, D), BF16),
        ],
        (entity, lists, lists_other, relation, near2, far, far2),
        cost=flops(15),
    )
    fetched_other = swap_core(fetched)
    given = swap_zh(fetched[:, TAIL0:LEG2])
    block = [pltpu.VMEM((ROWS, D), BF16), pltpu.VMEM((ROWS, D), BF16)]
    head_grad = call(
        head_kernel,
        ((ROWS, D), F32),
        (fetched, fetched_other, lists, lists_other, rel_rows, left_hi, left_lo),
        scratch=block,
        cost=flops(8),
    )
    keep, send = call(
        tail_kernel,
        [((HALF, D), F32), ((HALF, D), F32)],
        (fetched, fetched_other, given, entity, table_hi, table_lo, head_grad),
        scratch=block + [pltpu.VMEM((ROWS, D), F32)],
        cost=flops(10),
    )
    half = keep + swap_core(send)
    half = half + swap_zh(half)
    other = swap_core(half)
    updated, accum = call(
        update_kernel,
        [((ROWS, D), F32), ((4, 128), F32)],
        (half, other, entity, state.reshape(4, 128)),
    )
    return updated, accum.reshape(ROWS)


def solution(mesh):
    return jax.shard_map(
        shards,
        mesh=mesh,
        in_specs=(
            P("dom", None),
            P("dom"),
            P("edge", None),
            P(None, "dom", "edge", None),
            P(None, "dom", "edge", None),
            P(None, "dom", "edge", None),
            P(None, "dom", "edge", None),
            P(None, "dom", "edge"),
            P(),
        ),
        out_specs=(P("dom", None), P("dom")),
        check_vma=False,
    )
```

time: 446 us -> 181 us (0.41)
  the two profiles are of different devices: /device:TPU:1 before, /device:TPU:131 now
where the time goes in v1:
time: 181 us
  starting transfers between devices  80.4 us (44%)
  waiting for transfers between devices  55.6 us (31%)
  Pallas kernels  25.8 us (14%)
  local copies, waits for them, and re-layouts  17.7 us (10%)
    ppermute x1, waiting for transfers between devices, shards(): half = half + swap_zh(half)  27 us
    pallas_call x6, Pallas kernels, call(): pl.pallas_call(kernel, out_shape=out_shape, in_specs=specs, out_specs=jax...  25.8 us
    ppermute x1, starting transfers between devices, shards(): lists_other = swap_zh(lists)  19.9 us
    ppermute x3, waiting for transfers between devices, shards(): lax.ppermute(piece, 'dom', perm=[(d, (d + 32 * shift) % doms) for d in ra...  16.5 us
    all_to_all x1, starting transfers between devices, shards(): lax.all_to_all(payload, 'dom', split_axis=0, concat_axis=0, tiled=True)  14.6 us
    ppermute x3, starting transfers between devices, shards(): lax.ppermute(piece, 'dom', perm=[(d, (d + 32 * shift) % doms) for d in ra...  10 us
    all_to_all x1, starting transfers between devices, shards(): lax.all_to_all(routed, 'dom', split_axis=0, concat_axis=0, tiled=True)  10 us
    unnamed x27, local copies, waits for them, and re-layouts  8.01 us
  transfers between devices with their start and end apart: 14, of which 9 were waited for; matrix products, arithmetic and copies ran while one was open for 7% of the time, Pallas kernels for 7%

profile of v1, /device:TPU:131, one launch (start us, length us, event | category | flops | bytes accessed | tf_op | source)
XLA Modules:
  0.0 180.6 jit_solution(7707176216296105300)
XLA Ops:
  0.7 1.5 copy.20.entity_ref
  4.3 14.6 %all-to-all-start = ((f32[128,1,896]{2,1,0:T(1,128)}), f32[128,1,896]{2,1,0:T(1,128)S(1)}, u32[]{:S(2)}, u32[]{:S(2)}) async-start(f32[128,1,896]{2,1,0:T(1,128)} %copy.22), calls=%async_computation | async-start | bytes 917504 | tf_op jit(solution)/shard_map/all_to_all | solution.py:293
  18.9 1.6 copy.27.near_ref
  20.6 7.9 %collective-permute-start.4 = (f32[144,400]{1,0:T(8,128)S(1)}, f32[144,400]{1,0:T(8,128)}, u32[]{:S(2)}, u32[]{:S(2)}) collective-permute-start(f32[144,400]{1,0:T(8,128)S(1)} %constant_dynamic-slice_fusion), channel_id=1, source_target_pairs={{0,2},{2,0},{1,3},{3,1},{4,6},{6,4},{5,7},{7,5},{8,10},{10,8},{9,1... | collective-permute-start | bytes 691208 | tf_op jit(solution)/shard_map/ppermute | solution.py:297
  28.5 5.1 %all-to-all-done = f32[128,1,896]{2,1,0:T(1,128)S(1)} async-done(((f32[128,1,896]{2,1,0:T(1,128)}), f32[128,1,896]{2,1,0:T(1,128)S(1)}, u32[]{:S(2)}, u32[]{:S(2)}) %all-to-all-start) | async-done | bytes 458784 | tf_op jit(solution)/shard_map/all_to_all | solution.py:293
  34.5 1.8 %copy.23 = f32[128,1,1664]{2,1,0:T(1,128)} copy(f32[128,1,1664]{2,0,1:T(8,128)S(1)} %bitcast.10) | data formatting | bytes 1703936 | tf_op jit(solution)/shard_map/all_to_all | solution.py:306
  36.3 10.0 %all-to-all-start.1 = ((f32[128,1,1664]{2,1,0:T(1,128)}), f32[128,1,1664]{2,1,0:T(1,128)}, u32[]{:S(2)}, u32[]{:S(2)}) async-start(f32[128,1,1664]{2,1,0:T(1,128)} %copy.23), calls=%async_computation.1 | async-start | bytes 1703936 | tf_op jit(solution)/shard_map/all_to_all | solution.py:306
  47.2 3.3 %collective-permute-start.5 = (f32[144,400]{1,0:T(8,128)}, f32[144,400]{1,0:T(8,128)S(1)}, u32[]{:S(2)}, u32[]{:S(2)}) collective-permute-start(f32[144,400]{1,0:T(8,128)} %collective-permute-done.4), channel_id=1, source_target_pairs={{0,128},{4,132},{8,136},{12,140},{16,144},{20,148},{24,152},{28,15... | collective-permute-start | bytes 691208 | tf_op jit(solution)/shard_map/ppermute | solution.py:300
  50.5 2.7 %collective-permute-start.6 = (f32[144,400]{1,0:T(8,128)}, f32[144,400]{1,0:T(8,128)S(1)}, u32[]{:S(2)}, u32[]{:S(2)}) collective-permute-start(f32[144,400]{1,0:T(8,128)} %collective-permute-done.4), channel_id=1, source_target_pairs={{0,256},{4,260},{8,264},{12,268},{16,272},{20,276},{24,280},{28,28... | collective-permute-start | bytes 691208 | tf_op jit(solution)/shard_map/ppermute | solution.py:300
  53.2 4.0 %collective-permute-start.7 = (f32[144,400]{1,0:T(8,128)}, f32[144,400]{1,0:T(8,128)S(1)}, u32[]{:S(2)}, u32[]{:S(2)}) collective-permute-start(f32[144,400]{1,0:T(8,128)} %collective-permute-done.4), channel_id=1, source_target_pairs={{0,384},{4,388},{8,392},{12,396},{16,400},{20,404},{24,408},{28,41... | collective-permute-start | bytes 691208 | tf_op jit(solution)/shard_map/ppermute | solution.py:300
  58.2 3.6 %collective-permute-done.5 = f32[144,400]{1,0:T(8,128)S(1)} collective-permute-done((f32[144,400]{1,0:T(8,128)}, f32[144,400]{1,0:T(8,128)S(1)}, u32[]{:S(2)}, u32[]{:S(2)}) %collective-permute-start.5) | collective-permute-done | bytes 230432 | tf_op jit(solution)/shard_map/ppermute | solution.py:300
  61.8 5.0 %collective-permute-done.6 = f32[144,400]{1,0:T(8,128)S(1)} collective-permute-done((f32[144,400]{1,0:T(8,128)}, f32[144,400]{1,0:T(8,128)S(1)}, u32[]{:S(2)}, u32[]{:S(2)}) %collective-permute-start.6) | collective-permute-done | bytes 230432 | tf_op jit(solution)/shard_map/ppermute | solution.py:300
  66.8 7.9 %collective-permute-done.7 = f32[144,400]{1,0:T(8,128)S(1)} collective-permute-done((f32[144,400]{1,0:T(8,128)}, f32[144,400]{1,0:T(8,128)S(1)}, u32[]{:S(2)}, u32[]{:S(2)}) %collective-permute-start.7) | collective-permute-done | bytes 230432 | tf_op jit(solution)/shard_map/ppermute | solution.py:300
  74.8 1.3 copy.25
  76.1 2.4 %collective-permute-start.8 = (f32[576,400]{0,1:T(8,128)}, f32[576,400]{0,1:T(8,128)}, u32[]{:S(2)}, u32[]{:S(2)}) collective-permute-start(f32[576,400]{0,1:T(8,128)} %copy.25), channel_id=1, source_target_pairs={{0,1},{1,0},{2,3},{3,2},{4,5},{5,4},{6,7},{7,6},{8,9},{9,8},{10,11... | collective-permute-start | bytes 2764808 | tf_op jit(solution)/shard_map/ppermute | solution.py:303
  78.5 1.9 %collective-permute-start.3 = (f32[528,400]{0,1:T(8,128)}, f32[528,400]{0,1:T(8,128)}, u32[]{:S(2)}, u32[]{:S(2)}) collective-permute-start(f32[528,400]{0,1:T(8,128)} %param.11), channel_id=1, source_target_pairs={{0,1},{1,0},{2,3},{3,2},{4,5},{5,4},{6,7},{7,6},{8,9},{9,8},{10,11... | collective-permute-start | bytes 2534408 | tf_op jit(solution)/shard_map/ppermute | solution.py:302
  80.5 19.9 %collective-permute-start.2 = (f32[128,128]{1,0:T(8,128)S(1)}, f32[128,128]{1,0:T(8,128)S(1)}, u32[]{:S(2)}, u32[]{:S(2)}) collective-permute-start(f32[128,128]{1,0:T(8,128)S(1)} %get-tuple-element.14.mine_ref.lists_mine), channel_id=1, source_target_pairs={{0,2},{2,0},{1,3},{3,1},{4,6},{6,4},{5,7},{7,5},{8,10},{10,8},{9,1... | collective-permute-start | bytes 196616 | tf_op jit(solution)/shard_map/ppermute | solution.py:294
  100.3 2.6 %copy.28.near2_ref = f32[528,400]{1,0:T(8,128)} copy(f32[528,400]{0,1:T(8,128)} %collective-permute-done.3) | data formatting | bytes 1689600 | tf_op jit(solution)/shard_map/ppermute | solution.py:302
  102.9 2.6 %copy.29.far2_ref = f32[576,400]{1,0:T(8,128)} copy(f32[576,400]{0,1:T(8,128)} %collective-permute-done.8) | data formatting | bytes 1843200 | tf_op jit(solution)/shard_map/ppermute | solution.py:303
  106.9 2.9 %collective-permute-start = (f32[128,1664]{1,0:T(8,128)S(1)}, f32[128,1664]{1,0:T(8,128)S(1)}, u32[]{:S(2)}, u32[]{:S(2)}) collective-permute-start(f32[128,1664]{1,0:T(8,128)S(1)} %bitcast.12), channel_id=1, source_target_pairs={{0,1},{1,0},{2,3},{3,2},{4,5},{5,4},{6,7},{7,6},{8,9},{9,8},{10,11... | collective-permute-start | bytes 2555912 | tf_op jit(solution)/shard_map/ppermute | solution.py:319
  111.0 6.5 %left_kernel.1 = (f32[1024,400]{1,0:T(8,128)S(1)}, bf16[1024,400]{1,0:T(8,128)(2,1)S(1)}, bf16[1024,400]{1,0:T(8,128)(2,1)S(1)}, bf16[2208,400]{1,0:T(8,128)(2,1)S(1)}, bf16[2208,400]{1,0:T(8,128)(2,1)S(1)}) custom-call(f32[512,400]{1,0:T(8,128)S(1)} %copy.20.entity_ref, f32[128,128]{1,0:T(8,128)S(1)} %get-tuple-element.14.mine_ref.lists_mine, ...), custom_call_target="tpu_custom_call" | custom-call | flops 15000000512 | bytes 4000000 | tf_op jit(solution)/shard_map/left_kernel/pallas_call | solution.py:263
  117.5 2.3 %collective-permute-start.1 = (f32[128,128]{1,0:T(8,128)S(1)}, f32[128,128]{1,0:T(8,128)S(1)}, u32[]{:S(2)}, u32[]{:S(2)}) collective-permute-start(f32[128,128]{1,0:T(8,128)S(1)} %slice.4), channel_id=1, source_target_pairs={{0,2},{2,0},{1,3},{3,1},{4,6},{6,4},{5,7},{7,5},{8,10},{10,8},{9,1... | collective-permute-start | bytes 196616 | tf_op jit(solution)/shard_map/ppermute | solution.py:320
  119.8 5.6 %head_kernel.1.head_grad = f32[512,400]{1,0:T(8,128)S(1)} custom-call(f32[128,1664]{1,0:T(8,128)S(1)} %bitcast.14, f32[128,1664]{1,0:T(8,128)S(1)} %collective-permute-done.theirs_ref, f32[128,128]{1,0:T(8,128)S(1)} %get-tuple-element.14.mine_ref.lists_mine, f32[128,128]{1,0:T(8,128)S(1)} %collective-permute-done.2.theirs_ref.lists_theirs, ...), custom_call_target="tpu_custom_call" | custom-call | flops 8000000000 | bytes 4000000 | tf_op jit(solution)/shard_map/head_kernel/pallas_call | solution.py:263
  125.3 3.1 %collective-permute-done.1.given_ref = f32[128,128]{1,0:T(8,128)S(1)} collective-permute-done((f32[128,128]{1,0:T(8,128)S(1)}, f32[128,128]{1,0:T(8,128)S(1)}, u32[]{:S(2)}, u32[]{:S(2)}) %collective-permute-start.1) | collective-permute-done | bytes 65568 | tf_op jit(solution)/shard_map/ppermute | solution.py:320
  128.4 10.9 %tail_kernel.1 = (f32[256,400]{1,0:T(8,128)S(1)}, f32[256,400]{1,0:T(8,128)S(1)}) custom-call(f32[128,1664]{1,0:T(8,128)S(1)} %bitcast.15, f32[128,1664]{1,0:T(8,128)S(1)} %collective-permute-done.theirs_ref, f32[128,128]{1,0:T(8,128)S(1)} %collective-permute-done.1.given_ref, f32[512,400]{1,0:T(8,128)S(1)} %copy.20.entity_ref, ...), custom_call_target="tpu_custom_call" | custom-call | flops 10000000000 | bytes 4000000 | tf_op jit(solution)/shard_map/tail_kernel/pallas_call | solution.py:263
  139.3 2.7 %collective-permute-start.9 = (f32[256,400]{1,0:T(8,128)S(1)}, f32[256,400]{1,0:T(8,128)S(1)}, u32[]{:S(2)}, u32[]{:S(2)}) collective-permute-start(f32[256,400]{1,0:T(8,128)S(1)} %get-tuple-element.21), channel_id=1, source_target_pairs={{0,1},{1,0},{2,3},{3,2},{4,5},{5,4},{6,7},{7,6},{8,9},{9,8},{10,11... | collective-permute-start | bytes 1228808 | tf_op jit(solution)/shard_map/ppermute | solution.py:336
  142.0 1.5 collective-permute-done.9
  143.6 3.4 %collective-permute-start.10 = (f32[256,400]{1,0:T(8,128)S(1)}, f32[256,400]{1,0:T(8,128)S(1)}, u32[]{:S(2)}, u32[]{:S(2)}) collective-permute-start(f32[256,400]{1,0:T(8,128)S(1)} %add.11), channel_id=1, source_target_pairs={{0,2},{2,0},{1,3},{3,1},{4,6},{6,4},{5,7},{7,5},{8,10},{10,8},{9,1... | collective-permute-start | bytes 1228808 | tf_op jit(solution)/shard_map/ppermute | solution.py:337
  147.1 27.0 %collective-permute-done.10 = f32[256,400]{1,0:T(8,128)S(1)} collective-permute-done((f32[256,400]{1,0:T(8,128)S(1)}, f32[256,400]{1,0:T(8,128)S(1)}, u32[]{:S(2)}, u32[]{:S(2)}) %collective-permute-start.10) | collective-permute-done | bytes 409632 | tf_op jit(solution)/shard_map/ppermute | solution.py:337
  174.1 2.4 %collective-permute-start.11 = (f32[256,400]{1,0:T(8,128)S(1)}, f32[256,400]{1,0:T(8,128)S(1)}, u32[]{:S(2)}, u32[]{:S(2)}) collective-permute-start(f32[256,400]{1,0:T(8,128)S(1)} %add.12.mine_ref), channel_id=1, source_target_pairs={{0,1},{1,0},{2,3},{3,2},{4,5},{5,4},{6,7},{7,6},{8,9},{9,8},{10,11... | collective-permute-start | bytes 1228808 | tf_op jit(solution)/shard_map/ppermute | solution.py:338
  176.5 1.5 collective-permute-done.11.theirs_ref
  178.0 1.4 update_kernel.1
  (39 shorter events, 8.8 us)
Async XLA Ops:
  0.6 1.6 copy-start.8
  0.6 1.7 copy-start.2
  0.7 1.6 copy-start.3
  0.7 1.6 copy-start.4
  0.7 1.6 copy-start.5
  4.3 29.3 %all-to-all-start = ((f32[128,1,896]{2,1,0:T(1,128)}), f32[128,1,896]{2,1,0:T(1,128)S(1)}, u32[]{:S(2)}, u32[]{:S(2)}) async-start(f32[128,1,896]{2,1,0:T(1,128)} %copy.22), calls=%async_computation | async-start | bytes 917504 | tf_op jit(solution)/shard_map/all_to_all | solution.py:293
  20.5 13.2 %copy-start.7 = (s32[2,128]{1,0:T(2,128)S(1)}, s32[2,128]{1,0:T(2,128)}, u32[]{:S(2)}) copy-start(s32[2,128]{1,0:T(2,128)} %matching_ref.1) | copy-start | bytes 3076
  20.6 26.6 %collective-permute-start.4 = (f32[144,400]{1,0:T(8,128)S(1)}, f32[144,400]{1,0:T(8,128)}, u32[]{:S(2)}, u32[]{:S(2)}) collective-permute-start(f32[144,400]{1,0:T(8,128)S(1)} %constant_dynamic-slice_fusion), channel_id=1, source_target_pairs={{0,2},{2,0},{1,3},{3,1},{4,6},{6,4},{5,7},{7,5},{8,10},{10,8},{9,1... | collective-permute-start | bytes 691208 | tf_op jit(solution)/shard_map/ppermute | solution.py:297
  36.3 69.3 %all-to-all-start.1 = ((f32[128,1,1664]{2,1,0:T(1,128)}), f32[128,1,1664]{2,1,0:T(1,128)}, u32[]{:S(2)}, u32[]{:S(2)}) async-start(f32[128,1,1664]{2,1,0:T(1,128)} %copy.23), calls=%async_computation.1 | async-start | bytes 1703936 | tf_op jit(solution)/shard_map/all_to_all | solution.py:306
  47.2 14.6 %collective-permute-start.5 = (f32[144,400]{1,0:T(8,128)}, f32[144,400]{1,0:T(8,128)S(1)}, u32[]{:S(2)}, u32[]{:S(2)}) collective-permute-start(f32[144,400]{1,0:T(8,128)} %collective-permute-done.4), channel_id=1, source_target_pairs={{0,128},{4,132},{8,136},{12,140},{16,144},{20,148},{24,152},{28,15... | collective-permute-start | bytes 691208 | tf_op jit(solution)/shard_map/ppermute | solution.py:300
  50.5 16.3 %collective-permute-start.6 = (f32[144,400]{1,0:T(8,128)}, f32[144,400]{1,0:T(8,128)S(1)}, u32[]{:S(2)}, u32[]{:S(2)}) collective-permute-start(f32[144,400]{1,0:T(8,128)} %collective-permute-done.4), channel_id=1, source_target_pairs={{0,256},{4,260},{8,264},{12,268},{16,272},{20,276},{24,280},{28,28... | collective-permute-start | bytes 691208 | tf_op jit(solution)/shard_map/ppermute | solution.py:300
  53.2 21.5 %collective-permute-start.7 = (f32[144,400]{1,0:T(8,128)}, f32[144,400]{1,0:T(8,128)S(1)}, u32[]{:S(2)}, u32[]{:S(2)}) collective-permute-start(f32[144,400]{1,0:T(8,128)} %collective-permute-done.4), channel_id=1, source_target_pairs={{0,384},{4,388},{8,392},{12,396},{16,400},{20,404},{24,408},{28,41... | collective-permute-start | bytes 691208 | tf_op jit(solution)/shard_map/ppermute | solution.py:300
  76.1 26.8 %collective-permute-start.8 = (f32[576,400]{0,1:T(8,128)}, f32[576,400]{0,1:T(8,128)}, u32[]{:S(2)}, u32[]{:S(2)}) collective-permute-start(f32[576,400]{0,1:T(8,128)} %copy.25), channel_id=1, source_target_pairs={{0,1},{1,0},{2,3},{3,2},{4,5},{5,4},{6,7},{7,6},{8,9},{9,8},{10,11... | collective-permute-start | bytes 2764808 | tf_op jit(solution)/shard_map/ppermute | solution.py:303
  78.5 21.8 %collective-permute-start.3 = (f32[528,400]{0,1:T(8,128)}, f32[528,400]{0,1:T(8,128)}, u32[]{:S(2)}, u32[]{:S(2)}) collective-permute-start(f32[528,400]{0,1:T(8,128)} %param.11), channel_id=1, source_target_pairs={{0,1},{1,0},{2,3},{3,2},{4,5},{5,4},{6,7},{7,6},{8,9},{9,8},{10,11... | collective-permute-start | bytes 2534408 | tf_op jit(solution)/shard_map/ppermute | solution.py:302
  80.5 29.3 %collective-permute-start.2 = (f32[128,128]{1,0:T(8,128)S(1)}, f32[128,128]{1,0:T(8,128)S(1)}, u32[]{:S(2)}, u32[]{:S(2)}) collective-permute-start(f32[128,128]{1,0:T(8,128)S(1)} %get-tuple-element.14.mine_ref.lists_mine), channel_id=1, source_target_pairs={{0,2},{2,0},{1,3},{3,1},{4,6},{6,4},{5,7},{7,5},{8,10},{10,8},{9,1... | collective-permute-start | bytes 196616 | tf_op jit(solution)/shard_map/ppermute | solution.py:294
  105.6 4.2 %copy-start = (f32[576,400]{1,0:T(8,128)S(1)}, f32[576,400]{1,0:T(8,128)}, u32[]{:S(2)}) copy-start(f32[576,400]{1,0:T(8,128)} %copy.29.far2_ref) | copy-start | bytes 2764804
  106.9 12.9 %collective-permute-start = (f32[128,1664]{1,0:T(8,128)S(1)}, f32[128,1664]{1,0:T(8,128)S(1)}, u32[]{:S(2)}, u32[]{:S(2)}) collective-permute-start(f32[128,1664]{1,0:T(8,128)S(1)} %bitcast.12), channel_id=1, source_target_pairs={{0,1},{1,0},{2,3},{3,2},{4,5},{5,4},{6,7},{7,6},{8,9},{9,8},{10,11... | collective-permute-start | bytes 2555912 | tf_op jit(solution)/shard_map/ppermute | solution.py:319
  109.8 1.2 copy-start.1
  117.5 10.9 %collective-permute-start.1 = (f32[128,128]{1,0:T(8,128)S(1)}, f32[128,128]{1,0:T(8,128)S(1)}, u32[]{:S(2)}, u32[]{:S(2)}) collective-permute-start(f32[128,128]{1,0:T(8,128)S(1)} %slice.4), channel_id=1, source_target_pairs={{0,2},{2,0},{1,3},{3,1},{4,6},{6,4},{5,7},{7,5},{8,10},{10,8},{9,1... | collective-permute-start | bytes 196616 | tf_op jit(solution)/shard_map/ppermute | solution.py:320
  139.3 4.2 %collective-permute-start.9 = (f32[256,400]{1,0:T(8,128)S(1)}, f32[256,400]{1,0:T(8,128)S(1)}, u32[]{:S(2)}, u32[]{:S(2)}) collective-permute-start(f32[256,400]{1,0:T(8,128)S(1)} %get-tuple-element.21), channel_id=1, source_target_pairs={{0,1},{1,0},{2,3},{3,2},{4,5},{5,4},{6,7},{7,6},{8,9},{9,8},{10,11... | collective-permute-start | bytes 1228808 | tf_op jit(solution)/shard_map/ppermute | solution.py:336
  143.6 34.4 %copy-start.6 = (f32[512]{0:T(512)S(1)}, f32[512]{0:T(512)}, u32[]{:S(2)}) copy-start(f32[512]{0:T(512)} %param.10) | copy-start | bytes 6148
  143.6 30.4 %collective-permute-start.10 = (f32[256,400]{1,0:T(8,128)S(1)}, f32[256,400]{1,0:T(8,128)S(1)}, u32[]{:S(2)}, u32[]{:S(2)}) collective-permute-start(f32[256,400]{1,0:T(8,128)S(1)} %add.11), channel_id=1, source_target_pairs={{0,2},{2,0},{1,3},{3,1},{4,6},{6,4},{5,7},{7,5},{8,10},{10,8},{9,1... | collective-permute-start | bytes 1228808 | tf_op jit(solution)/shard_map/ppermute | solution.py:337
  174.1 3.9 %collective-permute-start.11 = (f32[256,400]{1,0:T(8,128)S(1)}, f32[256,400]{1,0:T(8,128)S(1)}, u32[]{:S(2)}, u32[]{:S(2)}) collective-permute-start(f32[256,400]{1,0:T(8,128)S(1)} %add.12.mine_ref), channel_id=1, source_target_pairs={{0,1},{1,0},{2,3},{3,2},{4,5},{5,4},{6,7},{7,6},{8,9},{9,8},{10,11... | collective-permute-start | bytes 1228808 | tf_op jit(solution)/shard_map/ppermute | solution.py:338

commit v2 on v1

v2 whole, which is shorter than its diff:
```python
import functools

import jax
import jax.numpy as jnp
from jax import lax
from jax.experimental import pallas as pl
from jax.experimental.pallas import tpu as pltpu
from jax.sharding import PartitionSpec as P


LEARN_RATE = 0.1
D = 400
ROWS = 512
HALF = 256
SLOTS = 512
REL_DEV = 528
PIECES = 4
PIECE = 112
TABLE = 4 * REL_DEV
FAR = 640
LIST = 16
LEG1 = 896
LEG2 = 1664
TAIL0 = 1536
F32 = jnp.float32
BF16 = jnp.bfloat16
VMEM_LIMIT = 40 * 1024 * 1024


def split2(x):
    hi = x.astype(BF16)
    return hi, (x - hi.astype(F32)).astype(BF16)


def split3(x):
    hi = x.astype(BF16)
    rest = x - hi.astype(F32)
    mid = rest.astype(BF16)
    return hi, mid, (rest - mid.astype(F32)).astype(BF16)


def dot_nn(a, b):
    return lax.dot_general(a, b, (((1,), (0,)), ((), ())), preferred_element_type=F32)


def dot_nt(a, b):
    return lax.dot_general(a, b, (((1,), (1,)), ((), ())), preferred_element_type=F32)


def iota(shape, dim):
    return lax.broadcasted_iota(jnp.int32, shape, dim)


def place():
    edge = lax.axis_index("edge")
    return edge // 2, lax.rem(edge, 2)


def onehot_cols(lists, first, count, columns):
    blocks = [(lists[:, first + j : first + j + 1] == columns) for j in range(count)]
    return jnp.concatenate([jnp.where(b, 1.0, 0.0) for b in blocks], axis=0).astype(BF16)


def pack_kernel(entity_ref, head_ref, rel_ref, tail_ref, neg_ref, count_ref, out_ref, cols_ref, give_ref, rows_ref):
    zh, core = place()
    rows_ref[...] = jnp.full((128, 128), -1.0, F32)
    lane = iota((1, 128), 1)
    for bucket in range(2):
        at = bucket * LIST
        live = count_ref[bucket, 0, 0]
        for j in range(4):
            span = pl.ds(128 * j, 128)
            head = jnp.where(lane + 128 * j < live, head_ref[bucket, 0, 0:1, span], -1)
            rows_ref[at + j : at + j + 1, :] = head.astype(F32)
            rows_ref[at + 4 + j : at + 5 + j, :] = rel_ref[bucket, 0, 0:1, span].astype(F32)
            rows_ref[at + 8 + j : at + 9 + j, :] = tail_ref[bucket, 0, 0:1, span].astype(F32)
        rows_ref[at + 12 : at + 13, :] = neg_ref[bucket, 0, 0:1, 0:128].astype(F32)
        rows_ref[at + 13 : at + 14, :] = neg_ref[bucket, 0, 0:1, 128:256].astype(F32)
        rows_ref[at + 14 : at + 15, 0:64] = neg_ref[bucket, 0, 0:1, 256:320].astype(F32)
    one, two = rows_ref[0:LIST, :], rows_ref[LIST : 2 * LIST, :]
    keep = jnp.where(zh == 0, one, two)
    give = jnp.where(zh == 0, two, one)
    both = jnp.concatenate([keep, give, rows_ref[2 * LIST :, :]], axis=0).T
    cols_ref[...] = both
    give_ref[...] = give
    half = jnp.where(core == 0, entity_ref[:, 0:HALF], entity_ref[:, HALF:ROWS]).T
    out_ref[:, 0, :] = jnp.concatenate([half[0:128, :], half[128:HALF, :], both[:, 0 : LEG1 - 2 * D]], axis=1)


def route_kernel(x_ref, matching_ref, out_ref):
    zh, _ = place()
    parts = split3(x_ref[:, 0, :])
    rows = iota((128, 128), 0)
    marks = [jnp.where(matching_ref[b : b + 1, :] == rows, 1.0, 0.0) for b in range(2)]
    back_keep = jnp.where(zh == 0, marks[0], marks[1])
    back_give = jnp.where(zh == 0, marks[1], marks[0])
    fore = back_keep.T.astype(BF16)
    back_keep, back_give = back_keep.astype(BF16), back_give.astype(BF16)
    partner = sum(dot_nn(fore, p) for p in reversed(parts))
    source = sum(dot_nn(back_keep, p) for p in reversed(parts))
    given = sum(dot_nn(back_give, p[:, 768:LEG1]) for p in reversed(parts))
    out_ref[:, 0, :] = jnp.concatenate(
        [partner[:, 0 : 2 * D], source[:, 0 : 2 * D + LIST], given[:, 48:64], jnp.zeros((128, LEG2 - 4 * D - 2 * LIST), F32)],
        axis=1,
    )


def table_row(rel, zh, core):
    owner = (rel >= REL_DEV).astype(jnp.int32) + (rel >= 2 * REL_DEV).astype(jnp.int32)
    owner = owner + (rel >= 3 * REL_DEV).astype(jnp.int32)
    off = rel - REL_DEV * owner
    owner_zh = (owner >= 2).astype(jnp.int32)
    other_core = (owner - 2 * owner_zh) != core
    return jnp.where(owner_zh == zh, 0, 2 * REL_DEV) + jnp.where(other_core, REL_DEV, 0) + off


def piece_start(spot):
    return pl.multiple_of(jnp.minimum(PIECE * spot, D - PIECE), 16)


def spot_of_device():
    return lax.axis_index("dom") // 32


def bundle_kernel(relation_ref, give_ref, out_ref):
    out_ref[0:PIECE, :] = relation_ref[pl.ds(piece_start(spot_of_device()), PIECE), :]
    out_ref[PIECE : PIECE + LIST, :] = jnp.zeros((LIST, REL_DEV), F32)
    out_ref[PIECE : PIECE + LIST, 0:128] = give_ref[...]


def table_kernel(relation_ref, piece0_ref, piece1_ref, piece2_ref, piece3_ref, out_ref):
    spot = spot_of_device()
    out_ref[:, 0:REL_DEV] = relation_ref[...]
    out_ref[:, REL_DEV:FAR] = jnp.zeros((D, FAR - REL_DEV), F32)
    for shift, ref in enumerate((piece0_ref, piece1_ref, piece2_ref, piece3_ref)):
        origin = jnp.where(spot < shift, spot - shift + PIECES, spot - shift)
        out_ref[pl.ds(piece_start(origin), PIECE), FAR : FAR + REL_DEV] = ref[0:PIECE, :]


def gather_relations(lists, zh, core, table_hi, table_lo):
    rel_at = table_row(lists[:, 4:8].astype(jnp.int32), zh, core)
    rels = onehot_cols(rel_at, 0, 4, iota((128, TABLE), 1))
    return dot_nn(rels, table_hi[...]) + dot_nn(rels, table_lo[...])


def left_kernel(
    entity_ref, cols_ref, bundle_ref, mine_ref, theirs_ref,
    rel_out, left_hi, left_lo, table_hi, table_lo, entity_hi, entity_lo, cols_out,
):
    zh, core = place()
    for k, (ref, first) in enumerate(((mine_ref, 0), (theirs_ref, 0), (mine_ref, FAR), (theirs_ref, FAR))):
        hi, lo = split2(ref[:, first : first + REL_DEV].T)
        table_hi[k * REL_DEV : (k + 1) * REL_DEV, :] = hi
        table_lo[k * REL_DEV : (k + 1) * REL_DEV, :] = lo
    hi, lo = split2(entity_ref[...].T)
    entity_hi[...] = hi
    entity_lo[...] = lo
    own = iota((128, ROWS), 1).astype(F32)
    theirs = jnp.concatenate([bundle_ref[PIECE : PIECE + LIST, 0:128], jnp.zeros((128 - LIST, 128), F32)], axis=0).T
    cols_out[...] = theirs
    for k, lists in enumerate((cols_ref[:, 0:LIST], theirs[:, 0:LIST])):
        heads = onehot_cols(lists, 0, 4, own)
        head_rows = dot_nn(heads, hi) + dot_nn(heads, lo)
        rel_rows = gather_relations(lists, zh, core, table_hi, table_lo)
        l_hi, l_lo = split2(head_rows * rel_rows)
        span = pl.ds(k * SLOTS, SLOTS)
        rel_out[span, :] = rel_rows
        left_hi[span, :] = l_hi
        left_lo[span, :] = l_lo


def fill_block(hi_ref, lo_ref, mine_ref, theirs_ref, first):
    for k, (ref, lane) in enumerate(((mine_ref, 0), (mine_ref, D), (theirs_ref, 0), (theirs_ref, D))):
        hi, lo = split2(ref[:, 0, first + lane : first + lane + D])
        hi_ref[128 * k : 128 * (k + 1), :] = hi
        lo_ref[128 * k : 128 * (k + 1), :] = lo


def lists_rows(lists):
    return jnp.concatenate([lists, jnp.zeros((128, 128 - LIST), F32)], axis=1).T


def head_kernel(mine_ref, theirs_ref, lists_mine, lists_theirs, rel_ref, left_hi, left_lo, grad_ref, block_hi, block_lo):
    _, core = place()
    fill_block(block_hi, block_lo, mine_ref, theirs_ref, 0)
    numbers = jnp.bitwise_xor(iota((128, ROWS), 1), core * HALF).astype(F32)
    heads_at = iota((ROWS, 128), 0).astype(F32)
    total = None
    for k in range(2):
        lists = (lists_mine, lists_theirs)[k][:, 0:LIST]
        span = pl.ds(k * SLOTS, SLOTS)
        hi, lo = left_hi[span, :], left_lo[span, :]
        b_hi, b_lo = block_hi[...], block_lo[...]
        scores = dot_nt(hi, b_lo) + dot_nt(lo, b_hi) + dot_nt(hi, b_hi)
        tails = jnp.concatenate(
            [jnp.where(lists[:, 8 + j : 9 + j] == numbers, 1.0, 0.0) for j in range(4)], axis=0
        )
        drawn = sum(jnp.where(lists[:, 12 + j : 13 + j] == numbers, 1.0, 0.0) for j in range(3))
        times = jnp.sum(drawn, axis=0, keepdims=True) + tails
        scores = jnp.where(times > 0.0, scores, -3.0e38)
        weights = times * jnp.exp(scores - jnp.max(scores, axis=1, keepdims=True))
        weights = weights / jnp.sum(weights, axis=1, keepdims=True) - tails
        w_hi, w_lo = split2(weights)
        grad_left = dot_nn(w_hi, b_lo) + dot_nn(w_lo, b_hi) + dot_nn(w_hi, b_hi)
        g_hi, g_lo = split2(grad_left * rel_ref[span, :])
        rows = lists_rows(lists)
        marks = jnp.concatenate(
            [jnp.where(rows[j : j + 1, :] == heads_at, 1.0, 0.0) for j in range(4)], axis=1
        ).astype(BF16)
        part = dot_nn(marks, g_lo) + dot_nn(marks, g_hi)
        total = part if total is None else total + part
    grad_ref[...] = total


def first_relations_kernel(mine_ref, table_hi, table_lo, rel_ref):
    zh, core = place()
    rel_ref[...] = gather_relations(mine_ref[:, 0, 4 * D : 4 * D + LIST], zh, core, table_hi, table_lo)


def tail_kernel(
    mine_ref, theirs_ref, given_ref, rel_ref, entity_hi, entity_lo, table_hi, table_lo, head_grad,
    keep_ref, send_ref, block_hi, block_lo,
):
    zh, core = place()
    fill_block(block_hi, block_lo, mine_ref, theirs_ref, 2 * D)
    e_hi, e_lo = entity_hi[...], entity_lo[...]
    numbers = jnp.bitwise_xor(iota((128, ROWS), 1), core * HALF).astype(F32)
    rows_at = iota((ROWS, 128), 0).astype(F32)
    total = head_grad[...]
    for k in range(2):
        if k == 0:
            lists = mine_ref[:, 0, 4 * D : 4 * D + LIST]
            rel_rows = rel_ref[...]
        else:
            lists = given_ref[:, 0, 4 * D + LIST - TAIL0 : 4 * D + 2 * LIST - TAIL0]
            rel_rows = gather_relations(lists, zh, core, table_hi, table_lo)
        heads = onehot_cols(lists, 0, 4, numbers)
        head_rows = dot_nn(heads, block_hi[...]) + dot_nn(heads, block_lo[...])
        l_hi, l_lo = split2(head_rows * rel_rows)
        scores = dot_nt(e_lo, l_hi) + dot_nt(e_hi, l_lo) + dot_nt(e_hi, l_hi)
        rows = lists_rows(lists)
        tails = jnp.concatenate(
            [jnp.where(rows[8 + j : 9 + j, :] == rows_at, 1.0, 0.0) for j in range(4)], axis=1
        )
        drawn = sum(jnp.where(rows[12 + j : 13 + j, :] == rows_at, 1.0, 0.0) for j in range(3))
        times = jnp.sum(drawn, axis=1, keepdims=True) + tails
        scores = jnp.where(times > 0.0, scores, -3.0e38)
        weights = times * jnp.exp(scores - jnp.max(scores, axis=0, keepdims=True))
        weights = weights / jnp.sum(weights, axis=0, keepdims=True) - tails
        w_hi, w_lo = split2(weights)
        total = total + (dot_nn(w_lo, l_hi) + dot_nn(w_hi, l_lo) + dot_nn(w_hi, l_hi))
    first, second = total[0:HALF, :].T, total[HALF:ROWS, :].T
    keep_ref[...] = jnp.where(core == 0, first, second)
    send_ref[...] = jnp.where(core == 0, second, first)


def update_kernel(mine_ref, theirs_ref, entity_ref, state_ref, updated_ref, accum_ref):
    _, core = place()
    mine, theirs = mine_ref[...], theirs_ref[...]
    for j, gradient in enumerate((jnp.where(core == 0, mine, theirs), jnp.where(core == 0, theirs, mine))):
        span = slice(HALF * j, HALF * (j + 1))
        accum = state_ref[:, span] + jnp.sum(gradient * gradient, axis=0, keepdims=True) / float(D)
        accum_ref[:, span] = accum
        updated_ref[:, span] = entity_ref[:, span] - LEARN_RATE * gradient / jnp.sqrt(accum)


def call(kernel, out_shape, args, scratch=(), cost=None, smem=()):
    out_shape = jax.tree.map(lambda s: jax.ShapeDtypeStruct(*s), out_shape, is_leaf=lambda s: isinstance(s, tuple))
    specs = [
        pl.BlockSpec(memory_space=pltpu.SMEM if i in smem else pltpu.VMEM) for i in range(len(args))
    ]
    return pl.pallas_call(
        kernel,
        out_shape=out_shape,
        in_specs=specs,
        out_specs=jax.tree.map(lambda _: pl.BlockSpec(memory_space=pltpu.VMEM), out_shape),
        scratch_shapes=list(scratch),
        compiler_params=pltpu.CompilerParams(vmem_limit_bytes=VMEM_LIMIT),
        cost_estimate=cost,
        name=kernel.__name__,
    )(*args)


def flops(us):
    return pl.CostEstimate(flops=int(us * 1.0e9), bytes_accessed=4_000_000, transcendentals=0)


def shards(entity, state, relation, edge_head, edge_rel, edge_tail, negatives, counts, matching):
    doms = lax.axis_size("dom")
    swap_core = functools.partial(lax.ppermute, axis_name="edge", perm=[(0, 1), (1, 0), (2, 3), (3, 2)])
    swap_zh = functools.partial(lax.ppermute, axis_name="edge", perm=[(0, 2), (2, 0), (1, 3), (3, 1)])
    entity_t, relation_t = entity.T, relation.T

    payload, cols, give = call(
        pack_kernel,
        [((128, 1, LEG1), F32), ((128, 128), F32), ((LIST, 128), F32)],
        (entity_t, edge_head, edge_rel, edge_tail, negatives, counts),
        scratch=[pltpu.VMEM((128, 128), F32)],
        smem=(5,),
    )
    spread = lax.all_to_all(payload, "dom", split_axis=0, concat_axis=0, tiled=True)

    bundle = call(bundle_kernel, ((PIECE + LIST, REL_DEV), F32), (relation_t, give))
    bundle = swap_zh(bundle)
    pieces = [bundle]
    for shift in range(1, PIECES):
        pieces.append(lax.ppermute(bundle, "dom", perm=[(d, (d + 32 * shift) % doms) for d in range(doms)]))
    spread, bundle = lax.optimization_barrier((spread, bundle))

    routed = call(route_kernel, ((128, 1, LEG2), F32), (spread, matching))
    fetched = lax.all_to_all(routed, "dom", split_axis=0, concat_axis=0, tiled=True)
    table = call(table_kernel, ((D, FAR + REL_DEV), F32), (relation_t, *pieces))
    table_other = swap_core(table)
    prepared = call(
        left_kernel,
        [
            ((2 * SLOTS, D), F32),
            ((2 * SLOTS, D), BF16),
            ((2 * SLOTS, D), BF16),
            ((TABLE, D), BF16),
            ((TABLE, D), BF16),
            ((ROWS, D), BF16),
            ((ROWS, D), BF16),
            ((128, 128), F32),
        ],
        (entity_t, cols, bundle, table, table_other),
        cost=flops(8),
    )
    fetched, prepared = lax.optimization_barrier((fetched, prepared))
    rel_rows, left_hi, left_lo, table_hi, table_lo, entity_hi, entity_lo, cols_other = prepared
    fetched_other = swap_core(fetched)
    given = swap_zh(fetched[:, :, TAIL0:LEG2])
    first_rel = call(first_relations_kernel, ((SLOTS, D), F32), (fetched, table_hi, table_lo), cost=flops(3))
    fetched_other, first_rel = lax.optimization_barrier((fetched_other, first_rel))
    block = [pltpu.VMEM((ROWS, D), BF16), pltpu.VMEM((ROWS, D), BF16)]
    head_grad = call(
        head_kernel,
        ((ROWS, D), F32),
        (fetched, fetched_other, cols, cols_other, rel_rows, left_hi, left_lo),
        scratch=block,
        cost=flops(6),
    )
    keep, send = call(
        tail_kernel,
        [((D, HALF), F32), ((D, HALF), F32)],
        (fetched, fetched_other, given, first_rel, entity_hi, entity_lo, table_hi, table_lo, head_grad),
        scratch=block,
        cost=flops(9),
    )
    half = keep + swap_core(send)
    half = half + swap_zh(half)
    other = swap_core(half)
    updated, accum = call(
        update_kernel,
        [((D, ROWS), F32), ((1, ROWS), F32)],
        (half, other, entity_t, state.reshape(1, ROWS)),
    )
    return updated.T, accum.reshape(ROWS)


def solution(mesh):
    return jax.shard_map(
        shards,
        mesh=mesh,
        in_specs=(
            P("dom", None),
            P("dom"),
            P("edge", None),
            P(None, "dom", "edge", None),
            P(None, "dom", "edge", None),
            P(None, "dom", "edge", None),
            P(None, "dom", "edge", None),
            P(None, "dom", "edge"),
            P(),
        ),
        out_specs=(P("dom", None), P("dom")),
        check_vma=False,
    )
```

time: 181 us -> 204 us (1.13)
  the two profiles are of different devices: /device:TPU:131 before, /device:TPU:65 now
where the time goes in v2:
time: 204 us; the launch traced here: 203 us
  waiting for transfers between devices  58.9 us (29%)
  starting transfers between devices  52.5 us (26%)
  Pallas kernels  43.5 us (21%)
  blocking collectives  29.8 us (15%)
  local copies, waits for them, and re-layouts  17.5 us (9%)
    pallas_call x9, Pallas kernels, call(): pl.pallas_call(kernel, out_shape=out_shape, in_specs=specs, out_specs=jax...  43.5 us
    all_to_all x1, blocking collectives, shards(): lax.all_to_all(payload, 'dom', split_axis=0, concat_axis=0, tiled=True)  29.8 us
    ppermute x1, waiting for transfers between devices, shards(): half = half + swap_zh(half)  23.2 us
    unnamed x51, local copies, waits for them, and re-layouts  16.6 us
    ppermute x1, waiting for transfers between devices, shards(): bundle = swap_zh(bundle)  14.4 us
    ppermute x3, starting transfers between devices, shards(): lax.ppermute(bundle, 'dom', perm=[(d, (d + 32 * shift) % doms) for d in r...  10.5 us
    ppermute x3, waiting for transfers between devices, shards(): lax.ppermute(bundle, 'dom', perm=[(d, (d + 32 * shift) % doms) for d in r...  10.1 us
    ppermute x1, starting transfers between devices, shards(): bundle = swap_zh(bundle)  9.74 us
  transfers between devices with their start and end apart: 11, of which 8 were waited for; matrix products, arithmetic and copies ran while one was open for 0% of the time, Pallas kernels for 13%

profile of v2, /device:TPU:65, one launch (start us, length us, event | category | flops | bytes accessed | tf_op | source)
XLA Modules:
  0.0 203.3 jit_solution(14322275100033201829)
XLA Ops:
  1.4 1.1 copy-done.2
  6.3 1.2 copy-done
  7.5 9.7 %collective-permute-start = (f32[128,528]{1,0:T(8,128)S(1)}, f32[128,528]{1,0:T(8,128)S(1)}, u32[]{:S(2)}, u32[]{:S(2)}) collective-permute-start(f32[128,528]{1,0:T(8,128)S(1)} %bundle_kernel.1), channel_id=1, source_target_pairs={{0,2},{2,0},{1,3},{3,1},{4,6},{6,4},{5,7},{7,5},{8,10},{10,8},{9,1... | collective-permute-start | bytes 811016 | tf_op jit(solution)/shard_map/ppermute | solution.py:304
  17.2 14.4 %collective-permute-done.piece0_ref.bundle_ref = f32[128,528]{1,0:T(8,128)S(1)} collective-permute-done((f32[128,528]{1,0:T(8,128)S(1)}, f32[128,528]{1,0:T(8,128)S(1)}, u32[]{:S(2)}, u32[]{:S(2)}) %collective-permute-start) | collective-permute-done | bytes 270368 | tf_op jit(solution)/shard_map/ppermute | solution.py:304
  31.7 3.1 %collective-permute-start.1 = (f32[128,528]{1,0:T(8,128)S(1)}, f32[128,528]{1,0:T(8,128)S(1)}, u32[]{:S(2)}, u32[]{:S(2)}) collective-permute-start(f32[128,528]{1,0:T(8,128)S(1)} %collective-permute-done.piece0_ref.bundle_ref), channel_id=1, source_target_pairs={{0,128},{4,132},{8,136},{12,140},{16,144},{20,148},{24,152},{28,15... | collective-permute-start | bytes 811016 | tf_op jit(solution)/shard_map/ppermute | solution.py:307
  34.8 4.4 %collective-permute-start.2 = (f32[128,528]{1,0:T(8,128)S(1)}, f32[128,528]{1,0:T(8,128)S(1)}, u32[]{:S(2)}, u32[]{:S(2)}) collective-permute-start(f32[128,528]{1,0:T(8,128)S(1)} %collective-permute-done.piece0_ref.bundle_ref), channel_id=1, source_target_pairs={{0,256},{4,260},{8,264},{12,268},{16,272},{20,276},{24,280},{28,28... | collective-permute-start | bytes 811016 | tf_op jit(solution)/shard_map/ppermute | solution.py:307
  39.2 3.1 %collective-permute-start.3 = (f32[128,528]{1,0:T(8,128)S(1)}, f32[128,528]{1,0:T(8,128)S(1)}, u32[]{:S(2)}, u32[]{:S(2)}) collective-permute-start(f32[128,528]{1,0:T(8,128)S(1)} %collective-permute-done.piece0_ref.bundle_ref), channel_id=1, source_target_pairs={{0,384},{4,388},{8,392},{12,396},{16,400},{20,404},{24,408},{28,41... | collective-permute-start | bytes 811016 | tf_op jit(solution)/shard_map/ppermute | solution.py:307
  42.7 8.0 %collective-permute-done.2.piece2_ref = f32[128,528]{1,0:T(8,128)S(1)} collective-permute-done((f32[128,528]{1,0:T(8,128)S(1)}, f32[128,528]{1,0:T(8,128)S(1)}, u32[]{:S(2)}, u32[]{:S(2)}) %collective-permute-start.2) | collective-permute-done | bytes 270368 | tf_op jit(solution)/shard_map/ppermute | solution.py:307
  50.7 1.7 collective-permute-done.3.piece3_ref
  52.4 1.2 copy-done.1
  53.8 4.1 %collective-permute-start.4 = (f32[400,1168]{1,0:T(8,128)S(1)}, f32[400,1168]{1,0:T(8,128)}, u32[]{:S(2)}, u32[]{:S(2)}) collective-permute-start(f32[400,1168]{1,0:T(8,128)S(1)} %table_kernel.1.mine_ref), channel_id=1, source_target_pairs={{0,1},{1,0},{2,3},{3,2},{4,5},{5,4},{6,7},{7,6},{8,9},{9,8},{10,11... | collective-permute-start | bytes 5606408 | tf_op jit(solution)/shard_map/ppermute | solution.py:313
  57.9 29.8 %all_to_all.10.x_ref = f32[128,1,896]{2,1,0:T(1,128)S(1)} all-to-all(f32[128,1,896]{2,1,0:T(1,128)S(1)} %get-tuple-element.30), channel_id=1, replica_groups=mesh['dom'=128,'edge'=4] {'dom'}, dimensions={0} | all-to-all | bytes 917504 | tf_op jit(solution)/shard_map/all_to_all | solution.py:301
  87.7 3.9 %route_kernel.1 = f32[128,1,1664]{2,1,0:T(1,128)} custom-call(f32[128,1,896]{2,1,0:T(1,128)S(1)} %all_to_all.10.x_ref, s32[2,128]{1,0:T(2,128)S(1)} %copy-done.9), custom_call_target="tpu_custom_call" | custom-call | tf_op jit(solution)/shard_map/route_kernel/pallas_call | solution.py:272
  91.5 8.3 %all-to-all-start.1 = ((f32[128,1,1664]{2,1,0:T(1,128)}), f32[128,1,1664]{2,1,0:T(1,128)}, u32[]{:S(2)}, u32[]{:S(2)}) async-start(f32[128,1,1664]{2,1,0:T(1,128)} %route_kernel.1), calls=%async_computation.1 | async-start | bytes 1703936 | tf_op jit(solution)/shard_map/all_to_all | solution.py:311
  99.8 8.2 %left_kernel.1 = (f32[1024,400]{1,0:T(8,128)S(1)}, bf16[1024,400]{1,0:T(8,128)(2,1)S(1)}, bf16[1024,400]{1,0:T(8,128)(2,1)S(1)}, bf16[2112,400]{1,0:T(8,128)(2,1...) custom-call(f32[400,512]{1,0:T(8,128)S(1)} %bitcast.8, ...), custom_call_target="tpu_custom_call" | custom-call | flops 8000000000 | bytes 4000000 | tf_op jit(solution)/shard_map/left_kernel/pallas_call | solution.py:272
  108.1 1.3 copy-done.10
  109.4 1.4 copy-done.15
  114.4 8.4 %all-to-all-done.1.mine_ref = f32[128,1,1664]{2,1,0:T(1,128)} async-done(((f32[128,1,1664]{2,1,0:T(1,128)}), f32[128,1,1664]{2,1,0:T(1,128)}, u32[]{:S(2)}, u32[]{:S(2)}) %all-to-all-start.1) | async-done | bytes 852000 | tf_op jit(solution)/shard_map/all_to_all | solution.py:311
  122.8 5.2 %collective-permute-start.5 = (f32[128,1,1664]{2,1,0:T(1,128)}, f32[128,1,1664]{2,1,0:T(1,128)S(1)}, u32[]{:S(2)}, u32[]{:S(2)}) collective-permute-start(f32[128,1,1664]{2,1,0:T(1,128)} %all-to-all-done.1.mine_ref), channel_id=1, source_target_pairs={{0,1},{1,0},{2,3},{3,2},{4,5},{5,4},{6,7},{7,6},{8,9},{9,8},{10,11... | collective-permute-start | bytes 2555912 | tf_op jit(solution)/shard_map/ppermute | solution.py:331
  128.9 7.3 %collective-permute-start.6 = (f32[128,1,128]{2,1,0:T(1,128)S(1)}, f32[128,1,128]{2,1,0:T(1,128)S(1)}, u32[]{:S(2)}, u32[]{:S(2)}) collective-permute-start(f32[128,1,128]{2,1,0:T(1,128)S(1)} %slice.3), channel_id=1, source_target_pairs={{0,2},{2,0},{1,3},{3,1},{4,6},{6,4},{5,7},{7,5},{8,10},{10,8},{9,1... | collective-permute-start | bytes 196616 | tf_op jit(solution)/shard_map/ppermute | solution.py:332
  136.2 1.6 copy-done.11
  137.8 1.6 copy-done.13
  139.4 5.2 %first_relations_kernel.1.rel_ref = f32[512,400]{1,0:T(8,128)S(1)} custom-call(f32[128,1,1664]{2,1,0:T(1,128)} %all-to-all-done.1.mine_ref, bf16[2112,400]{1,0:T(8,128)(2,1)S(1)} %copy-done.11, bf16[2112,400]{1,0:T(8,128)(2,1)S(1)} %copy-done.13), custom_call_target="tpu_custom_call" | custom-call | flops 3000000000 | bytes 4000000 | tf_op jit(solution)/shard_map/first_relations_kernel/pallas_call | solution.py:272
  144.7 9.6 %head_kernel.1.head_grad = f32[512,400]{1,0:T(8,128)S(1)} custom-call(f32[128,1,1664]{2,1,0:T(1,128)} %all-to-all-done.1.mine_ref, f32[128,1,1664]{2,1,0:T(1,128)S(1)} %collective-permute-done.5.theirs_ref, f32[128,128]{1,0:T(8,128)S(1)} %get-tuple-element.33.cols_ref.lists_mine, f32[128,128]{1,0:T(8,128)S(1)} %get-tuple-element.50.lists_theirs, ...), custom_call_target="tpu_custom_call" | custom-call | flops 6000000000 | bytes 4000000 | tf_op jit(solution)/shard_map/head_kernel/pallas_call | solution.py:272
  154.4 14.3 %tail_kernel.1 = (f32[400,256]{1,0:T(8,128)S(1)}, f32[400,256]{1,0:T(8,128)S(1)}) custom-call(f32[128,1,1664]{2,1,0:T(1,128)} %all-to-all-done.1.mine_ref, f32[128,1,1664]{2,1,0:T(1,128)S(1)} %collective-permute-done.5.theirs_ref, f32[128,1,128]{2,1,0:T(1,128)S(1)} %collective-permute-done.6.given_ref, f32[512,400]{1,0:T(8,128)S(1)} %first_relations_kernel.1.rel_ref, ...), custom_call_target="tpu_custom_call" | custom-call | flops 8999999488 | bytes 4000000 | tf_op jit(solution)/shard_map/tail_kernel/pallas_call | solution.py:272
  168.7 2.2 %collective-permute-start.7 = (f32[400,256]{1,0:T(8,128)S(1)}, f32[400,256]{1,0:T(8,128)S(1)}, u32[]{:S(2)}, u32[]{:S(2)}) collective-permute-start(f32[400,256]{1,0:T(8,128)S(1)} %get-tuple-element.55), channel_id=1, source_target_pairs={{0,1},{1,0},{2,3},{3,2},{4,5},{5,4},{6,7},{7,6},{8,9},{9,8},{10,11... | collective-permute-start | bytes 1228808 | tf_op jit(solution)/shard_map/ppermute | solution.py:350
  170.9 1.4 collective-permute-done.7
  172.4 2.1 %collective-permute-start.8 = (f32[400,256]{1,0:T(8,128)S(1)}, f32[400,256]{1,0:T(8,128)S(1)}, u32[]{:S(2)}, u32[]{:S(2)}) collective-permute-start(f32[400,256]{1,0:T(8,128)S(1)} %add.6), channel_id=1, source_target_pairs={{0,2},{2,0},{1,3},{3,1},{4,6},{6,4},{5,7},{7,5},{8,10},{10,8},{9,1... | collective-permute-start | bytes 1228808 | tf_op jit(solution)/shard_map/ppermute | solution.py:351
  174.5 23.2 %collective-permute-done.8 = f32[400,256]{1,0:T(8,128)S(1)} collective-permute-done((f32[400,256]{1,0:T(8,128)S(1)}, f32[400,256]{1,0:T(8,128)S(1)}, u32[]{:S(2)}, u32[]{:S(2)}) %collective-permute-start.8) | collective-permute-done | bytes 409632 | tf_op jit(solution)/shard_map/ppermute | solution.py:351
  197.8 3.0 %collective-permute-start.9 = (f32[400,256]{1,0:T(8,128)S(1)}, f32[400,256]{1,0:T(8,128)S(1)}, u32[]{:S(2)}, u32[]{:S(2)}) collective-permute-start(f32[400,256]{1,0:T(8,128)S(1)} %add.7.mine_ref), channel_id=1, source_target_pairs={{0,1},{1,0},{2,3},{3,2},{4,5},{5,4},{6,7},{7,6},{8,9},{9,8},{10,11... | collective-permute-start | bytes 1228808 | tf_op jit(solution)/shard_map/ppermute | solution.py:352
  200.8 1.4 collective-permute-done.9.theirs_ref
  202.2 1.2 update_kernel.1
  (54 shorter events, 9.7 us)
Async XLA Ops:
  1.4 1.1 copy-start.2
  6.2 1.2 copy-start
  7.5 80.2 %copy-start.9 = (s32[2,128]{1,0:T(2,128)S(1)}, s32[2,128]{1,0:T(2,128)}, u32[]{:S(2)}) copy-start(s32[2,128]{1,0:T(2,128)} %matching_ref.1) | copy-start | bytes 3076
  7.5 24.2 %collective-permute-start = (f32[128,528]{1,0:T(8,128)S(1)}, f32[128,528]{1,0:T(8,128)S(1)}, u32[]{:S(2)}, u32[]{:S(2)}) collective-permute-start(f32[128,528]{1,0:T(8,128)S(1)} %bundle_kernel.1), channel_id=1, source_target_pairs={{0,2},{2,0},{1,3},{3,1},{4,6},{6,4},{5,7},{7,5},{8,10},{10,8},{9,1... | collective-permute-start | bytes 811016 | tf_op jit(solution)/shard_map/ppermute | solution.py:304
  31.7 11.0 %collective-permute-start.1 = (f32[128,528]{1,0:T(8,128)S(1)}, f32[128,528]{1,0:T(8,128)S(1)}, u32[]{:S(2)}, u32[]{:S(2)}) collective-permute-start(f32[128,528]{1,0:T(8,128)S(1)} %collective-permute-done.piece0_ref.bundle_ref), channel_id=1, source_target_pairs={{0,128},{4,132},{8,136},{12,140},{16,144},{20,148},{24,152},{28,15... | collective-permute-start | bytes 811016 | tf_op jit(solution)/shard_map/ppermute | solution.py:307
  34.8 15.9 %collective-permute-start.2 = (f32[128,528]{1,0:T(8,128)S(1)}, f32[128,528]{1,0:T(8,128)S(1)}, u32[]{:S(2)}, u32[]{:S(2)}) collective-permute-start(f32[128,528]{1,0:T(8,128)S(1)} %collective-permute-done.piece0_ref.bundle_ref), channel_id=1, source_target_pairs={{0,256},{4,260},{8,264},{12,268},{16,272},{20,276},{24,280},{28,28... | collective-permute-start | bytes 811016 | tf_op jit(solution)/shard_map/ppermute | solution.py:307
  39.2 13.2 %collective-permute-start.3 = (f32[128,528]{1,0:T(8,128)S(1)}, f32[128,528]{1,0:T(8,128)S(1)}, u32[]{:S(2)}, u32[]{:S(2)}) collective-permute-start(f32[128,528]{1,0:T(8,128)S(1)} %collective-permute-done.piece0_ref.bundle_ref), channel_id=1, source_target_pairs={{0,384},{4,388},{8,392},{12,396},{16,400},{20,404},{24,408},{28,41... | collective-permute-start | bytes 811016 | tf_op jit(solution)/shard_map/ppermute | solution.py:307
  52.4 1.2 copy-start.1
  53.7 46.1 %copy-start.3 = (f32[512,400]{0,1:T(8,128)S(1)}, f32[512,400]{0,1:T(8,128)}, u32[]{:S(2)}) copy-start(f32[512,400]{0,1:T(8,128)} %param.9) | copy-start | bytes 2457604
  53.8 46.1 %collective-permute-start.4 = (f32[400,1168]{1,0:T(8,128)S(1)}, f32[400,1168]{1,0:T(8,128)}, u32[]{:S(2)}, u32[]{:S(2)}) collective-permute-start(f32[400,1168]{1,0:T(8,128)S(1)} %table_kernel.1.mine_ref), channel_id=1, source_target_pairs={{0,1},{1,0},{2,3},{3,2},{4,5},{5,4},{6,7},{7,6},{8,9},{9,8},{10,11... | collective-permute-start | bytes 5606408 | tf_op jit(solution)/shard_map/ppermute | solution.py:313
  91.5 31.2 %all-to-all-start.1 = ((f32[128,1,1664]{2,1,0:T(1,128)}), f32[128,1,1664]{2,1,0:T(1,128)}, u32[]{:S(2)}, u32[]{:S(2)}) async-start(f32[128,1,1664]{2,1,0:T(1,128)} %route_kernel.1), calls=%async_computation.1 | async-start | bytes 1703936 | tf_op jit(solution)/shard_map/all_to_all | solution.py:311
  108.0 1.4 copy-start.10
  109.4 1.4 copy-start.15
  110.8 1.0 copy-start.17
  111.7 1.0 copy-start.19
  112.8 0.8 copy-start.21
  113.6 0.8 copy-start.23
  122.8 21.9 %collective-permute-start.5 = (f32[128,1,1664]{2,1,0:T(1,128)}, f32[128,1,1664]{2,1,0:T(1,128)S(1)}, u32[]{:S(2)}, u32[]{:S(2)}) collective-permute-start(f32[128,1,1664]{2,1,0:T(1,128)} %all-to-all-done.1.mine_ref), channel_id=1, source_target_pairs={{0,1},{1,0},{2,3},{3,2},{4,5},{5,4},{6,7},{7,6},{8,9},{9,8},{10,11... | collective-permute-start | bytes 2555912 | tf_op jit(solution)/shard_map/ppermute | solution.py:331
  128.9 25.4 %collective-permute-start.6 = (f32[128,1,128]{2,1,0:T(1,128)S(1)}, f32[128,1,128]{2,1,0:T(1,128)S(1)}, u32[]{:S(2)}, u32[]{:S(2)}) collective-permute-start(f32[128,1,128]{2,1,0:T(1,128)S(1)} %slice.3), channel_id=1, source_target_pairs={{0,2},{2,0},{1,3},{3,1},{4,6},{6,4},{5,7},{7,5},{8,10},{10,8},{9,1... | collective-permute-start | bytes 196616 | tf_op jit(solution)/shard_map/ppermute | solution.py:332
  136.2 1.6 copy-start.11
  137.8 1.6 copy-start.13
  139.4 5.2 %copy-start.16 = (f32[1024,400]{1,0:T(8,128)S(1)}, f32[1024,400]{1,0:T(8,128)}, u32[]{:S(2)}) copy-start(f32[1024,400]{1,0:T(8,128)} %copy-done.15) | copy-start | bytes 4915204
  139.4 5.2 %copy-start.18 = (bf16[1024,400]{1,0:T(8,128)(2,1)S(1)}, bf16[1024,400]{1,0:T(8,128)(2,1)}, u32[]{:S(2)}) copy-start(bf16[1024,400]{1,0:T(8,128)(2,1)} %copy-done.17) | copy-start | bytes 2457604
  139.4 5.2 %copy-start.20 = (bf16[1024,400]{1,0:T(8,128)(2,1)S(1)}, bf16[1024,400]{1,0:T(8,128)(2,1)}, u32[]{:S(2)}) copy-start(bf16[1024,400]{1,0:T(8,128)(2,1)} %copy-done.19) | copy-start | bytes 2457604
  144.6 9.7 %copy-start.12 = (bf16[2112,400]{1,0:T(8,128)(2,1)S(1)}, bf16[2112,400]{1,0:T(8,128)(2,1)}, u32[]{:S(2)}) copy-start(bf16[2112,400]{1,0:T(8,128)(2,1)} %copy-done.10) | copy-start | bytes 5068804
  144.6 9.7 %copy-start.14 = (bf16[2112,400]{1,0:T(8,128)(2,1)S(1)}, bf16[2112,400]{1,0:T(8,128)(2,1)}, u32[]{:S(2)}) copy-start(bf16[2112,400]{1,0:T(8,128)(2,1)} %get-tuple-element.45.table_lo) | copy-start | bytes 5068804
  144.6 9.7 %copy-start.22 = (bf16[512,400]{1,0:T(8,128)(2,1)S(1)}, bf16[512,400]{1,0:T(8,128)(2,1)}, u32[]{:S(2)}) copy-start(bf16[512,400]{1,0:T(8,128)(2,1)} %copy-done.21) | copy-start | bytes 1228804
  144.6 9.7 %copy-start.24 = (bf16[512,400]{1,0:T(8,128)(2,1)S(1)}, bf16[512,400]{1,0:T(8,128)(2,1)}, u32[]{:S(2)}) copy-start(bf16[512,400]{1,0:T(8,128)(2,1)} %copy-done.23) | copy-start | bytes 1228804
  168.7 33.5 %copy-start.8 = (f32[512]{0:T(512)S(1)}, f32[512]{0:T(512)}, u32[]{:S(2)}) copy-start(f32[512]{0:T(512)} %param.10) | copy-start | bytes 6148
  168.7 3.6 %collective-permute-start.7 = (f32[400,256]{1,0:T(8,128)S(1)}, f32[400,256]{1,0:T(8,128)S(1)}, u32[]{:S(2)}, u32[]{:S(2)}) collective-permute-start(f32[400,256]{1,0:T(8,128)S(1)} %get-tuple-element.55), channel_id=1, source_target_pairs={{0,1},{1,0},{2,3},{3,2},{4,5},{5,4},{6,7},{7,6},{8,9},{9,8},{10,11... | collective-permute-start | bytes 1228808 | tf_op jit(solution)/shard_map/ppermute | solution.py:350
  172.4 25.3 %collective-permute-start.8 = (f32[400,256]{1,0:T(8,128)S(1)}, f32[400,256]{1,0:T(8,128)S(1)}, u32[]{:S(2)}, u32[]{:S(2)}) collective-permute-start(f32[400,256]{1,0:T(8,128)S(1)} %add.6), channel_id=1, source_target_pairs={{0,2},{2,0},{1,3},{3,1},{4,6},{6,4},{5,7},{7,5},{8,10},{10,8},{9,1... | collective-permute-start | bytes 1228808 | tf_op jit(solution)/shard_map/ppermute | solution.py:351
  197.8 4.4 %collective-permute-start.9 = (f32[400,256]{1,0:T(8,128)S(1)}, f32[400,256]{1,0:T(8,128)S(1)}, u32[]{:S(2)}, u32[]{:S(2)}) collective-permute-start(f32[400,256]{1,0:T(8,128)S(1)} %add.7.mine_ref), channel_id=1, source_target_pairs={{0,1},{1,0},{2,3},{3,2},{4,5},{5,4},{6,7},{7,6},{8,9},{9,8},{10,11... | collective-permute-start | bytes 1228808 | tf_op jit(solution)/shard_map/ppermute | solution.py:352
  (4 other events, 2.7 us)

commit v3 on v2

--- a/solution.py
+++ b/solution.py
@@ -13,18 +13,20 @@
 ROWS = 512
 HALF = 256
 SLOTS = 512
+NEGS = 320
 REL_DEV = 528
 PIECES = 4
 PIECE = 112
+REL_LANES = 640
 TABLE = 4 * REL_DEV
-FAR = 640
 LIST = 16
-LEG1 = 896
-LEG2 = 1664
-TAIL0 = 1536
+CHUNK1 = 7
+CHUNK2 = 13
+GIVEN_CHUNK = 12
+FIRST = 4 * D - 128 * GIVEN_CHUNK
 F32 = jnp.float32
 BF16 = jnp.bfloat16
-VMEM_LIMIT = 40 * 1024 * 1024
+MIB = 1024 * 1024
 
 
 def split2(x):
@@ -52,8 +54,16 @@
 
 
 def place():
-    edge = lax.axis_index("edge")
-    return edge // 2, lax.rem(edge, 2)
+    return lax.axis_index("zh"), lax.axis_index("core")
+
+
+def read_rows(ref, chunks):
+    return jnp.concatenate([ref[pl.ds(k, 128, stride=chunks), :] for k in range(chunks)], axis=1)
+
+
+def write_rows(ref, value, chunks):
+    for k in range(chunks):
+        ref[pl.ds(k, 128, stride=chunks), :] = value[:, 128 * k : 128 * (k + 1)]
 
 
 def onehot_cols(lists, first, count, columns):
@@ -61,13 +71,25 @@
     return jnp.concatenate([jnp.where(b, 1.0, 0.0) for b in blocks], axis=0).astype(BF16)
 
 
-def pack_kernel(entity_ref, head_ref, rel_ref, tail_ref, neg_ref, count_ref, out_ref, cols_ref, give_ref, rows_ref):
+def pack_kernel(
+    entity_hbm, head_hbm, rel_hbm, tail_hbm, neg_hbm, count_hbm, out_ref, cols_ref, give_ref,
+    rows_ref, entity_ref, head_ref, rel_ref, tail_ref, neg_ref, count_ref, sems,
+):
     zh, core = place()
+    pairs = (
+        (head_hbm, head_ref), (rel_hbm, rel_ref), (tail_hbm, tail_ref), (neg_hbm, neg_ref), (count_hbm, count_ref),
+        (entity_hbm, entity_ref),
+    )
+    copies = [pltpu.make_async_copy(a, b, sems.at[i]) for i, (a, b) in enumerate(pairs)]
+    for copy in copies:
+        copy.start()
     rows_ref[...] = jnp.full((128, 128), -1.0, F32)
     lane = iota((1, 128), 1)
+    for copy in copies[:-1]:
+        copy.wait()
     for bucket in range(2):
         at = bucket * LIST
-        live = count_ref[bucket, 0, 0]
+        live = count_ref[bucket]
         for j in range(4):
             span = pl.ds(128 * j, 128)
             head = jnp.where(lane + 128 * j < live, head_ref[bucket, 0, 0:1, span], -1)
@@ -83,13 +105,15 @@
     both = jnp.concatenate([keep, give, rows_ref[2 * LIST :, :]], axis=0).T
     cols_ref[...] = both
     give_ref[...] = give
+    copies[-1].wait()
     half = jnp.where(core == 0, entity_ref[:, 0:HALF], entity_ref[:, HALF:ROWS]).T
-    out_ref[:, 0, :] = jnp.concatenate([half[0:128, :], half[128:HALF, :], both[:, 0 : LEG1 - 2 * D]], axis=1)
+    payload = jnp.concatenate([half[0:128, :], half[128:HALF, :], both[:, 0 : 128 * CHUNK1 - 2 * D]], axis=1)
+    write_rows(out_ref, payload, CHUNK1)
 
 
 def route_kernel(x_ref, matching_ref, out_ref):
     zh, _ = place()
-    parts = split3(x_ref[:, 0, :])
+    parts = split3(read_rows(x_ref, CHUNK1))
     rows = iota((128, 128), 0)
     marks = [jnp.where(matching_ref[b : b + 1, :] == rows, 1.0, 0.0) for b in range(2)]
     back_keep = jnp.where(zh == 0, marks[0], marks[1])
@@ -98,11 +122,10 @@
     back_keep, back_give = back_keep.astype(BF16), back_give.astype(BF16)
     partner = sum(dot_nn(fore, p) for p in reversed(parts))
     source = sum(dot_nn(back_keep, p) for p in reversed(parts))
-    given = sum(dot_nn(back_give, p[:, 768:LEG1]) for p in reversed(parts))
-    out_ref[:, 0, :] = jnp.concatenate(
-        [partner[:, 0 : 2 * D], source[:, 0 : 2 * D + LIST], given[:, 48:64], jnp.zeros((128, LEG2 - 4 * D - 2 * LIST), F32)],
-        axis=1,
-    )
+    given = sum(dot_nn(back_give, p[:, 768 : 128 * CHUNK1]) for p in reversed(parts))
+    fill = jnp.zeros((128, 128 * CHUNK2 - 4 * D - 2 * LIST), F32)
+    routed = jnp.concatenate([partner[:, 0 : 2 * D], source[:, 0 : 2 * D + LIST], given[:, 48:64], fill], axis=1)
+    write_rows(out_ref, routed, CHUNK2)
 
 
 def table_row(rel, zh, core):
@@ -115,26 +138,16 @@
 
 
 def piece_start(spot):
-    return pl.multiple_of(jnp.minimum(PIECE * spot, D - PIECE), 16)
-
-
-def spot_of_device():
-    return lax.axis_index("dom") // 32
+    return min(PIECE * spot, D - PIECE)
 
 
 def bundle_kernel(relation_ref, give_ref, out_ref):
-    out_ref[0:PIECE, :] = relation_ref[pl.ds(piece_start(spot_of_device()), PIECE), :]
-    out_ref[PIECE : PIECE + LIST, :] = jnp.zeros((LIST, REL_DEV), F32)
+    spot = lax.axis_index("x")
+    start = pl.multiple_of(jnp.minimum(PIECE * spot, D - PIECE), 16)
+    out_ref[:, 512:REL_LANES] = jnp.zeros((PIECE + LIST, REL_LANES - 512), F32)
+    out_ref[0:PIECE, 0:REL_DEV] = relation_ref[pl.ds(start, PIECE), :]
+    out_ref[PIECE : PIECE + LIST, 128:512] = jnp.zeros((LIST, 384), F32)
     out_ref[PIECE : PIECE + LIST, 0:128] = give_ref[...]
-
-
-def table_kernel(relation_ref, piece0_ref, piece1_ref, piece2_ref, piece3_ref, out_ref):
-    spot = spot_of_device()
-    out_ref[:, 0:REL_DEV] = relation_ref[...]
-    out_ref[:, REL_DEV:FAR] = jnp.zeros((D, FAR - REL_DEV), F32)
-    for shift, ref in enumerate((piece0_ref, piece1_ref, piece2_ref, piece3_ref)):
-        origin = jnp.where(spot < shift, spot - shift + PIECES, spot - shift)
-        out_ref[pl.ds(piece_start(origin), PIECE), FAR : FAR + REL_DEV] = ref[0:PIECE, :]
 
 
 def gather_relations(lists, zh, core, table_hi, table_lo):
@@ -144,12 +157,16 @@
 
 
 def left_kernel(
-    entity_ref, cols_ref, bundle_ref, mine_ref, theirs_ref,
-    rel_out, left_hi, left_lo, table_hi, table_lo, entity_hi, entity_lo, cols_out,
+    entity_ref, cols_ref, bundle_ref, near_ref, near2_ref, far_ref,
+    rel_out, left_hi, left_lo, table_hi, table_lo, entity_hi, entity_lo, cols_out, far_table,
 ):
     zh, core = place()
-    for k, (ref, first) in enumerate(((mine_ref, 0), (theirs_ref, 0), (mine_ref, FAR), (theirs_ref, FAR))):
-        hi, lo = split2(ref[:, first : first + REL_DEV].T)
+    for c in range(2):
+        for spot in range(PIECES):
+            far_table[c, piece_start(spot) : piece_start(spot) + PIECE, :] = far_ref[2 * spot + c, :, 0:REL_DEV]
+    parts = (near_ref[...], near2_ref[...], far_table[core], far_table[1 - core])
+    for k, part in enumerate(parts):
+        hi, lo = split2(part.T)
         table_hi[k * REL_DEV : (k + 1) * REL_DEV, :] = hi
         table_lo[k * REL_DEV : (k + 1) * REL_DEV, :] = lo
     hi, lo = split2(entity_ref[...].T)
@@ -169,9 +186,9 @@
         left_lo[span, :] = l_lo
 
 
-def fill_block(hi_ref, lo_ref, mine_ref, theirs_ref, first):
-    for k, (ref, lane) in enumerate(((mine_ref, 0), (mine_ref, D), (theirs_ref, 0), (theirs_ref, D))):
-        hi, lo = split2(ref[:, 0, first + lane : first + lane + D])
+def fill_block(hi_ref, lo_ref, mine, theirs, first):
+    for k, (rows, lane) in enumerate(((mine, 0), (mine, D), (theirs, 0), (theirs, D))):
+        hi, lo = split2(rows[:, first + lane : first + lane + D])
         hi_ref[128 * k : 128 * (k + 1), :] = hi
         lo_ref[128 * k : 128 * (k + 1), :] = lo
 
@@ -182,7 +199,7 @@
 
 def head_kernel(mine_ref, theirs_ref, lists_mine, lists_theirs, rel_ref, left_hi, left_lo, grad_ref, block_hi, block_lo):
     _, core = place()
-    fill_block(block_hi, block_lo, mine_ref, theirs_ref, 0)
+    fill_block(block_hi, block_lo, read_rows(mine_ref, CHUNK2), read_rows(theirs_ref, CHUNK2), 0)
     numbers = jnp.bitwise_xor(iota((128, ROWS), 1), core * HALF).astype(F32)
     heads_at = iota((ROWS, 128), 0).astype(F32)
     total = None
@@ -214,7 +231,8 @@
 
 def first_relations_kernel(mine_ref, table_hi, table_lo, rel_ref):
     zh, core = place()
-    rel_ref[...] = gather_relations(mine_ref[:, 0, 4 * D : 4 * D + LIST], zh, core, table_hi, table_lo)
+    chunk = mine_ref[pl.ds(GIVEN_CHUNK, 128, stride=CHUNK2), :]
+    rel_ref[...] = gather_relations(chunk[:, FIRST : FIRST + LIST], zh, core, table_hi, table_lo)
 
 
 def tail_kernel(
@@ -222,17 +240,18 @@
     keep_ref, send_ref, block_hi, block_lo,
 ):
     zh, core = place()
-    fill_block(block_hi, block_lo, mine_ref, theirs_ref, 2 * D)
+    mine = read_rows(mine_ref, CHUNK2)
+    fill_block(block_hi, block_lo, mine, read_rows(theirs_ref, CHUNK2), 2 * D)
     e_hi, e_lo = entity_hi[...], entity_lo[...]
     numbers = jnp.bitwise_xor(iota((128, ROWS), 1), core * HALF).astype(F32)
     rows_at = iota((ROWS, 128), 0).astype(F32)
     total = head_grad[...]
     for k in range(2):
         if k == 0:
-            lists = mine_ref[:, 0, 4 * D : 4 * D + LIST]
+            lists = mine[:, 4 * D : 4 * D + LIST]
             rel_rows = rel_ref[...]
         else:
-            lists = given_ref[:, 0, 4 * D + LIST - TAIL0 : 4 * D + 2 * LIST - TAIL0]
+            lists = given_ref[:, FIRST + LIST : FIRST + 2 * LIST]
             rel_rows = gather_relations(lists, zh, core, table_hi, table_lo)
         heads = onehot_cols(lists, 0, 4, numbers)
         head_rows = dot_nn(heads, block_hi[...]) + dot_nn(heads, block_lo[...])
@@ -264,18 +283,15 @@
         updated_ref[:, span] = entity_ref[:, span] - LEARN_RATE * gradient / jnp.sqrt(accum)
 
 
-def call(kernel, out_shape, args, scratch=(), cost=None, smem=()):
+def call(kernel, out_shape, args, vmem, scratch=(), cost=None, space=pltpu.VMEM):
     out_shape = jax.tree.map(lambda s: jax.ShapeDtypeStruct(*s), out_shape, is_leaf=lambda s: isinstance(s, tuple))
-    specs = [
-        pl.BlockSpec(memory_space=pltpu.SMEM if i in smem else pltpu.VMEM) for i in range(len(args))
-    ]
     return pl.pallas_call(
         kernel,
         out_shape=out_shape,
-        in_specs=specs,
+        in_specs=[pl.BlockSpec(memory_space=space) for _ in args],
         out_specs=jax.tree.map(lambda _: pl.BlockSpec(memory_space=pltpu.VMEM), out_shape),
         scratch_shapes=list(scratch),
-        compiler_params=pltpu.CompilerParams(vmem_limit_bytes=VMEM_LIMIT),
+        compiler_params=pltpu.CompilerParams(vmem_limit_bytes=vmem * MIB),
         cost_estimate=cost,
         name=kernel.__name__,
     )(*args)
@@ -286,31 +302,30 @@
 
 
 def shards(entity, state, relation, edge_head, edge_rel, edge_tail, negatives, counts, matching):
-    doms = lax.axis_size("dom")
-    swap_core = functools.partial(lax.ppermute, axis_name="edge", perm=[(0, 1), (1, 0), (2, 3), (3, 2)])
-    swap_zh = functools.partial(lax.ppermute, axis_name="edge", perm=[(0, 2), (2, 0), (1, 3), (3, 1)])
+    swap_core = functools.partial(lax.ppermute, axis_name="core", perm=[(0, 1), (1, 0)])
+    swap_zh = functools.partial(lax.ppermute, axis_name="zh", perm=[(0, 1), (1, 0)])
+    exchange = functools.partial(lax.all_to_all, axis_name=("x", "yz"), split_axis=0, concat_axis=0, tiled=True)
     entity_t, relation_t = entity.T, relation.T
 
     payload, cols, give = call(
         pack_kernel,
-        [((128, 1, LEG1), F32), ((128, 128), F32), ((LIST, 128), F32)],
+        [((128 * CHUNK1, 128), F32), ((128, 128), F32), ((LIST, 128), F32)],
         (entity_t, edge_head, edge_rel, edge_tail, negatives, counts),
-        scratch=[pltpu.VMEM((128, 128), F32)],
-        smem=(5,),
-    )
-    spread = lax.all_to_all(payload, "dom", split_axis=0, concat_axis=0, tiled=True)
-
-    bundle = call(bundle_kernel, ((PIECE + LIST, REL_DEV), F32), (relation_t, give))
-    bundle = swap_zh(bundle)
-    pieces = [bundle]
-    for shift in range(1, PIECES):
-        pieces.append(lax.ppermute(bundle, "dom", perm=[(d, (d + 32 * shift) % doms) for d in range(doms)]))
+        vmem=60,
+        scratch=[pltpu.VMEM((128, 128), F32), pltpu.VMEM((D, ROWS), F32)]
+        + [pltpu.VMEM((2, 1, 1, n), jnp.int32) for n in (SLOTS, SLOTS, SLOTS, NEGS)]
+        + [pltpu.VMEM((2, 1, 1), jnp.int32), pltpu.SemaphoreType.DMA((6,))],
+        space=pltpu.HBM,
+    )
+    spread = exchange(payload.reshape(128, 1, 128 * CHUNK1)).reshape(128 * CHUNK1, 128)
+
+    bundle = swap_zh(call(bundle_kernel, ((PIECE + LIST, REL_LANES), F32), (relation_t, give), vmem=8))
+    near2 = swap_core(relation_t)
     spread, bundle = lax.optimization_barrier((spread, bundle))
-
-    routed = call(route_kernel, ((128, 1, LEG2), F32), (spread, matching))
-    fetched = lax.all_to_all(routed, "dom", split_axis=0, concat_axis=0, tiled=True)
-    table = call(table_kernel, ((D, FAR + REL_DEV), F32), (relation_t, *pieces))
-    table_other = swap_core(table)
+    far = lax.all_gather(bundle[0:PIECE], ("x", "core"), axis=0)
+
+    routed = call(route_kernel, ((128 * CHUNK2, 128), F32), (spread, matching), vmem=16)
+    fetched = exchange(routed.reshape(128, 1, 128 * CHUNK2)).reshape(128 * CHUNK2, 128)
     prepared = call(
         left_kernel,
         [
@@ -323,20 +338,23 @@
             ((ROWS, D), BF16),
             ((128, 128), F32),
         ],
-        (entity_t, cols, bundle, table, table_other),
+        (entity_t, cols, bundle, relation_t, near2, far),
+        vmem=36,
+        scratch=[pltpu.VMEM((2, D, REL_DEV), F32)],
         cost=flops(8),
     )
-    fetched, prepared = lax.optimization_barrier((fetched, prepared))
     rel_rows, left_hi, left_lo, table_hi, table_lo, entity_hi, entity_lo, cols_other = prepared
+    fetched, cols_other = lax.optimization_barrier((fetched, cols_other))
     fetched_other = swap_core(fetched)
-    given = swap_zh(fetched[:, :, TAIL0:LEG2])
-    first_rel = call(first_relations_kernel, ((SLOTS, D), F32), (fetched, table_hi, table_lo), cost=flops(3))
+    given = swap_zh(lax.slice(fetched, (GIVEN_CHUNK, 0), fetched.shape, (CHUNK2, 1)))
+    first_rel = call(first_relations_kernel, ((SLOTS, D), F32), (fetched, table_hi, table_lo), vmem=24, cost=flops(3))
     fetched_other, first_rel = lax.optimization_barrier((fetched_other, first_rel))
     block = [pltpu.VMEM((ROWS, D), BF16), pltpu.VMEM((ROWS, D), BF16)]
     head_grad = call(
         head_kernel,
         ((ROWS, D), F32),
         (fetched, fetched_other, cols, cols_other, rel_rows, left_hi, left_lo),
+        vmem=24,
         scratch=block,
         cost=flops(6),
     )
@@ -344,6 +362,7 @@
         tail_kernel,
         [((D, HALF), F32), ((D, HALF), F32)],
         (fetched, fetched_other, given, first_rel, entity_hi, entity_lo, table_hi, table_lo, head_grad),
+        vmem=32,
         scratch=block,
         cost=flops(9),
     )
@@ -354,25 +373,29 @@
         update_kernel,
         [((D, ROWS), F32), ((1, ROWS), F32)],
         (half, other, entity_t, state.reshape(1, ROWS)),
+        vmem=8,
     )
     return updated.T, accum.reshape(ROWS)
 
 
 def solution(mesh):
+    parts = (PIECES, mesh.shape["dom"] // PIECES, 2, 2)
+    fine = jax.sharding.Mesh(mesh.devices.reshape(parts), ("x", "yz", "zh", "core"))
+    dom, edge = ("x", "yz"), ("zh", "core")
     return jax.shard_map(
         shards,
-        mesh=mesh,
+        mesh=fine,
         in_specs=(
-            P("dom", None),
-            P("dom"),
-            P("edge", None),
-            P(None, "dom", "edge", None),
-            P(None, "dom", "edge", None),
-            P(None, "dom", "edge", None),
-            P(None, "dom", "edge", None),
-            P(None, "dom", "edge"),
+            P(dom, None),
+            P(dom),
+            P(edge, None),
+            P(None, dom, edge, None),
+            P(None, dom, edge, None),
+            P(None, dom, edge, None),
+            P(None, dom, edge, None),
+            P(None, dom, edge),
             P(),
         ),
-        out_specs=(P("dom", None), P("dom")),
+        out_specs=(P(dom, None), P(dom)),
         check_vma=False,
     )

time: 204 us -> 185 us (0.907)
  the two profiles are of different devices: /device:TPU:65 before, /device:TPU:1 now
where the time goes in v3:
time: 185 us; the launch traced here: 184 us
  starting transfers between devices  63.5 us (34%)
  waiting for transfers between devices  58.9 us (32%)
  Pallas kernels  29 us (16%)
  local copies, waits for them, and re-layouts  18.2 us (10%)
  between operations  14.4 us (8%)
    pallas_call x8, Pallas kernels, call(): pl.pallas_call(kernel, out_shape=out_shape, in_specs=[pl.BlockSpec(memory...  29 us
    ppermute x1, waiting for transfers between devices, shards(): swap_zh(call(bundle_kernel, ((PIECE + LIST, REL_LANES), F32), (relation_t...  21.6 us
    all_to_all x1, starting transfers between devices, shards(): exchange(payload.reshape(128, 1, 128 * CHUNK1)).reshape(128 * CHUNK1, 128)  17.8 us
    ppermute x1, waiting for transfers between devices, shards(): half = half + swap_zh(half)  17.7 us
    unnamed x55, local copies, waits for them, and re-layouts  17.4 us
    all_gather x1, waiting for transfers between devices, shards(): far = lax.all_gather(bundle[0:PIECE], ('x', 'core'), axis=0)  14.6 us
    all_to_all x1, starting transfers between devices, shards(): exchange(routed.reshape(128, 1, 128 * CHUNK2)).reshape(128 * CHUNK2, 128)  11.9 us
    ppermute x1, starting transfers between devices, shards(): swap_zh(lax.slice(fetched, (GIVEN_CHUNK, 0), fetched.shape, (CHUNK2, 1)))  8.66 us
  transfers between devices with their start and end apart: 10, of which 6 were waited for; matrix products, arithmetic and copies ran while one was open for 0% of the time, Pallas kernels for 9%

profile of v3, /device:TPU:1, one launch (start us, length us, event | category | flops | bytes accessed | tf_op | source)
XLA Modules:
  0.0 184.1 jit_solution(10645709516397370449)
XLA Ops:
  7.2 1.4 copy.12.count_hbm
  8.6 2.4 %pack_kernel.1 = (f32[896,128]{1,0:T(8,128)}, f32[128,128]{1,0:T(8,128)}, f32[16,128]{1,0:T(8,128)}) custom-call(f32[400,512]{1,0:T(8,128)} %bitcast.10, s32[2,1,1,512]{3,2,1,0:T(1,128)} %head_hbm.1, s32[2,1,1,512]{3,2,1,0:T(1,128)} %rel_hbm.1, s32[2,1,1,512]{3,2,1,0:T(1,128)} %tail_hbm.1, s32[2,1,1,320]{3,2,1,0:T(1,128)} %neg_hbm.1, s32[2,1,1]{2,1,0:T(1,128)} %copy.12.count_hbm), custom_call_target="tpu_custom_call" | custom-call | tf_op jit(solution)/shard_map/pack_kernel/pallas_call | solution.py:288
  10.9 17.8 %all-to-all-start = ((f32[128,1,896]{2,1,0:T(1,128)}), f32[128,1,896]{2,1,0:T(1,128)S(1)}, u32[]{:S(2)}, u32[]{:S(2)}) async-start(f32[128,1,896]{2,1,0:T(1,128)} %bitcast.24), calls=%async_computation | async-start | bytes 917504 | tf_op jit(solution)/shard_map/all_to_all | solution.py:320
  29.5 8.1 %collective-permute-start = (f32[128,640]{1,0:T(8,128)S(1)}, f32[128,640]{1,0:T(8,128)S(1)}, u32[]{:S(2)}, u32[]{:S(2)}) collective-permute-start(f32[128,640]{1,0:T(8,128)S(1)} %bundle_kernel.1), channel_id=1, source_target_pairs={{0,2},{2,0},{1,3},{3,1},{4,6},{6,4},{5,7},{7,5},{8,10},{10,8},{9,1... | collective-permute-start | bytes 983048 | tf_op jit(solution)/shard_map/ppermute | solution.py:322
  37.6 21.6 %collective-permute-done.bundle_ref = f32[128,640]{1,0:T(8,128)S(1)} collective-permute-done((f32[128,640]{1,0:T(8,128)S(1)}, f32[128,640]{1,0:T(8,128)S(1)}, u32[]{:S(2)}, u32[]{:S(2)}) %collective-permute-start) | collective-permute-done | bytes 327712 | tf_op jit(solution)/shard_map/ppermute | solution.py:322
  60.0 1.7 route_kernel.1
  61.7 11.9 %all-to-all-start.1 = ((f32[128,1,1664]{2,1,0:T(1,128)}), f32[128,1,1664]{2,1,0:T(1,128)S(1)}, u32[]{:S(2)}, u32[]{:S(2)}) async-start(f32[128,1,1664]{2,1,0:T(1,128)} %bitcast.4), calls=%async_computation.1 | async-start | bytes 1703936 | tf_op jit(solution)/shard_map/all_to_all | solution.py:328
  73.6 3.2 %collective-permute-start.1 = (f32[400,528]{1,0:T(8,128)S(1)}, f32[400,528]{1,0:T(8,128)S(1)}, u32[]{:S(2)}, u32[]{:S(2)}) collective-permute-start(f32[400,528]{1,0:T(8,128)S(1)} %bitcast.15), channel_id=1, source_target_pairs={{0,1},{1,0},{2,3},{3,2},{4,5},{5,4},{6,7},{7,6},{8,9},{9,8},{10,11... | collective-permute-start | bytes 2534408 | tf_op jit(solution)/shard_map/ppermute | solution.py:323
  76.8 2.2 %collective-permute-done.1.near2_ref = f32[400,528]{1,0:T(8,128)S(1)} collective-permute-done((f32[400,528]{1,0:T(8,128)S(1)}, f32[400,528]{1,0:T(8,128)S(1)}, u32[]{:S(2)}, u32[]{:S(2)}) %collective-permute-start.1) | collective-permute-done | bytes 844832 | tf_op jit(solution)/shard_map/ppermute | solution.py:323
  80.0 14.6 %all-gather.3.cloned.1.call-done = f32[896,640]{1,0:T(8,128)} async-done(((f32[112,640]{1,0:T(8,128)}), f32[896,640]{1,0:T(8,128)}) %all-gather.3.cloned.1.call-update) | async-done | bytes 2293776 | tf_op jit(solution)/shard_map/all_gather | solution.py:325
  94.6 1.6 copy-done.5
  96.2 1.2 copy-done.7
  97.4 7.0 %left_kernel.1 = (f32[1024,400]{1,0:T(8,128)S(1)}, bf16[1024,400]{1,0:T(8,128)(2,1)S(1)}, bf16[1024,400]{1,0:T(8,128)(2,1)S(1)}, bf16[2112,400]{1,0:T(8,128)(2,1...) custom-call(f32[400,512]{1,0:T(8,128)S(1)} %bitcast.11, ...), custom_call_target="tpu_custom_call" | custom-call | flops 8000000000 | bytes 4000000 | tf_op jit(solution)/shard_map/left_kernel/pallas_call | solution.py:288
  104.4 1.3 copy-done.9
  105.8 1.4 copy-done.12
  107.1 1.4 copy-done.15
  108.5 1.0 copy-done.17
  109.5 1.0 copy-done.19
  112.7 2.2 %collective-permute-start.2 = (f32[1664,128]{1,0:T(8,128)S(1)}, f32[1664,128]{1,0:T(8,128)S(1)}, u32[]{:S(2)}, u32[]{:S(2)}) collective-permute-start(f32[1664,128]{1,0:T(8,128)S(1)} %bitcast.17), channel_id=1, source_target_pairs={{0,1},{1,0},{2,3},{3,2},{4,5},{5,4},{6,7},{7,6},{8,9},{9,8},{10,11... | collective-permute-start | bytes 2555912 | tf_op jit(solution)/shard_map/ppermute | solution.py:348
  114.9 8.7 %collective-permute-start.3 = (f32[128,128]{1,0:T(8,128)S(1)}, f32[128,128]{1,0:T(8,128)S(1)}, u32[]{:S(2)}, u32[]{:S(2)}) collective-permute-start(f32[128,128]{1,0:T(8,128)S(1)} %slice.7), channel_id=1, source_target_pairs={{0,2},{2,0},{1,3},{3,1},{4,6},{6,4},{5,7},{7,5},{8,10},{10,8},{9,1... | collective-permute-start | bytes 196616 | tf_op jit(solution)/shard_map/ppermute | solution.py:349
  123.6 1.6 copy-done.10
  125.2 1.6 copy-done.13
  126.8 2.7 %first_relations_kernel.1.rel_ref = f32[512,400]{1,0:T(8,128)S(1)} custom-call(f32[1664,128]{1,0:T(8,128)S(1)} %bitcast.19, bf16[2112,400]{1,0:T(8,128)(2,1)S(1)} %copy-done.10, bf16[2112,400]{1,0:T(8,128)(2,1)S(1)} %copy-done.13), custom_call_target="tpu_custom_call" | custom-call | flops 3000000000 | bytes 4000000 | tf_op jit(solution)/shard_map/first_relations_kernel/pallas_call | solution.py:288
  129.6 5.6 %head_kernel.1.head_grad = f32[512,400]{1,0:T(8,128)S(1)} custom-call(f32[1664,128]{1,0:T(8,128)S(1)} %bitcast.20, f32[1664,128]{1,0:T(8,128)S(1)} %collective-permute-done.2.theirs_ref, f32[128,128]{1,0:T(8,128)S(1)} %copy-done.8, f32[128,128]{1,0:T(8,128)S(1)} %copy-done.26, f32[1024,400]{1,0:T(8,128)S(1)} %copy-done.16, bf16[1024,400]{1,0:T(8,128)(2,1)S(1)} %copy-done.18, ...), custom_call_target="tpu_custom_call" | custom-call | flops 6000000000 | bytes 4000000 | tf_op jit(solution)/shard_map/head_kernel/pallas_call | solution.py:288
  135.2 8.6 %tail_kernel.1 = (f32[400,256]{1,0:T(8,128)S(1)}, f32[400,256]{1,0:T(8,128)S(1)}) custom-call(f32[1664,128]{1,0:T(8,128)S(1)} %bitcast.21, f32[1664,128]{1,0:T(8,128)S(1)} %collective-permute-done.2.theirs_ref, f32[128,128]{1,0:T(8,128)S(1)} %collective-permute-done.3.given_ref, f32[512,400]{1,0:T(8,128)S(1)} %first_relations_kernel.1.rel_ref, ...), custom_call_target="tpu_custom_call" | custom-call | flops 8999999488 | bytes 4000000 | tf_op jit(solution)/shard_map/tail_kernel/pallas_call | solution.py:288
  143.8 2.4 %collective-permute-start.4 = (f32[400,256]{1,0:T(8,128)S(1)}, f32[400,256]{1,0:T(8,128)S(1)}, u32[]{:S(2)}, u32[]{:S(2)}) collective-permute-start(f32[400,256]{1,0:T(8,128)S(1)} %get-tuple-element.41), channel_id=1, source_target_pairs={{0,1},{1,0},{2,3},{3,2},{4,5},{5,4},{6,7},{7,6},{8,9},{9,8},{10,11... | collective-permute-start | bytes 1228808 | tf_op jit(solution)/shard_map/ppermute | solution.py:369
  146.3 1.4 collective-permute-done.4
  147.7 1.9 %collective-permute-start.5 = (f32[400,256]{1,0:T(8,128)S(1)}, f32[400,256]{1,0:T(8,128)S(1)}, u32[]{:S(2)}, u32[]{:S(2)}) collective-permute-start(f32[400,256]{1,0:T(8,128)S(1)} %add.6), channel_id=1, source_target_pairs={{0,2},{2,0},{1,3},{3,1},{4,6},{6,4},{5,7},{7,5},{8,10},{10,8},{9,1... | collective-permute-start | bytes 1228808 | tf_op jit(solution)/shard_map/ppermute | solution.py:370
  149.6 17.7 %collective-permute-done.5 = f32[400,256]{1,0:T(8,128)S(1)} collective-permute-done((f32[400,256]{1,0:T(8,128)S(1)}, f32[400,256]{1,0:T(8,128)S(1)}, u32[]{:S(2)}, u32[]{:S(2)}) %collective-permute-start.5) | collective-permute-done | bytes 409632 | tf_op jit(solution)/shard_map/ppermute | solution.py:370
  167.4 7.4 %collective-permute-start.6 = (f32[400,256]{1,0:T(8,128)S(1)}, f32[400,256]{1,0:T(8,128)S(1)}, u32[]{:S(2)}, u32[]{:S(2)}) collective-permute-start(f32[400,256]{1,0:T(8,128)S(1)} %add.7.mine_ref), channel_id=1, source_target_pairs={{0,1},{1,0},{2,3},{3,2},{4,5},{5,4},{6,7},{7,6},{8,9},{9,8},{10,11... | collective-permute-start | bytes 1228808 | tf_op jit(solution)/shard_map/ppermute | solution.py:371
  174.7 1.4 collective-permute-done.6.theirs_ref
  176.1 1.2 update_kernel.1
  (56 shorter events, 4.9 us)
Async XLA Ops:
  7.2 21.6 %copy-start.1 = (f32[528,400]{0,1:T(8,128)S(1)}, f32[528,400]{0,1:T(8,128)}, u32[]{:S(2)}) copy-start(f32[528,400]{0,1:T(8,128)} %param.11) | copy-start | bytes 2534404
  7.2 52.8 %copy-start.4 = (s32[2,128]{1,0:T(2,128)S(1)}, s32[2,128]{1,0:T(2,128)}, u32[]{:S(2)}) copy-start(s32[2,128]{1,0:T(2,128)} %matching_ref.1) | copy-start | bytes 3076
  10.9 48.3 %all-to-all-start = ((f32[128,1,896]{2,1,0:T(1,128)}), f32[128,1,896]{2,1,0:T(1,128)S(1)}, u32[]{:S(2)}, u32[]{:S(2)}) async-start(f32[128,1,896]{2,1,0:T(1,128)} %bitcast.24), calls=%async_computation | async-start | bytes 917504 | tf_op jit(solution)/shard_map/all_to_all | solution.py:320
  28.7 65.8 %all-gather.3.cloned.1.call-start = ((), (), s32[]{:S(2)}) async-start(), calls=%async_computation.2 | async-start | bytes 2580480 | tf_op jit(solution)/shard_map/all_gather | solution.py:325
  29.5 65.1 %copy-start = (f32[512,400]{0,1:T(8,128)S(1)}, f32[512,400]{0,1:T(8,128)}, u32[]{:S(2)}) copy-start(f32[512,400]{0,1:T(8,128)} %param.9) | copy-start | bytes 2457604
  29.5 65.0 %copy-start.8 = (f32[128,128]{1,0:T(8,128)S(1)}, f32[128,128]{1,0:T(8,128)}, u32[]{:S(2)}) copy-start(f32[128,128]{1,0:T(8,128)} %get-tuple-element.26.cols_ref.lists_mine) | copy-start | bytes 196612
  29.5 29.7 %collective-permute-start = (f32[128,640]{1,0:T(8,128)S(1)}, f32[128,640]{1,0:T(8,128)S(1)}, u32[]{:S(2)}, u32[]{:S(2)}) collective-permute-start(f32[128,640]{1,0:T(8,128)S(1)} %bundle_kernel.1), channel_id=1, source_target_pairs={{0,2},{2,0},{1,3},{3,1},{4,6},{6,4},{5,7},{7,5},{8,10},{10,8},{9,1... | collective-permute-start | bytes 983048 | tf_op jit(solution)/shard_map/ppermute | solution.py:322
  61.7 51.0 %all-to-all-start.1 = ((f32[128,1,1664]{2,1,0:T(1,128)}), f32[128,1,1664]{2,1,0:T(1,128)S(1)}, u32[]{:S(2)}, u32[]{:S(2)}) async-start(f32[128,1,1664]{2,1,0:T(1,128)} %bitcast.4), calls=%async_computation.1 | async-start | bytes 1703936 | tf_op jit(solution)/shard_map/all_to_all | solution.py:328
  73.6 5.5 %collective-permute-start.1 = (f32[400,528]{1,0:T(8,128)S(1)}, f32[400,528]{1,0:T(8,128)S(1)}, u32[]{:S(2)}, u32[]{:S(2)}) collective-permute-start(f32[400,528]{1,0:T(8,128)S(1)} %bitcast.15), channel_id=1, source_target_pairs={{0,1},{1,0},{2,3},{3,2},{4,5},{5,4},{6,7},{7,6},{8,9},{9,8},{10,11... | collective-permute-start | bytes 2534408 | tf_op jit(solution)/shard_map/ppermute | solution.py:323
  94.6 1.6 copy-start.5
  96.2 1.2 copy-start.7
  104.4 1.4 copy-start.9
  105.8 1.4 copy-start.12
  107.1 1.4 copy-start.15
  108.5 1.0 copy-start.17
  109.5 1.0 copy-start.19
  112.7 16.8 %collective-permute-start.2 = (f32[1664,128]{1,0:T(8,128)S(1)}, f32[1664,128]{1,0:T(8,128)S(1)}, u32[]{:S(2)}, u32[]{:S(2)}) collective-permute-start(f32[1664,128]{1,0:T(8,128)S(1)} %bitcast.17), channel_id=1, source_target_pairs={{0,1},{1,0},{2,3},{3,2},{4,5},{5,4},{6,7},{7,6},{8,9},{9,8},{10,11... | collective-permute-start | bytes 2555912 | tf_op jit(solution)/shard_map/ppermute | solution.py:348
  114.9 20.2 %collective-permute-start.3 = (f32[128,128]{1,0:T(8,128)S(1)}, f32[128,128]{1,0:T(8,128)S(1)}, u32[]{:S(2)}, u32[]{:S(2)}) collective-permute-start(f32[128,128]{1,0:T(8,128)S(1)} %slice.7), channel_id=1, source_target_pairs={{0,2},{2,0},{1,3},{3,1},{4,6},{6,4},{5,7},{7,5},{8,10},{10,8},{9,1... | collective-permute-start | bytes 196616 | tf_op jit(solution)/shard_map/ppermute | solution.py:349
  123.6 1.6 copy-start.10
  125.2 1.6 copy-start.13
  126.8 2.7 %copy-start.16 = (f32[1024,400]{1,0:T(8,128)S(1)}, f32[1024,400]{1,0:T(8,128)}, u32[]{:S(2)}) copy-start(f32[1024,400]{1,0:T(8,128)} %copy-done.15) | copy-start | bytes 4915204
  126.8 2.7 %copy-start.18 = (bf16[1024,400]{1,0:T(8,128)(2,1)S(1)}, bf16[1024,400]{1,0:T(8,128)(2,1)}, u32[]{:S(2)}) copy-start(bf16[1024,400]{1,0:T(8,128)(2,1)} %copy-done.17) | copy-start | bytes 2457604
  126.8 2.7 %copy-start.20 = (bf16[1024,400]{1,0:T(8,128)(2,1)S(1)}, bf16[1024,400]{1,0:T(8,128)(2,1)}, u32[]{:S(2)}) copy-start(bf16[1024,400]{1,0:T(8,128)(2,1)} %copy-done.19) | copy-start | bytes 2457604
  126.8 2.7 %copy-start.26 = (f32[128,128]{1,0:T(8,128)S(1)}, f32[128,128]{1,0:T(8,128)}, u32[]{:S(2)}) copy-start(f32[128,128]{1,0:T(8,128)} %copy-done.25) | copy-start | bytes 196612
  129.5 5.6 %copy-start.11 = (bf16[2112,400]{1,0:T(8,128)(2,1)S(1)}, bf16[2112,400]{1,0:T(8,128)(2,1)}, u32[]{:S(2)}) copy-start(bf16[2112,400]{1,0:T(8,128)(2,1)} %copy-done.9) | copy-start | bytes 5068804
  129.5 5.6 %copy-start.14 = (bf16[2112,400]{1,0:T(8,128)(2,1)S(1)}, bf16[2112,400]{1,0:T(8,128)(2,1)}, u32[]{:S(2)}) copy-start(bf16[2112,400]{1,0:T(8,128)(2,1)} %copy-done.12) | copy-start | bytes 5068804
  129.6 5.6 %copy-start.22 = (bf16[512,400]{1,0:T(8,128)(2,1)S(1)}, bf16[512,400]{1,0:T(8,128)(2,1)}, u32[]{:S(2)}) copy-start(bf16[512,400]{1,0:T(8,128)(2,1)} %copy-done.21) | copy-start | bytes 1228804
  129.6 5.6 %copy-start.24 = (bf16[512,400]{1,0:T(8,128)(2,1)S(1)}, bf16[512,400]{1,0:T(8,128)(2,1)}, u32[]{:S(2)}) copy-start(bf16[512,400]{1,0:T(8,128)(2,1)} %copy-done.23) | copy-start | bytes 1228804
  143.8 32.3 %copy-start.3 = (f32[512]{0:T(512)S(1)}, f32[512]{0:T(512)}, u32[]{:S(2)}) copy-start(f32[512]{0:T(512)} %param.10) | copy-start | bytes 6148
  143.8 3.8 %collective-permute-start.4 = (f32[400,256]{1,0:T(8,128)S(1)}, f32[400,256]{1,0:T(8,128)S(1)}, u32[]{:S(2)}, u32[]{:S(2)}) collective-permute-start(f32[400,256]{1,0:T(8,128)S(1)} %get-tuple-element.41), channel_id=1, source_target_pairs={{0,1},{1,0},{2,3},{3,2},{4,5},{5,4},{6,7},{7,6},{8,9},{9,8},{10,11... | collective-permute-start | bytes 1228808 | tf_op jit(solution)/shard_map/ppermute | solution.py:369
  147.7 19.6 %collective-permute-start.5 = (f32[400,256]{1,0:T(8,128)S(1)}, f32[400,256]{1,0:T(8,128)S(1)}, u32[]{:S(2)}, u32[]{:S(2)}) collective-permute-start(f32[400,256]{1,0:T(8,128)S(1)} %add.6), channel_id=1, source_target_pairs={{0,2},{2,0},{1,3},{3,1},{4,6},{6,4},{5,7},{7,5},{8,10},{10,8},{9,1... | collective-permute-start | bytes 1228808 | tf_op jit(solution)/shard_map/ppermute | solution.py:370
  167.4 8.7 %collective-permute-start.6 = (f32[400,256]{1,0:T(8,128)S(1)}, f32[400,256]{1,0:T(8,128)S(1)}, u32[]{:S(2)}, u32[]{:S(2)}) collective-permute-start(f32[400,256]{1,0:T(8,128)S(1)} %add.7.mine_ref), channel_id=1, source_target_pairs={{0,1},{1,0},{2,3},{3,2},{4,5},{5,4},{6,7},{7,6},{8,9},{9,8},{10,11... | collective-permute-start | bytes 1228808 | tf_op jit(solution)/shard_map/ppermute | solution.py:371
  (5 other events, 3.9 us)
Sparse Core Ops, SparseCore 0:
  60.1 34.3 all-gather.2

commit v4 on v3

--- a/solution.py
+++ b/solution.py
@@ -17,7 +17,7 @@
 REL_DEV = 528
 PIECES = 4
 PIECE = 112
-REL_LANES = 640
+REL_LANES = 576
 TABLE = 4 * REL_DEV
 LIST = 16
 CHUNK1 = 7
@@ -68,7 +68,7 @@
 
 def onehot_cols(lists, first, count, columns):
     blocks = [(lists[:, first + j : first + j + 1] == columns) for j in range(count)]
-    return jnp.concatenate([jnp.where(b, 1.0, 0.0) for b in blocks], axis=0).astype(BF16)
+    return jnp.concatenate([jnp.where(b, 1.0, 0.0).astype(BF16) for b in blocks], axis=0)
 
 
 def pack_kernel(
@@ -89,7 +89,7 @@
         copy.wait()
     for bucket in range(2):
         at = bucket * LIST
-        live = count_ref[bucket]
+        live = count_ref[0, :, bucket : bucket + 1]
         for j in range(4):
             span = pl.ds(128 * j, 128)
             head = jnp.where(lane + 128 * j < live, head_ref[bucket, 0, 0:1, span], -1)
@@ -157,14 +157,14 @@
 
 
 def left_kernel(
-    entity_ref, cols_ref, bundle_ref, near_ref, near2_ref, far_ref,
+    entity_ref, cols_ref, bundle_ref, near_ref, near2_ref, far_ref, far2_ref,
     rel_out, left_hi, left_lo, table_hi, table_lo, entity_hi, entity_lo, cols_out, far_table,
 ):
     zh, core = place()
-    for c in range(2):
+    for c, ref in enumerate((far_ref, far2_ref)):
         for spot in range(PIECES):
-            far_table[c, piece_start(spot) : piece_start(spot) + PIECE, :] = far_ref[2 * spot + c, :, 0:REL_DEV]
-    parts = (near_ref[...], near2_ref[...], far_table[core], far_table[1 - core])
+            far_table[c, piece_start(spot) : piece_start(spot) + PIECE, :] = ref[spot, :, 0:REL_DEV]
+    parts = (near_ref[...], near2_ref[...], far_table[0], far_table[1])
     for k, part in enumerate(parts):
         hi, lo = split2(part.T)
         table_hi[k * REL_DEV : (k + 1) * REL_DEV, :] = hi
@@ -310,22 +310,23 @@
     payload, cols, give = call(
         pack_kernel,
         [((128 * CHUNK1, 128), F32), ((128, 128), F32), ((LIST, 128), F32)],
-        (entity_t, edge_head, edge_rel, edge_tail, negatives, counts),
+        (entity_t, edge_head, edge_rel, edge_tail, negatives, counts.transpose(1, 2, 0)),
         vmem=60,
         scratch=[pltpu.VMEM((128, 128), F32), pltpu.VMEM((D, ROWS), F32)]
         + [pltpu.VMEM((2, 1, 1, n), jnp.int32) for n in (SLOTS, SLOTS, SLOTS, NEGS)]
-        + [pltpu.VMEM((2, 1, 1), jnp.int32), pltpu.SemaphoreType.DMA((6,))],
+        + [pltpu.VMEM((1, 1, 2), jnp.int32), pltpu.SemaphoreType.DMA((6,))],
         space=pltpu.HBM,
     )
     spread = exchange(payload.reshape(128, 1, 128 * CHUNK1)).reshape(128 * CHUNK1, 128)
 
     bundle = swap_zh(call(bundle_kernel, ((PIECE + LIST, REL_LANES), F32), (relation_t, give), vmem=8))
     near2 = swap_core(relation_t)
-    spread, bundle = lax.optimization_barrier((spread, bundle))
-    far = lax.all_gather(bundle[0:PIECE], ("x", "core"), axis=0)
 
     routed = call(route_kernel, ((128 * CHUNK2, 128), F32), (spread, matching), vmem=16)
     fetched = exchange(routed.reshape(128, 1, 128 * CHUNK2)).reshape(128 * CHUNK2, 128)
+    bundle, _ = lax.optimization_barrier((bundle, routed))
+    far = lax.all_gather(bundle[0:PIECE], "x", axis=0)
+    far2 = swap_core(far)
     prepared = call(
         left_kernel,
         [
@@ -338,13 +339,12 @@
             ((ROWS, D), BF16),
             ((128, 128), F32),
         ],
-        (entity_t, cols, bundle, relation_t, near2, far),
+        (entity_t, cols, bundle, relation_t, near2, far, far2),
         vmem=36,
         scratch=[pltpu.VMEM((2, D, REL_DEV), F32)],
         cost=flops(8),
     )
     rel_rows, left_hi, left_lo, table_hi, table_lo, entity_hi, entity_lo, cols_other = prepared
-    fetched, cols_other = lax.optimization_barrier((fetched, cols_other))
     fetched_other = swap_core(fetched)
     given = swap_zh(lax.slice(fetched, (GIVEN_CHUNK, 0), fetched.shape, (CHUNK2, 1)))
     first_rel = call(first_relations_kernel, ((SLOTS, D), F32), (fetched, table_hi, table_lo), vmem=24, cost=flops(3))

time: 185 us -> 176 us (0.951)
  waiting for transfers between devices: 58.9 us -> 25.2 us
  blocking collectives: 0 us -> 19.1 us
  starting transfers between devices: 63.5 us -> 82.2 us
  between operations: 14.4 us -> 0.95 us
  Pallas kernels: 29 us -> 34.6 us
  local copies, waits for them, and re-layouts: 18.2 us -> 12.9 us
    ppermute x1, waiting for transfers between devices: 21.6 us -> 0.01 us  [shards(): swap_zh(call(bundle_kernel, ((PIECE + LIST, REL_LANES), F32), (relation_t...]
    all_gather x0 -> x1, blocking collectives: none -> 19.1 us  [shards(): far = lax.all_gather(bundle[0:PIECE], 'x', axis=0)]
    all_gather x1 -> x0, waiting for transfers between devices: 14.6 us -> none  [shards(): far = lax.all_gather(bundle[0:PIECE], ('x', 'core'), axis=0)]
    all_to_all x1, waiting for transfers between devices: 0.01 us -> 7.24 us  [shards(): exchange(payload.reshape(128, 1, 128 * CHUNK1)).reshape(128 * CHUNK1, 128)]
    all_to_all x1, starting transfers between devices: 11.9 us -> 19.1 us  [shards(): exchange(routed.reshape(128, 1, 128 * CHUNK2)).reshape(128 * CHUNK2, 128)]
    ppermute x0 -> x1, starting transfers between devices: none -> 7.06 us  [shards(): far2 = swap_core(far)]
    unnamed x55 -> x44, local copies, waits for them, and re-layouts: 17.4 us -> 11.7 us
    pallas_call x8, Pallas kernels: 29 us -> 34.6 us  [call(): pl.pallas_call(kernel, out_shape=out_shape, in_specs=[pl.BlockSpec(memory...]
  transfers between devices with their start and end apart: 10 -> 10, of which waited for: 6 -> 5; matrix products, arithmetic and copies ran while one was open for 0% -> 1% of each run, Pallas kernels for 9% -> 12%
where the time goes in v4:
time: 176 us; the launch traced here: 175 us
  starting transfers between devices  82.2 us (47%)
  Pallas kernels  34.6 us (20%)
  waiting for transfers between devices  25.2 us (14%)
  blocking collectives  19.1 us (11%)
  local copies, waits for them, and re-layouts  12.9 us (7%)
    pallas_call x8, Pallas kernels, call(): pl.pallas_call(kernel, out_shape=out_shape, in_specs=[pl.BlockSpec(memory...  34.6 us
    all_gather x1, blocking collectives, shards(): far = lax.all_gather(bundle[0:PIECE], 'x', axis=0)  19.1 us
    all_to_all x1, starting transfers between devices, shards(): exchange(routed.reshape(128, 1, 128 * CHUNK2)).reshape(128 * CHUNK2, 128)  19.1 us
    all_to_all x1, starting transfers between devices, shards(): exchange(payload.reshape(128, 1, 128 * CHUNK1)).reshape(128 * CHUNK1, 128)  17.8 us
    ppermute x1, waiting for transfers between devices, shards(): half = half + swap_zh(half)  15 us
    unnamed x44, local copies, waits for them, and re-layouts  11.7 us
    ppermute x1, starting transfers between devices, shards(): other = swap_core(half)  11.1 us
    ppermute x1, starting transfers between devices, shards(): swap_zh(lax.slice(fetched, (GIVEN_CHUNK, 0), fetched.shape, (CHUNK2, 1)))  10.7 us
  transfers between devices with their start and end apart: 10, of which 5 were waited for; matrix products, arithmetic and copies ran while one was open for 1% of the time, Pallas kernels for 12%

profile of v4, /device:TPU:1, one launch (start us, length us, event | category | flops | bytes accessed | tf_op | source)
XLA Modules:
  0.0 175.0 jit_solution(4159226912899761203)
XLA Ops:
  0.7 2.5 %pack_kernel.1 = (f32[896,128]{1,0:T(8,128)}, f32[128,128]{1,0:T(8,128)}, f32[16,128]{1,0:T(8,128)}) custom-call(f32[400,512]{1,0:T(8,128)} %bitcast.11, s32[2,1,1,512]{3,2,1,0:T(1,128)} %head_hbm.1, s32[2,1,1,512]{3,2,1,0:T(1,128)} %rel_hbm.1, s32[2,1,1,512]{3,2,1,0:T(1,128)} %tail_hbm.1, s32[2,1,1,320]{3,2,1,0:T(1,128)} %neg_hbm.1, s32[1,1,2]{2,1,0:T(1,128)} %bitcast.22), custom_call_target="tpu_custom_call" | custom-call | tf_op jit(solution)/shard_map/pack_kernel/pallas_call | solution.py:288
  3.1 17.8 %all-to-all-start = ((f32[128,1,896]{2,1,0:T(1,128)}), f32[128,1,896]{2,1,0:T(1,128)S(1)}, u32[]{:S(2)}, u32[]{:S(2)}) async-start(f32[128,1,896]{2,1,0:T(1,128)} %bitcast.21), calls=%async_computation | async-start | bytes 917504 | tf_op jit(solution)/shard_map/all_to_all | solution.py:320
  21.6 7.9 %collective-permute-start.1 = (f32[128,576]{1,0:T(8,128)S(1)}, f32[128,576]{1,0:T(8,128)S(1)}, u32[]{:S(2)}, u32[]{:S(2)}) collective-permute-start(f32[128,576]{1,0:T(8,128)S(1)} %bundle_kernel.1), channel_id=1, source_target_pairs={{0,2},{2,0},{1,3},{3,1},{4,6},{6,4},{5,7},{7,5},{8,10},{10,8},{9,1... | collective-permute-start | bytes 884744 | tf_op jit(solution)/shard_map/ppermute | solution.py:322
  29.6 7.2 %all-to-all-done = f32[128,1,896]{2,1,0:T(1,128)S(1)} async-done(((f32[128,1,896]{2,1,0:T(1,128)}), f32[128,1,896]{2,1,0:T(1,128)S(1)}, u32[]{:S(2)}, u32[]{:S(2)}) %all-to-all-start) | async-done | bytes 458784 | tf_op jit(solution)/shard_map/all_to_all | solution.py:320
  36.8 1.7 route_kernel.1
  38.5 19.1 %all-to-all-start.1 = ((f32[128,1,1664]{2,1,0:T(1,128)}), f32[128,1,1664]{2,1,0:T(1,128)}, u32[]{:S(2)}, u32[]{:S(2)}) async-start(f32[128,1,1664]{2,1,0:T(1,128)} %bitcast.4), calls=%async_computation.1 | async-start | bytes 1703936 | tf_op jit(solution)/shard_map/all_to_all | solution.py:326
  57.6 19.1 %all-gather = f32[448,576]{1,0:T(8,128)S(1)} all-gather(f32[112,576]{1,0:T(8,128)S(1)} %slice.6), channel_id=2, replica_groups=mesh['x'=4,'yz'=32,'zh'=2,'core'=2] {'x'}, dimensions={0}, use_global_device_ids=true | all-gather | bytes 1290240 | tf_op jit(solution)/shard_map/all_gather | solution.py:328
  76.7 7.1 %collective-permute-start.3 = (f32[4,112,576]{2,1,0:T(8,128)S(1)}, f32[4,112,576]{2,1,0:T(8,128)}, u32[]{:S(2)}, u32[]{:S(2)}) collective-permute-start(f32[4,112,576]{2,1,0:T(8,128)S(1)} %bitcast.15), channel_id=1, source_target_pairs={{0,1},{1,0},{2,3},{3,2},{4,5},{5,4},{6,7},{7,6},{8,9},{9,8},{10,11... | collective-permute-start | bytes 3096584 | tf_op jit(solution)/shard_map/ppermute | solution.py:329
  83.8 1.9 %collective-permute-start.2 = (f32[400,528]{1,0:T(8,128)S(1)}, f32[400,528]{1,0:T(8,128)}, u32[]{:S(2)}, u32[]{:S(2)}) collective-permute-start(f32[400,528]{1,0:T(8,128)S(1)} %bitcast.18), channel_id=1, source_target_pairs={{0,1},{1,0},{2,3},{3,2},{4,5},{5,4},{6,7},{7,6},{8,9},{9,8},{10,11... | collective-permute-start | bytes 2534408 | tf_op jit(solution)/shard_map/ppermute | solution.py:323
  85.7 2.4 %collective-permute-start = (f32[1664,128]{1,0:T(8,128)}, f32[1664,128]{1,0:T(8,128)}, u32[]{:S(2)}, u32[]{:S(2)}) collective-permute-start(f32[1664,128]{1,0:T(8,128)} %bitcast.5.mine_ref), channel_id=1, source_target_pairs={{0,1},{1,0},{2,3},{3,2},{4,5},{5,4},{6,7},{7,6},{8,9},{9,8},{10,11... | collective-permute-start | bytes 2555912 | tf_op jit(solution)/shard_map/ppermute | solution.py:348
  88.4 8.2 %left_kernel.1 = (f32[1024,400]{1,0:T(8,128)S(1)}, bf16[1024,400]{1,0:T(8,128)(2,1)S(1)}, bf16[1024,400]{1,0:T(8,128)(2,1)S(1)}, bf16[2112,400]{1,0:T(8,128)(2,1...) custom-call(f32[400,512]{1,0:T(8,128)S(1)} %bitcast.12, ...), custom_call_target="tpu_custom_call" | custom-call | flops 8000000000 | bytes 4000000 | tf_op jit(solution)/shard_map/left_kernel/pallas_call | solution.py:288
  96.7 1.4 copy-done.6
  98.1 1.4 copy-done.9
  99.4 1.4 copy-done.12
  100.8 1.0 copy-done.14
  101.8 1.1 copy-done.16
  102.8 0.8 copy-done.18
  103.6 0.8 copy-done.20
  104.4 1.2 slice.7
  105.6 10.7 %collective-permute-start.4 = (f32[128,128]{1,0:T(8,128)S(1)}, f32[128,128]{1,0:T(8,128)S(1)}, u32[]{:S(2)}, u32[]{:S(2)}) collective-permute-start(f32[128,128]{1,0:T(8,128)S(1)} %slice.7), channel_id=1, source_target_pairs={{0,2},{2,0},{1,3},{3,1},{4,6},{6,4},{5,7},{7,5},{8,10},{10,8},{9,1... | collective-permute-start | bytes 196616 | tf_op jit(solution)/shard_map/ppermute | solution.py:349
  116.3 1.6 copy-done.7
  117.9 1.6 copy-done.10
  119.5 4.0 %first_relations_kernel.1.rel_ref = f32[512,400]{1,0:T(8,128)S(1)} custom-call(f32[1664,128]{1,0:T(8,128)} %bitcast.5.mine_ref, bf16[2112,400]{1,0:T(8,128)(2,1)S(1)} %copy-done.7, bf16[2112,400]{1,0:T(8,128)(2,1)S(1)} %copy-done.10), custom_call_target="tpu_custom_call" | custom-call | flops 3000000000 | bytes 4000000 | tf_op jit(solution)/shard_map/first_relations_kernel/pallas_call | solution.py:288
  123.5 7.1 %head_kernel.1.head_grad = f32[512,400]{1,0:T(8,128)S(1)} custom-call(f32[1664,128]{1,0:T(8,128)} %bitcast.5.mine_ref, f32[1664,128]{1,0:T(8,128)} %collective-permute-done.theirs_ref, f32[128,128]{1,0:T(8,128)S(1)} %copy-done.5, f32[128,128]{1,0:T(8,128)S(1)} %get-tuple-element.30.lists_theirs, f32[1024,400]{1,0:T(8,128)S(1)} %copy-done.13, ...), custom_call_target="tpu_custom_call" | custom-call | flops 6000000000 | bytes 4000000 | tf_op jit(solution)/shard_map/head_kernel/pallas_call | solution.py:288
  130.7 10.0 %tail_kernel.1 = (f32[400,256]{1,0:T(8,128)S(1)}, f32[400,256]{1,0:T(8,128)S(1)}) custom-call(f32[1664,128]{1,0:T(8,128)} %bitcast.5.mine_ref, f32[1664,128]{1,0:T(8,128)} %collective-permute-done.theirs_ref, f32[128,128]{1,0:T(8,128)S(1)} %collective-permute-done.4.given_ref, f32[512,400]{1,0:T(8,128)S(1)} %first_relations_kernel.1.rel_ref, ...), custom_call_target="tpu_custom_call" | custom-call | flops 8999999488 | bytes 4000000 | tf_op jit(solution)/shard_map/tail_kernel/pallas_call | solution.py:288
  140.7 2.4 %collective-permute-start.5 = (f32[400,256]{1,0:T(8,128)S(1)}, f32[400,256]{1,0:T(8,128)S(1)}, u32[]{:S(2)}, u32[]{:S(2)}) collective-permute-start(f32[400,256]{1,0:T(8,128)S(1)} %get-tuple-element.35), channel_id=1, source_target_pairs={{0,1},{1,0},{2,3},{3,2},{4,5},{5,4},{6,7},{7,6},{8,9},{9,8},{10,11... | collective-permute-start | bytes 1228808 | tf_op jit(solution)/shard_map/ppermute | solution.py:369
  143.0 1.4 collective-permute-done.5
  144.5 1.9 %collective-permute-start.6 = (f32[400,256]{1,0:T(8,128)S(1)}, f32[400,256]{1,0:T(8,128)S(1)}, u32[]{:S(2)}, u32[]{:S(2)}) collective-permute-start(f32[400,256]{1,0:T(8,128)S(1)} %add.6), channel_id=1, source_target_pairs={{0,2},{2,0},{1,3},{3,1},{4,6},{6,4},{5,7},{7,5},{8,10},{10,8},{9,1... | collective-permute-start | bytes 1228808 | tf_op jit(solution)/shard_map/ppermute | solution.py:370
  146.4 15.0 %collective-permute-done.6 = f32[400,256]{1,0:T(8,128)S(1)} collective-permute-done((f32[400,256]{1,0:T(8,128)S(1)}, f32[400,256]{1,0:T(8,128)S(1)}, u32[]{:S(2)}, u32[]{:S(2)}) %collective-permute-start.6) | collective-permute-done | bytes 409632 | tf_op jit(solution)/shard_map/ppermute | solution.py:370
  161.4 11.1 %collective-permute-start.7 = (f32[400,256]{1,0:T(8,128)S(1)}, f32[400,256]{1,0:T(8,128)S(1)}, u32[]{:S(2)}, u32[]{:S(2)}) collective-permute-start(f32[400,256]{1,0:T(8,128)S(1)} %add.7.mine_ref), channel_id=1, source_target_pairs={{0,1},{1,0},{2,3},{3,2},{4,5},{5,4},{6,7},{7,6},{8,9},{9,8},{10,11... | collective-permute-start | bytes 1228808 | tf_op jit(solution)/shard_map/ppermute | solution.py:371
  172.5 1.4 collective-permute-done.7.theirs_ref
  173.9 1.2 update_kernel.1
  (45 shorter events, 1.2 us)
Async XLA Ops:
  0.6 20.3 %copy-start.1 = (f32[528,400]{0,1:T(8,128)S(1)}, f32[528,400]{0,1:T(8,128)}, u32[]{:S(2)}) copy-start(f32[528,400]{0,1:T(8,128)} %param.11) | copy-start | bytes 2534404
  0.6 36.2 %copy-start.4 = (s32[2,128]{1,0:T(2,128)S(1)}, s32[2,128]{1,0:T(2,128)}, u32[]{:S(2)}) copy-start(s32[2,128]{1,0:T(2,128)} %matching_ref.1) | copy-start | bytes 3076
  3.1 33.7 %all-to-all-start = ((f32[128,1,896]{2,1,0:T(1,128)}), f32[128,1,896]{2,1,0:T(1,128)S(1)}, u32[]{:S(2)}, u32[]{:S(2)}) async-start(f32[128,1,896]{2,1,0:T(1,128)} %bitcast.21), calls=%async_computation | async-start | bytes 917504 | tf_op jit(solution)/shard_map/all_to_all | solution.py:320
  20.9 0.7 copy-start.2
  21.6 35.9 %collective-permute-start.1 = (f32[128,576]{1,0:T(8,128)S(1)}, f32[128,576]{1,0:T(8,128)S(1)}, u32[]{:S(2)}, u32[]{:S(2)}) collective-permute-start(f32[128,576]{1,0:T(8,128)S(1)} %bundle_kernel.1), channel_id=1, source_target_pairs={{0,2},{2,0},{1,3},{3,1},{4,6},{6,4},{5,7},{7,5},{8,10},{10,8},{9,1... | collective-permute-start | bytes 884744 | tf_op jit(solution)/shard_map/ppermute | solution.py:322
  38.5 49.9 %copy-start = (f32[512,400]{0,1:T(8,128)S(1)}, f32[512,400]{0,1:T(8,128)}, u32[]{:S(2)}) copy-start(f32[512,400]{0,1:T(8,128)} %param.9) | copy-start | bytes 2457604
  38.5 49.9 %copy-start.5 = (f32[128,128]{1,0:T(8,128)S(1)}, f32[128,128]{1,0:T(8,128)}, u32[]{:S(2)}) copy-start(f32[128,128]{1,0:T(8,128)} %get-tuple-element.21.cols_ref.lists_mine) | copy-start | bytes 196612
  38.5 47.2 %all-to-all-start.1 = ((f32[128,1,1664]{2,1,0:T(1,128)}), f32[128,1,1664]{2,1,0:T(1,128)}, u32[]{:S(2)}, u32[]{:S(2)}) async-start(f32[128,1,1664]{2,1,0:T(1,128)} %bitcast.4), calls=%async_computation.1 | async-start | bytes 1703936 | tf_op jit(solution)/shard_map/all_to_all | solution.py:326
  76.7 11.7 %collective-permute-start.3 = (f32[4,112,576]{2,1,0:T(8,128)S(1)}, f32[4,112,576]{2,1,0:T(8,128)}, u32[]{:S(2)}, u32[]{:S(2)}) collective-permute-start(f32[4,112,576]{2,1,0:T(8,128)S(1)} %bitcast.15), channel_id=1, source_target_pairs={{0,1},{1,0},{2,3},{3,2},{4,5},{5,4},{6,7},{7,6},{8,9},{9,8},{10,11... | collective-permute-start | bytes 3096584 | tf_op jit(solution)/shard_map/ppermute | solution.py:329
  83.8 4.7 %collective-permute-start.2 = (f32[400,528]{1,0:T(8,128)S(1)}, f32[400,528]{1,0:T(8,128)}, u32[]{:S(2)}, u32[]{:S(2)}) collective-permute-start(f32[400,528]{1,0:T(8,128)S(1)} %bitcast.18), channel_id=1, source_target_pairs={{0,1},{1,0},{2,3},{3,2},{4,5},{5,4},{6,7},{7,6},{8,9},{9,8},{10,11... | collective-permute-start | bytes 2534408 | tf_op jit(solution)/shard_map/ppermute | solution.py:323
  85.7 37.7 %collective-permute-start = (f32[1664,128]{1,0:T(8,128)}, f32[1664,128]{1,0:T(8,128)}, u32[]{:S(2)}, u32[]{:S(2)}) collective-permute-start(f32[1664,128]{1,0:T(8,128)} %bitcast.5.mine_ref), channel_id=1, source_target_pairs={{0,1},{1,0},{2,3},{3,2},{4,5},{5,4},{6,7},{7,6},{8,9},{9,8},{10,11... | collective-permute-start | bytes 2555912 | tf_op jit(solution)/shard_map/ppermute | solution.py:348
  96.7 1.4 copy-start.6
  98.1 1.4 copy-start.9
  99.4 1.4 copy-start.12
  100.8 1.0 copy-start.14
  101.8 1.1 copy-start.16
  102.8 0.8 copy-start.18
  103.6 0.8 copy-start.20
  105.6 25.1 %collective-permute-start.4 = (f32[128,128]{1,0:T(8,128)S(1)}, f32[128,128]{1,0:T(8,128)S(1)}, u32[]{:S(2)}, u32[]{:S(2)}) collective-permute-start(f32[128,128]{1,0:T(8,128)S(1)} %slice.7), channel_id=1, source_target_pairs={{0,2},{2,0},{1,3},{3,1},{4,6},{6,4},{5,7},{7,5},{8,10},{10,8},{9,1... | collective-permute-start | bytes 196616 | tf_op jit(solution)/shard_map/ppermute | solution.py:349
  116.3 1.6 copy-start.7
  117.9 1.6 copy-start.10
  119.5 4.0 %copy-start.13 = (f32[1024,400]{1,0:T(8,128)S(1)}, f32[1024,400]{1,0:T(8,128)}, u32[]{:S(2)}) copy-start(f32[1024,400]{1,0:T(8,128)} %copy-done.12) | copy-start | bytes 4915204
  119.5 4.0 %copy-start.15 = (bf16[1024,400]{1,0:T(8,128)(2,1)S(1)}, bf16[1024,400]{1,0:T(8,128)(2,1)}, u32[]{:S(2)}) copy-start(bf16[1024,400]{1,0:T(8,128)(2,1)} %copy-done.14) | copy-start | bytes 2457604
  119.5 4.0 %copy-start.17 = (bf16[1024,400]{1,0:T(8,128)(2,1)S(1)}, bf16[1024,400]{1,0:T(8,128)(2,1)}, u32[]{:S(2)}) copy-start(bf16[1024,400]{1,0:T(8,128)(2,1)} %copy-done.16) | copy-start | bytes 2457604
  123.5 7.2 %copy-start.8 = (bf16[2112,400]{1,0:T(8,128)(2,1)S(1)}, bf16[2112,400]{1,0:T(8,128)(2,1)}, u32[]{:S(2)}) copy-start(bf16[2112,400]{1,0:T(8,128)(2,1)} %copy-done.6) | copy-start | bytes 5068804
  123.5 7.2 %copy-start.11 = (bf16[2112,400]{1,0:T(8,128)(2,1)S(1)}, bf16[2112,400]{1,0:T(8,128)(2,1)}, u32[]{:S(2)}) copy-start(bf16[2112,400]{1,0:T(8,128)(2,1)} %copy-done.9) | copy-start | bytes 5068804
  123.5 7.2 %copy-start.19 = (bf16[512,400]{1,0:T(8,128)(2,1)S(1)}, bf16[512,400]{1,0:T(8,128)(2,1)}, u32[]{:S(2)}) copy-start(bf16[512,400]{1,0:T(8,128)(2,1)} %copy-done.18) | copy-start | bytes 1228804
  123.5 7.2 %copy-start.21 = (bf16[512,400]{1,0:T(8,128)(2,1)S(1)}, bf16[512,400]{1,0:T(8,128)(2,1)}, u32[]{:S(2)}) copy-start(bf16[512,400]{1,0:T(8,128)(2,1)} %copy-done.20) | copy-start | bytes 1228804
  140.7 33.2 %copy-start.3 = (f32[512]{0:T(512)S(1)}, f32[512]{0:T(512)}, u32[]{:S(2)}) copy-start(f32[512]{0:T(512)} %param.10) | copy-start | bytes 6148
  140.7 3.7 %collective-permute-start.5 = (f32[400,256]{1,0:T(8,128)S(1)}, f32[400,256]{1,0:T(8,128)S(1)}, u32[]{:S(2)}, u32[]{:S(2)}) collective-permute-start(f32[400,256]{1,0:T(8,128)S(1)} %get-tuple-element.35), channel_id=1, source_target_pairs={{0,1},{1,0},{2,3},{3,2},{4,5},{5,4},{6,7},{7,6},{8,9},{9,8},{10,11... | collective-permute-start | bytes 1228808 | tf_op jit(solution)/shard_map/ppermute | solution.py:369
  144.5 16.9 %collective-permute-start.6 = (f32[400,256]{1,0:T(8,128)S(1)}, f32[400,256]{1,0:T(8,128)S(1)}, u32[]{:S(2)}, u32[]{:S(2)}) collective-permute-start(f32[400,256]{1,0:T(8,128)S(1)} %add.6), channel_id=1, source_target_pairs={{0,2},{2,0},{1,3},{3,1},{4,6},{6,4},{5,7},{7,5},{8,10},{10,8},{9,1... | collective-permute-start | bytes 1228808 | tf_op jit(solution)/shard_map/ppermute | solution.py:370
  161.4 12.5 %collective-permute-start.7 = (f32[400,256]{1,0:T(8,128)S(1)}, f32[400,256]{1,0:T(8,128)S(1)}, u32[]{:S(2)}, u32[]{:S(2)}) collective-permute-start(f32[400,256]{1,0:T(8,128)S(1)} %add.7.mine_ref), channel_id=1, source_target_pairs={{0,1},{1,0},{2,3},{3,2},{4,5},{5,4},{6,7},{7,6},{8,9},{9,8},{10,11... | collective-permute-start | bytes 1228808 | tf_op jit(solution)/shard_map/ppermute | solution.py:371

commit v5 on v4

--- a/solution.py
+++ b/solution.py
@@ -16,8 +16,9 @@
 NEGS = 320
 REL_DEV = 528
 PIECES = 4
-PIECE = 112
-REL_LANES = 576
+PIECE = 104
+MAIN = 512
+REST = REL_DEV - MAIN
 TABLE = 4 * REL_DEV
 LIST = 16
 CHUNK1 = 7
@@ -143,11 +144,18 @@
 
 def bundle_kernel(relation_ref, give_ref, out_ref):
     spot = lax.axis_index("x")
-    start = pl.multiple_of(jnp.minimum(PIECE * spot, D - PIECE), 16)
-    out_ref[:, 512:REL_LANES] = jnp.zeros((PIECE + LIST, REL_LANES - 512), F32)
-    out_ref[0:PIECE, 0:REL_DEV] = relation_ref[pl.ds(start, PIECE), :]
-    out_ref[PIECE : PIECE + LIST, 128:512] = jnp.zeros((LIST, 384), F32)
-    out_ref[PIECE : PIECE + LIST, 0:128] = give_ref[...]
+    start = pl.multiple_of(jnp.minimum(PIECE * spot, D - PIECE), 8)
+    piece = relation_ref[pl.ds(start, PIECE), :]
+    out_ref[0:PIECE, :] = piece[:, 0:MAIN]
+    rest = jnp.concatenate([piece[:, MAIN:REL_DEV], jnp.zeros((PIECE, 128 - REST), F32)], axis=1)
+    rest = jnp.concatenate([rest, jnp.zeros((128 - PIECE, 128), F32)], axis=0).T
+    for g in range(4):
+        out_ref[PIECE : PIECE + 4, 128 * g : 128 * (g + 1)] = rest[4 * g : 4 * g + 4, :]
+        out_ref[PIECE + 4 : PIECE + 8, 128 * g : 128 * (g + 1)] = give_ref[4 * g : 4 * g + 4, :]
+
+
+def unfold(rows):
+    return jnp.concatenate([rows[:, 128 * g : 128 * (g + 1)] for g in range(4)], axis=0)
 
 
 def gather_relations(lists, zh, core, table_hi, table_lo):
@@ -156,24 +164,32 @@
     return dot_nn(rels, table_hi[...]) + dot_nn(rels, table_lo[...])
 
 
-def left_kernel(
-    entity_ref, cols_ref, bundle_ref, near_ref, near2_ref, far_ref, far2_ref,
-    rel_out, left_hi, left_lo, table_hi, table_lo, entity_hi, entity_lo, cols_out, far_table,
+def relations_kernel(
+    entity_ref, cols_ref, bundle_ref, near_ref, near2_ref, far_ref, far2_ref, fetched_ref,
+    rel_out, left_hi, left_lo, first_out, table_hi, table_lo, entity_hi, entity_lo, cols_out, far_table,
 ):
     zh, core = place()
-    for c, ref in enumerate((far_ref, far2_ref)):
-        for spot in range(PIECES):
-            far_table[c, piece_start(spot) : piece_start(spot) + PIECE, :] = ref[spot, :, 0:REL_DEV]
-    parts = (near_ref[...], near2_ref[...], far_table[0], far_table[1])
-    for k, part in enumerate(parts):
-        hi, lo = split2(part.T)
+    for k, ref in enumerate((near_ref, near2_ref)):
+        hi, lo = split2(ref[...].T)
         table_hi[k * REL_DEV : (k + 1) * REL_DEV, :] = hi
         table_lo[k * REL_DEV : (k + 1) * REL_DEV, :] = lo
+    for k, ref in enumerate((far_ref, far2_ref)):
+        for spot in range(PIECES):
+            far_table[k, piece_start(spot) : piece_start(spot) + PIECE, :] = ref[spot, 0:PIECE, :]
+        at = (2 + k) * REL_DEV
+        hi, lo = split2(far_table[k].T)
+        table_hi[at : at + MAIN, :] = hi
+        table_lo[at : at + MAIN, :] = lo
+        rest = [unfold(ref[spot, PIECE : PIECE + 4, :]) for spot in range(PIECES)]
+        rest = [rest[spot][:, 0:PIECE] for spot in range(PIECES - 1)] + [rest[-1][:, PIECES * PIECE - D : PIECE]]
+        hi, lo = split2(jnp.concatenate(rest, axis=1))
+        table_hi[at + MAIN : at + REL_DEV, :] = hi
+        table_lo[at + MAIN : at + REL_DEV, :] = lo
     hi, lo = split2(entity_ref[...].T)
     entity_hi[...] = hi
     entity_lo[...] = lo
     own = iota((128, ROWS), 1).astype(F32)
-    theirs = jnp.concatenate([bundle_ref[PIECE : PIECE + LIST, 0:128], jnp.zeros((128 - LIST, 128), F32)], axis=0).T
+    theirs = jnp.concatenate([unfold(bundle_ref[PIECE + 4 : PIECE + 8, :]), jnp.zeros((128 - LIST, 128), F32)], axis=0).T
     cols_out[...] = theirs
     for k, lists in enumerate((cols_ref[:, 0:LIST], theirs[:, 0:LIST])):
         heads = onehot_cols(lists, 0, 4, own)
@@ -184,6 +200,8 @@
         rel_out[span, :] = rel_rows
         left_hi[span, :] = l_hi
         left_lo[span, :] = l_lo
+    chunk = fetched_ref[pl.ds(GIVEN_CHUNK, 128, stride=CHUNK2), :]
+    first_out[...] = gather_relations(chunk[:, FIRST : FIRST + LIST], zh, core, table_hi, table_lo)
 
 
 def fill_block(hi_ref, lo_ref, mine, theirs, first):
@@ -229,10 +247,8 @@
     grad_ref[...] = total
 
 
-def first_relations_kernel(mine_ref, table_hi, table_lo, rel_ref):
-    zh, core = place()
-    chunk = mine_ref[pl.ds(GIVEN_CHUNK, 128, stride=CHUNK2), :]
-    rel_ref[...] = gather_relations(chunk[:, FIRST : FIRST + LIST], zh, core, table_hi, table_lo)
+def given_kernel(fetched_ref, out_ref):
+    out_ref[...] = fetched_ref[pl.ds(GIVEN_CHUNK, 128, stride=CHUNK2), :].T[FIRST + LIST : FIRST + 2 * LIST, :]
 
 
 def tail_kernel(
@@ -251,7 +267,7 @@
             lists = mine[:, 4 * D : 4 * D + LIST]
             rel_rows = rel_ref[...]
         else:
-            lists = given_ref[:, FIRST + LIST : FIRST + 2 * LIST]
+            lists = jnp.concatenate([given_ref[...], jnp.zeros((128 - LIST, 128), F32)], axis=0).T[:, 0:LIST]
             rel_rows = gather_relations(lists, zh, core, table_hi, table_lo)
         heads = onehot_cols(lists, 0, 4, numbers)
         head_rows = dot_nn(heads, block_hi[...]) + dot_nn(heads, block_lo[...])
@@ -319,42 +335,40 @@
     )
     spread = exchange(payload.reshape(128, 1, 128 * CHUNK1)).reshape(128 * CHUNK1, 128)
 
-    bundle = swap_zh(call(bundle_kernel, ((PIECE + LIST, REL_LANES), F32), (relation_t, give), vmem=8))
+    bundle = swap_zh(call(bundle_kernel, ((PIECE + 8, MAIN), F32), (relation_t, give), vmem=8))
     near2 = swap_core(relation_t)
 
     routed = call(route_kernel, ((128 * CHUNK2, 128), F32), (spread, matching), vmem=16)
     fetched = exchange(routed.reshape(128, 1, 128 * CHUNK2)).reshape(128 * CHUNK2, 128)
     bundle, _ = lax.optimization_barrier((bundle, routed))
-    far = lax.all_gather(bundle[0:PIECE], "x", axis=0)
+    far = lax.all_gather(bundle, "x", axis=0)
     far2 = swap_core(far)
-    prepared = call(
-        left_kernel,
+    fetched_other = swap_core(fetched)
+    given = swap_zh(call(given_kernel, ((LIST, 128), F32), (fetched,), vmem=4))
+    rel_rows, left_hi, left_lo, first_rel, table_hi, table_lo, entity_hi, entity_lo, cols_other = call(
+        relations_kernel,
         [
             ((2 * SLOTS, D), F32),
             ((2 * SLOTS, D), BF16),
             ((2 * SLOTS, D), BF16),
+            ((SLOTS, D), F32),
             ((TABLE, D), BF16),
             ((TABLE, D), BF16),
             ((ROWS, D), BF16),
             ((ROWS, D), BF16),
             ((128, 128), F32),
         ],
-        (entity_t, cols, bundle, relation_t, near2, far, far2),
-        vmem=36,
-        scratch=[pltpu.VMEM((2, D, REL_DEV), F32)],
-        cost=flops(8),
-    )
-    rel_rows, left_hi, left_lo, table_hi, table_lo, entity_hi, entity_lo, cols_other = prepared
-    fetched_other = swap_core(fetched)
-    given = swap_zh(lax.slice(fetched, (GIVEN_CHUNK, 0), fetched.shape, (CHUNK2, 1)))
-    first_rel = call(first_relations_kernel, ((SLOTS, D), F32), (fetched, table_hi, table_lo), vmem=24, cost=flops(3))
-    fetched_other, first_rel = lax.optimization_barrier((fetched_other, first_rel))
+        (entity_t, cols, bundle, relation_t, near2, far, far2, fetched),
+        vmem=32,
+        scratch=[pltpu.VMEM((2, D, MAIN), F32)],
+        cost=flops(10),
+    )
     block = [pltpu.VMEM((ROWS, D), BF16), pltpu.VMEM((ROWS, D), BF16)]
     head_grad = call(
         head_kernel,
         ((ROWS, D), F32),
         (fetched, fetched_other, cols, cols_other, rel_rows, left_hi, left_lo),
-        vmem=24,
+        vmem=20,
         scratch=block,
         cost=flops(6),
     )
@@ -362,7 +376,7 @@
         tail_kernel,
         [((D, HALF), F32), ((D, HALF), F32)],
         (fetched, fetched_other, given, first_rel, entity_hi, entity_lo, table_hi, table_lo, head_grad),
-        vmem=32,
+        vmem=28,
         scratch=block,
         cost=flops(9),
     )

time: 176 us -> 163 us (0.926)
  starting transfers between devices: 82.2 us -> 39 us
  blocking collectives: 19.1 us -> 47.5 us
  waiting for transfers between devices: 25.2 us -> 43.6 us
  local copies, waits for them, and re-layouts: 12.9 us -> 0.7 us
  Pallas kernels: 34.6 us -> 30.6 us
    all_to_all x0 -> x1, blocking collectives: none -> 33.3 us  [shards(): exchange(payload.reshape(128, 1, 128 * CHUNK1)).reshape(128 * CHUNK1, 128)]
    ppermute x2, waiting for transfers between devices: 0.01 us -> 25.3 us  [the longest x1 25.3 us: shards(): swap_zh(call(bundle_kernel, ((PIECE + 8, MAIN), F32), (relation_t, give),...]
    all_to_all x1 -> x0, starting transfers between devices: 17.8 us -> none  [shards(): exchange(payload.reshape(128, 1, 128 * CHUNK1)).reshape(128 * CHUNK1, 128)]
    unnamed x44 -> x12, local copies, waits for them, and re-layouts: 11.7 us -> 0.7 us
    all_to_all x1, starting transfers between devices: 19.1 us -> 8.85 us  [shards(): exchange(routed.reshape(128, 1, 128 * CHUNK2)).reshape(128 * CHUNK2, 128)]
    ppermute x1, starting transfers between devices: 11.1 us -> 2.45 us  [shards(): other = swap_core(half)]
    ppermute x2, starting transfers between devices: 18.6 us -> 10.1 us  [the longest x1 7.94 us: shards(): swap_zh(call(bundle_kernel, ((PIECE + 8, MAIN), F32), (relation_t, give),...]
    all_to_all x1 -> x0, waiting for transfers between devices: 7.24 us -> none  [shards(): exchange(payload.reshape(128, 1, 128 * CHUNK1)).reshape(128 * CHUNK1, 128)]
  transfers between devices with their start and end apart: 10 -> 9, of which waited for: 5 -> 4; matrix products, arithmetic and copies ran while one was open for 1% -> 0% of each run, Pallas kernels for 12% -> 10%
where the time goes in v5:
time: 163 us; the launch traced here: 162 us
  blocking collectives  47.5 us (29%)
  waiting for transfers between devices  43.6 us (27%)
  starting transfers between devices  39 us (24%)
  Pallas kernels  30.6 us (19%)
    all_to_all x1, blocking collectives, shards(): exchange(payload.reshape(128, 1, 128 * CHUNK1)).reshape(128 * CHUNK1, 128)  33.3 us
    pallas_call x8, Pallas kernels, call(): pl.pallas_call(kernel, out_shape=out_shape, in_specs=[pl.BlockSpec(memory...  30.6 us
    ppermute x1, waiting for transfers between devices, shards(): swap_zh(call(bundle_kernel, ((PIECE + 8, MAIN), F32), (relation_t, give),...  25.3 us
    ppermute x1, waiting for transfers between devices, shards(): half = half + swap_zh(half)  15.2 us
    all_gather x1, blocking collectives, shards(): far = lax.all_gather(bundle, 'x', axis=0)  14.2 us
    all_to_all x1, starting transfers between devices, shards(): exchange(routed.reshape(128, 1, 128 * CHUNK2)).reshape(128 * CHUNK2, 128)  8.85 us
    ppermute x1, starting transfers between devices, shards(): swap_zh(call(bundle_kernel, ((PIECE + 8, MAIN), F32), (relation_t, give),...  7.94 us
    ppermute x1, starting transfers between devices, shards(): half = half + swap_zh(half)  7.27 us
  transfers between devices with their start and end apart: 9, of which 4 were waited for; matrix products, arithmetic and copies ran while one was open for 0% of the time, Pallas kernels for 10%

profile of v5, /device:TPU:1, one launch (start us, length us, event | category | flops | bytes accessed | tf_op | source)
XLA Modules:
  0.0 162.2 jit_solution(11202462577684963075)
XLA Ops:
  0.6 2.4 %pack_kernel.1 = (f32[896,128]{1,0:T(8,128)}, f32[128,128]{1,0:T(8,128)}, f32[16,128]{1,0:T(8,128)}) custom-call(f32[400,512]{1,0:T(8,128)} %bitcast.16, s32[2,1,1,512]{3,2,1,0:T(1,128)} %head_hbm.1, s32[2,1,1,512]{3,2,1,0:T(1,128)} %rel_hbm.1, s32[2,1,1,512]{3,2,1,0:T(1,128)} %tail_hbm.1, s32[2,1,1,320]{3,2,1,0:T(1,128)} %neg_hbm.1, s32[1,1,2]{2,1,0:T(1,128)} %bitcast.25), custom_call_target="tpu_custom_call" | custom-call | tf_op jit(solution)/shard_map/pack_kernel/pallas_call | solution.py:304
  3.0 0.0 copy-start.1
  3.0 33.3 %all_to_all.10 = f32[128,1,896]{2,1,0:T(1,128)S(1)} all-to-all(f32[128,1,896]{2,1,0:T(1,128)} %bitcast.24), channel_id=1, replica_groups=mesh['x'=4,'yz'=32,'zh'=2,'core'=2] {'x','yz'}, dimensions={0} | all-to-all | bytes 917504 | tf_op jit(solution)/shard_map/all_to_all | solution.py:336
  36.3 0.7 copy-done.4
  37.0 1.7 %route_kernel.1 = f32[1664,128]{1,0:T(8,128)} custom-call(f32[896,128]{1,0:T(8,128)S(1)} %bitcast.19, s32[2,128]{1,0:T(2,128)S(1)} %copy-done.4), custom_call_target="tpu_custom_call" | custom-call | tf_op jit(solution)/shard_map/route_kernel/pallas_call | solution.py:304
  38.7 8.8 %all-to-all-start.1 = ((f32[128,1,1664]{2,1,0:T(1,128)}), f32[128,1,1664]{2,1,0:T(1,128)S(1)}, u32[]{:S(2)}, u32[]{:S(2)}) async-start(f32[128,1,1664]{2,1,0:T(1,128)} %bitcast.4), calls=%async_computation.1 | async-start | bytes 1703936 | tf_op jit(solution)/shard_map/all_to_all | solution.py:342
  47.5 0.1 bundle_kernel.1
  47.6 7.9 %collective-permute-start.2 = (f32[112,512]{1,0:T(8,128)S(1)}, f32[112,512]{1,0:T(8,128)S(1)}, u32[]{:S(2)}, u32[]{:S(2)}) collective-permute-start(f32[112,512]{1,0:T(8,128)S(1)} %bundle_kernel.1), channel_id=1, source_target_pairs={{0,2},{2,0},{1,3},{3,1},{4,6},{6,4},{5,7},{7,5},{8,10},{10,8},{9,1... | collective-permute-start | bytes 688136 | tf_op jit(solution)/shard_map/ppermute | solution.py:338
  55.6 25.3 %collective-permute-done.2.bundle_ref = f32[112,512]{1,0:T(8,128)S(1)} collective-permute-done((f32[112,512]{1,0:T(8,128)S(1)}, f32[112,512]{1,0:T(8,128)S(1)}, u32[]{:S(2)}, u32[]{:S(2)}) %collective-permute-start.2) | collective-permute-done | bytes 229408 | tf_op jit(solution)/shard_map/ppermute | solution.py:338
  80.9 14.2 %all-gather = f32[448,512]{1,0:T(8,128)} all-gather(f32[112,512]{1,0:T(8,128)S(1)} %collective-permute-done.2.bundle_ref), channel_id=2, replica_groups=mesh['x'=4,'yz'=32,'zh'=2,'core'=2] {'x'}, dimensions={0}, use_global_device_ids=true | all-gather | bytes 1146880 | tf_op jit(solution)/shard_map/all_gather | solution.py:344
  95.1 4.1 %collective-permute-start.4 = (f32[4,112,512]{2,1,0:T(8,128)}, f32[4,112,512]{2,1,0:T(8,128)}, u32[]{:S(2)}, u32[]{:S(2)}) collective-permute-start(f32[4,112,512]{2,1,0:T(8,128)} %bitcast.7.far_ref), channel_id=1, source_target_pairs={{0,1},{1,0},{2,3},{3,2},{4,5},{5,4},{6,7},{7,6},{8,9},{9,8},{10,11... | collective-permute-start | bytes 2752520 | tf_op jit(solution)/shard_map/ppermute | solution.py:345
  99.2 1.9 %collective-permute-start.3 = (f32[400,528]{1,0:T(8,128)S(1)}, f32[400,528]{1,0:T(8,128)}, u32[]{:S(2)}, u32[]{:S(2)}) collective-permute-start(f32[400,528]{1,0:T(8,128)S(1)} %bitcast.21), channel_id=1, source_target_pairs={{0,1},{1,0},{2,3},{3,2},{4,5},{5,4},{6,7},{7,6},{8,9},{9,8},{10,11... | collective-permute-start | bytes 2534408 | tf_op jit(solution)/shard_map/ppermute | solution.py:339
  101.1 0.0 all-to-all-done.1
  101.1 2.4 %collective-permute-start = (f32[1664,128]{1,0:T(8,128)S(1)}, f32[1664,128]{1,0:T(8,128)S(1)}, u32[]{:S(2)}, u32[]{:S(2)}) collective-permute-start(f32[1664,128]{1,0:T(8,128)S(1)} %bitcast.11), channel_id=1, source_target_pairs={{0,1},{1,0},{2,3},{3,2},{4,5},{5,4},{6,7},{7,6},{8,9},{9,8},{10,11... | collective-permute-start | bytes 2555912 | tf_op jit(solution)/shard_map/ppermute | solution.py:346
  103.5 2.1 %collective-permute-start.1 = (f32[16,128]{1,0:T(8,128)S(1)}, f32[16,128]{1,0:T(8,128)S(1)}, u32[]{:S(2)}, u32[]{:S(2)}) collective-permute-start(f32[16,128]{1,0:T(8,128)S(1)} %given_kernel.1), channel_id=1, source_target_pairs={{0,2},{2,0},{1,3},{3,1},{4,6},{6,4},{5,7},{7,5},{8,10},{10,8},{9,1... | collective-permute-start | bytes 24584 | tf_op jit(solution)/shard_map/ppermute | solution.py:347
  105.7 0.0 collective-permute-done.3.near2_ref
  105.7 0.0 collective-permute-done.4.far2_ref
  105.7 11.0 %relations_kernel.1 = (f32[1024,400]{1,0:T(8,128)S(1)}, bf16[1024,400]{1,0:T(8,128)(2,1)S(1)}, bf16[1024,400]{1,0:T(8,128)(2,1)S(1)}, f32[512,400]{1,0:T(8,128)S...) custom-call(f32[400,512]{1,0:T(8,128)S(1)} %bitcast.17, ...), custom_call_target="tpu_custom_call" | custom-call | flops 10000000000 | bytes 4000000 | tf_op jit(solution)/shard_map/relations_kernel/pallas_call | solution.py:304
  116.7 0.0 collective-permute-done.theirs_ref
  116.7 5.6 %head_kernel.1.head_grad = f32[512,400]{1,0:T(8,128)S(1)} custom-call(f32[1664,128]{1,0:T(8,128)S(1)} %bitcast.14, f32[1664,128]{1,0:T(8,128)S(1)} %collective-permute-done.theirs_ref, f32[128,128]{1,0:T(8,128)S(1)} %copy-done.5, f32[128,128]{1,0:T(8,128)S(1)} %get-tuple-element.28.lists_theirs, f32[1024,400]{1,0:T(8,128)S(1)} %get-tuple-element.29.rel_ref, ...), custom_call_target="tpu_custom_call" | custom-call | flops 6000000000 | bytes 4000000 | tf_op jit(solution)/shard_map/head_kernel/pallas_call | solution.py:304
  122.3 0.0 collective-permute-done.1.given_ref
  122.3 8.7 %tail_kernel.1 = (f32[400,256]{1,0:T(8,128)S(1)}, f32[400,256]{1,0:T(8,128)S(1)}) custom-call(f32[1664,128]{1,0:T(8,128)S(1)} %bitcast.15, f32[1664,128]{1,0:T(8,128)S(1)} %collective-permute-done.theirs_ref, f32[16,128]{1,0:T(8,128)S(1)} %collective-permute-done.1.given_ref, f32[512,400]{1,0:T(8,128)S(1)} %get-tuple-element.23.rel_ref, ...), custom_call_target="tpu_custom_call" | custom-call | flops 8999999488 | bytes 4000000 | tf_op jit(solution)/shard_map/tail_kernel/pallas_call | solution.py:304
  131.0 0.0 copy-start.3
  131.0 1.9 %collective-permute-start.5 = (f32[400,256]{1,0:T(8,128)S(1)}, f32[400,256]{1,0:T(8,128)S(1)}, u32[]{:S(2)}, u32[]{:S(2)}) collective-permute-start(f32[400,256]{1,0:T(8,128)S(1)} %get-tuple-element.33), channel_id=1, source_target_pairs={{0,1},{1,0},{2,3},{3,2},{4,5},{5,4},{6,7},{7,6},{8,9},{9,8},{10,11... | collective-permute-start | bytes 1228808 | tf_op jit(solution)/shard_map/ppermute | solution.py:383
  133.0 1.7 %collective-permute-done.5 = f32[400,256]{1,0:T(8,128)S(1)} collective-permute-done((f32[400,256]{1,0:T(8,128)S(1)}, f32[400,256]{1,0:T(8,128)S(1)}, u32[]{:S(2)}, u32[]{:S(2)}) %collective-permute-start.5) | collective-permute-done | bytes 409632 | tf_op jit(solution)/shard_map/ppermute | solution.py:383
  134.7 0.1 add.6
  134.7 7.3 %collective-permute-start.6 = (f32[400,256]{1,0:T(8,128)S(1)}, f32[400,256]{1,0:T(8,128)S(1)}, u32[]{:S(2)}, u32[]{:S(2)}) collective-permute-start(f32[400,256]{1,0:T(8,128)S(1)} %add.6), channel_id=1, source_target_pairs={{0,2},{2,0},{1,3},{3,1},{4,6},{6,4},{5,7},{7,5},{8,10},{10,8},{9,1... | collective-permute-start | bytes 1228808 | tf_op jit(solution)/shard_map/ppermute | solution.py:384
  142.0 15.2 %collective-permute-done.6 = f32[400,256]{1,0:T(8,128)S(1)} collective-permute-done((f32[400,256]{1,0:T(8,128)S(1)}, f32[400,256]{1,0:T(8,128)S(1)}, u32[]{:S(2)}, u32[]{:S(2)}) %collective-permute-start.6) | collective-permute-done | bytes 409632 | tf_op jit(solution)/shard_map/ppermute | solution.py:384
  157.2 0.1 add.7.mine_ref
  157.2 2.4 %collective-permute-start.7 = (f32[400,256]{1,0:T(8,128)S(1)}, f32[400,256]{1,0:T(8,128)S(1)}, u32[]{:S(2)}, u32[]{:S(2)}) collective-permute-start(f32[400,256]{1,0:T(8,128)S(1)} %add.7.mine_ref), channel_id=1, source_target_pairs={{0,1},{1,0},{2,3},{3,2},{4,5},{5,4},{6,7},{7,6},{8,9},{9,8},{10,11... | collective-permute-start | bytes 1228808 | tf_op jit(solution)/shard_map/ppermute | solution.py:385
  159.7 1.4 collective-permute-done.7.theirs_ref
  161.0 1.2 update_kernel.1
  (10 shorter events, 0.0 us)
Async XLA Ops:
  3.0 44.5 %copy-start.1 = (f32[528,400]{0,1:T(8,128)S(1)}, f32[528,400]{0,1:T(8,128)}, u32[]{:S(2)}) copy-start(f32[528,400]{0,1:T(8,128)} %param.11) | copy-start | bytes 2534404
  3.0 44.5 %copy-start.2 = (f32[16,128]{1,0:T(8,128)S(1)}, f32[16,128]{1,0:T(8,128)}, u32[]{:S(2)}) copy-start(f32[16,128]{1,0:T(8,128)} %get-tuple-element.21.give_ref) | copy-start | bytes 24580
  36.3 0.7 copy-start.4
  38.7 67.1 %copy-start = (f32[512,400]{0,1:T(8,128)S(1)}, f32[512,400]{0,1:T(8,128)}, u32[]{:S(2)}) copy-start(f32[512,400]{0,1:T(8,128)} %param.9) | copy-start | bytes 2457604
  38.7 67.1 %copy-start.5 = (f32[128,128]{1,0:T(8,128)S(1)}, f32[128,128]{1,0:T(8,128)}, u32[]{:S(2)}) copy-start(f32[128,128]{1,0:T(8,128)} %get-tuple-element.20.cols_ref.lists_mine) | copy-start | bytes 196612
  38.7 62.4 %all-to-all-start.1 = ((f32[128,1,1664]{2,1,0:T(1,128)}), f32[128,1,1664]{2,1,0:T(1,128)S(1)}, u32[]{:S(2)}, u32[]{:S(2)}) async-start(f32[128,1,1664]{2,1,0:T(1,128)} %bitcast.4), calls=%async_computation.1 | async-start | bytes 1703936 | tf_op jit(solution)/shard_map/all_to_all | solution.py:342
  47.6 33.3 %collective-permute-start.2 = (f32[112,512]{1,0:T(8,128)S(1)}, f32[112,512]{1,0:T(8,128)S(1)}, u32[]{:S(2)}, u32[]{:S(2)}) collective-permute-start(f32[112,512]{1,0:T(8,128)S(1)} %bundle_kernel.1), channel_id=1, source_target_pairs={{0,2},{2,0},{1,3},{3,1},{4,6},{6,4},{5,7},{7,5},{8,10},{10,8},{9,1... | collective-permute-start | bytes 688136 | tf_op jit(solution)/shard_map/ppermute | solution.py:338
  95.1 10.6 %collective-permute-start.4 = (f32[4,112,512]{2,1,0:T(8,128)}, f32[4,112,512]{2,1,0:T(8,128)}, u32[]{:S(2)}, u32[]{:S(2)}) collective-permute-start(f32[4,112,512]{2,1,0:T(8,128)} %bitcast.7.far_ref), channel_id=1, source_target_pairs={{0,1},{1,0},{2,3},{3,2},{4,5},{5,4},{6,7},{7,6},{8,9},{9,8},{10,11... | collective-permute-start | bytes 2752520 | tf_op jit(solution)/shard_map/ppermute | solution.py:345
  99.2 6.5 %collective-permute-start.3 = (f32[400,528]{1,0:T(8,128)S(1)}, f32[400,528]{1,0:T(8,128)}, u32[]{:S(2)}, u32[]{:S(2)}) collective-permute-start(f32[400,528]{1,0:T(8,128)S(1)} %bitcast.21), channel_id=1, source_target_pairs={{0,1},{1,0},{2,3},{3,2},{4,5},{5,4},{6,7},{7,6},{8,9},{9,8},{10,11... | collective-permute-start | bytes 2534408 | tf_op jit(solution)/shard_map/ppermute | solution.py:339
  101.1 15.6 %collective-permute-start = (f32[1664,128]{1,0:T(8,128)S(1)}, f32[1664,128]{1,0:T(8,128)S(1)}, u32[]{:S(2)}, u32[]{:S(2)}) collective-permute-start(f32[1664,128]{1,0:T(8,128)S(1)} %bitcast.11), channel_id=1, source_target_pairs={{0,1},{1,0},{2,3},{3,2},{4,5},{5,4},{6,7},{7,6},{8,9},{9,8},{10,11... | collective-permute-start | bytes 2555912 | tf_op jit(solution)/shard_map/ppermute | solution.py:346
  103.5 18.7 %collective-permute-start.1 = (f32[16,128]{1,0:T(8,128)S(1)}, f32[16,128]{1,0:T(8,128)S(1)}, u32[]{:S(2)}, u32[]{:S(2)}) collective-permute-start(f32[16,128]{1,0:T(8,128)S(1)} %given_kernel.1), channel_id=1, source_target_pairs={{0,2},{2,0},{1,3},{3,1},{4,6},{6,4},{5,7},{7,5},{8,10},{10,8},{9,1... | collective-permute-start | bytes 24584 | tf_op jit(solution)/shard_map/ppermute | solution.py:347
  131.0 30.0 %copy-start.3 = (f32[512]{0:T(512)S(1)}, f32[512]{0:T(512)}, u32[]{:S(2)}) copy-start(f32[512]{0:T(512)} %param.10) | copy-start | bytes 6148
  131.0 3.6 %collective-permute-start.5 = (f32[400,256]{1,0:T(8,128)S(1)}, f32[400,256]{1,0:T(8,128)S(1)}, u32[]{:S(2)}, u32[]{:S(2)}) collective-permute-start(f32[400,256]{1,0:T(8,128)S(1)} %get-tuple-element.33), channel_id=1, source_target_pairs={{0,1},{1,0},{2,3},{3,2},{4,5},{5,4},{6,7},{7,6},{8,9},{9,8},{10,11... | collective-permute-start | bytes 1228808 | tf_op jit(solution)/shard_map/ppermute | solution.py:383
  134.7 22.4 %collective-permute-start.6 = (f32[400,256]{1,0:T(8,128)S(1)}, f32[400,256]{1,0:T(8,128)S(1)}, u32[]{:S(2)}, u32[]{:S(2)}) collective-permute-start(f32[400,256]{1,0:T(8,128)S(1)} %add.6), channel_id=1, source_target_pairs={{0,2},{2,0},{1,3},{3,1},{4,6},{6,4},{5,7},{7,5},{8,10},{10,8},{9,1... | collective-permute-start | bytes 1228808 | tf_op jit(solution)/shard_map/ppermute | solution.py:384
  157.2 3.8 %collective-permute-start.7 = (f32[400,256]{1,0:T(8,128)S(1)}, f32[400,256]{1,0:T(8,128)S(1)}, u32[]{:S(2)}, u32[]{:S(2)}) collective-permute-start(f32[400,256]{1,0:T(8,128)S(1)} %add.7.mine_ref), channel_id=1, source_target_pairs={{0,1},{1,0},{2,3},{3,2},{4,5},{5,4},{6,7},{7,6},{8,9},{9,8},{10,11... | collective-permute-start | bytes 1228808 | tf_op jit(solution)/shard_map/ppermute | solution.py:385

commit v6 on v5

--- a/solution.py
+++ b/solution.py
@@ -253,11 +253,12 @@
 
 def tail_kernel(
     mine_ref, theirs_ref, given_ref, rel_ref, entity_hi, entity_lo, table_hi, table_lo, head_grad,
-    keep_ref, send_ref, block_hi, block_lo,
+    keep0_ref, keep1_ref, send0_ref, send1_ref, block_hi, block_lo,
 ):
     zh, core = place()
     mine = read_rows(mine_ref, CHUNK2)
     fill_block(block_hi, block_lo, mine, read_rows(theirs_ref, CHUNK2), 2 * D)
+    keep_refs, send_refs = (keep0_ref, keep1_ref), (send0_ref, send1_ref)
     e_hi, e_lo = entity_hi[...], entity_lo[...]
     numbers = jnp.bitwise_xor(iota((128, ROWS), 1), core * HALF).astype(F32)
     rows_at = iota((ROWS, 128), 0).astype(F32)
@@ -285,13 +286,16 @@
         w_hi, w_lo = split2(weights)
         total = total + (dot_nn(w_lo, l_hi) + dot_nn(w_hi, l_lo) + dot_nn(w_hi, l_hi))
     first, second = total[0:HALF, :].T, total[HALF:ROWS, :].T
-    keep_ref[...] = jnp.where(core == 0, first, second)
-    send_ref[...] = jnp.where(core == 0, second, first)
-
-
-def update_kernel(mine_ref, theirs_ref, entity_ref, state_ref, updated_ref, accum_ref):
+    keep, send = jnp.where(core == 0, first, second), jnp.where(core == 0, second, first)
+    for k in range(2):
+        keep_refs[k][...] = keep[k * D // 2 : (k + 1) * D // 2, :]
+        send_refs[k][...] = send[k * D // 2 : (k + 1) * D // 2, :]
+
+
+def update_kernel(mine0_ref, mine1_ref, theirs0_ref, theirs1_ref, entity_ref, state_ref, updated_ref, accum_ref):
     _, core = place()
-    mine, theirs = mine_ref[...], theirs_ref[...]
+    mine = jnp.concatenate([mine0_ref[...], mine1_ref[...]], axis=0)
+    theirs = jnp.concatenate([theirs0_ref[...], theirs1_ref[...]], axis=0)
     for j, gradient in enumerate((jnp.where(core == 0, mine, theirs), jnp.where(core == 0, theirs, mine))):
         span = slice(HALF * j, HALF * (j + 1))
         accum = state_ref[:, span] + jnp.sum(gradient * gradient, axis=0, keepdims=True) / float(D)
@@ -337,6 +341,7 @@
 
     bundle = swap_zh(call(bundle_kernel, ((PIECE + 8, MAIN), F32), (relation_t, give), vmem=8))
     near2 = swap_core(relation_t)
+    spread, bundle = lax.optimization_barrier((spread, bundle))
 
     routed = call(route_kernel, ((128 * CHUNK2, 128), F32), (spread, matching), vmem=16)
     fetched = exchange(routed.reshape(128, 1, 128 * CHUNK2)).reshape(128 * CHUNK2, 128)
@@ -372,21 +377,21 @@
         scratch=block,
         cost=flops(6),
     )
-    keep, send = call(
+    parts = call(
         tail_kernel,
-        [((D, HALF), F32), ((D, HALF), F32)],
+        [((D // 2, HALF), F32)] * 4,
         (fetched, fetched_other, given, first_rel, entity_hi, entity_lo, table_hi, table_lo, head_grad),
         vmem=28,
         scratch=block,
         cost=flops(9),
     )
-    half = keep + swap_core(send)
-    half = half + swap_zh(half)
-    other = swap_core(half)
+    halves = [keep + swap_core(send) for keep, send in zip(parts[:2], parts[2:])]
+    halves = [half + swap_zh(half) for half in halves]
+    others = [swap_core(half) for half in halves]
     updated, accum = call(
         update_kernel,
         [((D, ROWS), F32), ((1, ROWS), F32)],
-        (half, other, entity_t, state.reshape(1, ROWS)),
+        (*halves, *others, entity_t, state.reshape(1, ROWS)),
         vmem=8,
     )
     return updated.T, accum.reshape(ROWS)

time: 163 us -> 153 us (0.939)
  the two profiles are of different devices: /device:TPU:1 before, /device:TPU:19 now
where the time goes in v6:
time: 153 us; the launch traced here: 152 us
  starting transfers between devices  79.9 us (52%)
  Pallas kernels  30.7 us (20%)
  waiting for transfers between devices  23.4 us (15%)
  blocking collectives  16.3 us (11%)
    pallas_call x8, Pallas kernels, call(): pl.pallas_call(kernel, out_shape=out_shape, in_specs=[pl.BlockSpec(memory...  30.7 us
    all_to_all x1, starting transfers between devices, shards(): exchange(routed.reshape(128, 1, 128 * CHUNK2)).reshape(128 * CHUNK2, 128)  16.6 us
    all_gather x1, blocking collectives, shards(): far = lax.all_gather(bundle, 'x', axis=0)  16.3 us
    all_to_all x1, starting transfers between devices, shards(): exchange(payload.reshape(128, 1, 128 * CHUNK1)).reshape(128 * CHUNK1, 128)  16.2 us
    ppermute x1, waiting for transfers between devices, shards(): swap_zh(call(bundle_kernel, ((PIECE + 8, MAIN), F32), (relation_t, give),...  13 us
    ppermute x2, starting transfers between devices, shards(): others = [swap_core(half) for half in halves]  9.81 us
    ppermute x2, waiting for transfers between devices, shards(): halves = [half + swap_zh(half) for half in halves]  9.32 us
    ppermute x2, starting transfers between devices, shards(): halves = [half + swap_zh(half) for half in halves]  9.19 us
  transfers between devices with their start and end apart: 13, of which 4 were waited for; matrix products, arithmetic and copies ran while one was open for 0% of the time, Pallas kernels for 11%

profile of v6, /device:TPU:19, one launch (start us, length us, event | category | flops | bytes accessed | tf_op | source)
XLA Modules:
  0.0 152.0 jit_solution(17281214944158819247)
XLA Ops:
  0.7 2.5 %pack_kernel.1 = (f32[896,128]{1,0:T(8,128)}, f32[128,128]{1,0:T(8,128)}, f32[16,128]{1,0:T(8,128)}) custom-call(f32[400,512]{1,0:T(8,128)} %bitcast.16, s32[2,1,1,512]{3,2,1,0:T(1,128)} %head_hbm.1, s32[2,1,1,512]{3,2,1,0:T(1,128)} %rel_hbm.1, s32[2,1,1,512]{3,2,1,0:T(1,128)} %tail_hbm.1, s32[2,1,1,320]{3,2,1,0:T(1,128)} %neg_hbm.1, s32[1,1,2]{2,1,0:T(1,128)} %bitcast.25), custom_call_target="tpu_custom_call" | custom-call | tf_op jit(solution)/shard_map/pack_kernel/pallas_call | solution.py:308
  3.1 16.2 %all-to-all-start = ((f32[128,1,896]{2,1,0:T(1,128)}), f32[128,1,896]{2,1,0:T(1,128)S(1)}, u32[]{:S(2)}, u32[]{:S(2)}) async-start(f32[128,1,896]{2,1,0:T(1,128)} %bitcast.24), calls=%async_computation | async-start | bytes 917504 | tf_op jit(solution)/shard_map/all_to_all | solution.py:340
  19.4 0.7 copy-done.2
  20.1 0.1 bundle_kernel.1
  20.1 7.9 %collective-permute-start = (f32[112,512]{1,0:T(8,128)S(1)}, f32[112,512]{1,0:T(8,128)S(1)}, u32[]{:S(2)}, u32[]{:S(2)}) collective-permute-start(f32[112,512]{1,0:T(8,128)S(1)} %bundle_kernel.1), channel_id=1, source_target_pairs={{0,2},{2,0},{1,3},{3,1},{4,6},{6,4},{5,7},{7,5},{8,10},{10,8},{9,1... | collective-permute-start | bytes 688136 | tf_op jit(solution)/shard_map/ppermute | solution.py:342
  28.1 13.0 %collective-permute-done.bundle_ref = f32[112,512]{1,0:T(8,128)S(1)} collective-permute-done((f32[112,512]{1,0:T(8,128)S(1)}, f32[112,512]{1,0:T(8,128)S(1)}, u32[]{:S(2)}, u32[]{:S(2)}) %collective-permute-start) | collective-permute-done | bytes 229408 | tf_op jit(solution)/shard_map/ppermute | solution.py:342
  41.1 1.7 %route_kernel.1 = f32[1664,128]{1,0:T(8,128)} custom-call(f32[896,128]{1,0:T(8,128)S(1)} %bitcast.19, s32[2,128]{1,0:T(2,128)S(1)} %copy-done.4), custom_call_target="tpu_custom_call" | custom-call | tf_op jit(solution)/shard_map/route_kernel/pallas_call | solution.py:308
  42.8 16.6 %all-to-all-start.1 = ((f32[128,1,1664]{2,1,0:T(1,128)}), f32[128,1,1664]{2,1,0:T(1,128)S(1)}, u32[]{:S(2)}, u32[]{:S(2)}) async-start(f32[128,1,1664]{2,1,0:T(1,128)} %bitcast.5), calls=%async_computation.1 | async-start | bytes 1703936 | tf_op jit(solution)/shard_map/all_to_all | solution.py:347
  59.4 16.3 %all-gather = f32[448,512]{1,0:T(8,128)} all-gather(f32[112,512]{1,0:T(8,128)S(1)} %collective-permute-done.bundle_ref), channel_id=2, replica_groups=mesh['x'=4,'yz'=32,'zh'=2,'core'=2] {'x'}, dimensions={0}, use_global_device_ids=true | all-gather | bytes 1146880 | tf_op jit(solution)/shard_map/all_gather | solution.py:349
  75.7 5.8 %collective-permute-start.4 = (f32[4,112,512]{2,1,0:T(8,128)}, f32[4,112,512]{2,1,0:T(8,128)}, u32[]{:S(2)}, u32[]{:S(2)}) collective-permute-start(f32[4,112,512]{2,1,0:T(8,128)} %bitcast.7.far_ref), channel_id=1, source_target_pairs={{0,1},{1,0},{2,3},{3,2},{4,5},{5,4},{6,7},{7,6},{8,9},{9,8},{10,11... | collective-permute-start | bytes 2752520 | tf_op jit(solution)/shard_map/ppermute | solution.py:350
  81.5 1.9 %collective-permute-start.3 = (f32[400,528]{1,0:T(8,128)S(1)}, f32[400,528]{1,0:T(8,128)}, u32[]{:S(2)}, u32[]{:S(2)}) collective-permute-start(f32[400,528]{1,0:T(8,128)S(1)} %bitcast.21), channel_id=1, source_target_pairs={{0,1},{1,0},{2,3},{3,2},{4,5},{5,4},{6,7},{7,6},{8,9},{9,8},{10,11... | collective-permute-start | bytes 2534408 | tf_op jit(solution)/shard_map/ppermute | solution.py:343
  83.4 0.0 all-to-all-done.1
  83.4 4.0 %collective-permute-start.1 = (f32[1664,128]{1,0:T(8,128)S(1)}, f32[1664,128]{1,0:T(8,128)S(1)}, u32[]{:S(2)}, u32[]{:S(2)}) collective-permute-start(f32[1664,128]{1,0:T(8,128)S(1)} %bitcast.11), channel_id=1, source_target_pairs={{0,1},{1,0},{2,3},{3,2},{4,5},{5,4},{6,7},{7,6},{8,9},{9,8},{10,11... | collective-permute-start | bytes 2555912 | tf_op jit(solution)/shard_map/ppermute | solution.py:351
  87.4 4.1 %collective-permute-start.2 = (f32[16,128]{1,0:T(8,128)S(1)}, f32[16,128]{1,0:T(8,128)S(1)}, u32[]{:S(2)}, u32[]{:S(2)}) collective-permute-start(f32[16,128]{1,0:T(8,128)S(1)} %given_kernel.1), channel_id=1, source_target_pairs={{0,2},{2,0},{1,3},{3,1},{4,6},{6,4},{5,7},{7,5},{8,10},{10,8},{9,1... | collective-permute-start | bytes 24584 | tf_op jit(solution)/shard_map/ppermute | solution.py:352
  91.6 0.0 collective-permute-done.3.near2_ref
  91.6 0.0 collective-permute-done.4.far2_ref
  91.6 11.0 %relations_kernel.1 = (f32[1024,400]{1,0:T(8,128)S(1)}, bf16[1024,400]{1,0:T(8,128)(2,1)S(1)}, bf16[1024,400]{1,0:T(8,128)(2,1)S(1)}, f32[512,400]{1,0:T(8,128)S...) custom-call(f32[400,512]{1,0:T(8,128)S(1)} %bitcast.17, ...), custom_call_target="tpu_custom_call" | custom-call | flops 10000000000 | bytes 4000000 | tf_op jit(solution)/shard_map/relations_kernel/pallas_call | solution.py:308
  102.6 0.0 collective-permute-done.1.theirs_ref
  102.6 5.6 %head_kernel.1.head_grad = f32[512,400]{1,0:T(8,128)S(1)} custom-call(f32[1664,128]{1,0:T(8,128)S(1)} %bitcast.14, f32[1664,128]{1,0:T(8,128)S(1)} %collective-permute-done.1.theirs_ref, f32[128,128]{1,0:T(8,128)S(1)} %copy-done.5, f32[128,128]{1,0:T(8,128)S(1)} %get-tuple-element.34.lists_theirs, f32[1024,400]{1,0:T(8,128)S(1)} %get-tuple-element.35.rel_ref, ...), custom_call_target="tpu_custom_call" | custom-call | flops 6000000000 | bytes 4000000 | tf_op jit(solution)/shard_map/head_kernel/pallas_call | solution.py:308
  108.2 0.0 collective-permute-done.2.given_ref
  108.2 8.7 %tail_kernel.1 = (f32[200,256]{1,0:T(8,128)S(1)}, f32[200,256]{1,0:T(8,128)S(1)}, f32[200,256]{1,0:T(8,128)S(1)}, f32[200,256]{1,0:T(8,128)S(1)}) custom-call(f32[1664,128]{1,0:T(8,128)S(1)} %bitcast.15, f32[1664,128]{1,0:T(8,128)S(1)} %collective-permute-done.1.theirs_ref, f32[16,128]{1,0:T(8,128)S(1)} %collective-permute-done.2.given_ref, ...), custom_call_target="tpu_custom_call" | custom-call | flops 8999999488 | bytes 4000000 | tf_op jit(solution)/shard_map/tail_kernel/pallas_call | solution.py:308
  116.9 0.0 copy-start.3
  116.9 2.2 %collective-permute-start.7 = (f32[200,256]{1,0:T(8,128)S(1)}, f32[200,256]{1,0:T(8,128)S(1)}, u32[]{:S(2)}, u32[]{:S(2)}) collective-permute-start(f32[200,256]{1,0:T(8,128)S(1)} %get-tuple-element.41), channel_id=1, source_target_pairs={{0,1},{1,0},{2,3},{3,2},{4,5},{5,4},{6,7},{7,6},{8,9},{9,8},{10,11... | collective-permute-start | bytes 614408 | tf_op jit(solution)/shard_map/ppermute | solution.py:388
  119.1 2.1 %collective-permute-start.5 = (f32[200,256]{1,0:T(8,128)S(1)}, f32[200,256]{1,0:T(8,128)S(1)}, u32[]{:S(2)}, u32[]{:S(2)}) collective-permute-start(f32[200,256]{1,0:T(8,128)S(1)} %get-tuple-element.39), channel_id=1, source_target_pairs={{0,1},{1,0},{2,3},{3,2},{4,5},{5,4},{6,7},{7,6},{8,9},{9,8},{10,11... | collective-permute-start | bytes 614408 | tf_op jit(solution)/shard_map/ppermute | solution.py:388
  121.3 5.3 %collective-permute-start.8 = (f32[200,256]{1,0:T(8,128)S(1)}, f32[200,256]{1,0:T(8,128)S(1)}, u32[]{:S(2)}, u32[]{:S(2)}) collective-permute-start(f32[200,256]{1,0:T(8,128)S(1)} %add.14), channel_id=1, source_target_pairs={{0,2},{2,0},{1,3},{3,1},{4,6},{6,4},{5,7},{7,5},{8,10},{10,8},{9,1... | collective-permute-start | bytes 614408 | tf_op jit(solution)/shard_map/ppermute | solution.py:389
  126.7 3.9 %collective-permute-start.6 = (f32[200,256]{1,0:T(8,128)S(1)}, f32[200,256]{1,0:T(8,128)S(1)}, u32[]{:S(2)}, u32[]{:S(2)}) collective-permute-start(f32[200,256]{1,0:T(8,128)S(1)} %add.12), channel_id=1, source_target_pairs={{0,2},{2,0},{1,3},{3,1},{4,6},{6,4},{5,7},{7,5},{8,10},{10,8},{9,1... | collective-permute-start | bytes 614408 | tf_op jit(solution)/shard_map/ppermute | solution.py:389
  130.6 6.0 %collective-permute-done.8 = f32[200,256]{1,0:T(8,128)S(1)} collective-permute-done((f32[200,256]{1,0:T(8,128)S(1)}, f32[200,256]{1,0:T(8,128)S(1)}, u32[]{:S(2)}, u32[]{:S(2)}) %collective-permute-start.8) | collective-permute-done | bytes 204832 | tf_op jit(solution)/shard_map/ppermute | solution.py:389
  136.6 6.7 %collective-permute-start.10 = (f32[200,256]{1,0:T(8,128)S(1)}, f32[200,256]{1,0:T(8,128)S(1)}, u32[]{:S(2)}, u32[]{:S(2)}) collective-permute-start(f32[200,256]{1,0:T(8,128)S(1)} %add.15.mine1_ref), channel_id=1, source_target_pairs={{0,1},{1,0},{2,3},{3,2},{4,5},{5,4},{6,7},{7,6},{8,9},{9,8},{10,11... | collective-permute-start | bytes 614408 | tf_op jit(solution)/shard_map/ppermute | solution.py:390
  143.4 3.3 %collective-permute-done.6 = f32[200,256]{1,0:T(8,128)S(1)} collective-permute-done((f32[200,256]{1,0:T(8,128)S(1)}, f32[200,256]{1,0:T(8,128)S(1)}, u32[]{:S(2)}, u32[]{:S(2)}) %collective-permute-start.6) | collective-permute-done | bytes 204832 | tf_op jit(solution)/shard_map/ppermute | solution.py:389
  146.7 3.1 %collective-permute-start.9 = (f32[200,256]{1,0:T(8,128)S(1)}, f32[200,256]{1,0:T(8,128)S(1)}, u32[]{:S(2)}, u32[]{:S(2)}) collective-permute-start(f32[200,256]{1,0:T(8,128)S(1)} %add.13.mine0_ref), channel_id=1, source_target_pairs={{0,1},{1,0},{2,3},{3,2},{4,5},{5,4},{6,7},{7,6},{8,9},{9,8},{10,11... | collective-permute-start | bytes 614408 | tf_op jit(solution)/shard_map/ppermute | solution.py:390
  149.8 1.0 collective-permute-done.9.theirs0_ref
  150.9 1.2 update_kernel.1
  (19 shorter events, 0.2 us)
Async XLA Ops:
  0.6 18.7 %copy-start.1 = (f32[528,400]{0,1:T(8,128)S(1)}, f32[528,400]{0,1:T(8,128)}, u32[]{:S(2)}) copy-start(f32[528,400]{0,1:T(8,128)} %param.11) | copy-start | bytes 2534404
  0.6 40.5 %copy-start.4 = (s32[2,128]{1,0:T(2,128)S(1)}, s32[2,128]{1,0:T(2,128)}, u32[]{:S(2)}) copy-start(s32[2,128]{1,0:T(2,128)} %matching_ref.1) | copy-start | bytes 3076
  3.1 38.0 %all-to-all-start = ((f32[128,1,896]{2,1,0:T(1,128)}), f32[128,1,896]{2,1,0:T(1,128)S(1)}, u32[]{:S(2)}, u32[]{:S(2)}) async-start(f32[128,1,896]{2,1,0:T(1,128)} %bitcast.24), calls=%async_computation | async-start | bytes 917504 | tf_op jit(solution)/shard_map/all_to_all | solution.py:340
  19.4 0.7 copy-start.2
  20.1 21.0 %collective-permute-start = (f32[112,512]{1,0:T(8,128)S(1)}, f32[112,512]{1,0:T(8,128)S(1)}, u32[]{:S(2)}, u32[]{:S(2)}) collective-permute-start(f32[112,512]{1,0:T(8,128)S(1)} %bundle_kernel.1), channel_id=1, source_target_pairs={{0,2},{2,0},{1,3},{3,1},{4,6},{6,4},{5,7},{7,5},{8,10},{10,8},{9,1... | collective-permute-start | bytes 688136 | tf_op jit(solution)/shard_map/ppermute | solution.py:342
  42.8 48.8 %copy-start = (f32[512,400]{0,1:T(8,128)S(1)}, f32[512,400]{0,1:T(8,128)}, u32[]{:S(2)}) copy-start(f32[512,400]{0,1:T(8,128)} %param.9) | copy-start | bytes 2457604
  42.8 48.8 %copy-start.5 = (f32[128,128]{1,0:T(8,128)S(1)}, f32[128,128]{1,0:T(8,128)}, u32[]{:S(2)}) copy-start(f32[128,128]{1,0:T(8,128)} %get-tuple-element.26.cols_ref.lists_mine) | copy-start | bytes 196612
  42.8 40.6 %all-to-all-start.1 = ((f32[128,1,1664]{2,1,0:T(1,128)}), f32[128,1,1664]{2,1,0:T(1,128)S(1)}, u32[]{:S(2)}, u32[]{:S(2)}) async-start(f32[128,1,1664]{2,1,0:T(1,128)} %bitcast.5), calls=%async_computation.1 | async-start | bytes 1703936 | tf_op jit(solution)/shard_map/all_to_all | solution.py:347
  75.7 15.9 %collective-permute-start.4 = (f32[4,112,512]{2,1,0:T(8,128)}, f32[4,112,512]{2,1,0:T(8,128)}, u32[]{:S(2)}, u32[]{:S(2)}) collective-permute-start(f32[4,112,512]{2,1,0:T(8,128)} %bitcast.7.far_ref), channel_id=1, source_target_pairs={{0,1},{1,0},{2,3},{3,2},{4,5},{5,4},{6,7},{7,6},{8,9},{9,8},{10,11... | collective-permute-start | bytes 2752520 | tf_op jit(solution)/shard_map/ppermute | solution.py:350
  81.5 10.1 %collective-permute-start.3 = (f32[400,528]{1,0:T(8,128)S(1)}, f32[400,528]{1,0:T(8,128)}, u32[]{:S(2)}, u32[]{:S(2)}) collective-permute-start(f32[400,528]{1,0:T(8,128)S(1)} %bitcast.21), channel_id=1, source_target_pairs={{0,1},{1,0},{2,3},{3,2},{4,5},{5,4},{6,7},{7,6},{8,9},{9,8},{10,11... | collective-permute-start | bytes 2534408 | tf_op jit(solution)/shard_map/ppermute | solution.py:343
  83.4 19.2 %collective-permute-start.1 = (f32[1664,128]{1,0:T(8,128)S(1)}, f32[1664,128]{1,0:T(8,128)S(1)}, u32[]{:S(2)}, u32[]{:S(2)}) collective-permute-start(f32[1664,128]{1,0:T(8,128)S(1)} %bitcast.11), channel_id=1, source_target_pairs={{0,1},{1,0},{2,3},{3,2},{4,5},{5,4},{6,7},{7,6},{8,9},{9,8},{10,11... | collective-permute-start | bytes 2555912 | tf_op jit(solution)/shard_map/ppermute | solution.py:351
  87.4 20.8 %collective-permute-start.2 = (f32[16,128]{1,0:T(8,128)S(1)}, f32[16,128]{1,0:T(8,128)S(1)}, u32[]{:S(2)}, u32[]{:S(2)}) collective-permute-start(f32[16,128]{1,0:T(8,128)S(1)} %given_kernel.1), channel_id=1, source_target_pairs={{0,2},{2,0},{1,3},{3,1},{4,6},{6,4},{5,7},{7,5},{8,10},{10,8},{9,1... | collective-permute-start | bytes 24584 | tf_op jit(solution)/shard_map/ppermute | solution.py:352
  116.9 33.9 %copy-start.3 = (f32[512]{0:T(512)S(1)}, f32[512]{0:T(512)}, u32[]{:S(2)}) copy-start(f32[512]{0:T(512)} %param.10) | copy-start | bytes 6148
  116.9 4.3 %collective-permute-start.7 = (f32[200,256]{1,0:T(8,128)S(1)}, f32[200,256]{1,0:T(8,128)S(1)}, u32[]{:S(2)}, u32[]{:S(2)}) collective-permute-start(f32[200,256]{1,0:T(8,128)S(1)} %get-tuple-element.41), channel_id=1, source_target_pairs={{0,1},{1,0},{2,3},{3,2},{4,5},{5,4},{6,7},{7,6},{8,9},{9,8},{10,11... | collective-permute-start | bytes 614408 | tf_op jit(solution)/shard_map/ppermute | solution.py:388
  119.1 7.5 %collective-permute-start.5 = (f32[200,256]{1,0:T(8,128)S(1)}, f32[200,256]{1,0:T(8,128)S(1)}, u32[]{:S(2)}, u32[]{:S(2)}) collective-permute-start(f32[200,256]{1,0:T(8,128)S(1)} %get-tuple-element.39), channel_id=1, source_target_pairs={{0,1},{1,0},{2,3},{3,2},{4,5},{5,4},{6,7},{7,6},{8,9},{9,8},{10,11... | collective-permute-start | bytes 614408 | tf_op jit(solution)/shard_map/ppermute | solution.py:388
  121.3 15.3 %collective-permute-start.8 = (f32[200,256]{1,0:T(8,128)S(1)}, f32[200,256]{1,0:T(8,128)S(1)}, u32[]{:S(2)}, u32[]{:S(2)}) collective-permute-start(f32[200,256]{1,0:T(8,128)S(1)} %add.14), channel_id=1, source_target_pairs={{0,2},{2,0},{1,3},{3,1},{4,6},{6,4},{5,7},{7,5},{8,10},{10,8},{9,1... | collective-permute-start | bytes 614408 | tf_op jit(solution)/shard_map/ppermute | solution.py:389
  126.7 20.0 %collective-permute-start.6 = (f32[200,256]{1,0:T(8,128)S(1)}, f32[200,256]{1,0:T(8,128)S(1)}, u32[]{:S(2)}, u32[]{:S(2)}) collective-permute-start(f32[200,256]{1,0:T(8,128)S(1)} %add.12), channel_id=1, source_target_pairs={{0,2},{2,0},{1,3},{3,1},{4,6},{6,4},{5,7},{7,5},{8,10},{10,8},{9,1... | collective-permute-start | bytes 614408 | tf_op jit(solution)/shard_map/ppermute | solution.py:389
  136.6 13.2 %collective-permute-start.10 = (f32[200,256]{1,0:T(8,128)S(1)}, f32[200,256]{1,0:T(8,128)S(1)}, u32[]{:S(2)}, u32[]{:S(2)}) collective-permute-start(f32[200,256]{1,0:T(8,128)S(1)} %add.15.mine1_ref), channel_id=1, source_target_pairs={{0,1},{1,0},{2,3},{3,2},{4,5},{5,4},{6,7},{7,6},{8,9},{9,8},{10,11... | collective-permute-start | bytes 614408 | tf_op jit(solution)/shard_map/ppermute | solution.py:390
  146.7 4.1 %collective-permute-start.9 = (f32[200,256]{1,0:T(8,128)S(1)}, f32[200,256]{1,0:T(8,128)S(1)}, u32[]{:S(2)}, u32[]{:S(2)}) collective-permute-start(f32[200,256]{1,0:T(8,128)S(1)} %add.13.mine0_ref), channel_id=1, source_target_pairs={{0,1},{1,0},{2,3},{3,2},{4,5},{5,4},{6,7},{7,6},{8,9},{9,8},{10,11... | collective-permute-start | bytes 614408 | tf_op jit(solution)/shard_map/ppermute | solution.py:390

commit v7 on v6

--- a/solution.py
+++ b/solution.py
@@ -158,50 +158,72 @@
     return jnp.concatenate([rows[:, 128 * g : 128 * (g + 1)] for g in range(4)], axis=0)
 
 
-def gather_relations(lists, zh, core, table_hi, table_lo):
-    rel_at = table_row(lists[:, 4:8].astype(jnp.int32), zh, core)
-    rels = onehot_cols(rel_at, 0, 4, iota((128, TABLE), 1))
-    return dot_nn(rels, table_hi[...]) + dot_nn(rels, table_lo[...])
+def store_relations(table_ref, first, rows):
+    padded = jnp.concatenate([rows, jnp.zeros((rows.shape[0], 512 - D), F32)], axis=1)
+    for k in range(4):
+        table_ref[pl.ds(4 * first + k, rows.shape[0], stride=4), :] = padded[:, 128 * k : 128 * (k + 1)]
+
+
+def load_indices(rels, zh, core, index_vmem, index_smem, sem):
+    rels = jnp.concatenate([rels, jnp.zeros((16 - rels.shape[0], 128), F32)], axis=0)
+    index_vmem[...] = table_row(rels.astype(jnp.int32), zh, core)
+    copy = pltpu.make_async_copy(index_vmem, index_smem, sem)
+    copy.start()
+    copy.wait()
+
+
+def gather_relations(table_ref, index_smem, first, out_ref):
+    def body(step, _):
+        for j in range(4):
+            for u in range(8):
+                lane = step * 8 + u
+                at = pl.multiple_of(4 * index_smem[first + j, lane], 4)
+                to = pl.multiple_of(512 * j + 4 * lane, 4)
+                out_ref[pl.ds(to, 4), :] = table_ref[pl.ds(at, 4), :]
+        return 0
+
+    lax.fori_loop(0, 16, body, 0)
+    return jnp.concatenate([out_ref[pl.ds(k, SLOTS, stride=4), :] for k in range(4)], axis=1)[:, 0:D]
+
+
+def gather_heads(lists, hi, lo):
+    heads = onehot_cols(lists, 0, 4, iota((128, ROWS), 1).astype(F32))
+    return dot_nn(heads, hi) + dot_nn(heads, lo)
 
 
 def relations_kernel(
     entity_ref, cols_ref, bundle_ref, near_ref, near2_ref, far_ref, far2_ref, fetched_ref,
-    rel_out, left_hi, left_lo, first_out, table_hi, table_lo, entity_hi, entity_lo, cols_out, far_table,
+    rel_out, left_hi, left_lo, first_out, table_ref, entity_hi, entity_lo, cols_out,
+    far_table, gathered, index_vmem, index_smem, sem,
 ):
     zh, core = place()
+    theirs = unfold(bundle_ref[PIECE + 4 : PIECE + 8, :])
+    chunk = fetched_ref[pl.ds(GIVEN_CHUNK, 128, stride=CHUNK2), :].T
+    rels = jnp.concatenate([cols_ref[...].T[4:8, :], theirs[4:8, :], chunk[FIRST + 4 : FIRST + 8, :]], axis=0)
+    load_indices(rels, zh, core, index_vmem, index_smem, sem)
     for k, ref in enumerate((near_ref, near2_ref)):
-        hi, lo = split2(ref[...].T)
-        table_hi[k * REL_DEV : (k + 1) * REL_DEV, :] = hi
-        table_lo[k * REL_DEV : (k + 1) * REL_DEV, :] = lo
+        store_relations(table_ref, k * REL_DEV, ref[...].T)
     for k, ref in enumerate((far_ref, far2_ref)):
         for spot in range(PIECES):
             far_table[k, piece_start(spot) : piece_start(spot) + PIECE, :] = ref[spot, 0:PIECE, :]
-        at = (2 + k) * REL_DEV
-        hi, lo = split2(far_table[k].T)
-        table_hi[at : at + MAIN, :] = hi
-        table_lo[at : at + MAIN, :] = lo
+        store_relations(table_ref, (2 + k) * REL_DEV, far_table[k].T)
         rest = [unfold(ref[spot, PIECE : PIECE + 4, :]) for spot in range(PIECES)]
         rest = [rest[spot][:, 0:PIECE] for spot in range(PIECES - 1)] + [rest[-1][:, PIECES * PIECE - D : PIECE]]
-        hi, lo = split2(jnp.concatenate(rest, axis=1))
-        table_hi[at + MAIN : at + REL_DEV, :] = hi
-        table_lo[at + MAIN : at + REL_DEV, :] = lo
+        store_relations(table_ref, (2 + k) * REL_DEV + MAIN, jnp.concatenate(rest, axis=1))
+    theirs = jnp.concatenate([theirs, jnp.zeros((128 - LIST, 128), F32)], axis=0).T
+    cols_out[...] = theirs
     hi, lo = split2(entity_ref[...].T)
     entity_hi[...] = hi
     entity_lo[...] = lo
-    own = iota((128, ROWS), 1).astype(F32)
-    theirs = jnp.concatenate([unfold(bundle_ref[PIECE + 4 : PIECE + 8, :]), jnp.zeros((128 - LIST, 128), F32)], axis=0).T
-    cols_out[...] = theirs
-    for k, lists in enumerate((cols_ref[:, 0:LIST], theirs[:, 0:LIST])):
-        heads = onehot_cols(lists, 0, 4, own)
-        head_rows = dot_nn(heads, hi) + dot_nn(heads, lo)
-        rel_rows = gather_relations(lists, zh, core, table_hi, table_lo)
+    for k in range(2):
+        head_rows = gather_heads((cols_ref, theirs)[k][:, 0:LIST], hi, lo)
+        rel_rows = gather_relations(table_ref, index_smem, 4 * k, gathered)
         l_hi, l_lo = split2(head_rows * rel_rows)
         span = pl.ds(k * SLOTS, SLOTS)
         rel_out[span, :] = rel_rows
         left_hi[span, :] = l_hi
         left_lo[span, :] = l_lo
-    chunk = fetched_ref[pl.ds(GIVEN_CHUNK, 128, stride=CHUNK2), :]
-    first_out[...] = gather_relations(chunk[:, FIRST : FIRST + LIST], zh, core, table_hi, table_lo)
+    first_out[...] = gather_relations(table_ref, index_smem, 8, gathered)
 
 
 def fill_block(hi_ref, lo_ref, mine, theirs, first):
@@ -252,8 +274,8 @@
 
 
 def tail_kernel(
-    mine_ref, theirs_ref, given_ref, rel_ref, entity_hi, entity_lo, table_hi, table_lo, head_grad,
-    keep0_ref, keep1_ref, send0_ref, send1_ref, block_hi, block_lo,
+    mine_ref, theirs_ref, given_ref, rel_ref, entity_hi, entity_lo, table_ref, head_grad,
+    keep0_ref, keep1_ref, send0_ref, send1_ref, block_hi, block_lo, gathered, index_vmem, index_smem, sem,
 ):
     zh, core = place()
     mine = read_rows(mine_ref, CHUNK2)
@@ -269,7 +291,8 @@
             rel_rows = rel_ref[...]
         else:
             lists = jnp.concatenate([given_ref[...], jnp.zeros((128 - LIST, 128), F32)], axis=0).T[:, 0:LIST]
-            rel_rows = gather_relations(lists, zh, core, table_hi, table_lo)
+            load_indices(given_ref[4:8, :], zh, core, index_vmem, index_smem, sem)
+            rel_rows = gather_relations(table_ref, index_smem, 0, gathered)
         heads = onehot_cols(lists, 0, 4, numbers)
         head_rows = dot_nn(heads, block_hi[...]) + dot_nn(heads, block_lo[...])
         l_hi, l_lo = split2(head_rows * rel_rows)
@@ -350,23 +373,28 @@
     far2 = swap_core(far)
     fetched_other = swap_core(fetched)
     given = swap_zh(call(given_kernel, ((LIST, 128), F32), (fetched,), vmem=4))
-    rel_rows, left_hi, left_lo, first_rel, table_hi, table_lo, entity_hi, entity_lo, cols_other = call(
+    gather = [
+        pltpu.VMEM((4 * SLOTS, 128), F32),
+        pltpu.VMEM((16, 128), jnp.int32),
+        pltpu.SMEM((16, 128), jnp.int32),
+        pltpu.SemaphoreType.DMA,
+    ]
+    rel_rows, left_hi, left_lo, first_rel, table, entity_hi, entity_lo, cols_other = call(
         relations_kernel,
         [
             ((2 * SLOTS, D), F32),
             ((2 * SLOTS, D), BF16),
             ((2 * SLOTS, D), BF16),
             ((SLOTS, D), F32),
-            ((TABLE, D), BF16),
-            ((TABLE, D), BF16),
+            ((4 * TABLE, 128), F32),
             ((ROWS, D), BF16),
             ((ROWS, D), BF16),
             ((128, 128), F32),
         ],
         (entity_t, cols, bundle, relation_t, near2, far, far2, fetched),
         vmem=32,
-        scratch=[pltpu.VMEM((2, D, MAIN), F32)],
-        cost=flops(10),
+        scratch=[pltpu.VMEM((2, D, MAIN), F32)] + gather,
+        cost=flops(6),
     )
     block = [pltpu.VMEM((ROWS, D), BF16), pltpu.VMEM((ROWS, D), BF16)]
     head_grad = call(
@@ -380,9 +408,9 @@
     parts = call(
         tail_kernel,
         [((D // 2, HALF), F32)] * 4,
-        (fetched, fetched_other, given, first_rel, entity_hi, entity_lo, table_hi, table_lo, head_grad),
+        (fetched, fetched_other, given, first_rel, entity_hi, entity_lo, table, head_grad),
         vmem=28,
-        scratch=block,
+        scratch=block + gather,
         cost=flops(9),
     )
     halves = [keep + swap_core(send) for keep, send in zip(parts[:2], parts[2:])]

time: 153 us -> 149 us (0.974)
  the two profiles are of different devices: /device:TPU:19 before, /device:TPU:1 now
where the time goes in v7:
time: 149 us; the launch traced here: 147 us
  starting transfers between devices  75.5 us (51%)
  Pallas kernels  27.6 us (19%)
  waiting for transfers between devices  23.2 us (16%)
  blocking collectives  16.6 us (11%)
  local copies, waits for them, and re-layouts  2.61 us (2%)
    pallas_call x8, Pallas kernels, call(): pl.pallas_call(kernel, out_shape=out_shape, in_specs=[pl.BlockSpec(memory...  27.6 us
    all_to_all x1, starting transfers between devices, shards(): exchange(payload.reshape(128, 1, 128 * CHUNK1)).reshape(128 * CHUNK1, 128)  17.9 us
    all_gather x1, blocking collectives, shards(): far = lax.all_gather(bundle, 'x', axis=0)  16.6 us
    ppermute x1, waiting for transfers between devices, shards(): swap_zh(call(bundle_kernel, ((PIECE + 8, MAIN), F32), (relation_t, give),...  15 us
    all_to_all x1, starting transfers between devices, shards(): exchange(routed.reshape(128, 1, 128 * CHUNK2)).reshape(128 * CHUNK2, 128)  13.5 us
    ppermute x2, starting transfers between devices, shards(): halves = [half + swap_zh(half) for half in halves]  9.19 us
    ppermute x2, starting transfers between devices, shards(): others = [swap_core(half) for half in halves]  8.58 us
    ppermute x1, starting transfers between devices, shards(): swap_zh(call(bundle_kernel, ((PIECE + 8, MAIN), F32), (relation_t, give),...  8.07 us
  transfers between devices with their start and end apart: 13, of which 4 were waited for; matrix products, arithmetic and copies ran while one was open for 0% of the time, Pallas kernels for 10%

profile of v7, /device:TPU:1, one launch (start us, length us, event | category | flops | bytes accessed | tf_op | source)
XLA Modules:
  0.0 146.5 jit_solution(5501858686884106812)
XLA Ops:
  0.6 2.4 %pack_kernel.1 = (f32[896,128]{1,0:T(8,128)}, f32[128,128]{1,0:T(8,128)}, f32[16,128]{1,0:T(8,128)}) custom-call(f32[400,512]{1,0:T(8,128)} %bitcast.16, s32[2,1,1,512]{3,2,1,0:T(1,128)} %head_hbm.1, s32[2,1,1,512]{3,2,1,0:T(1,128)} %rel_hbm.1, s32[2,1,1,512]{3,2,1,0:T(1,128)} %tail_hbm.1, s32[2,1,1,320]{3,2,1,0:T(1,128)} %neg_hbm.1, s32[1,1,2]{2,1,0:T(1,128)} %bitcast.25), custom_call_target="tpu_custom_call" | custom-call | tf_op jit(solution)/shard_map/pack_kernel/pallas_call | solution.py:331
  3.1 17.9 %all-to-all-start = ((f32[128,1,896]{2,1,0:T(1,128)}), f32[128,1,896]{2,1,0:T(1,128)S(1)}, u32[]{:S(2)}, u32[]{:S(2)}) async-start(f32[128,1,896]{2,1,0:T(1,128)} %bitcast.24), calls=%async_computation | async-start | bytes 917504 | tf_op jit(solution)/shard_map/all_to_all | solution.py:363
  21.0 0.0 copy-start.1
  21.0 1.2 copy-done.1
  22.2 0.7 copy-done.3
  22.9 0.1 bundle_kernel.1
  23.0 8.1 %collective-permute-start = (f32[112,512]{1,0:T(8,128)S(1)}, f32[112,512]{1,0:T(8,128)S(1)}, u32[]{:S(2)}, u32[]{:S(2)}) collective-permute-start(f32[112,512]{1,0:T(8,128)S(1)} %bundle_kernel.1), channel_id=1, source_target_pairs={{0,2},{2,0},{1,3},{3,1},{4,6},{6,4},{5,7},{7,5},{8,10},{10,8},{9,1... | collective-permute-start | bytes 688136 | tf_op jit(solution)/shard_map/ppermute | solution.py:365
  31.1 15.0 %collective-permute-done.bundle_ref = f32[112,512]{1,0:T(8,128)S(1)} collective-permute-done((f32[112,512]{1,0:T(8,128)S(1)}, f32[112,512]{1,0:T(8,128)S(1)}, u32[]{:S(2)}, u32[]{:S(2)}) %collective-permute-start) | collective-permute-done | bytes 229408 | tf_op jit(solution)/shard_map/ppermute | solution.py:365
  46.1 0.0 all-to-all-done
  46.1 0.7 copy-done.5
  46.7 1.7 %route_kernel.1 = f32[1664,128]{1,0:T(8,128)} custom-call(f32[896,128]{1,0:T(8,128)S(1)} %bitcast.19, s32[2,128]{1,0:T(2,128)S(1)} %copy-done.5), custom_call_target="tpu_custom_call" | custom-call | tf_op jit(solution)/shard_map/route_kernel/pallas_call | solution.py:331
  48.4 13.5 %all-to-all-start.1 = ((f32[128,1,1664]{2,1,0:T(1,128)}), f32[128,1,1664]{2,1,0:T(1,128)S(1)}, u32[]{:S(2)}, u32[]{:S(2)}) async-start(f32[128,1,1664]{2,1,0:T(1,128)} %bitcast.5), calls=%async_computation.1 | async-start | bytes 1703936 | tf_op jit(solution)/shard_map/all_to_all | solution.py:370
  61.9 16.6 %all-gather = f32[448,512]{1,0:T(8,128)} all-gather(f32[112,512]{1,0:T(8,128)S(1)} %collective-permute-done.bundle_ref), channel_id=2, replica_groups=mesh['x'=4,'yz'=32,'zh'=2,'core'=2] {'x'}, dimensions={0}, use_global_device_ids=true | all-gather | bytes 1146880 | tf_op jit(solution)/shard_map/all_gather | solution.py:372
  78.5 6.1 %collective-permute-start.4 = (f32[4,112,512]{2,1,0:T(8,128)}, f32[4,112,512]{2,1,0:T(8,128)}, u32[]{:S(2)}, u32[]{:S(2)}) collective-permute-start(f32[4,112,512]{2,1,0:T(8,128)} %bitcast.7.far_ref), channel_id=1, source_target_pairs={{0,1},{1,0},{2,3},{3,2},{4,5},{5,4},{6,7},{7,6},{8,9},{9,8},{10,11... | collective-permute-start | bytes 2752520 | tf_op jit(solution)/shard_map/ppermute | solution.py:373
  84.7 1.9 %collective-permute-start.3 = (f32[400,528]{1,0:T(8,128)S(1)}, f32[400,528]{1,0:T(8,128)}, u32[]{:S(2)}, u32[]{:S(2)}) collective-permute-start(f32[400,528]{1,0:T(8,128)S(1)} %bitcast.21), channel_id=1, source_target_pairs={{0,1},{1,0},{2,3},{3,2},{4,5},{5,4},{6,7},{7,6},{8,9},{9,8},{10,11... | collective-permute-start | bytes 2534408 | tf_op jit(solution)/shard_map/ppermute | solution.py:366
  86.6 0.0 all-to-all-done.1
  86.6 3.4 %collective-permute-start.1 = (f32[1664,128]{1,0:T(8,128)S(1)}, f32[1664,128]{1,0:T(8,128)S(1)}, u32[]{:S(2)}, u32[]{:S(2)}) collective-permute-start(f32[1664,128]{1,0:T(8,128)S(1)} %bitcast.11), channel_id=1, source_target_pairs={{0,1},{1,0},{2,3},{3,2},{4,5},{5,4},{6,7},{7,6},{8,9},{9,8},{10,11... | collective-permute-start | bytes 2555912 | tf_op jit(solution)/shard_map/ppermute | solution.py:374
  90.1 2.5 %collective-permute-start.2 = (f32[16,128]{1,0:T(8,128)S(1)}, f32[16,128]{1,0:T(8,128)S(1)}, u32[]{:S(2)}, u32[]{:S(2)}) collective-permute-start(f32[16,128]{1,0:T(8,128)S(1)} %given_kernel.1), channel_id=1, source_target_pairs={{0,2},{2,0},{1,3},{3,1},{4,6},{6,4},{5,7},{7,5},{8,10},{10,8},{9,1... | collective-permute-start | bytes 24584 | tf_op jit(solution)/shard_map/ppermute | solution.py:375
  92.6 9.0 %relations_kernel.1 = (f32[1024,400]{1,0:T(8,128)S(1)}, bf16[1024,400]{1,0:T(8,128)(2,1)S(1)}, bf16[1024,400]{1,0:T(8,128)(2,1)S(1)}, f32[512,400]{1,0:T(8,128)S...) custom-call(f32[400,512]{1,0:T(8,128)S(1)} %bitcast.17, ...), custom_call_target="tpu_custom_call" | custom-call | flops 6000000000 | bytes 4000000 | tf_op jit(solution)/shard_map/relations_kernel/pallas_call | solution.py:331
  101.6 5.6 %head_kernel.1.head_grad = f32[512,400]{1,0:T(8,128)S(1)} custom-call(f32[1664,128]{1,0:T(8,128)S(1)} %bitcast.14, f32[1664,128]{1,0:T(8,128)S(1)} %collective-permute-done.1.theirs_ref, f32[128,128]{1,0:T(8,128)S(1)} %copy-done.6, f32[128,128]{1,0:T(8,128)S(1)} %get-tuple-element.32.lists_theirs, f32[1024,400]{1,0:T(8,128)S(1)} %get-tuple-element.33.rel_ref, ...), custom_call_target="tpu_custom_call" | custom-call | flops 6000000000 | bytes 4000000 | tf_op jit(solution)/shard_map/head_kernel/pallas_call | solution.py:331
  107.2 0.0 copy-start.4
  107.2 7.6 %tail_kernel.1 = (f32[200,256]{1,0:T(8,128)S(1)}, f32[200,256]{1,0:T(8,128)S(1)}, f32[200,256]{1,0:T(8,128)S(1)}, f32[200,256]{1,0:T(8,128)S(1)}) custom-call(f32[1664,128]{1,0:T(8,128)S(1)} %bitcast.15, f32[1664,128]{1,0:T(8,128)S(1)} %collective-permute-done.1.theirs_ref, f32[16,128]{1,0:T(8,128)S(1)} %collective-permute-done.2.given_ref, ...), custom_call_target="tpu_custom_call" | custom-call | flops 8999999488 | bytes 4000000 | tf_op jit(solution)/shard_map/tail_kernel/pallas_call | solution.py:331
  114.8 2.2 %collective-permute-start.7 = (f32[200,256]{1,0:T(8,128)S(1)}, f32[200,256]{1,0:T(8,128)S(1)}, u32[]{:S(2)}, u32[]{:S(2)}) collective-permute-start(f32[200,256]{1,0:T(8,128)S(1)} %get-tuple-element.39), channel_id=1, source_target_pairs={{0,1},{1,0},{2,3},{3,2},{4,5},{5,4},{6,7},{7,6},{8,9},{9,8},{10,11... | collective-permute-start | bytes 614408 | tf_op jit(solution)/shard_map/ppermute | solution.py:416
  117.0 2.2 %collective-permute-start.5 = (f32[200,256]{1,0:T(8,128)S(1)}, f32[200,256]{1,0:T(8,128)S(1)}, u32[]{:S(2)}, u32[]{:S(2)}) collective-permute-start(f32[200,256]{1,0:T(8,128)S(1)} %get-tuple-element.37), channel_id=1, source_target_pairs={{0,1},{1,0},{2,3},{3,2},{4,5},{5,4},{6,7},{7,6},{8,9},{9,8},{10,11... | collective-permute-start | bytes 614408 | tf_op jit(solution)/shard_map/ppermute | solution.py:416
  119.2 7.0 %collective-permute-start.8 = (f32[200,256]{1,0:T(8,128)S(1)}, f32[200,256]{1,0:T(8,128)S(1)}, u32[]{:S(2)}, u32[]{:S(2)}) collective-permute-start(f32[200,256]{1,0:T(8,128)S(1)} %add.14), channel_id=1, source_target_pairs={{0,2},{2,0},{1,3},{3,1},{4,6},{6,4},{5,7},{7,5},{8,10},{10,8},{9,1... | collective-permute-start | bytes 614408 | tf_op jit(solution)/shard_map/ppermute | solution.py:417
  126.2 2.2 %collective-permute-start.6 = (f32[200,256]{1,0:T(8,128)S(1)}, f32[200,256]{1,0:T(8,128)S(1)}, u32[]{:S(2)}, u32[]{:S(2)}) collective-permute-start(f32[200,256]{1,0:T(8,128)S(1)} %add.12), channel_id=1, source_target_pairs={{0,2},{2,0},{1,3},{3,1},{4,6},{6,4},{5,7},{7,5},{8,10},{10,8},{9,1... | collective-permute-start | bytes 614408 | tf_op jit(solution)/shard_map/ppermute | solution.py:417
  128.4 3.0 %collective-permute-done.8 = f32[200,256]{1,0:T(8,128)S(1)} collective-permute-done((f32[200,256]{1,0:T(8,128)S(1)}, f32[200,256]{1,0:T(8,128)S(1)}, u32[]{:S(2)}, u32[]{:S(2)}) %collective-permute-start.8) | collective-permute-done | bytes 204832 | tf_op jit(solution)/shard_map/ppermute | solution.py:417
  131.4 5.1 %collective-permute-start.10 = (f32[200,256]{1,0:T(8,128)S(1)}, f32[200,256]{1,0:T(8,128)S(1)}, u32[]{:S(2)}, u32[]{:S(2)}) collective-permute-start(f32[200,256]{1,0:T(8,128)S(1)} %add.15.mine1_ref), channel_id=1, source_target_pairs={{0,1},{1,0},{2,3},{3,2},{4,5},{5,4},{6,7},{7,6},{8,9},{9,8},{10,11... | collective-permute-start | bytes 614408 | tf_op jit(solution)/shard_map/ppermute | solution.py:418
  136.5 4.2 %collective-permute-done.6 = f32[200,256]{1,0:T(8,128)S(1)} collective-permute-done((f32[200,256]{1,0:T(8,128)S(1)}, f32[200,256]{1,0:T(8,128)S(1)}, u32[]{:S(2)}, u32[]{:S(2)}) %collective-permute-start.6) | collective-permute-done | bytes 204832 | tf_op jit(solution)/shard_map/ppermute | solution.py:417
  140.8 3.5 %collective-permute-start.9 = (f32[200,256]{1,0:T(8,128)S(1)}, f32[200,256]{1,0:T(8,128)S(1)}, u32[]{:S(2)}, u32[]{:S(2)}) collective-permute-start(f32[200,256]{1,0:T(8,128)S(1)} %add.13.mine0_ref), channel_id=1, source_target_pairs={{0,1},{1,0},{2,3},{3,2},{4,5},{5,4},{6,7},{7,6},{8,9},{9,8},{10,11... | collective-permute-start | bytes 614408 | tf_op jit(solution)/shard_map/ppermute | solution.py:418
  144.3 1.0 collective-permute-done.9.theirs0_ref
  145.3 1.2 update_kernel.1
  (21 shorter events, 0.2 us)
Async XLA Ops:
  0.6 91.9 %copy-start = (f32[512,400]{0,1:T(8,128)S(1)}, f32[512,400]{0,1:T(8,128)}, u32[]{:S(2)}) copy-start(f32[512,400]{0,1:T(8,128)} %param.9) | copy-start | bytes 2457604
  3.1 89.5 %copy-start.6 = (f32[128,128]{1,0:T(8,128)S(1)}, f32[128,128]{1,0:T(8,128)}, u32[]{:S(2)}) copy-start(f32[128,128]{1,0:T(8,128)} %get-tuple-element.25.cols_ref.lists_mine) | copy-start | bytes 196612
  3.1 43.0 %all-to-all-start = ((f32[128,1,896]{2,1,0:T(1,128)}), f32[128,1,896]{2,1,0:T(1,128)S(1)}, u32[]{:S(2)}, u32[]{:S(2)}) async-start(f32[128,1,896]{2,1,0:T(1,128)} %bitcast.24), calls=%async_computation | async-start | bytes 917504 | tf_op jit(solution)/shard_map/all_to_all | solution.py:363
  21.0 1.2 copy-start.1
  22.2 0.7 copy-start.3
  22.9 61.7 %copy-start.2 = (f32[528,400]{0,1:T(8,128)S(1)}, f32[528,400]{0,1:T(8,128)}, u32[]{:S(2)}) copy-start(f32[528,400]{0,1:T(8,128)} %param.11) | copy-start | bytes 2534404
  23.0 23.0 %collective-permute-start = (f32[112,512]{1,0:T(8,128)S(1)}, f32[112,512]{1,0:T(8,128)S(1)}, u32[]{:S(2)}, u32[]{:S(2)}) collective-permute-start(f32[112,512]{1,0:T(8,128)S(1)} %bundle_kernel.1), channel_id=1, source_target_pairs={{0,2},{2,0},{1,3},{3,1},{4,6},{6,4},{5,7},{7,5},{8,10},{10,8},{9,1... | collective-permute-start | bytes 688136 | tf_op jit(solution)/shard_map/ppermute | solution.py:365
  46.1 0.7 copy-start.5
  48.4 38.2 %all-to-all-start.1 = ((f32[128,1,1664]{2,1,0:T(1,128)}), f32[128,1,1664]{2,1,0:T(1,128)S(1)}, u32[]{:S(2)}, u32[]{:S(2)}) async-start(f32[128,1,1664]{2,1,0:T(1,128)} %bitcast.5), calls=%async_computation.1 | async-start | bytes 1703936 | tf_op jit(solution)/shard_map/all_to_all | solution.py:370
  78.5 14.1 %collective-permute-start.4 = (f32[4,112,512]{2,1,0:T(8,128)}, f32[4,112,512]{2,1,0:T(8,128)}, u32[]{:S(2)}, u32[]{:S(2)}) collective-permute-start(f32[4,112,512]{2,1,0:T(8,128)} %bitcast.7.far_ref), channel_id=1, source_target_pairs={{0,1},{1,0},{2,3},{3,2},{4,5},{5,4},{6,7},{7,6},{8,9},{9,8},{10,11... | collective-permute-start | bytes 2752520 | tf_op jit(solution)/shard_map/ppermute | solution.py:373
  84.7 7.9 %collective-permute-start.3 = (f32[400,528]{1,0:T(8,128)S(1)}, f32[400,528]{1,0:T(8,128)}, u32[]{:S(2)}, u32[]{:S(2)}) collective-permute-start(f32[400,528]{1,0:T(8,128)S(1)} %bitcast.21), channel_id=1, source_target_pairs={{0,1},{1,0},{2,3},{3,2},{4,5},{5,4},{6,7},{7,6},{8,9},{9,8},{10,11... | collective-permute-start | bytes 2534408 | tf_op jit(solution)/shard_map/ppermute | solution.py:366
  86.6 15.0 %collective-permute-start.1 = (f32[1664,128]{1,0:T(8,128)S(1)}, f32[1664,128]{1,0:T(8,128)S(1)}, u32[]{:S(2)}, u32[]{:S(2)}) collective-permute-start(f32[1664,128]{1,0:T(8,128)S(1)} %bitcast.11), channel_id=1, source_target_pairs={{0,1},{1,0},{2,3},{3,2},{4,5},{5,4},{6,7},{7,6},{8,9},{9,8},{10,11... | collective-permute-start | bytes 2555912 | tf_op jit(solution)/shard_map/ppermute | solution.py:374
  90.1 17.1 %collective-permute-start.2 = (f32[16,128]{1,0:T(8,128)S(1)}, f32[16,128]{1,0:T(8,128)S(1)}, u32[]{:S(2)}, u32[]{:S(2)}) collective-permute-start(f32[16,128]{1,0:T(8,128)S(1)} %given_kernel.1), channel_id=1, source_target_pairs={{0,2},{2,0},{1,3},{3,1},{4,6},{6,4},{5,7},{7,5},{8,10},{10,8},{9,1... | collective-permute-start | bytes 24584 | tf_op jit(solution)/shard_map/ppermute | solution.py:375
  107.2 38.2 %copy-start.4 = (f32[512]{0:T(512)S(1)}, f32[512]{0:T(512)}, u32[]{:S(2)}) copy-start(f32[512]{0:T(512)} %param.10) | copy-start | bytes 6148
  114.8 4.3 %collective-permute-start.7 = (f32[200,256]{1,0:T(8,128)S(1)}, f32[200,256]{1,0:T(8,128)S(1)}, u32[]{:S(2)}, u32[]{:S(2)}) collective-permute-start(f32[200,256]{1,0:T(8,128)S(1)} %get-tuple-element.39), channel_id=1, source_target_pairs={{0,1},{1,0},{2,3},{3,2},{4,5},{5,4},{6,7},{7,6},{8,9},{9,8},{10,11... | collective-permute-start | bytes 614408 | tf_op jit(solution)/shard_map/ppermute | solution.py:416
  117.0 9.2 %collective-permute-start.5 = (f32[200,256]{1,0:T(8,128)S(1)}, f32[200,256]{1,0:T(8,128)S(1)}, u32[]{:S(2)}, u32[]{:S(2)}) collective-permute-start(f32[200,256]{1,0:T(8,128)S(1)} %get-tuple-element.37), channel_id=1, source_target_pairs={{0,1},{1,0},{2,3},{3,2},{4,5},{5,4},{6,7},{7,6},{8,9},{9,8},{10,11... | collective-permute-start | bytes 614408 | tf_op jit(solution)/shard_map/ppermute | solution.py:416
  119.2 12.2 %collective-permute-start.8 = (f32[200,256]{1,0:T(8,128)S(1)}, f32[200,256]{1,0:T(8,128)S(1)}, u32[]{:S(2)}, u32[]{:S(2)}) collective-permute-start(f32[200,256]{1,0:T(8,128)S(1)} %add.14), channel_id=1, source_target_pairs={{0,2},{2,0},{1,3},{3,1},{4,6},{6,4},{5,7},{7,5},{8,10},{10,8},{9,1... | collective-permute-start | bytes 614408 | tf_op jit(solution)/shard_map/ppermute | solution.py:417
  126.2 14.6 %collective-permute-start.6 = (f32[200,256]{1,0:T(8,128)S(1)}, f32[200,256]{1,0:T(8,128)S(1)}, u32[]{:S(2)}, u32[]{:S(2)}) collective-permute-start(f32[200,256]{1,0:T(8,128)S(1)} %add.12), channel_id=1, source_target_pairs={{0,2},{2,0},{1,3},{3,1},{4,6},{6,4},{5,7},{7,5},{8,10},{10,8},{9,1... | collective-permute-start | bytes 614408 | tf_op jit(solution)/shard_map/ppermute | solution.py:417
  131.4 12.9 %collective-permute-start.10 = (f32[200,256]{1,0:T(8,128)S(1)}, f32[200,256]{1,0:T(8,128)S(1)}, u32[]{:S(2)}, u32[]{:S(2)}) collective-permute-start(f32[200,256]{1,0:T(8,128)S(1)} %add.15.mine1_ref), channel_id=1, source_target_pairs={{0,1},{1,0},{2,3},{3,2},{4,5},{5,4},{6,7},{7,6},{8,9},{9,8},{10,11... | collective-permute-start | bytes 614408 | tf_op jit(solution)/shard_map/ppermute | solution.py:418
  140.8 4.5 %collective-permute-start.9 = (f32[200,256]{1,0:T(8,128)S(1)}, f32[200,256]{1,0:T(8,128)S(1)}, u32[]{:S(2)}, u32[]{:S(2)}) collective-permute-start(f32[200,256]{1,0:T(8,128)S(1)} %add.13.mine0_ref), channel_id=1, source_target_pairs={{0,1},{1,0},{2,3},{3,2},{4,5},{5,4},{6,7},{7,6},{8,9},{9,8},{10,11... | collective-permute-start | bytes 614408 | tf_op jit(solution)/shard_map/ppermute | solution.py:418

commit v8 on v7

--- a/solution.py
+++ b/solution.py
@@ -169,7 +169,7 @@
     index_vmem[...] = table_row(rels.astype(jnp.int32), zh, core)
     copy = pltpu.make_async_copy(index_vmem, index_smem, sem)
     copy.start()
-    copy.wait()
+    return copy
 
 
 def gather_relations(table_ref, index_smem, first, out_ref):
@@ -192,33 +192,40 @@
 
 
 def relations_kernel(
-    entity_ref, cols_ref, bundle_ref, near_ref, near2_ref, far_ref, far2_ref, fetched_ref,
+    entity_ref, cols_ref, bundle_ref, near_ref, near2_hbm, far_hbm, far2_hbm, fetched_ref,
     rel_out, left_hi, left_lo, first_out, table_ref, entity_hi, entity_lo, cols_out,
-    far_table, gathered, index_vmem, index_smem, sem,
+    near2_ref, far_ref, far2_ref, far_table, gathered, index_vmem, index_smem, sem, sems,
 ):
     zh, core = place()
+    pairs = ((near2_hbm, near2_ref), (far_hbm, far_ref), (far2_hbm, far2_ref))
+    copies = [pltpu.make_async_copy(a, b, sems.at[i]) for i, (a, b) in enumerate(pairs)]
+    for copy in copies:
+        copy.start()
     theirs = unfold(bundle_ref[PIECE + 4 : PIECE + 8, :])
     chunk = fetched_ref[pl.ds(GIVEN_CHUNK, 128, stride=CHUNK2), :].T
     rels = jnp.concatenate([cols_ref[...].T[4:8, :], theirs[4:8, :], chunk[FIRST + 4 : FIRST + 8, :]], axis=0)
-    load_indices(rels, zh, core, index_vmem, index_smem, sem)
-    for k, ref in enumerate((near_ref, near2_ref)):
-        store_relations(table_ref, k * REL_DEV, ref[...].T)
+    indices = load_indices(rels, zh, core, index_vmem, index_smem, sem)
+    theirs = jnp.concatenate([theirs, jnp.zeros((128 - LIST, 128), F32)], axis=0).T
+    cols_out[...] = theirs
+    hi, lo = split2(entity_ref[...].T)
+    entity_hi[...] = hi
+    entity_lo[...] = lo
+    head_rows = [gather_heads(lists[:, 0:LIST], hi, lo) for lists in (cols_ref, theirs)]
+    store_relations(table_ref, 0, near_ref[...].T)
+    copies[0].wait()
+    store_relations(table_ref, REL_DEV, near2_ref[...].T)
     for k, ref in enumerate((far_ref, far2_ref)):
+        copies[1 + k].wait()
         for spot in range(PIECES):
             far_table[k, piece_start(spot) : piece_start(spot) + PIECE, :] = ref[spot, 0:PIECE, :]
         store_relations(table_ref, (2 + k) * REL_DEV, far_table[k].T)
         rest = [unfold(ref[spot, PIECE : PIECE + 4, :]) for spot in range(PIECES)]
         rest = [rest[spot][:, 0:PIECE] for spot in range(PIECES - 1)] + [rest[-1][:, PIECES * PIECE - D : PIECE]]
         store_relations(table_ref, (2 + k) * REL_DEV + MAIN, jnp.concatenate(rest, axis=1))
-    theirs = jnp.concatenate([theirs, jnp.zeros((128 - LIST, 128), F32)], axis=0).T
-    cols_out[...] = theirs
-    hi, lo = split2(entity_ref[...].T)
-    entity_hi[...] = hi
-    entity_lo[...] = lo
+    indices.wait()
     for k in range(2):
-        head_rows = gather_heads((cols_ref, theirs)[k][:, 0:LIST], hi, lo)
         rel_rows = gather_relations(table_ref, index_smem, 4 * k, gathered)
-        l_hi, l_lo = split2(head_rows * rel_rows)
+        l_hi, l_lo = split2(head_rows[k] * rel_rows)
         span = pl.ds(k * SLOTS, SLOTS)
         rel_out[span, :] = rel_rows
         left_hi[span, :] = l_hi
@@ -237,82 +244,93 @@
     return jnp.concatenate([lists, jnp.zeros((128, 128 - LIST), F32)], axis=1).T
 
 
-def head_kernel(mine_ref, theirs_ref, lists_mine, lists_theirs, rel_ref, left_hi, left_lo, grad_ref, block_hi, block_lo):
-    _, core = place()
-    fill_block(block_hi, block_lo, read_rows(mine_ref, CHUNK2), read_rows(theirs_ref, CHUNK2), 0)
+def given_kernel(fetched_ref, out_ref):
+    out_ref[...] = fetched_ref[pl.ds(GIVEN_CHUNK, 128, stride=CHUNK2), :].T[FIRST + LIST : FIRST + 2 * LIST, :]
+
+
+def softmax_weights(scores, times, tails, axis):
+    scores = jnp.where(times > 0.0, scores, -3.0e38)
+    weights = times * jnp.exp(scores - jnp.max(scores, axis=axis, keepdims=True))
+    return split2(weights / jnp.sum(weights, axis=axis, keepdims=True) - tails)
+
+
+def weights_kernel(
+    mine_ref, theirs_ref, given_ref, cols_mine, cols_theirs, left_hi, left_lo, rel_ref, entity_hi, entity_lo, table_ref,
+    head_hi, head_lo, tail_hi, tail_lo, source_hi, source_lo, block_hi, block_lo,
+    other_hi, other_lo, gathered, index_vmem, index_smem, sem,
+):
+    zh, core = place()
+    indices = load_indices(given_ref[4:8, :], zh, core, index_vmem, index_smem, sem)
+    mine, theirs = read_rows(mine_ref, CHUNK2), read_rows(theirs_ref, CHUNK2)
+    fill_block(block_hi, block_lo, mine, theirs, 0)
+    fill_block(other_hi, other_lo, mine, theirs, 2 * D)
     numbers = jnp.bitwise_xor(iota((128, ROWS), 1), core * HALF).astype(F32)
-    heads_at = iota((ROWS, 128), 0).astype(F32)
-    total = None
+    rows_at = iota((ROWS, 128), 0).astype(F32)
+    b_hi, b_lo = block_hi[...], block_lo[...]
+    e_hi, e_lo = entity_hi[...], entity_lo[...]
     for k in range(2):
-        lists = (lists_mine, lists_theirs)[k][:, 0:LIST]
+        lists = (cols_mine, cols_theirs)[k][:, 0:LIST]
         span = pl.ds(k * SLOTS, SLOTS)
         hi, lo = left_hi[span, :], left_lo[span, :]
-        b_hi, b_lo = block_hi[...], block_lo[...]
         scores = dot_nt(hi, b_lo) + dot_nt(lo, b_hi) + dot_nt(hi, b_hi)
         tails = jnp.concatenate(
             [jnp.where(lists[:, 8 + j : 9 + j] == numbers, 1.0, 0.0) for j in range(4)], axis=0
         )
         drawn = sum(jnp.where(lists[:, 12 + j : 13 + j] == numbers, 1.0, 0.0) for j in range(3))
         times = jnp.sum(drawn, axis=0, keepdims=True) + tails
-        scores = jnp.where(times > 0.0, scores, -3.0e38)
-        weights = times * jnp.exp(scores - jnp.max(scores, axis=1, keepdims=True))
-        weights = weights / jnp.sum(weights, axis=1, keepdims=True) - tails
-        w_hi, w_lo = split2(weights)
-        grad_left = dot_nn(w_hi, b_lo) + dot_nn(w_lo, b_hi) + dot_nn(w_hi, b_hi)
-        g_hi, g_lo = split2(grad_left * rel_ref[span, :])
-        rows = lists_rows(lists)
-        marks = jnp.concatenate(
-            [jnp.where(rows[j : j + 1, :] == heads_at, 1.0, 0.0) for j in range(4)], axis=1
-        ).astype(BF16)
-        part = dot_nn(marks, g_lo) + dot_nn(marks, g_hi)
-        total = part if total is None else total + part
-    grad_ref[...] = total
-
-
-def given_kernel(fetched_ref, out_ref):
-    out_ref[...] = fetched_ref[pl.ds(GIVEN_CHUNK, 128, stride=CHUNK2), :].T[FIRST + LIST : FIRST + 2 * LIST, :]
-
-
-def tail_kernel(
-    mine_ref, theirs_ref, given_ref, rel_ref, entity_hi, entity_lo, table_ref, head_grad,
-    keep0_ref, keep1_ref, send0_ref, send1_ref, block_hi, block_lo, gathered, index_vmem, index_smem, sem,
-):
-    zh, core = place()
-    mine = read_rows(mine_ref, CHUNK2)
-    fill_block(block_hi, block_lo, mine, read_rows(theirs_ref, CHUNK2), 2 * D)
-    keep_refs, send_refs = (keep0_ref, keep1_ref), (send0_ref, send1_ref)
-    e_hi, e_lo = entity_hi[...], entity_lo[...]
-    numbers = jnp.bitwise_xor(iota((128, ROWS), 1), core * HALF).astype(F32)
-    rows_at = iota((ROWS, 128), 0).astype(F32)
-    total = head_grad[...]
+        w_hi, w_lo = softmax_weights(scores, times, tails, 1)
+        head_hi[span, :] = w_hi
+        head_lo[span, :] = w_lo
     for k in range(2):
+        span = pl.ds(k * SLOTS, SLOTS)
         if k == 0:
             lists = mine[:, 4 * D : 4 * D + LIST]
             rel_rows = rel_ref[...]
         else:
             lists = jnp.concatenate([given_ref[...], jnp.zeros((128 - LIST, 128), F32)], axis=0).T[:, 0:LIST]
-            load_indices(given_ref[4:8, :], zh, core, index_vmem, index_smem, sem)
+            indices.wait()
             rel_rows = gather_relations(table_ref, index_smem, 0, gathered)
         heads = onehot_cols(lists, 0, 4, numbers)
-        head_rows = dot_nn(heads, block_hi[...]) + dot_nn(heads, block_lo[...])
-        l_hi, l_lo = split2(head_rows * rel_rows)
-        scores = dot_nt(e_lo, l_hi) + dot_nt(e_hi, l_lo) + dot_nt(e_hi, l_hi)
+        hi, lo = split2((dot_nn(heads, other_hi[...]) + dot_nn(heads, other_lo[...])) * rel_rows)
+        source_hi[span, :] = hi
+        source_lo[span, :] = lo
+        scores = dot_nt(e_lo, hi) + dot_nt(e_hi, lo) + dot_nt(e_hi, hi)
         rows = lists_rows(lists)
         tails = jnp.concatenate(
             [jnp.where(rows[8 + j : 9 + j, :] == rows_at, 1.0, 0.0) for j in range(4)], axis=1
         )
         drawn = sum(jnp.where(rows[12 + j : 13 + j, :] == rows_at, 1.0, 0.0) for j in range(3))
         times = jnp.sum(drawn, axis=1, keepdims=True) + tails
-        scores = jnp.where(times > 0.0, scores, -3.0e38)
-        weights = times * jnp.exp(scores - jnp.max(scores, axis=0, keepdims=True))
-        weights = weights / jnp.sum(weights, axis=0, keepdims=True) - tails
-        w_hi, w_lo = split2(weights)
-        total = total + (dot_nn(w_lo, l_hi) + dot_nn(w_hi, l_lo) + dot_nn(w_hi, l_hi))
-    first, second = total[0:HALF, :].T, total[HALF:ROWS, :].T
-    keep, send = jnp.where(core == 0, first, second), jnp.where(core == 0, second, first)
+        w_hi, w_lo = softmax_weights(scores, times, tails, 0)
+        tail_hi[span, :] = w_hi
+        tail_lo[span, :] = w_lo
+
+
+def gradient_kernel(
+    first, last, cols_mine, cols_theirs, rel_ref, head_hi, head_lo, tail_hi, tail_lo, source_hi, source_lo, block_hi, block_lo,
+    keep_ref, send_ref,
+):
+    _, core = place()
+    heads_at = iota((ROWS, 128), 0).astype(F32)
+    b_hi, b_lo = block_hi[:, first:last], block_lo[:, first:last]
+    total = None
     for k in range(2):
-        keep_refs[k][...] = keep[k * D // 2 : (k + 1) * D // 2, :]
-        send_refs[k][...] = send[k * D // 2 : (k + 1) * D // 2, :]
+        span = pl.ds(k * SLOTS, SLOTS)
+        w_hi, w_lo = head_hi[span, :], head_lo[span, :]
+        grad_left = dot_nn(w_hi, b_lo) + dot_nn(w_lo, b_hi) + dot_nn(w_hi, b_hi)
+        g_hi, g_lo = split2(grad_left * rel_ref[span, first:last])
+        rows = lists_rows((cols_mine, cols_theirs)[k][:, 0:LIST])
+        marks = jnp.concatenate(
+            [jnp.where(rows[j : j + 1, :] == heads_at, 1.0, 0.0).astype(BF16) for j in range(4)], axis=1
+        )
+        part = dot_nn(marks, g_lo) + dot_nn(marks, g_hi)
+        hi, lo = source_hi[span, first:last], source_lo[span, first:last]
+        w_hi, w_lo = tail_hi[span, :], tail_lo[span, :]
+        part = part + (dot_nn(w_lo, hi) + dot_nn(w_hi, lo) + dot_nn(w_hi, hi))
+        total = part if total is None else total + part
+    one, two = total[0:HALF, :].T, total[HALF:ROWS, :].T
+    keep_ref[...] = jnp.where(core == 0, one, two)
+    send_ref[...] = jnp.where(core == 0, two, one)
 
 
 def update_kernel(mine0_ref, mine1_ref, theirs0_ref, theirs1_ref, entity_ref, state_ref, updated_ref, accum_ref):
@@ -326,17 +344,17 @@
         updated_ref[:, span] = entity_ref[:, span] - LEARN_RATE * gradient / jnp.sqrt(accum)
 
 
-def call(kernel, out_shape, args, vmem, scratch=(), cost=None, space=pltpu.VMEM):
+def call(kernel, out_shape, args, vmem, scratch=(), cost=None, space=pltpu.VMEM, in_hbm=()):
     out_shape = jax.tree.map(lambda s: jax.ShapeDtypeStruct(*s), out_shape, is_leaf=lambda s: isinstance(s, tuple))
     return pl.pallas_call(
         kernel,
         out_shape=out_shape,
-        in_specs=[pl.BlockSpec(memory_space=space) for _ in args],
+        in_specs=[pl.BlockSpec(memory_space=pltpu.HBM if i in in_hbm else space) for i in range(len(args))],
         out_specs=jax.tree.map(lambda _: pl.BlockSpec(memory_space=pltpu.VMEM), out_shape),
         scratch_shapes=list(scratch),
         compiler_params=pltpu.CompilerParams(vmem_limit_bytes=vmem * MIB),
         cost_estimate=cost,
-        name=kernel.__name__,
+        name=getattr(kernel, "func", kernel).__name__,
     )(*args)
 
 
@@ -379,12 +397,13 @@
         pltpu.SMEM((16, 128), jnp.int32),
         pltpu.SemaphoreType.DMA,
     ]
+    wide, square = (2 * SLOTS, D), (2 * SLOTS, ROWS)
     rel_rows, left_hi, left_lo, first_rel, table, entity_hi, entity_lo, cols_other = call(
         relations_kernel,
         [
-            ((2 * SLOTS, D), F32),
-            ((2 * SLOTS, D), BF16),
-            ((2 * SLOTS, D), BF16),
+            (wide, F32),
+            (wide, BF16),
+            (wide, BF16),
             ((SLOTS, D), F32),
             ((4 * TABLE, 128), F32),
             ((ROWS, D), BF16),
@@ -393,29 +412,39 @@
         ],
         (entity_t, cols, bundle, relation_t, near2, far, far2, fetched),
         vmem=32,
-        scratch=[pltpu.VMEM((2, D, MAIN), F32)] + gather,
-        cost=flops(6),
-    )
-    block = [pltpu.VMEM((ROWS, D), BF16), pltpu.VMEM((ROWS, D), BF16)]
-    head_grad = call(
-        head_kernel,
-        ((ROWS, D), F32),
-        (fetched, fetched_other, cols, cols_other, rel_rows, left_hi, left_lo),
-        vmem=20,
-        scratch=block,
-        cost=flops(6),
-    )
-    parts = call(
-        tail_kernel,
-        [((D // 2, HALF), F32)] * 4,
-        (fetched, fetched_other, given, first_rel, entity_hi, entity_lo, table, head_grad),
-        vmem=28,
-        scratch=block + gather,
-        cost=flops(9),
-    )
-    halves = [keep + swap_core(send) for keep, send in zip(parts[:2], parts[2:])]
-    halves = [half + swap_zh(half) for half in halves]
-    others = [swap_core(half) for half in halves]
+        scratch=[pltpu.VMEM((D, REL_DEV), F32)]
+        + [pltpu.VMEM((PIECES, PIECE + 8, MAIN), F32)] * 2
+        + [pltpu.VMEM((2, D, MAIN), F32)]
+        + gather
+        + [pltpu.SemaphoreType.DMA((3,))],
+        cost=flops(8),
+        in_hbm=(4, 5, 6),
+    )
+    weights = call(
+        weights_kernel,
+        [(square, BF16)] * 4 + [(wide, BF16)] * 2 + [((ROWS, D), BF16)] * 2,
+        (fetched, fetched_other, given, cols, cols_other, left_hi, left_lo, first_rel, entity_hi, entity_lo, table),
+        vmem=32,
+        scratch=[pltpu.VMEM((ROWS, D), BF16)] * 2 + gather,
+        cost=flops(8),
+    )
+    halves, others = [], []
+    for first, last in ((0, 256), (256, D)):
+        keep, send = call(
+            functools.partial(gradient_kernel, first, last),
+            [((last - first, HALF), F32)] * 2,
+            (cols, cols_other, rel_rows, *weights),
+            vmem=28,
+            cost=flops(3),
+        )
+        recv = swap_core(send)
+        if first == 0:
+            recv, first_weight = lax.optimization_barrier((recv, weights[0]))
+            weights = (first_weight, *weights[1:])
+        half = keep + recv
+        half = half + swap_zh(half)
+        halves.append(half)
+        others.append(swap_core(half))
     updated, accum = call(
         update_kernel,
         [((D, ROWS), F32), ((1, ROWS), F32)],

time: 149 us -> 149 us (level)
  waiting for transfers between devices: 23.2 us -> 26.1 us
  starting transfers between devices: 75.5 us -> 72.8 us
    ppermute x6, waiting for transfers between devices: 8.24 us -> 11.1 us  [the longest x2 8 us: shards(): half = half + swap_zh(half)]
    ppermute x6, starting transfers between devices: 22.1 us -> 19.3 us  [the longest x2 9.49 us: shards(): half = half + swap_zh(half)]
    pallas_call x8 -> x9, Pallas kernels: 27.6 us -> 27.8 us  [call(): pl.pallas_call(kernel, out_shape=out_shape, in_specs=[pl.BlockSpec(memory...]
  transfers between devices with their start and end apart: 13 -> 13, of which waited for: 4 -> 5; matrix products, arithmetic and copies ran while one was open for 0% -> 0% of each run, Pallas kernels for 10% -> 7%
where the time goes in v8:
time: 149 us; the launch traced here: 147 us
  starting transfers between devices  72.8 us (49%)
  Pallas kernels  27.8 us (19%)
  waiting for transfers between devices  26.1 us (18%)
  blocking collectives  16.6 us (11%)
  local copies, waits for them, and re-layouts  2.61 us (2%)
    pallas_call x9, Pallas kernels, call(): pl.pallas_call(kernel, out_shape=out_shape, in_specs=[pl.BlockSpec(memory...  27.8 us
    all_to_all x1, starting transfers between devices, shards(): exchange(payload.reshape(128, 1, 128 * CHUNK1)).reshape(128 * CHUNK1, 128)  17.9 us
    all_gather x1, blocking collectives, shards(): far = lax.all_gather(bundle, 'x', axis=0)  16.6 us
    ppermute x1, waiting for transfers between devices, shards(): swap_zh(call(bundle_kernel, ((PIECE + 8, MAIN), F32), (relation_t, give),...  15 us
    all_to_all x1, starting transfers between devices, shards(): exchange(routed.reshape(128, 1, 128 * CHUNK2)).reshape(128 * CHUNK2, 128)  13.5 us
    ppermute x2, starting transfers between devices, shards(): half = half + swap_zh(half)  9.49 us
    ppermute x1, starting transfers between devices, shards(): swap_zh(call(bundle_kernel, ((PIECE + 8, MAIN), F32), (relation_t, give),...  8.07 us
    ppermute x2, waiting for transfers between devices, shards(): half = half + swap_zh(half)  8 us
  transfers between devices with their start and end apart: 13, of which 5 were waited for; matrix products, arithmetic and copies ran while one was open for 0% of the time, Pallas kernels for 7%

profile of v8, /device:TPU:1, one launch (start us, length us, event | category | flops | bytes accessed | tf_op | source)
XLA Modules:
  0.0 146.9 jit_solution(15504016316168599437)
XLA Ops:
  0.6 2.4 %pack_kernel.1 = (f32[896,128]{1,0:T(8,128)}, f32[128,128]{1,0:T(8,128)}, f32[16,128]{1,0:T(8,128)}) custom-call(f32[400,512]{1,0:T(8,128)} %bitcast.15, s32[2,1,1,512]{3,2,1,0:T(1,128)} %head_hbm.1, s32[2,1,1,512]{3,2,1,0:T(1,128)} %rel_hbm.1, s32[2,1,1,512]{3,2,1,0:T(1,128)} %tail_hbm.1, s32[2,1,1,320]{3,2,1,0:T(1,128)} %neg_hbm.1, s32[1,1,2]{2,1,0:T(1,128)} %bitcast.24), custom_call_target="tpu_custom_call" | custom-call | tf_op jit(solution)/shard_map/pack_kernel/pallas_call | solution.py:349
  3.1 17.9 %all-to-all-start = ((f32[128,1,896]{2,1,0:T(1,128)}), f32[128,1,896]{2,1,0:T(1,128)S(1)}, u32[]{:S(2)}, u32[]{:S(2)}) async-start(f32[128,1,896]{2,1,0:T(1,128)} %bitcast.23), calls=%async_computation | async-start | bytes 917504 | tf_op jit(solution)/shard_map/all_to_all | solution.py:381
  21.0 0.0 copy-start.1
  21.0 1.2 copy-done.1
  22.2 0.7 copy-done.3
  22.9 0.1 bundle_kernel.1
  23.0 8.1 %collective-permute-start = (f32[112,512]{1,0:T(8,128)S(1)}, f32[112,512]{1,0:T(8,128)S(1)}, u32[]{:S(2)}, u32[]{:S(2)}) collective-permute-start(f32[112,512]{1,0:T(8,128)S(1)} %bundle_kernel.1), channel_id=1, source_target_pairs={{0,2},{2,0},{1,3},{3,1},{4,6},{6,4},{5,7},{7,5},{8,10},{10,8},{9,1... | collective-permute-start | bytes 688136 | tf_op jit(solution)/shard_map/ppermute | solution.py:383
  31.1 15.0 %collective-permute-done.bundle_ref = f32[112,512]{1,0:T(8,128)S(1)} collective-permute-done((f32[112,512]{1,0:T(8,128)S(1)}, f32[112,512]{1,0:T(8,128)S(1)}, u32[]{:S(2)}, u32[]{:S(2)}) %collective-permute-start) | collective-permute-done | bytes 229408 | tf_op jit(solution)/shard_map/ppermute | solution.py:383
  46.1 0.7 copy-done.5
  46.7 1.7 %route_kernel.1 = f32[1664,128]{1,0:T(8,128)} custom-call(f32[896,128]{1,0:T(8,128)S(1)} %bitcast.18, s32[2,128]{1,0:T(2,128)S(1)} %copy-done.5), custom_call_target="tpu_custom_call" | custom-call | tf_op jit(solution)/shard_map/route_kernel/pallas_call | solution.py:349
  48.4 13.5 %all-to-all-start.1 = ((f32[128,1,1664]{2,1,0:T(1,128)}), f32[128,1,1664]{2,1,0:T(1,128)S(1)}, u32[]{:S(2)}, u32[]{:S(2)}) async-start(f32[128,1,1664]{2,1,0:T(1,128)} %bitcast.6), calls=%async_computation.1 | async-start | bytes 1703936 | tf_op jit(solution)/shard_map/all_to_all | solution.py:388
  61.9 16.6 %all-gather = f32[448,512]{1,0:T(8,128)} all-gather(f32[112,512]{1,0:T(8,128)S(1)} %collective-permute-done.bundle_ref), channel_id=2, replica_groups=mesh['x'=4,'yz'=32,'zh'=2,'core'=2] {'x'}, dimensions={0}, use_global_device_ids=true | all-gather | bytes 1146880 | tf_op jit(solution)/shard_map/all_gather | solution.py:390
  78.5 6.1 %collective-permute-start.2 = (f32[4,112,512]{2,1,0:T(8,128)}, f32[4,112,512]{2,1,0:T(8,128)}, u32[]{:S(2)}, u32[]{:S(2)}) collective-permute-start(f32[4,112,512]{2,1,0:T(8,128)} %bitcast.5.far_hbm), channel_id=1, source_target_pairs={{0,1},{1,0},{2,3},{3,2},{4,5},{5,4},{6,7},{7,6},{8,9},{9,8},{10,11... | collective-permute-start | bytes 2752520 | tf_op jit(solution)/shard_map/ppermute | solution.py:391
  84.6 1.9 %collective-permute-start.1 = (f32[400,528]{1,0:T(8,128)S(1)}, f32[400,528]{1,0:T(8,128)}, u32[]{:S(2)}, u32[]{:S(2)}) collective-permute-start(f32[400,528]{1,0:T(8,128)S(1)} %bitcast.20), channel_id=1, source_target_pairs={{0,1},{1,0},{2,3},{3,2},{4,5},{5,4},{6,7},{7,6},{8,9},{9,8},{10,11... | collective-permute-start | bytes 2534408 | tf_op jit(solution)/shard_map/ppermute | solution.py:384
  86.6 3.4 %collective-permute-start.3 = (f32[1664,128]{1,0:T(8,128)S(1)}, f32[1664,128]{1,0:T(8,128)S(1)}, u32[]{:S(2)}, u32[]{:S(2)}) collective-permute-start(f32[1664,128]{1,0:T(8,128)S(1)} %bitcast.11), channel_id=1, source_target_pairs={{0,1},{1,0},{2,3},{3,2},{4,5},{5,4},{6,7},{7,6},{8,9},{9,8},{10,11... | collective-permute-start | bytes 2555912 | tf_op jit(solution)/shard_map/ppermute | solution.py:392
  90.1 2.5 %collective-permute-start.4 = (f32[16,128]{1,0:T(8,128)S(1)}, f32[16,128]{1,0:T(8,128)S(1)}, u32[]{:S(2)}, u32[]{:S(2)}) collective-permute-start(f32[16,128]{1,0:T(8,128)S(1)} %given_kernel.1), channel_id=1, source_target_pairs={{0,2},{2,0},{1,3},{3,1},{4,6},{6,4},{5,7},{7,5},{8,10},{10,8},{9,1... | collective-permute-start | bytes 24584 | tf_op jit(solution)/shard_map/ppermute | solution.py:393
  92.6 6.5 %relations_kernel.1 = (f32[1024,400]{1,0:T(8,128)S(1)}, bf16[1024,400]{1,0:T(8,128)(2,1)S(1)}, bf16[1024,400]{1,0:T(8,128)(2,1)S(1)}, f32[512,400]{1,0:T(8,128)S...) custom-call(f32[400,512]{1,0:T(8,128)S(1)} %bitcast.16, ...), custom_call_target="tpu_custom_call" | custom-call | flops 8000000000 | bytes 4000000 | tf_op jit(solution)/shard_map/relations_kernel/pallas_call | solution.py:349
  99.1 8.3 %weights_kernel.1 = (bf16[1024,512]{1,0:T(8,128)(2,1)S(1)}, bf16[1024,512]{1,0:T(8,128)(2,1)S(1)}, bf16[1024,512]{1,0:T(8,128)(2,1)S(1)}, bf16[1024,512]{1,0:T(8...) custom-call(f32[1664,128]{1,0:T(8,128)S(1)} %bitcast.14, ...), custom_call_target="tpu_custom_call" | custom-call | flops 8000000000 | bytes 4000000 | tf_op jit(solution)/shard_map/weights_kernel/pallas_call | solution.py:349
  107.4 3.8 %gradient_kernel.2 = (f32[256,256]{1,0:T(8,128)S(1)}, f32[256,256]{1,0:T(8,128)S(1)}) custom-call(f32[128,128]{1,0:T(8,128)S(1)} %copy-done.6, f32[128,128]{1,0:T(8,128)S(1)} %get-tuple-element.38.cols_theirs, f32[1024,400]{1,0:T(8,128)S(1)} %get-tuple-element.39.rel_ref, bf16[1024,512]{1,0:T(8,128)(2,1)S(1)} %get-tuple-element.57.head_hi, ...), custom_call_target="tpu_custom_call" | custom-call | flops 3000000000 | bytes 4000000 | tf_op jit(solution)/shard_map/gradient_kernel/pallas_call | solution.py:349
  111.2 2.4 %collective-permute-start.5 = (f32[256,256]{1,0:T(8,128)S(1)}, f32[256,256]{1,0:T(8,128)S(1)}, u32[]{:S(2)}, u32[]{:S(2)}) collective-permute-start(f32[256,256]{1,0:T(8,128)S(1)} %get-tuple-element.55), channel_id=1, source_target_pairs={{0,1},{1,0},{2,3},{3,2},{4,5},{5,4},{6,7},{7,6},{8,9},{9,8},{10,11... | collective-permute-start | bytes 786440 | tf_op jit(solution)/shard_map/ppermute | solution.py:440
  113.7 1.1 collective-permute-done.5
  114.8 0.0 copy-start.4
  114.8 7.0 %collective-permute-start.6 = (f32[256,256]{1,0:T(8,128)S(1)}, f32[256,256]{1,0:T(8,128)S(1)}, u32[]{:S(2)}, u32[]{:S(2)}) collective-permute-start(f32[256,256]{1,0:T(8,128)S(1)} %add.12), channel_id=1, source_target_pairs={{0,2},{2,0},{1,3},{3,1},{4,6},{6,4},{5,7},{7,5},{8,10},{10,8},{9,1... | collective-permute-start | bytes 786440 | tf_op jit(solution)/shard_map/ppermute | solution.py:445
  121.9 3.8 %gradient_kernel.3 = (f32[144,256]{1,0:T(8,128)S(1)}, f32[144,256]{1,0:T(8,128)S(1)}) custom-call(f32[128,128]{1,0:T(8,128)S(1)} %copy-done.6, f32[128,128]{1,0:T(8,128)S(1)} %get-tuple-element.38.cols_theirs, f32[1024,400]{1,0:T(8,128)S(1)} %get-tuple-element.39.rel_ref, bf16[1024,512]{1,0:T(8,128)(2,1)S(1)} %get-tuple-element.57.head_hi, ...), custom_call_target="tpu_custom_call" | custom-call | flops 3000000000 | bytes 4000000 | tf_op jit(solution)/shard_map/gradient_kernel/pallas_call | solution.py:349
  125.7 2.5 %collective-permute-start.7 = (f32[144,256]{1,0:T(8,128)S(1)}, f32[144,256]{1,0:T(8,128)S(1)}, u32[]{:S(2)}, u32[]{:S(2)}) collective-permute-start(f32[144,256]{1,0:T(8,128)S(1)} %get-tuple-element.59), channel_id=1, source_target_pairs={{0,1},{1,0},{2,3},{3,2},{4,5},{5,4},{6,7},{7,6},{8,9},{9,8},{10,11... | collective-permute-start | bytes 442376 | tf_op jit(solution)/shard_map/ppermute | solution.py:440
  128.2 1.0 collective-permute-done.7
  129.2 2.5 %collective-permute-start.8 = (f32[144,256]{1,0:T(8,128)S(1)}, f32[144,256]{1,0:T(8,128)S(1)}, u32[]{:S(2)}, u32[]{:S(2)}) collective-permute-start(f32[144,256]{1,0:T(8,128)S(1)} %add.14), channel_id=1, source_target_pairs={{0,2},{2,0},{1,3},{3,1},{4,6},{6,4},{5,7},{7,5},{8,10},{10,8},{9,1... | collective-permute-start | bytes 442376 | tf_op jit(solution)/shard_map/ppermute | solution.py:445
  131.7 2.6 %collective-permute-start.9 = (f32[256,256]{1,0:T(8,128)S(1)}, f32[256,256]{1,0:T(8,128)S(1)}, u32[]{:S(2)}, u32[]{:S(2)}) collective-permute-start(f32[256,256]{1,0:T(8,128)S(1)} %add.13.mine0_ref), channel_id=1, source_target_pairs={{0,1},{1,0},{2,3},{3,2},{4,5},{5,4},{6,7},{7,6},{8,9},{9,8},{10,11... | collective-permute-start | bytes 786440 | tf_op jit(solution)/shard_map/ppermute | solution.py:447
  134.3 8.0 %collective-permute-done.8 = f32[144,256]{1,0:T(8,128)S(1)} collective-permute-done((f32[144,256]{1,0:T(8,128)S(1)}, f32[144,256]{1,0:T(8,128)S(1)}, u32[]{:S(2)}, u32[]{:S(2)}) %collective-permute-start.8) | collective-permute-done | bytes 147488 | tf_op jit(solution)/shard_map/ppermute | solution.py:445
  142.3 2.4 %collective-permute-start.10 = (f32[144,256]{1,0:T(8,128)S(1)}, f32[144,256]{1,0:T(8,128)S(1)}, u32[]{:S(2)}, u32[]{:S(2)}) collective-permute-start(f32[144,256]{1,0:T(8,128)S(1)} %add.15.mine1_ref), channel_id=1, source_target_pairs={{0,1},{1,0},{2,3},{3,2},{4,5},{5,4},{6,7},{7,6},{8,9},{9,8},{10,11... | collective-permute-start | bytes 442376 | tf_op jit(solution)/shard_map/ppermute | solution.py:447
  144.7 1.0 collective-permute-done.10.theirs1_ref
  145.7 1.2 update_kernel.1
  (22 shorter events, 0.2 us)
Async XLA Ops:
  0.6 91.9 %copy-start = (f32[512,400]{0,1:T(8,128)S(1)}, f32[512,400]{0,1:T(8,128)}, u32[]{:S(2)}) copy-start(f32[512,400]{0,1:T(8,128)} %param.9) | copy-start | bytes 2457604
  3.1 89.5 %copy-start.6 = (f32[128,128]{1,0:T(8,128)S(1)}, f32[128,128]{1,0:T(8,128)}, u32[]{:S(2)}) copy-start(f32[128,128]{1,0:T(8,128)} %get-tuple-element.32.cols_ref.cols_mine) | copy-start | bytes 196612
  3.1 43.0 %all-to-all-start = ((f32[128,1,896]{2,1,0:T(1,128)}), f32[128,1,896]{2,1,0:T(1,128)S(1)}, u32[]{:S(2)}, u32[]{:S(2)}) async-start(f32[128,1,896]{2,1,0:T(1,128)} %bitcast.23), calls=%async_computation | async-start | bytes 917504 | tf_op jit(solution)/shard_map/all_to_all | solution.py:381
  21.0 1.2 copy-start.1
  22.2 0.7 copy-start.3
  22.9 61.7 %copy-start.2 = (f32[528,400]{0,1:T(8,128)S(1)}, f32[528,400]{0,1:T(8,128)}, u32[]{:S(2)}) copy-start(f32[528,400]{0,1:T(8,128)} %param.11) | copy-start | bytes 2534404
  23.0 23.0 %collective-permute-start = (f32[112,512]{1,0:T(8,128)S(1)}, f32[112,512]{1,0:T(8,128)S(1)}, u32[]{:S(2)}, u32[]{:S(2)}) collective-permute-start(f32[112,512]{1,0:T(8,128)S(1)} %bundle_kernel.1), channel_id=1, source_target_pairs={{0,2},{2,0},{1,3},{3,1},{4,6},{6,4},{5,7},{7,5},{8,10},{10,8},{9,1... | collective-permute-start | bytes 688136 | tf_op jit(solution)/shard_map/ppermute | solution.py:383
  46.1 0.7 copy-start.5
  48.4 38.2 %all-to-all-start.1 = ((f32[128,1,1664]{2,1,0:T(1,128)}), f32[128,1,1664]{2,1,0:T(1,128)S(1)}, u32[]{:S(2)}, u32[]{:S(2)}) async-start(f32[128,1,1664]{2,1,0:T(1,128)} %bitcast.6), calls=%async_computation.1 | async-start | bytes 1703936 | tf_op jit(solution)/shard_map/all_to_all | solution.py:388
  78.5 14.1 %collective-permute-start.2 = (f32[4,112,512]{2,1,0:T(8,128)}, f32[4,112,512]{2,1,0:T(8,128)}, u32[]{:S(2)}, u32[]{:S(2)}) collective-permute-start(f32[4,112,512]{2,1,0:T(8,128)} %bitcast.5.far_hbm), channel_id=1, source_target_pairs={{0,1},{1,0},{2,3},{3,2},{4,5},{5,4},{6,7},{7,6},{8,9},{9,8},{10,11... | collective-permute-start | bytes 2752520 | tf_op jit(solution)/shard_map/ppermute | solution.py:391
  84.6 7.9 %collective-permute-start.1 = (f32[400,528]{1,0:T(8,128)S(1)}, f32[400,528]{1,0:T(8,128)}, u32[]{:S(2)}, u32[]{:S(2)}) collective-permute-start(f32[400,528]{1,0:T(8,128)S(1)} %bitcast.20), channel_id=1, source_target_pairs={{0,1},{1,0},{2,3},{3,2},{4,5},{5,4},{6,7},{7,6},{8,9},{9,8},{10,11... | collective-permute-start | bytes 2534408 | tf_op jit(solution)/shard_map/ppermute | solution.py:384
  86.6 12.5 %collective-permute-start.3 = (f32[1664,128]{1,0:T(8,128)S(1)}, f32[1664,128]{1,0:T(8,128)S(1)}, u32[]{:S(2)}, u32[]{:S(2)}) collective-permute-start(f32[1664,128]{1,0:T(8,128)S(1)} %bitcast.11), channel_id=1, source_target_pairs={{0,1},{1,0},{2,3},{3,2},{4,5},{5,4},{6,7},{7,6},{8,9},{9,8},{10,11... | collective-permute-start | bytes 2555912 | tf_op jit(solution)/shard_map/ppermute | solution.py:392
  90.1 9.0 %collective-permute-start.4 = (f32[16,128]{1,0:T(8,128)S(1)}, f32[16,128]{1,0:T(8,128)S(1)}, u32[]{:S(2)}, u32[]{:S(2)}) collective-permute-start(f32[16,128]{1,0:T(8,128)S(1)} %given_kernel.1), channel_id=1, source_target_pairs={{0,2},{2,0},{1,3},{3,1},{4,6},{6,4},{5,7},{7,5},{8,10},{10,8},{9,1... | collective-permute-start | bytes 24584 | tf_op jit(solution)/shard_map/ppermute | solution.py:393
  111.2 3.6 %collective-permute-start.5 = (f32[256,256]{1,0:T(8,128)S(1)}, f32[256,256]{1,0:T(8,128)S(1)}, u32[]{:S(2)}, u32[]{:S(2)}) collective-permute-start(f32[256,256]{1,0:T(8,128)S(1)} %get-tuple-element.55), channel_id=1, source_target_pairs={{0,1},{1,0},{2,3},{3,2},{4,5},{5,4},{6,7},{7,6},{8,9},{9,8},{10,11... | collective-permute-start | bytes 786440 | tf_op jit(solution)/shard_map/ppermute | solution.py:440
  114.8 30.9 %copy-start.4 = (f32[512]{0:T(512)S(1)}, f32[512]{0:T(512)}, u32[]{:S(2)}) copy-start(f32[512]{0:T(512)} %param.10) | copy-start | bytes 6148
  114.8 16.8 %collective-permute-start.6 = (f32[256,256]{1,0:T(8,128)S(1)}, f32[256,256]{1,0:T(8,128)S(1)}, u32[]{:S(2)}, u32[]{:S(2)}) collective-permute-start(f32[256,256]{1,0:T(8,128)S(1)} %add.12), channel_id=1, source_target_pairs={{0,2},{2,0},{1,3},{3,1},{4,6},{6,4},{5,7},{7,5},{8,10},{10,8},{9,1... | collective-permute-start | bytes 786440 | tf_op jit(solution)/shard_map/ppermute | solution.py:445
  125.7 3.5 %collective-permute-start.7 = (f32[144,256]{1,0:T(8,128)S(1)}, f32[144,256]{1,0:T(8,128)S(1)}, u32[]{:S(2)}, u32[]{:S(2)}) collective-permute-start(f32[144,256]{1,0:T(8,128)S(1)} %get-tuple-element.59), channel_id=1, source_target_pairs={{0,1},{1,0},{2,3},{3,2},{4,5},{5,4},{6,7},{7,6},{8,9},{9,8},{10,11... | collective-permute-start | bytes 442376 | tf_op jit(solution)/shard_map/ppermute | solution.py:440
  129.2 13.1 %collective-permute-start.8 = (f32[144,256]{1,0:T(8,128)S(1)}, f32[144,256]{1,0:T(8,128)S(1)}, u32[]{:S(2)}, u32[]{:S(2)}) collective-permute-start(f32[144,256]{1,0:T(8,128)S(1)} %add.14), channel_id=1, source_target_pairs={{0,2},{2,0},{1,3},{3,1},{4,6},{6,4},{5,7},{7,5},{8,10},{10,8},{9,1... | collective-permute-start | bytes 442376 | tf_op jit(solution)/shard_map/ppermute | solution.py:445
  131.7 14.0 %collective-permute-start.9 = (f32[256,256]{1,0:T(8,128)S(1)}, f32[256,256]{1,0:T(8,128)S(1)}, u32[]{:S(2)}, u32[]{:S(2)}) collective-permute-start(f32[256,256]{1,0:T(8,128)S(1)} %add.13.mine0_ref), channel_id=1, source_target_pairs={{0,1},{1,0},{2,3},{3,2},{4,5},{5,4},{6,7},{7,6},{8,9},{9,8},{10,11... | collective-permute-start | bytes 786440 | tf_op jit(solution)/shard_map/ppermute | solution.py:447
  142.3 3.4 %collective-permute-start.10 = (f32[144,256]{1,0:T(8,128)S(1)}, f32[144,256]{1,0:T(8,128)S(1)}, u32[]{:S(2)}, u32[]{:S(2)}) collective-permute-start(f32[144,256]{1,0:T(8,128)S(1)} %add.15.mine1_ref), channel_id=1, source_target_pairs={{0,1},{1,0},{2,3},{3,2},{4,5},{5,4},{6,7},{7,6},{8,9},{9,8},{10,11... | collective-permute-start | bytes 442376 | tf_op jit(solution)/shard_map/ppermute | solution.py:447

commit v9 on v7

--- a/solution.py
+++ b/solution.py
@@ -112,10 +112,13 @@
     write_rows(out_ref, payload, CHUNK1)
 
 
-def route_kernel(x_ref, matching_ref, out_ref):
+def route_kernel(x_ref, matching_hbm, out_ref, matching_ref, sem):
     zh, _ = place()
+    copy = pltpu.make_async_copy(matching_hbm, matching_ref, sem)
+    copy.start()
     parts = split3(read_rows(x_ref, CHUNK1))
     rows = iota((128, 128), 0)
+    copy.wait()
     marks = [jnp.where(matching_ref[b : b + 1, :] == rows, 1.0, 0.0) for b in range(2)]
     back_keep = jnp.where(zh == 0, marks[0], marks[1])
     back_give = jnp.where(zh == 0, marks[1], marks[0])
@@ -169,7 +172,7 @@
     index_vmem[...] = table_row(rels.astype(jnp.int32), zh, core)
     copy = pltpu.make_async_copy(index_vmem, index_smem, sem)
     copy.start()
-    copy.wait()
+    return copy
 
 
 def gather_relations(table_ref, index_smem, first, out_ref):
@@ -192,33 +195,40 @@
 
 
 def relations_kernel(
-    entity_ref, cols_ref, bundle_ref, near_ref, near2_ref, far_ref, far2_ref, fetched_ref,
+    entity_ref, cols_ref, bundle_ref, near_ref, near2_hbm, far_hbm, far2_hbm, fetched_ref,
     rel_out, left_hi, left_lo, first_out, table_ref, entity_hi, entity_lo, cols_out,
-    far_table, gathered, index_vmem, index_smem, sem,
+    near2_ref, far_ref, far2_ref, far_table, gathered, index_vmem, index_smem, sem, sems,
 ):
     zh, core = place()
+    pairs = ((near2_hbm, near2_ref), (far_hbm, far_ref), (far2_hbm, far2_ref))
+    copies = [pltpu.make_async_copy(a, b, sems.at[i]) for i, (a, b) in enumerate(pairs)]
+    for copy in copies:
+        copy.start()
     theirs = unfold(bundle_ref[PIECE + 4 : PIECE + 8, :])
     chunk = fetched_ref[pl.ds(GIVEN_CHUNK, 128, stride=CHUNK2), :].T
     rels = jnp.concatenate([cols_ref[...].T[4:8, :], theirs[4:8, :], chunk[FIRST + 4 : FIRST + 8, :]], axis=0)
-    load_indices(rels, zh, core, index_vmem, index_smem, sem)
-    for k, ref in enumerate((near_ref, near2_ref)):
-        store_relations(table_ref, k * REL_DEV, ref[...].T)
+    indices = load_indices(rels, zh, core, index_vmem, index_smem, sem)
+    theirs = jnp.concatenate([theirs, jnp.zeros((128 - LIST, 128), F32)], axis=0).T
+    cols_out[...] = theirs
+    hi, lo = split2(entity_ref[...].T)
+    entity_hi[...] = hi
+    entity_lo[...] = lo
+    head_rows = [gather_heads(lists[:, 0:LIST], hi, lo) for lists in (cols_ref, theirs)]
+    store_relations(table_ref, 0, near_ref[...].T)
+    copies[0].wait()
+    store_relations(table_ref, REL_DEV, near2_ref[...].T)
     for k, ref in enumerate((far_ref, far2_ref)):
+        copies[1 + k].wait()
         for spot in range(PIECES):
             far_table[k, piece_start(spot) : piece_start(spot) + PIECE, :] = ref[spot, 0:PIECE, :]
         store_relations(table_ref, (2 + k) * REL_DEV, far_table[k].T)
         rest = [unfold(ref[spot, PIECE : PIECE + 4, :]) for spot in range(PIECES)]
         rest = [rest[spot][:, 0:PIECE] for spot in range(PIECES - 1)] + [rest[-1][:, PIECES * PIECE - D : PIECE]]
         store_relations(table_ref, (2 + k) * REL_DEV + MAIN, jnp.concatenate(rest, axis=1))
-    theirs = jnp.concatenate([theirs, jnp.zeros((128 - LIST, 128), F32)], axis=0).T
-    cols_out[...] = theirs
-    hi, lo = split2(entity_ref[...].T)
-    entity_hi[...] = hi
-    entity_lo[...] = lo
+    indices.wait()
     for k in range(2):
-        head_rows = gather_heads((cols_ref, theirs)[k][:, 0:LIST], hi, lo)
         rel_rows = gather_relations(table_ref, index_smem, 4 * k, gathered)
-        l_hi, l_lo = split2(head_rows * rel_rows)
+        l_hi, l_lo = split2(head_rows[k] * rel_rows)
         span = pl.ds(k * SLOTS, SLOTS)
         rel_out[span, :] = rel_rows
         left_hi[span, :] = l_hi
@@ -275,12 +285,12 @@
 
 def tail_kernel(
     mine_ref, theirs_ref, given_ref, rel_ref, entity_hi, entity_lo, table_ref, head_grad,
-    keep0_ref, keep1_ref, send0_ref, send1_ref, block_hi, block_lo, gathered, index_vmem, index_smem, sem,
+    keep_ref, send_ref, block_hi, block_lo, gathered, index_vmem, index_smem, sem,
 ):
     zh, core = place()
     mine = read_rows(mine_ref, CHUNK2)
     fill_block(block_hi, block_lo, mine, read_rows(theirs_ref, CHUNK2), 2 * D)
-    keep_refs, send_refs = (keep0_ref, keep1_ref), (send0_ref, send1_ref)
+    indices = load_indices(given_ref[4:8, :], zh, core, index_vmem, index_smem, sem)
     e_hi, e_lo = entity_hi[...], entity_lo[...]
     numbers = jnp.bitwise_xor(iota((128, ROWS), 1), core * HALF).astype(F32)
     rows_at = iota((ROWS, 128), 0).astype(F32)
@@ -291,7 +301,7 @@
             rel_rows = rel_ref[...]
         else:
             lists = jnp.concatenate([given_ref[...], jnp.zeros((128 - LIST, 128), F32)], axis=0).T[:, 0:LIST]
-            load_indices(given_ref[4:8, :], zh, core, index_vmem, index_smem, sem)
+            indices.wait()
             rel_rows = gather_relations(table_ref, index_smem, 0, gathered)
         heads = onehot_cols(lists, 0, 4, numbers)
         head_rows = dot_nn(heads, block_hi[...]) + dot_nn(heads, block_lo[...])
@@ -309,34 +319,35 @@
         w_hi, w_lo = split2(weights)
         total = total + (dot_nn(w_lo, l_hi) + dot_nn(w_hi, l_lo) + dot_nn(w_hi, l_hi))
     first, second = total[0:HALF, :].T, total[HALF:ROWS, :].T
-    keep, send = jnp.where(core == 0, first, second), jnp.where(core == 0, second, first)
-    for k in range(2):
-        keep_refs[k][...] = keep[k * D // 2 : (k + 1) * D // 2, :]
-        send_refs[k][...] = send[k * D // 2 : (k + 1) * D // 2, :]
-
-
-def update_kernel(mine0_ref, mine1_ref, theirs0_ref, theirs1_ref, entity_ref, state_ref, updated_ref, accum_ref):
+    keep_ref[...] = jnp.where(core == 0, first, second)
+    send_ref[...] = jnp.where(core == 0, second, first)
+
+
+def combine_kernel(keep_ref, sent_ref, out_ref):
     _, core = place()
-    mine = jnp.concatenate([mine0_ref[...], mine1_ref[...]], axis=0)
-    theirs = jnp.concatenate([theirs0_ref[...], theirs1_ref[...]], axis=0)
-    for j, gradient in enumerate((jnp.where(core == 0, mine, theirs), jnp.where(core == 0, theirs, mine))):
+    out_ref[...] = keep_ref[...] + sent_ref[1 - core]
+
+
+def update_kernel(gradient_ref, entity_ref, state_ref, updated_ref, accum_ref):
+    for j in range(2):
+        gradient = gradient_ref[j]
         span = slice(HALF * j, HALF * (j + 1))
         accum = state_ref[:, span] + jnp.sum(gradient * gradient, axis=0, keepdims=True) / float(D)
         accum_ref[:, span] = accum
         updated_ref[:, span] = entity_ref[:, span] - LEARN_RATE * gradient / jnp.sqrt(accum)
 
 
-def call(kernel, out_shape, args, vmem, scratch=(), cost=None, space=pltpu.VMEM):
+def call(kernel, out_shape, args, vmem, scratch=(), cost=None, space=pltpu.VMEM, in_hbm=()):
     out_shape = jax.tree.map(lambda s: jax.ShapeDtypeStruct(*s), out_shape, is_leaf=lambda s: isinstance(s, tuple))
     return pl.pallas_call(
         kernel,
         out_shape=out_shape,
-        in_specs=[pl.BlockSpec(memory_space=space) for _ in args],
+        in_specs=[pl.BlockSpec(memory_space=pltpu.HBM if i in in_hbm else space) for i in range(len(args))],
         out_specs=jax.tree.map(lambda _: pl.BlockSpec(memory_space=pltpu.VMEM), out_shape),
         scratch_shapes=list(scratch),
         compiler_params=pltpu.CompilerParams(vmem_limit_bytes=vmem * MIB),
         cost_estimate=cost,
-        name=kernel.__name__,
+        name=getattr(kernel, "func", kernel).__name__,
     )(*args)
 
 
@@ -366,7 +377,14 @@
     near2 = swap_core(relation_t)
     spread, bundle = lax.optimization_barrier((spread, bundle))
 
-    routed = call(route_kernel, ((128 * CHUNK2, 128), F32), (spread, matching), vmem=16)
+    routed = call(
+        route_kernel,
+        ((128 * CHUNK2, 128), F32),
+        (spread, matching),
+        vmem=16,
+        scratch=[pltpu.VMEM((2, 128), jnp.int32), pltpu.SemaphoreType.DMA],
+        in_hbm=(1,),
+    )
     fetched = exchange(routed.reshape(128, 1, 128 * CHUNK2)).reshape(128 * CHUNK2, 128)
     bundle, _ = lax.optimization_barrier((bundle, routed))
     far = lax.all_gather(bundle, "x", axis=0)
@@ -393,8 +411,13 @@
         ],
         (entity_t, cols, bundle, relation_t, near2, far, far2, fetched),
         vmem=32,
-        scratch=[pltpu.VMEM((2, D, MAIN), F32)] + gather,
-        cost=flops(6),
+        scratch=[pltpu.VMEM((D, REL_DEV), F32)]
+        + [pltpu.VMEM((PIECES, PIECE + 8, MAIN), F32)] * 2
+        + [pltpu.VMEM((2, D, MAIN), F32)]
+        + gather
+        + [pltpu.SemaphoreType.DMA((3,))],
+        cost=flops(8),
+        in_hbm=(4, 5, 6),
     )
     block = [pltpu.VMEM((ROWS, D), BF16), pltpu.VMEM((ROWS, D), BF16)]
     head_grad = call(
@@ -405,21 +428,22 @@
         scratch=block,
         cost=flops(6),
     )
-    parts = call(
+    keep, send = call(
         tail_kernel,
-        [((D // 2, HALF), F32)] * 4,
+        [((D, HALF), F32)] * 2,
         (fetched, fetched_other, given, first_rel, entity_hi, entity_lo, table, head_grad),
         vmem=28,
         scratch=block + gather,
         cost=flops(9),
     )
-    halves = [keep + swap_core(send) for keep, send in zip(parts[:2], parts[2:])]
-    halves = [half + swap_zh(half) for half in halves]
-    others = [swap_core(half) for half in halves]
+    sent = lax.all_gather(send, "core", axis=0)
+    half = call(combine_kernel, ((D, HALF), F32), (keep, sent), vmem=8)
+    chips = lax.all_gather(half, "zh", axis=0)
+    gradient = lax.all_gather(chips[0] + chips[1], "core", axis=0)
     updated, accum = call(
         update_kernel,
         [((D, ROWS), F32), ((1, ROWS), F32)],
-        (*halves, *others, entity_t, state.reshape(1, ROWS)),
+        (gradient, entity_t, state.reshape(1, ROWS)),
         vmem=8,
     )
     return updated.T, accum.reshape(ROWS)

time: 149 us -> 142 us (0.953)
  the two profiles are of different devices: /device:TPU:1 before, /device:TPU:65 now
where the time goes in v9:
time: 142 us; the launch traced here: 141 us
  starting transfers between devices  54.1 us (38%)
  blocking collectives  47 us (33%)
  Pallas kernels  25.1 us (18%)
  waiting for transfers between devices  11.5 us (8%)
  local copies, waits for them, and re-layouts  2.61 us (2%)
    pallas_call x9, Pallas kernels, call(): pl.pallas_call(kernel, out_shape=out_shape, in_specs=[pl.BlockSpec(memory...  25.1 us
    all_gather x1, blocking collectives, shards(): chips = lax.all_gather(half, 'zh', axis=0)  24.1 us
    all_gather x1, blocking collectives, shards(): far = lax.all_gather(bundle, 'x', axis=0)  17.3 us
    all_to_all x1, starting transfers between devices, shards(): exchange(routed.reshape(128, 1, 128 * CHUNK2)).reshape(128 * CHUNK2, 128)  16.9 us
    all_to_all x1, starting transfers between devices, shards(): exchange(payload.reshape(128, 1, 128 * CHUNK1)).reshape(128 * CHUNK1, 128)  15.6 us
    ppermute x1, waiting for transfers between devices, shards(): swap_zh(call(bundle_kernel, ((PIECE + 8, MAIN), F32), (relation_t, give),...  11.5 us
    ppermute x1, starting transfers between devices, shards(): swap_zh(call(bundle_kernel, ((PIECE + 8, MAIN), F32), (relation_t, give),...  8.07 us
    ppermute x1, starting transfers between devices, shards(): far2 = swap_core(far)  5.65 us
  transfers between devices with their start and end apart: 7, of which 1 were waited for; matrix products, arithmetic and copies ran while one was open for 0% of the time, Pallas kernels for 9%

profile of v9, /device:TPU:65, one launch (start us, length us, event | category | flops | bytes accessed | tf_op | source)
XLA Modules:
  0.0 141.2 jit_solution(12281659614159050062)
XLA Ops:
  0.6 2.4 %pack_kernel.1 = (f32[896,128]{1,0:T(8,128)}, f32[128,128]{1,0:T(8,128)}, f32[16,128]{1,0:T(8,128)}) custom-call(f32[400,512]{1,0:T(8,128)} %bitcast.18, s32[2,1,1,512]{3,2,1,0:T(1,128)} %head_hbm.1, s32[2,1,1,512]{3,2,1,0:T(1,128)} %rel_hbm.1, s32[2,1,1,512]{3,2,1,0:T(1,128)} %tail_hbm.1, s32[2,1,1,320]{3,2,1,0:T(1,128)} %neg_hbm.1, s32[1,1,2]{2,1,0:T(1,128)} %bitcast.29), custom_call_target="tpu_custom_call" | custom-call | tf_op jit(solution)/shard_map/pack_kernel/pallas_call | solution.py:342
  3.1 15.6 %all-to-all-start = ((f32[128,1,896]{2,1,0:T(1,128)}), f32[128,1,896]{2,1,0:T(1,128)S(1)}, u32[]{:S(2)}, u32[]{:S(2)}) async-start(f32[128,1,896]{2,1,0:T(1,128)} %bitcast.28), calls=%async_computation | async-start | bytes 917504 | tf_op jit(solution)/shard_map/all_to_all | solution.py:374
  18.7 0.0 copy-start.1
  18.7 1.2 copy-done.1
  19.9 0.7 copy-done.3
  20.6 0.1 bundle_kernel.1
  20.7 8.1 %collective-permute-start = (f32[112,512]{1,0:T(8,128)S(1)}, f32[112,512]{1,0:T(8,128)S(1)}, u32[]{:S(2)}, u32[]{:S(2)}) collective-permute-start(f32[112,512]{1,0:T(8,128)S(1)} %bundle_kernel.1), channel_id=1, source_target_pairs={{0,2},{2,0},{1,3},{3,1},{4,6},{6,4},{5,7},{7,5},{8,10},{10,8},{9,1... | collective-permute-start | bytes 688136 | tf_op jit(solution)/shard_map/ppermute | solution.py:376
  28.7 11.5 %collective-permute-done.bundle_ref = f32[112,512]{1,0:T(8,128)S(1)} collective-permute-done((f32[112,512]{1,0:T(8,128)S(1)}, f32[112,512]{1,0:T(8,128)S(1)}, u32[]{:S(2)}, u32[]{:S(2)}) %collective-permute-start) | collective-permute-done | bytes 229408 | tf_op jit(solution)/shard_map/ppermute | solution.py:376
  40.2 0.0 all-to-all-done
  40.2 0.7 copy-done.5
  40.9 1.8 %route_kernel.1 = f32[1664,128]{1,0:T(8,128)} custom-call(f32[896,128]{1,0:T(8,128)S(1)} %bitcast.23, s32[2,128]{1,0:T(2,128)S(1)} %copy-done.5), custom_call_target="tpu_custom_call" | custom-call | tf_op jit(solution)/shard_map/route_kernel/pallas_call | solution.py:342
  42.7 16.9 %all-to-all-start.1 = ((f32[128,1,1664]{2,1,0:T(1,128)}), f32[128,1,1664]{2,1,0:T(1,128)S(1)}, u32[]{:S(2)}, u32[]{:S(2)}) async-start(f32[128,1,1664]{2,1,0:T(1,128)} %bitcast.5), calls=%async_computation.1 | async-start | bytes 1703936 | tf_op jit(solution)/shard_map/all_to_all | solution.py:388
  59.7 17.3 %all-gather = f32[448,512]{1,0:T(8,128)} all-gather(f32[112,512]{1,0:T(8,128)S(1)} %collective-permute-done.bundle_ref), channel_id=2, replica_groups=mesh['x'=4,'yz'=32,'zh'=2,'core'=2] {'x'}, dimensions={0}, use_global_device_ids=true | all-gather | bytes 1146880 | tf_op jit(solution)/shard_map/all_gather | solution.py:390
  76.9 5.6 %collective-permute-start.4 = (f32[4,112,512]{2,1,0:T(8,128)}, f32[4,112,512]{2,1,0:T(8,128)}, u32[]{:S(2)}, u32[]{:S(2)}) collective-permute-start(f32[4,112,512]{2,1,0:T(8,128)} %bitcast.7.far_hbm), channel_id=1, source_target_pairs={{0,1},{1,0},{2,3},{3,2},{4,5},{5,4},{6,7},{7,6},{8,9},{9,8},{10,11... | collective-permute-start | bytes 2752520 | tf_op jit(solution)/shard_map/ppermute | solution.py:391
  82.6 0.0 copy-done.2
  82.6 1.9 %collective-permute-start.3 = (f32[400,528]{1,0:T(8,128)S(1)}, f32[400,528]{1,0:T(8,128)}, u32[]{:S(2)}, u32[]{:S(2)}) collective-permute-start(f32[400,528]{1,0:T(8,128)S(1)} %bitcast.25), channel_id=1, source_target_pairs={{0,1},{1,0},{2,3},{3,2},{4,5},{5,4},{6,7},{7,6},{8,9},{9,8},{10,11... | collective-permute-start | bytes 2534408 | tf_op jit(solution)/shard_map/ppermute | solution.py:377
  84.5 0.0 all-to-all-done.1
  84.6 3.5 %collective-permute-start.1 = (f32[1664,128]{1,0:T(8,128)S(1)}, f32[1664,128]{1,0:T(8,128)S(1)}, u32[]{:S(2)}, u32[]{:S(2)}) collective-permute-start(f32[1664,128]{1,0:T(8,128)S(1)} %bitcast.13), channel_id=1, source_target_pairs={{0,1},{1,0},{2,3},{3,2},{4,5},{5,4},{6,7},{7,6},{8,9},{9,8},{10,11... | collective-permute-start | bytes 2555912 | tf_op jit(solution)/shard_map/ppermute | solution.py:392
  88.1 2.5 %collective-permute-start.2 = (f32[16,128]{1,0:T(8,128)S(1)}, f32[16,128]{1,0:T(8,128)S(1)}, u32[]{:S(2)}, u32[]{:S(2)}) collective-permute-start(f32[16,128]{1,0:T(8,128)S(1)} %given_kernel.1), channel_id=1, source_target_pairs={{0,2},{2,0},{1,3},{3,1},{4,6},{6,4},{5,7},{7,5},{8,10},{10,8},{9,1... | collective-permute-start | bytes 24584 | tf_op jit(solution)/shard_map/ppermute | solution.py:393
  90.5 0.0 collective-permute-done.3.near2_hbm
  90.6 0.0 collective-permute-done.4.far2_hbm
  90.6 6.5 %relations_kernel.1 = (f32[1024,400]{1,0:T(8,128)S(1)}, bf16[1024,400]{1,0:T(8,128)(2,1)S(1)}, bf16[1024,400]{1,0:T(8,128)(2,1)S(1)}, f32[512,400]{1,0:T(8,128)S...) custom-call(f32[400,512]{1,0:T(8,128)S(1)} %bitcast.19, ...), custom_call_target="tpu_custom_call" | custom-call | flops 8000000000 | bytes 4000000 | tf_op jit(solution)/shard_map/relations_kernel/pallas_call | solution.py:342
  97.1 0.0 collective-permute-done.1.theirs_ref
  97.1 5.6 %head_kernel.1.head_grad = f32[512,400]{1,0:T(8,128)S(1)} custom-call(f32[1664,128]{1,0:T(8,128)S(1)} %bitcast.16, f32[1664,128]{1,0:T(8,128)S(1)} %collective-permute-done.1.theirs_ref, f32[128,128]{1,0:T(8,128)S(1)} %copy-done.6, f32[128,128]{1,0:T(8,128)S(1)} %get-tuple-element.30.lists_theirs, f32[1024,400]{1,0:T(8,128)S(1)} %get-tuple-element.31.rel_ref, ...), custom_call_target="tpu_custom_call" | custom-call | flops 6000000000 | bytes 4000000 | tf_op jit(solution)/shard_map/head_kernel/pallas_call | solution.py:342
  102.6 0.0 collective-permute-done.2.given_ref
  102.6 7.6 %tail_kernel.1 = (f32[400,256]{1,0:T(8,128)S(1)}, f32[400,256]{1,0:T(8,128)S(1)}) custom-call(f32[1664,128]{1,0:T(8,128)S(1)} %bitcast.17, f32[1664,128]{1,0:T(8,128)S(1)} %collective-permute-done.1.theirs_ref, f32[16,128]{1,0:T(8,128)S(1)} %collective-permute-done.2.given_ref, f32[512,400]{1,0:T(8,128)S(1)} %get-tuple-element.26.rel_ref, ...), custom_call_target="tpu_custom_call" | custom-call | flops 8999999488 | bytes 4000000 | tf_op jit(solution)/shard_map/tail_kernel/pallas_call | solution.py:342
  110.3 0.0 copy-start.4
  110.3 2.4 %all-gather.1 = f32[800,256]{1,0:T(8,128)S(1)} all-gather(f32[400,256]{1,0:T(8,128)S(1)} %get-tuple-element.35), channel_id=3, replica_groups=mesh['x'=4,'yz'=32,'zh'=2,'core'=2] {'core'}, dimensions={0}, use_global_device_ids=true | all-gather | bytes 1228800 | tf_op jit(solution)/shard_map/all_gather | solution.py:439
  112.7 24.1 %all-gather.2 = f32[800,256]{1,0:T(8,128)S(1)} all-gather(f32[400,256]{1,0:T(8,128)S(1)} %combine_kernel.1), channel_id=4, replica_groups=mesh['x'=4,'yz'=32,'zh'=2,'core'=2] {'zh'}, dimensions={0}, use_global_device_ids=true | all-gather | bytes 1228800 | tf_op jit(solution)/shard_map/all_gather | solution.py:441
  136.8 0.1 slice_add_fusion
  136.9 3.3 %all-gather.3 = f32[800,256]{1,0:T(8,128)S(1)} all-gather(f32[400,256]{1,0:T(8,128)S(1)} %slice_add_fusion), channel_id=5, replica_groups=mesh['x'=4,'yz'=32,'zh'=2,'core'=2] {'core'}, dimensions={0}, use_global_device_ids=true | all-gather | bytes 1228800 | tf_op jit(solution)/shard_map/all_gather | solution.py:442
  140.2 1.1 update_kernel.1
  (10 shorter events, 0.1 us)
Async XLA Ops:
  0.6 89.9 %copy-start = (f32[512,400]{0,1:T(8,128)S(1)}, f32[512,400]{0,1:T(8,128)}, u32[]{:S(2)}) copy-start(f32[512,400]{0,1:T(8,128)} %param.9) | copy-start | bytes 2457604
  3.1 87.5 %copy-start.6 = (f32[128,128]{1,0:T(8,128)S(1)}, f32[128,128]{1,0:T(8,128)}, u32[]{:S(2)}) copy-start(f32[128,128]{1,0:T(8,128)} %get-tuple-element.23.cols_ref.lists_mine) | copy-start | bytes 196612
  3.1 37.1 %all-to-all-start = ((f32[128,1,896]{2,1,0:T(1,128)}), f32[128,1,896]{2,1,0:T(1,128)S(1)}, u32[]{:S(2)}, u32[]{:S(2)}) async-start(f32[128,1,896]{2,1,0:T(1,128)} %bitcast.28), calls=%async_computation | async-start | bytes 917504 | tf_op jit(solution)/shard_map/all_to_all | solution.py:374
  18.7 1.2 copy-start.1
  19.9 0.7 copy-start.3
  20.6 62.0 %copy-start.2 = (f32[528,400]{0,1:T(8,128)S(1)}, f32[528,400]{0,1:T(8,128)}, u32[]{:S(2)}) copy-start(f32[528,400]{0,1:T(8,128)} %param.11) | copy-start | bytes 2534404
  20.7 19.6 %collective-permute-start = (f32[112,512]{1,0:T(8,128)S(1)}, f32[112,512]{1,0:T(8,128)S(1)}, u32[]{:S(2)}, u32[]{:S(2)}) collective-permute-start(f32[112,512]{1,0:T(8,128)S(1)} %bundle_kernel.1), channel_id=1, source_target_pairs={{0,2},{2,0},{1,3},{3,1},{4,6},{6,4},{5,7},{7,5},{8,10},{10,8},{9,1... | collective-permute-start | bytes 688136 | tf_op jit(solution)/shard_map/ppermute | solution.py:376
  40.2 0.7 copy-start.5
  42.7 41.8 %all-to-all-start.1 = ((f32[128,1,1664]{2,1,0:T(1,128)}), f32[128,1,1664]{2,1,0:T(1,128)S(1)}, u32[]{:S(2)}, u32[]{:S(2)}) async-start(f32[128,1,1664]{2,1,0:T(1,128)} %bitcast.5), calls=%async_computation.1 | async-start | bytes 1703936 | tf_op jit(solution)/shard_map/all_to_all | solution.py:388
  76.9 13.6 %collective-permute-start.4 = (f32[4,112,512]{2,1,0:T(8,128)}, f32[4,112,512]{2,1,0:T(8,128)}, u32[]{:S(2)}, u32[]{:S(2)}) collective-permute-start(f32[4,112,512]{2,1,0:T(8,128)} %bitcast.7.far_hbm), channel_id=1, source_target_pairs={{0,1},{1,0},{2,3},{3,2},{4,5},{5,4},{6,7},{7,6},{8,9},{9,8},{10,11... | collective-permute-start | bytes 2752520 | tf_op jit(solution)/shard_map/ppermute | solution.py:391
  82.6 7.9 %collective-permute-start.3 = (f32[400,528]{1,0:T(8,128)S(1)}, f32[400,528]{1,0:T(8,128)}, u32[]{:S(2)}, u32[]{:S(2)}) collective-permute-start(f32[400,528]{1,0:T(8,128)S(1)} %bitcast.25), channel_id=1, source_target_pairs={{0,1},{1,0},{2,3},{3,2},{4,5},{5,4},{6,7},{7,6},{8,9},{9,8},{10,11... | collective-permute-start | bytes 2534408 | tf_op jit(solution)/shard_map/ppermute | solution.py:377
  84.6 12.5 %collective-permute-start.1 = (f32[1664,128]{1,0:T(8,128)S(1)}, f32[1664,128]{1,0:T(8,128)S(1)}, u32[]{:S(2)}, u32[]{:S(2)}) collective-permute-start(f32[1664,128]{1,0:T(8,128)S(1)} %bitcast.13), channel_id=1, source_target_pairs={{0,1},{1,0},{2,3},{3,2},{4,5},{5,4},{6,7},{7,6},{8,9},{9,8},{10,11... | collective-permute-start | bytes 2555912 | tf_op jit(solution)/shard_map/ppermute | solution.py:392
  88.1 14.6 %collective-permute-start.2 = (f32[16,128]{1,0:T(8,128)S(1)}, f32[16,128]{1,0:T(8,128)S(1)}, u32[]{:S(2)}, u32[]{:S(2)}) collective-permute-start(f32[16,128]{1,0:T(8,128)S(1)} %given_kernel.1), channel_id=1, source_target_pairs={{0,2},{2,0},{1,3},{3,1},{4,6},{6,4},{5,7},{7,5},{8,10},{10,8},{9,1... | collective-permute-start | bytes 24584 | tf_op jit(solution)/shard_map/ppermute | solution.py:393
  110.3 29.9 %copy-start.4 = (f32[512]{0:T(512)S(1)}, f32[512]{0:T(512)}, u32[]{:S(2)}) copy-start(f32[512]{0:T(512)} %param.10) | copy-start | bytes 6148

commit v10 on v9

--- a/solution.py
+++ b/solution.py
@@ -48,6 +48,10 @@
 
 def dot_nt(a, b):
     return lax.dot_general(a, b, (((1,), (1,)), ((), ())), preferred_element_type=F32)
+
+
+def dot3_nt(a_hi, a_lo, b_hi, b_lo):
+    return dot_nt(jnp.concatenate([a_hi, a_lo, a_hi], axis=1), jnp.concatenate([b_lo, b_hi, b_hi], axis=1))
 
 
 def iota(shape, dim):
@@ -112,13 +116,10 @@
     write_rows(out_ref, payload, CHUNK1)
 
 
-def route_kernel(x_ref, matching_hbm, out_ref, matching_ref, sem):
+def route_kernel(x_ref, matching_ref, out_ref):
     zh, _ = place()
-    copy = pltpu.make_async_copy(matching_hbm, matching_ref, sem)
-    copy.start()
     parts = split3(read_rows(x_ref, CHUNK1))
     rows = iota((128, 128), 0)
-    copy.wait()
     marks = [jnp.where(matching_ref[b : b + 1, :] == rows, 1.0, 0.0) for b in range(2)]
     back_keep = jnp.where(zh == 0, marks[0], marks[1])
     back_give = jnp.where(zh == 0, marks[1], marks[0])
@@ -145,7 +146,7 @@
     return min(PIECE * spot, D - PIECE)
 
 
-def bundle_kernel(relation_ref, give_ref, out_ref):
+def bundle_kernel(relation_ref, matching_ref, out_ref, matching_out):
     spot = lax.axis_index("x")
     start = pl.multiple_of(jnp.minimum(PIECE * spot, D - PIECE), 8)
     piece = relation_ref[pl.ds(start, PIECE), :]
@@ -154,7 +155,8 @@
     rest = jnp.concatenate([rest, jnp.zeros((128 - PIECE, 128), F32)], axis=0).T
     for g in range(4):
         out_ref[PIECE : PIECE + 4, 128 * g : 128 * (g + 1)] = rest[4 * g : 4 * g + 4, :]
-        out_ref[PIECE + 4 : PIECE + 8, 128 * g : 128 * (g + 1)] = give_ref[4 * g : 4 * g + 4, :]
+    out_ref[PIECE + 4 : PIECE + 8, :] = jnp.zeros((4, MAIN), F32)
+    matching_out[...] = matching_ref[...]
 
 
 def unfold(rows):
@@ -195,7 +197,7 @@
 
 
 def relations_kernel(
-    entity_ref, cols_ref, bundle_ref, near_ref, near2_hbm, far_hbm, far2_hbm, fetched_ref,
+    entity_ref, cols_ref, theirs_ref, near_ref, near2_hbm, far_hbm, far2_hbm, fetched_ref,
     rel_out, left_hi, left_lo, first_out, table_ref, entity_hi, entity_lo, cols_out,
     near2_ref, far_ref, far2_ref, far_table, gathered, index_vmem, index_smem, sem, sems,
 ):
@@ -204,7 +206,7 @@
     copies = [pltpu.make_async_copy(a, b, sems.at[i]) for i, (a, b) in enumerate(pairs)]
     for copy in copies:
         copy.start()
-    theirs = unfold(bundle_ref[PIECE + 4 : PIECE + 8, :])
+    theirs = theirs_ref[...]
     chunk = fetched_ref[pl.ds(GIVEN_CHUNK, 128, stride=CHUNK2), :].T
     rels = jnp.concatenate([cols_ref[...].T[4:8, :], theirs[4:8, :], chunk[FIRST + 4 : FIRST + 8, :]], axis=0)
     indices = load_indices(rels, zh, core, index_vmem, index_smem, sem)
@@ -258,7 +260,7 @@
         span = pl.ds(k * SLOTS, SLOTS)
         hi, lo = left_hi[span, :], left_lo[span, :]
         b_hi, b_lo = block_hi[...], block_lo[...]
-        scores = dot_nt(hi, b_lo) + dot_nt(lo, b_hi) + dot_nt(hi, b_hi)
+        scores = dot3_nt(hi, lo, b_hi, b_lo)
         tails = jnp.concatenate(
             [jnp.where(lists[:, 8 + j : 9 + j] == numbers, 1.0, 0.0) for j in range(4)], axis=0
         )
@@ -306,7 +308,7 @@
         heads = onehot_cols(lists, 0, 4, numbers)
         head_rows = dot_nn(heads, block_hi[...]) + dot_nn(heads, block_lo[...])
         l_hi, l_lo = split2(head_rows * rel_rows)
-        scores = dot_nt(e_lo, l_hi) + dot_nt(e_hi, l_lo) + dot_nt(e_hi, l_hi)
+        scores = dot3_nt(e_hi, e_lo, l_hi, l_lo)
         rows = lists_rows(lists)
         tails = jnp.concatenate(
             [jnp.where(rows[8 + j : 9 + j, :] == rows_at, 1.0, 0.0) for j in range(4)], axis=1
@@ -373,17 +375,24 @@
     )
     spread = exchange(payload.reshape(128, 1, 128 * CHUNK1)).reshape(128 * CHUNK1, 128)
 
-    bundle = swap_zh(call(bundle_kernel, ((PIECE + 8, MAIN), F32), (relation_t, give), vmem=8))
+    bundle, matching = call(
+        bundle_kernel,
+        [((PIECE + 8, MAIN), F32), ((2, 128), jnp.int32)],
+        (relation_t, matching),
+        vmem=8,
+    )
+    lines = lax.axis_size("yz") // 4
+    mirror = [((4 * y + z) * 2 + h, (4 * y + 3 - z) * 2 + 1 - h) for y in range(lines) for z in range(4) for h in range(2)]
+    bundle = lax.ppermute(bundle, ("yz", "zh"), perm=mirror)
+    theirs = swap_zh(give)
     near2 = swap_core(relation_t)
-    spread, bundle = lax.optimization_barrier((spread, bundle))
+    spread, bundle, theirs = lax.optimization_barrier((spread, bundle, theirs))
 
     routed = call(
         route_kernel,
         ((128 * CHUNK2, 128), F32),
         (spread, matching),
         vmem=16,
-        scratch=[pltpu.VMEM((2, 128), jnp.int32), pltpu.SemaphoreType.DMA],
-        in_hbm=(1,),
     )
     fetched = exchange(routed.reshape(128, 1, 128 * CHUNK2)).reshape(128 * CHUNK2, 128)
     bundle, _ = lax.optimization_barrier((bundle, routed))
@@ -409,7 +418,7 @@
             ((ROWS, D), BF16),
             ((128, 128), F32),
         ],
-        (entity_t, cols, bundle, relation_t, near2, far, far2, fetched),
+        (entity_t, cols, theirs, relation_t, near2, far, far2, fetched),
         vmem=32,
         scratch=[pltpu.VMEM((D, REL_DEV), F32)]
         + [pltpu.VMEM((PIECES, PIECE + 8, MAIN), F32)] * 2

time: 142 us -> 139 us (0.979)
  the two profiles are of different devices: /device:TPU:65 before, /device:TPU:83 now
where the time goes in v10:
time: 139 us; the launch traced here: 138 us
  starting transfers between devices  55.2 us (40%)
  blocking collectives  46.6 us (34%)
  Pallas kernels  25.6 us (18%)
  waiting for transfers between devices  7.84 us (6%)
  local copies, waits for them, and re-layouts  1.91 us (1%)
    pallas_call x9, Pallas kernels, call(): pl.pallas_call(kernel, out_shape=out_shape, in_specs=[pl.BlockSpec(memory...  25.6 us
    all_gather x1, blocking collectives, shards(): chips = lax.all_gather(half, 'zh', axis=0)  24.1 us
    all_gather x1, blocking collectives, shards(): far = lax.all_gather(bundle, 'x', axis=0)  17 us
    all_to_all x1, starting transfers between devices, shards(): exchange(payload.reshape(128, 1, 128 * CHUNK1)).reshape(128 * CHUNK1, 128)  15.5 us
    all_to_all x1, starting transfers between devices, shards(): exchange(routed.reshape(128, 1, 128 * CHUNK2)).reshape(128 * CHUNK2, 128)  14.6 us
    ppermute x1, starting transfers between devices, shards(): bundle = lax.ppermute(bundle, ('yz', 'zh'), perm=mirror)  8.07 us
    ppermute x1, waiting for transfers between devices, shards(): theirs = swap_zh(give)  7.82 us
    ppermute x1, starting transfers between devices, shards(): far2 = swap_core(far)  4.81 us
  transfers between devices with their start and end apart: 8, of which 1 were waited for; matrix products, arithmetic and copies ran while one was open for 0% of the time, Pallas kernels for 9%

profile of v10, /device:TPU:83, one launch (start us, length us, event | category | flops | bytes accessed | tf_op | source)
XLA Modules:
  0.0 138.0 jit_solution(2813449005463860500)
XLA Ops:
  0.6 2.4 %pack_kernel.1 = (f32[896,128]{1,0:T(8,128)}, f32[128,128]{1,0:T(8,128)}, f32[16,128]{1,0:T(8,128)}) custom-call(f32[400,512]{1,0:T(8,128)} %bitcast.18, s32[2,1,1,512]{3,2,1,0:T(1,128)} %head_hbm.1, s32[2,1,1,512]{3,2,1,0:T(1,128)} %rel_hbm.1, s32[2,1,1,512]{3,2,1,0:T(1,128)} %tail_hbm.1, s32[2,1,1,320]{3,2,1,0:T(1,128)} %neg_hbm.1, s32[1,1,2]{2,1,0:T(1,128)} %bitcast.29), custom_call_target="tpu_custom_call" | custom-call | tf_op jit(solution)/shard_map/pack_kernel/pallas_call | solution.py:344
  3.1 15.5 %all-to-all-start = ((f32[128,1,896]{2,1,0:T(1,128)}), f32[128,1,896]{2,1,0:T(1,128)S(1)}, u32[]{:S(2)}, u32[]{:S(2)}) async-start(f32[128,1,896]{2,1,0:T(1,128)} %bitcast.28), calls=%async_computation | async-start | bytes 917504 | tf_op jit(solution)/shard_map/all_to_all | solution.py:376
  18.6 0.0 copy-start.1
  18.6 1.2 copy-done.1
  19.8 0.7 copy-done.4
  20.5 0.1 bundle_kernel.1
  20.5 8.1 %collective-permute-start = (f32[112,512]{1,0:T(8,128)S(1)}, f32[112,512]{1,0:T(8,128)S(1)}, u32[]{:S(2)}, u32[]{:S(2)}) collective-permute-start(f32[112,512]{1,0:T(8,128)S(1)} %get-tuple-element.24), channel_id=1, source_target_pairs={{0,14},{2,12},{4,10},{6,8},{8,6},{10,4},{12,2},{14,0},{16,30},{18,... | collective-permute-start | bytes 688136 | tf_op jit(solution)/shard_map/ppermute | solution.py:386
  28.6 1.9 %collective-permute-start.1 = (f32[16,128]{1,0:T(8,128)}, f32[16,128]{1,0:T(8,128)S(1)}, u32[]{:S(2)}, u32[]{:S(2)}) collective-permute-start(f32[16,128]{1,0:T(8,128)} %get-tuple-element.25), channel_id=1, source_target_pairs={{0,2},{2,0},{1,3},{3,1},{4,6},{6,4},{5,7},{7,5},{8,10},{10,8},{9,1... | collective-permute-start | bytes 24584 | tf_op jit(solution)/shard_map/ppermute | solution.py:387
  30.6 7.8 %collective-permute-done.1.theirs_ref = f32[16,128]{1,0:T(8,128)S(1)} collective-permute-done((f32[16,128]{1,0:T(8,128)}, f32[16,128]{1,0:T(8,128)S(1)}, u32[]{:S(2)}, u32[]{:S(2)}) %collective-permute-start.1) | collective-permute-done | bytes 8224 | tf_op jit(solution)/shard_map/ppermute | solution.py:387
  38.4 0.0 collective-permute-done
  38.4 0.0 all-to-all-done
  38.4 1.7 %route_kernel.1 = f32[1664,128]{1,0:T(8,128)} custom-call(f32[896,128]{1,0:T(8,128)S(1)} %bitcast.23, s32[2,128]{1,0:T(2,128)S(1)} %get-tuple-element.27.matching_ref), custom_call_target="tpu_custom_call" | custom-call | tf_op jit(solution)/shard_map/route_kernel/pallas_call | solution.py:344
  40.0 14.6 %all-to-all-start.1 = ((f32[128,1,1664]{2,1,0:T(1,128)}), f32[128,1,1664]{2,1,0:T(1,128)S(1)}, u32[]{:S(2)}, u32[]{:S(2)}) async-start(f32[128,1,1664]{2,1,0:T(1,128)} %bitcast.5), calls=%async_computation.1 | async-start | bytes 1703936 | tf_op jit(solution)/shard_map/all_to_all | solution.py:397
  54.6 17.0 %all-gather = f32[448,512]{1,0:T(8,128)} all-gather(f32[112,512]{1,0:T(8,128)S(1)} %collective-permute-done), channel_id=2, replica_groups=mesh['x'=4,'yz'=32,'zh'=2,'core'=2] {'x'}, dimensions={0}, use_global_device_ids=true | all-gather | bytes 1146880 | tf_op jit(solution)/shard_map/all_gather | solution.py:399
  71.6 4.8 %collective-permute-start.5 = (f32[4,112,512]{2,1,0:T(8,128)}, f32[4,112,512]{2,1,0:T(8,128)}, u32[]{:S(2)}, u32[]{:S(2)}) collective-permute-start(f32[4,112,512]{2,1,0:T(8,128)} %bitcast.7.far_hbm), channel_id=1, source_target_pairs={{0,1},{1,0},{2,3},{3,2},{4,5},{5,4},{6,7},{7,6},{8,9},{9,8},{10,11... | collective-permute-start | bytes 2752520 | tf_op jit(solution)/shard_map/ppermute | solution.py:400
  76.4 1.9 %collective-permute-start.4 = (f32[400,528]{1,0:T(8,128)S(1)}, f32[400,528]{1,0:T(8,128)}, u32[]{:S(2)}, u32[]{:S(2)}) collective-permute-start(f32[400,528]{1,0:T(8,128)S(1)} %bitcast.25), channel_id=1, source_target_pairs={{0,1},{1,0},{2,3},{3,2},{4,5},{5,4},{6,7},{7,6},{8,9},{9,8},{10,11... | collective-permute-start | bytes 2534408 | tf_op jit(solution)/shard_map/ppermute | solution.py:388
  78.3 0.0 all-to-all-done.1
  78.3 4.2 %collective-permute-start.2 = (f32[1664,128]{1,0:T(8,128)S(1)}, f32[1664,128]{1,0:T(8,128)S(1)}, u32[]{:S(2)}, u32[]{:S(2)}) collective-permute-start(f32[1664,128]{1,0:T(8,128)S(1)} %bitcast.13), channel_id=1, source_target_pairs={{0,1},{1,0},{2,3},{3,2},{4,5},{5,4},{6,7},{7,6},{8,9},{9,8},{10,11... | collective-permute-start | bytes 2555912 | tf_op jit(solution)/shard_map/ppermute | solution.py:401
  82.5 4.3 %collective-permute-start.3 = (f32[16,128]{1,0:T(8,128)S(1)}, f32[16,128]{1,0:T(8,128)S(1)}, u32[]{:S(2)}, u32[]{:S(2)}) collective-permute-start(f32[16,128]{1,0:T(8,128)S(1)} %given_kernel.1), channel_id=1, source_target_pairs={{0,2},{2,0},{1,3},{3,1},{4,6},{6,4},{5,7},{7,5},{8,10},{10,8},{9,1... | collective-permute-start | bytes 24584 | tf_op jit(solution)/shard_map/ppermute | solution.py:402
  86.8 0.0 collective-permute-done.4.near2_hbm
  86.9 0.0 collective-permute-done.5.far2_hbm
  86.9 7.2 %relations_kernel.1 = (f32[1024,400]{1,0:T(8,128)S(1)}, bf16[1024,400]{1,0:T(8,128)(2,1)S(1)}, bf16[1024,400]{1,0:T(8,128)(2,1)S(1)}, f32[512,400]{1,0:T(8,128)S...) custom-call(f32[400,512]{1,0:T(8,128)S(1)} %bitcast.19, ...), custom_call_target="tpu_custom_call" | custom-call | flops 8000000000 | bytes 4000000 | tf_op jit(solution)/shard_map/relations_kernel/pallas_call | solution.py:344
  94.0 0.0 collective-permute-done.2.theirs_ref
  94.1 5.6 %head_kernel.1.head_grad = f32[512,400]{1,0:T(8,128)S(1)} custom-call(f32[1664,128]{1,0:T(8,128)S(1)} %bitcast.16, f32[1664,128]{1,0:T(8,128)S(1)} %collective-permute-done.2.theirs_ref, f32[128,128]{1,0:T(8,128)S(1)} %copy-done.5, f32[128,128]{1,0:T(8,128)S(1)} %get-tuple-element.36.lists_theirs, f32[1024,400]{1,0:T(8,128)S(1)} %get-tuple-element.37.rel_ref, ...), custom_call_target="tpu_custom_call" | custom-call | flops 6000000000 | bytes 4000000 | tf_op jit(solution)/shard_map/head_kernel/pallas_call | solution.py:344
  99.7 0.0 collective-permute-done.3.given_ref
  99.7 7.4 %tail_kernel.1 = (f32[400,256]{1,0:T(8,128)S(1)}, f32[400,256]{1,0:T(8,128)S(1)}) custom-call(f32[1664,128]{1,0:T(8,128)S(1)} %bitcast.17, f32[1664,128]{1,0:T(8,128)S(1)} %collective-permute-done.2.theirs_ref, f32[16,128]{1,0:T(8,128)S(1)} %collective-permute-done.3.given_ref, f32[512,400]{1,0:T(8,128)S(1)} %get-tuple-element.32.rel_ref, ...), custom_call_target="tpu_custom_call" | custom-call | flops 8999999488 | bytes 4000000 | tf_op jit(solution)/shard_map/tail_kernel/pallas_call | solution.py:344
  107.2 0.0 copy-start.3
  107.2 2.4 %all-gather.1 = f32[800,256]{1,0:T(8,128)S(1)} all-gather(f32[400,256]{1,0:T(8,128)S(1)} %get-tuple-element.41), channel_id=3, replica_groups=mesh['x'=4,'yz'=32,'zh'=2,'core'=2] {'core'}, dimensions={0}, use_global_device_ids=true | all-gather | bytes 1228800 | tf_op jit(solution)/shard_map/all_gather | solution.py:448
  109.6 24.1 %all-gather.2 = f32[800,256]{1,0:T(8,128)S(1)} all-gather(f32[400,256]{1,0:T(8,128)S(1)} %combine_kernel.1), channel_id=4, replica_groups=mesh['x'=4,'yz'=32,'zh'=2,'core'=2] {'zh'}, dimensions={0}, use_global_device_ids=true | all-gather | bytes 1228800 | tf_op jit(solution)/shard_map/all_gather | solution.py:450
  133.8 0.1 slice_add_fusion
  133.8 3.1 %all-gather.3 = f32[800,256]{1,0:T(8,128)S(1)} all-gather(f32[400,256]{1,0:T(8,128)S(1)} %slice_add_fusion), channel_id=5, replica_groups=mesh['x'=4,'yz'=32,'zh'=2,'core'=2] {'core'}, dimensions={0}, use_global_device_ids=true | all-gather | bytes 1228800 | tf_op jit(solution)/shard_map/all_gather | solution.py:451
  136.9 1.1 update_kernel.1
  (10 shorter events, 0.1 us)
Async XLA Ops:
  0.6 86.2 %copy-start = (f32[512,400]{0,1:T(8,128)S(1)}, f32[512,400]{0,1:T(8,128)}, u32[]{:S(2)}) copy-start(f32[512,400]{0,1:T(8,128)} %param.9) | copy-start | bytes 2457604
  3.1 83.8 %copy-start.5 = (f32[128,128]{1,0:T(8,128)S(1)}, f32[128,128]{1,0:T(8,128)}, u32[]{:S(2)}) copy-start(f32[128,128]{1,0:T(8,128)} %get-tuple-element.28.cols_ref.lists_mine) | copy-start | bytes 196612
  3.1 35.3 %all-to-all-start = ((f32[128,1,896]{2,1,0:T(1,128)}), f32[128,1,896]{2,1,0:T(1,128)S(1)}, u32[]{:S(2)}, u32[]{:S(2)}) async-start(f32[128,1,896]{2,1,0:T(1,128)} %bitcast.28), calls=%async_computation | async-start | bytes 917504 | tf_op jit(solution)/shard_map/all_to_all | solution.py:376
  18.6 1.2 copy-start.1
  19.8 0.7 copy-start.4
  20.5 55.9 %copy-start.2 = (f32[528,400]{0,1:T(8,128)S(1)}, f32[528,400]{0,1:T(8,128)}, u32[]{:S(2)}) copy-start(f32[528,400]{0,1:T(8,128)} %param.11) | copy-start | bytes 2534404
  20.5 17.8 %collective-permute-start = (f32[112,512]{1,0:T(8,128)S(1)}, f32[112,512]{1,0:T(8,128)S(1)}, u32[]{:S(2)}, u32[]{:S(2)}) collective-permute-start(f32[112,512]{1,0:T(8,128)S(1)} %get-tuple-element.24), channel_id=1, source_target_pairs={{0,14},{2,12},{4,10},{6,8},{8,6},{10,4},{12,2},{14,0},{16,30},{18,... | collective-permute-start | bytes 688136 | tf_op jit(solution)/shard_map/ppermute | solution.py:386
  28.6 9.7 %collective-permute-start.1 = (f32[16,128]{1,0:T(8,128)}, f32[16,128]{1,0:T(8,128)S(1)}, u32[]{:S(2)}, u32[]{:S(2)}) collective-permute-start(f32[16,128]{1,0:T(8,128)} %get-tuple-element.25), channel_id=1, source_target_pairs={{0,2},{2,0},{1,3},{3,1},{4,6},{6,4},{5,7},{7,5},{8,10},{10,8},{9,1... | collective-permute-start | bytes 24584 | tf_op jit(solution)/shard_map/ppermute | solution.py:387
  40.0 38.3 %all-to-all-start.1 = ((f32[128,1,1664]{2,1,0:T(1,128)}), f32[128,1,1664]{2,1,0:T(1,128)S(1)}, u32[]{:S(2)}, u32[]{:S(2)}) async-start(f32[128,1,1664]{2,1,0:T(1,128)} %bitcast.5), calls=%async_computation.1 | async-start | bytes 1703936 | tf_op jit(solution)/shard_map/all_to_all | solution.py:397
  71.6 15.3 %collective-permute-start.5 = (f32[4,112,512]{2,1,0:T(8,128)}, f32[4,112,512]{2,1,0:T(8,128)}, u32[]{:S(2)}, u32[]{:S(2)}) collective-permute-start(f32[4,112,512]{2,1,0:T(8,128)} %bitcast.7.far_hbm), channel_id=1, source_target_pairs={{0,1},{1,0},{2,3},{3,2},{4,5},{5,4},{6,7},{7,6},{8,9},{9,8},{10,11... | collective-permute-start | bytes 2752520 | tf_op jit(solution)/shard_map/ppermute | solution.py:400
  76.4 10.5 %collective-permute-start.4 = (f32[400,528]{1,0:T(8,128)S(1)}, f32[400,528]{1,0:T(8,128)}, u32[]{:S(2)}, u32[]{:S(2)}) collective-permute-start(f32[400,528]{1,0:T(8,128)S(1)} %bitcast.25), channel_id=1, source_target_pairs={{0,1},{1,0},{2,3},{3,2},{4,5},{5,4},{6,7},{7,6},{8,9},{9,8},{10,11... | collective-permute-start | bytes 2534408 | tf_op jit(solution)/shard_map/ppermute | solution.py:388
  78.3 15.7 %collective-permute-start.2 = (f32[1664,128]{1,0:T(8,128)S(1)}, f32[1664,128]{1,0:T(8,128)S(1)}, u32[]{:S(2)}, u32[]{:S(2)}) collective-permute-start(f32[1664,128]{1,0:T(8,128)S(1)} %bitcast.13), channel_id=1, source_target_pairs={{0,1},{1,0},{2,3},{3,2},{4,5},{5,4},{6,7},{7,6},{8,9},{9,8},{10,11... | collective-permute-start | bytes 2555912 | tf_op jit(solution)/shard_map/ppermute | solution.py:401
  82.5 17.2 %collective-permute-start.3 = (f32[16,128]{1,0:T(8,128)S(1)}, f32[16,128]{1,0:T(8,128)S(1)}, u32[]{:S(2)}, u32[]{:S(2)}) collective-permute-start(f32[16,128]{1,0:T(8,128)S(1)} %given_kernel.1), channel_id=1, source_target_pairs={{0,2},{2,0},{1,3},{3,1},{4,6},{6,4},{5,7},{7,5},{8,10},{10,8},{9,1... | collective-permute-start | bytes 24584 | tf_op jit(solution)/shard_map/ppermute | solution.py:402
  107.2 29.8 %copy-start.3 = (f32[512]{0:T(512)S(1)}, f32[512]{0:T(512)}, u32[]{:S(2)}) copy-start(f32[512]{0:T(512)} %param.10) | copy-start | bytes 6148

commit v11 on v10

--- a/solution.py
+++ b/solution.py
@@ -146,16 +146,23 @@
     return min(PIECE * spot, D - PIECE)
 
 
-def bundle_kernel(relation_ref, matching_ref, out_ref, matching_out):
+def bundle_kernel(relation_hbm, out_ref, piece_ref, sem):
     spot = lax.axis_index("x")
     start = pl.multiple_of(jnp.minimum(PIECE * spot, D - PIECE), 8)
-    piece = relation_ref[pl.ds(start, PIECE), :]
+    copy = pltpu.make_async_copy(relation_hbm.at[pl.ds(start, PIECE), :], piece_ref, sem)
+    copy.start()
+    copy.wait()
+    piece = piece_ref[...]
     out_ref[0:PIECE, :] = piece[:, 0:MAIN]
     rest = jnp.concatenate([piece[:, MAIN:REL_DEV], jnp.zeros((PIECE, 128 - REST), F32)], axis=1)
     rest = jnp.concatenate([rest, jnp.zeros((128 - PIECE, 128), F32)], axis=0).T
     for g in range(4):
         out_ref[PIECE : PIECE + 4, 128 * g : 128 * (g + 1)] = rest[4 * g : 4 * g + 4, :]
     out_ref[PIECE + 4 : PIECE + 8, :] = jnp.zeros((4, MAIN), F32)
+
+
+def lists_kernel(give_ref, matching_ref, give_out, matching_out):
+    give_out[...] = give_ref[...]
     matching_out[...] = matching_ref[...]
 
 
@@ -171,7 +178,7 @@
 
 def load_indices(rels, zh, core, index_vmem, index_smem, sem):
     rels = jnp.concatenate([rels, jnp.zeros((16 - rels.shape[0], 128), F32)], axis=0)
-    index_vmem[...] = table_row(rels.astype(jnp.int32), zh, core)
+    index_vmem[...] = 4 * table_row(rels.astype(jnp.int32), zh, core)
     copy = pltpu.make_async_copy(index_vmem, index_smem, sem)
     copy.start()
     return copy
@@ -182,7 +189,7 @@
         for j in range(4):
             for u in range(8):
                 lane = step * 8 + u
-                at = pl.multiple_of(4 * index_smem[first + j, lane], 4)
+                at = pl.multiple_of(index_smem[first + j, lane], 4)
                 to = pl.multiple_of(512 * j + 4 * lane, 4)
                 out_ref[pl.ds(to, 4), :] = table_ref[pl.ds(at, 4), :]
         return 0
@@ -375,12 +382,15 @@
     )
     spread = exchange(payload.reshape(128, 1, 128 * CHUNK1)).reshape(128 * CHUNK1, 128)
 
-    bundle, matching = call(
+    bundle = call(
         bundle_kernel,
-        [((PIECE + 8, MAIN), F32), ((2, 128), jnp.int32)],
-        (relation_t, matching),
-        vmem=8,
-    )
+        ((PIECE + 8, MAIN), F32),
+        (relation_t,),
+        vmem=60,
+        scratch=[pltpu.VMEM((PIECE, REL_DEV), F32), pltpu.SemaphoreType.DMA],
+        in_hbm=(0,),
+    )
+    give, matching = call(lists_kernel, [((LIST, 128), F32), ((2, 128), jnp.int32)], (give, matching), vmem=4)
     lines = lax.axis_size("yz") // 4
     mirror = [((4 * y + z) * 2 + h, (4 * y + 3 - z) * 2 + 1 - h) for y in range(lines) for z in range(4) for h in range(2)]
     bundle = lax.ppermute(bundle, ("yz", "zh"), perm=mirror)

time: 139 us -> 138 us (level)
    pallas_call x9 -> x10, Pallas kernels: 25.6 us -> 26.8 us  [call(): pl.pallas_call(kernel, out_shape=out_shape, in_specs=[pl.BlockSpec(memory...]
  transfers between devices with their start and end apart: 8 -> 8, of which waited for: 1 -> 1; matrix products, arithmetic and copies ran while one was open for 0% -> 0% of each run, Pallas kernels for 9% -> 10%
where the time goes in v11:
time: 138 us; the launch traced here: 137 us
  starting transfers between devices  54.8 us (40%)
  blocking collectives  46.6 us (34%)
  Pallas kernels  26.8 us (19%)
  waiting for transfers between devices  6.92 us (5%)
  local copies, waits for them, and re-layouts  1.39 us (1%)
    pallas_call x10, Pallas kernels, call(): pl.pallas_call(kernel, out_shape=out_shape, in_specs=[pl.BlockSpec(memory...  26.8 us
    all_gather x1, blocking collectives, shards(): chips = lax.all_gather(half, 'zh', axis=0)  24.1 us
    all_gather x1, blocking collectives, shards(): far = lax.all_gather(bundle, 'x', axis=0)  17 us
    all_to_all x1, starting transfers between devices, shards(): exchange(payload.reshape(128, 1, 128 * CHUNK1)).reshape(128 * CHUNK1, 128)  15.5 us
    all_to_all x1, starting transfers between devices, shards(): exchange(routed.reshape(128, 1, 128 * CHUNK2)).reshape(128 * CHUNK2, 128)  14.4 us
    ppermute x1, starting transfers between devices, shards(): bundle = lax.ppermute(bundle, ('yz', 'zh'), perm=mirror)  7.95 us
    ppermute x1, waiting for transfers between devices, shards(): theirs = swap_zh(give)  6.91 us
    ppermute x1, starting transfers between devices, shards(): far2 = swap_core(far)  4.81 us
  transfers between devices with their start and end apart: 8, of which 1 were waited for; matrix products, arithmetic and copies ran while one was open for 0% of the time, Pallas kernels for 10%

profile of v11, /device:TPU:83, one launch (start us, length us, event | category | flops | bytes accessed | tf_op | source)
XLA Modules:
  0.0 137.4 jit_solution(4323961264081983181)
XLA Ops:
  0.6 0.0 copy-start.1
  0.7 2.5 %pack_kernel.1 = (f32[896,128]{1,0:T(8,128)}, f32[128,128]{1,0:T(8,128)}, f32[16,128]{1,0:T(8,128)}) custom-call(f32[400,512]{1,0:T(8,128)} %bitcast.18, s32[2,1,1,512]{3,2,1,0:T(1,128)} %head_hbm.1, s32[2,1,1,512]{3,2,1,0:T(1,128)} %rel_hbm.1, s32[2,1,1,512]{3,2,1,0:T(1,128)} %tail_hbm.1, s32[2,1,1,320]{3,2,1,0:T(1,128)} %neg_hbm.1, s32[1,1,2]{2,1,0:T(1,128)} %bitcast.29), custom_call_target="tpu_custom_call" | custom-call | tf_op jit(solution)/shard_map/pack_kernel/pallas_call | solution.py:351
  3.2 15.5 %all-to-all-start = ((f32[128,1,896]{2,1,0:T(1,128)}), f32[128,1,896]{2,1,0:T(1,128)S(1)}, u32[]{:S(2)}, u32[]{:S(2)}) async-start(f32[128,1,896]{2,1,0:T(1,128)} %bitcast.28), calls=%async_computation | async-start | bytes 917504 | tf_op jit(solution)/shard_map/all_to_all | solution.py:383
  18.6 1.7 %bundle_kernel.1 = f32[112,512]{1,0:T(8,128)} custom-call(f32[400,528]{1,0:T(8,128)} %bitcast.24), custom_call_target="tpu_custom_call" | custom-call | tf_op jit(solution)/shard_map/bundle_kernel/pallas_call | solution.py:351
  20.4 7.9 %collective-permute-start = (f32[112,512]{1,0:T(8,128)}, f32[112,512]{1,0:T(8,128)S(1)}, u32[]{:S(2)}, u32[]{:S(2)}) collective-permute-start(f32[112,512]{1,0:T(8,128)} %bundle_kernel.1), channel_id=1, source_target_pairs={{0,14},{2,12},{4,10},{6,8},{8,6},{10,4},{12,2},{14,0},{16,30},{18,... | collective-permute-start | bytes 688136 | tf_op jit(solution)/shard_map/ppermute | solution.py:396
  28.3 0.7 copy-done.2
  29.0 0.7 copy-done.4
  29.7 1.9 %collective-permute-start.1 = (f32[16,128]{1,0:T(8,128)S(1)}, f32[16,128]{1,0:T(8,128)S(1)}, u32[]{:S(2)}, u32[]{:S(2)}) collective-permute-start(f32[16,128]{1,0:T(8,128)S(1)} %get-tuple-element.25), channel_id=1, source_target_pairs={{0,2},{2,0},{1,3},{3,1},{4,6},{6,4},{5,7},{7,5},{8,10},{10,8},{9,1... | collective-permute-start | bytes 24584 | tf_op jit(solution)/shard_map/ppermute | solution.py:397
  31.6 6.9 %collective-permute-done.1.theirs_ref = f32[16,128]{1,0:T(8,128)S(1)} collective-permute-done((f32[16,128]{1,0:T(8,128)S(1)}, f32[16,128]{1,0:T(8,128)S(1)}, u32[]{:S(2)}, u32[]{:S(2)}) %collective-permute-start.1) | collective-permute-done | bytes 8224 | tf_op jit(solution)/shard_map/ppermute | solution.py:397
  38.5 0.0 collective-permute-done
  38.5 0.0 all-to-all-done
  38.5 1.7 %route_kernel.1 = f32[1664,128]{1,0:T(8,128)} custom-call(f32[896,128]{1,0:T(8,128)S(1)} %bitcast.23, s32[2,128]{1,0:T(2,128)S(1)} %get-tuple-element.27.matching_ref), custom_call_target="tpu_custom_call" | custom-call | tf_op jit(solution)/shard_map/route_kernel/pallas_call | solution.py:351
  40.2 14.4 %all-to-all-start.1 = ((f32[128,1,1664]{2,1,0:T(1,128)}), f32[128,1,1664]{2,1,0:T(1,128)S(1)}, u32[]{:S(2)}, u32[]{:S(2)}) async-start(f32[128,1,1664]{2,1,0:T(1,128)} %bitcast.5), calls=%async_computation.1 | async-start | bytes 1703936 | tf_op jit(solution)/shard_map/all_to_all | solution.py:407
  54.6 17.0 %all-gather = f32[448,512]{1,0:T(8,128)} all-gather(f32[112,512]{1,0:T(8,128)S(1)} %collective-permute-done), channel_id=2, replica_groups=mesh['x'=4,'yz'=32,'zh'=2,'core'=2] {'x'}, dimensions={0}, use_global_device_ids=true | all-gather | bytes 1146880 | tf_op jit(solution)/shard_map/all_gather | solution.py:409
  71.6 4.8 %collective-permute-start.5 = (f32[4,112,512]{2,1,0:T(8,128)}, f32[4,112,512]{2,1,0:T(8,128)}, u32[]{:S(2)}, u32[]{:S(2)}) collective-permute-start(f32[4,112,512]{2,1,0:T(8,128)} %bitcast.7.far_hbm), channel_id=1, source_target_pairs={{0,1},{1,0},{2,3},{3,2},{4,5},{5,4},{6,7},{7,6},{8,9},{9,8},{10,11... | collective-permute-start | bytes 2752520 | tf_op jit(solution)/shard_map/ppermute | solution.py:410
  76.4 1.9 %collective-permute-start.4 = (f32[400,528]{1,0:T(8,128)S(1)}, f32[400,528]{1,0:T(8,128)}, u32[]{:S(2)}, u32[]{:S(2)}) collective-permute-start(f32[400,528]{1,0:T(8,128)S(1)} %bitcast.25), channel_id=1, source_target_pairs={{0,1},{1,0},{2,3},{3,2},{4,5},{5,4},{6,7},{7,6},{8,9},{9,8},{10,11... | collective-permute-start | bytes 2534408 | tf_op jit(solution)/shard_map/ppermute | solution.py:398
  78.3 0.0 all-to-all-done.1
  78.3 4.2 %collective-permute-start.2 = (f32[1664,128]{1,0:T(8,128)S(1)}, f32[1664,128]{1,0:T(8,128)S(1)}, u32[]{:S(2)}, u32[]{:S(2)}) collective-permute-start(f32[1664,128]{1,0:T(8,128)S(1)} %bitcast.13), channel_id=1, source_target_pairs={{0,1},{1,0},{2,3},{3,2},{4,5},{5,4},{6,7},{7,6},{8,9},{9,8},{10,11... | collective-permute-start | bytes 2555912 | tf_op jit(solution)/shard_map/ppermute | solution.py:411
  82.5 4.2 %collective-permute-start.3 = (f32[16,128]{1,0:T(8,128)S(1)}, f32[16,128]{1,0:T(8,128)S(1)}, u32[]{:S(2)}, u32[]{:S(2)}) collective-permute-start(f32[16,128]{1,0:T(8,128)S(1)} %given_kernel.1), channel_id=1, source_target_pairs={{0,2},{2,0},{1,3},{3,1},{4,6},{6,4},{5,7},{7,5},{8,10},{10,8},{9,1... | collective-permute-start | bytes 24584 | tf_op jit(solution)/shard_map/ppermute | solution.py:412
  86.8 0.0 collective-permute-done.5.far2_hbm
  86.8 6.8 %relations_kernel.1 = (f32[1024,400]{1,0:T(8,128)S(1)}, bf16[1024,400]{1,0:T(8,128)(2,1)S(1)}, bf16[1024,400]{1,0:T(8,128)(2,1)S(1)}, f32[512,400]{1,0:T(8,128)S...) custom-call(f32[400,512]{1,0:T(8,128)S(1)} %bitcast.19, ...), custom_call_target="tpu_custom_call" | custom-call | flops 8000000000 | bytes 4000000 | tf_op jit(solution)/shard_map/relations_kernel/pallas_call | solution.py:351
  93.6 0.0 collective-permute-done.2.theirs_ref
  93.6 5.6 %head_kernel.1.head_grad = f32[512,400]{1,0:T(8,128)S(1)} custom-call(f32[1664,128]{1,0:T(8,128)S(1)} %bitcast.16, f32[1664,128]{1,0:T(8,128)S(1)} %collective-permute-done.2.theirs_ref, f32[128,128]{1,0:T(8,128)S(1)} %copy-done.5, f32[128,128]{1,0:T(8,128)S(1)} %get-tuple-element.36.lists_theirs, f32[1024,400]{1,0:T(8,128)S(1)} %get-tuple-element.37.rel_ref, ...), custom_call_target="tpu_custom_call" | custom-call | flops 6000000000 | bytes 4000000 | tf_op jit(solution)/shard_map/head_kernel/pallas_call | solution.py:351
  99.2 0.0 collective-permute-done.3.given_ref
  99.2 7.3 %tail_kernel.1 = (f32[400,256]{1,0:T(8,128)S(1)}, f32[400,256]{1,0:T(8,128)S(1)}) custom-call(f32[1664,128]{1,0:T(8,128)S(1)} %bitcast.17, f32[1664,128]{1,0:T(8,128)S(1)} %collective-permute-done.2.theirs_ref, f32[16,128]{1,0:T(8,128)S(1)} %collective-permute-done.3.given_ref, f32[512,400]{1,0:T(8,128)S(1)} %get-tuple-element.32.rel_ref, ...), custom_call_target="tpu_custom_call" | custom-call | flops 8999999488 | bytes 4000000 | tf_op jit(solution)/shard_map/tail_kernel/pallas_call | solution.py:351
  106.6 0.0 copy-start.3
  106.6 2.4 %all-gather.1 = f32[800,256]{1,0:T(8,128)S(1)} all-gather(f32[400,256]{1,0:T(8,128)S(1)} %get-tuple-element.41), channel_id=3, replica_groups=mesh['x'=4,'yz'=32,'zh'=2,'core'=2] {'core'}, dimensions={0}, use_global_device_ids=true | all-gather | bytes 1228800 | tf_op jit(solution)/shard_map/all_gather | solution.py:458
  109.0 0.1 combine_kernel.1
  109.0 24.1 %all-gather.2 = f32[800,256]{1,0:T(8,128)S(1)} all-gather(f32[400,256]{1,0:T(8,128)S(1)} %combine_kernel.1), channel_id=4, replica_groups=mesh['x'=4,'yz'=32,'zh'=2,'core'=2] {'zh'}, dimensions={0}, use_global_device_ids=true | all-gather | bytes 1228800 | tf_op jit(solution)/shard_map/all_gather | solution.py:460
  133.1 0.1 slice_add_fusion
  133.2 3.1 %all-gather.3 = f32[800,256]{1,0:T(8,128)S(1)} all-gather(f32[400,256]{1,0:T(8,128)S(1)} %slice_add_fusion), channel_id=5, replica_groups=mesh['x'=4,'yz'=32,'zh'=2,'core'=2] {'core'}, dimensions={0}, use_global_device_ids=true | all-gather | bytes 1228800 | tf_op jit(solution)/shard_map/all_gather | solution.py:461
  136.3 1.1 update_kernel.1
  (11 shorter events, 0.1 us)
Async XLA Ops:
  0.6 86.1 %copy-start = (f32[512,400]{0,1:T(8,128)S(1)}, f32[512,400]{0,1:T(8,128)}, u32[]{:S(2)}) copy-start(f32[512,400]{0,1:T(8,128)} %param.9) | copy-start | bytes 2457604
  0.6 75.7 %copy-start.1 = (f32[528,400]{0,1:T(8,128)S(1)}, f32[528,400]{0,1:T(8,128)}, u32[]{:S(2)}) copy-start(f32[528,400]{0,1:T(8,128)} %param.11) | copy-start | bytes 2534404
  3.2 83.6 %copy-start.5 = (f32[128,128]{1,0:T(8,128)S(1)}, f32[128,128]{1,0:T(8,128)}, u32[]{:S(2)}) copy-start(f32[128,128]{1,0:T(8,128)} %get-tuple-element.28.cols_ref.lists_mine) | copy-start | bytes 196612
  3.2 35.4 %all-to-all-start = ((f32[128,1,896]{2,1,0:T(1,128)}), f32[128,1,896]{2,1,0:T(1,128)S(1)}, u32[]{:S(2)}, u32[]{:S(2)}) async-start(f32[128,1,896]{2,1,0:T(1,128)} %bitcast.28), calls=%async_computation | async-start | bytes 917504 | tf_op jit(solution)/shard_map/all_to_all | solution.py:383
  20.4 18.2 %collective-permute-start = (f32[112,512]{1,0:T(8,128)}, f32[112,512]{1,0:T(8,128)S(1)}, u32[]{:S(2)}, u32[]{:S(2)}) collective-permute-start(f32[112,512]{1,0:T(8,128)} %bundle_kernel.1), channel_id=1, source_target_pairs={{0,14},{2,12},{4,10},{6,8},{8,6},{10,4},{12,2},{14,0},{16,30},{18,... | collective-permute-start | bytes 688136 | tf_op jit(solution)/shard_map/ppermute | solution.py:396
  28.3 0.7 copy-start.2
  29.0 0.7 copy-start.4
  29.7 8.8 %collective-permute-start.1 = (f32[16,128]{1,0:T(8,128)S(1)}, f32[16,128]{1,0:T(8,128)S(1)}, u32[]{:S(2)}, u32[]{:S(2)}) collective-permute-start(f32[16,128]{1,0:T(8,128)S(1)} %get-tuple-element.25), channel_id=1, source_target_pairs={{0,2},{2,0},{1,3},{3,1},{4,6},{6,4},{5,7},{7,5},{8,10},{10,8},{9,1... | collective-permute-start | bytes 24584 | tf_op jit(solution)/shard_map/ppermute | solution.py:397
  40.2 38.1 %all-to-all-start.1 = ((f32[128,1,1664]{2,1,0:T(1,128)}), f32[128,1,1664]{2,1,0:T(1,128)S(1)}, u32[]{:S(2)}, u32[]{:S(2)}) async-start(f32[128,1,1664]{2,1,0:T(1,128)} %bitcast.5), calls=%async_computation.1 | async-start | bytes 1703936 | tf_op jit(solution)/shard_map/all_to_all | solution.py:407
  71.6 15.2 %collective-permute-start.5 = (f32[4,112,512]{2,1,0:T(8,128)}, f32[4,112,512]{2,1,0:T(8,128)}, u32[]{:S(2)}, u32[]{:S(2)}) collective-permute-start(f32[4,112,512]{2,1,0:T(8,128)} %bitcast.7.far_hbm), channel_id=1, source_target_pairs={{0,1},{1,0},{2,3},{3,2},{4,5},{5,4},{6,7},{7,6},{8,9},{9,8},{10,11... | collective-permute-start | bytes 2752520 | tf_op jit(solution)/shard_map/ppermute | solution.py:410
  76.4 10.4 %collective-permute-start.4 = (f32[400,528]{1,0:T(8,128)S(1)}, f32[400,528]{1,0:T(8,128)}, u32[]{:S(2)}, u32[]{:S(2)}) collective-permute-start(f32[400,528]{1,0:T(8,128)S(1)} %bitcast.25), channel_id=1, source_target_pairs={{0,1},{1,0},{2,3},{3,2},{4,5},{5,4},{6,7},{7,6},{8,9},{9,8},{10,11... | collective-permute-start | bytes 2534408 | tf_op jit(solution)/shard_map/ppermute | solution.py:398
  78.3 15.3 %collective-permute-start.2 = (f32[1664,128]{1,0:T(8,128)S(1)}, f32[1664,128]{1,0:T(8,128)S(1)}, u32[]{:S(2)}, u32[]{:S(2)}) collective-permute-start(f32[1664,128]{1,0:T(8,128)S(1)} %bitcast.13), channel_id=1, source_target_pairs={{0,1},{1,0},{2,3},{3,2},{4,5},{5,4},{6,7},{7,6},{8,9},{9,8},{10,11... | collective-permute-start | bytes 2555912 | tf_op jit(solution)/shard_map/ppermute | solution.py:411
  82.5 16.7 %collective-permute-start.3 = (f32[16,128]{1,0:T(8,128)S(1)}, f32[16,128]{1,0:T(8,128)S(1)}, u32[]{:S(2)}, u32[]{:S(2)}) collective-permute-start(f32[16,128]{1,0:T(8,128)S(1)} %given_kernel.1), channel_id=1, source_target_pairs={{0,2},{2,0},{1,3},{3,1},{4,6},{6,4},{5,7},{7,5},{8,10},{10,8},{9,1... | collective-permute-start | bytes 24584 | tf_op jit(solution)/shard_map/ppermute | solution.py:412
  106.6 29.8 %copy-start.3 = (f32[512]{0:T(512)S(1)}, f32[512]{0:T(512)}, u32[]{:S(2)}) copy-start(f32[512]{0:T(512)} %param.10) | copy-start | bytes 6148

commit v12 on v11

--- a/solution.py
+++ b/solution.py
@@ -396,7 +396,6 @@
     bundle = lax.ppermute(bundle, ("yz", "zh"), perm=mirror)
     theirs = swap_zh(give)
     near2 = swap_core(relation_t)
-    spread, bundle, theirs = lax.optimization_barrier((spread, bundle, theirs))
 
     routed = call(
         route_kernel,
@@ -404,8 +403,8 @@
         (spread, matching),
         vmem=16,
     )
+    routed, bundle, theirs = lax.optimization_barrier((routed, bundle, theirs))
     fetched = exchange(routed.reshape(128, 1, 128 * CHUNK2)).reshape(128 * CHUNK2, 128)
-    bundle, _ = lax.optimization_barrier((bundle, routed))
     far = lax.all_gather(bundle, "x", axis=0)
     far2 = swap_core(far)
     fetched_other = swap_core(fetched)

time: 138 us -> 136 us (0.986)
  waiting for transfers between devices: 6.92 us -> 5.27 us
    ppermute x1, waiting for transfers between devices: 6.91 us -> 2.96 us  [shards(): theirs = swap_zh(give)]
    all_to_all x1, waiting for transfers between devices: 0.01 us -> 2.29 us  [shards(): exchange(payload.reshape(128, 1, 128 * CHUNK1)).reshape(128 * CHUNK1, 128)]
  transfers between devices with their start and end apart: 8 -> 8, of which waited for: 1 -> 2; matrix products, arithmetic and copies ran while one was open for 0% -> 0% of each run, Pallas kernels for 10% -> 12%
where the time goes in v12:
time: 136 us
  starting transfers between devices  54.8 us (40%)
  blocking collectives  46.6 us (34%)
  Pallas kernels  26.8 us (20%)
  waiting for transfers between devices  5.27 us (4%)
  local copies, waits for them, and re-layouts  1.39 us (1%)
    pallas_call x10, Pallas kernels, call(): pl.pallas_call(kernel, out_shape=out_shape, in_specs=[pl.BlockSpec(memory...  26.8 us
    all_gather x1, blocking collectives, shards(): chips = lax.all_gather(half, 'zh', axis=0)  24.1 us
    all_gather x1, blocking collectives, shards(): far = lax.all_gather(bundle, 'x', axis=0)  17 us
    all_to_all x1, starting transfers between devices, shards(): exchange(payload.reshape(128, 1, 128 * CHUNK1)).reshape(128 * CHUNK1, 128)  15.5 us
    all_to_all x1, starting transfers between devices, shards(): exchange(routed.reshape(128, 1, 128 * CHUNK2)).reshape(128 * CHUNK2, 128)  14.4 us
    ppermute x1, starting transfers between devices, shards(): bundle = lax.ppermute(bundle, ('yz', 'zh'), perm=mirror)  7.95 us
    ppermute x1, starting transfers between devices, shards(): far2 = swap_core(far)  4.81 us
    ppermute x1, starting transfers between devices, shards(): given = swap_zh(call(given_kernel, ((LIST, 128), F32), (fetched,), vmem=4))  4.22 us
  transfers between devices with their start and end apart: 8, of which 2 were waited for; matrix products, arithmetic and copies ran while one was open for 0% of the time, Pallas kernels for 12%

profile of v12, /device:TPU:83, one launch (start us, length us, event | category | flops | bytes accessed | tf_op | source)
XLA Modules:
  0.0 135.8 jit_solution(16207291508421156888)
XLA Ops:
  0.6 0.0 copy-start.1
  0.7 2.5 %pack_kernel.1 = (f32[896,128]{1,0:T(8,128)}, f32[128,128]{1,0:T(8,128)}, f32[16,128]{1,0:T(8,128)}) custom-call(f32[400,512]{1,0:T(8,128)} %bitcast.18, s32[2,1,1,512]{3,2,1,0:T(1,128)} %head_hbm.1, s32[2,1,1,512]{3,2,1,0:T(1,128)} %rel_hbm.1, s32[2,1,1,512]{3,2,1,0:T(1,128)} %tail_hbm.1, s32[2,1,1,320]{3,2,1,0:T(1,128)} %neg_hbm.1, s32[1,1,2]{2,1,0:T(1,128)} %bitcast.29), custom_call_target="tpu_custom_call" | custom-call | tf_op jit(solution)/shard_map/pack_kernel/pallas_call | solution.py:351
  3.2 15.5 %all-to-all-start = ((f32[128,1,896]{2,1,0:T(1,128)}), f32[128,1,896]{2,1,0:T(1,128)S(1)}, u32[]{:S(2)}, u32[]{:S(2)}) async-start(f32[128,1,896]{2,1,0:T(1,128)} %bitcast.28), calls=%async_computation | async-start | bytes 917504 | tf_op jit(solution)/shard_map/all_to_all | solution.py:383
  18.6 1.7 %bundle_kernel.1 = f32[112,512]{1,0:T(8,128)} custom-call(f32[400,528]{1,0:T(8,128)} %bitcast.24), custom_call_target="tpu_custom_call" | custom-call | tf_op jit(solution)/shard_map/bundle_kernel/pallas_call | solution.py:351
  20.4 7.9 %collective-permute-start = (f32[112,512]{1,0:T(8,128)}, f32[112,512]{1,0:T(8,128)S(1)}, u32[]{:S(2)}, u32[]{:S(2)}) collective-permute-start(f32[112,512]{1,0:T(8,128)} %bundle_kernel.1), channel_id=1, source_target_pairs={{0,14},{2,12},{4,10},{6,8},{8,6},{10,4},{12,2},{14,0},{16,30},{18,... | collective-permute-start | bytes 688136 | tf_op jit(solution)/shard_map/ppermute | solution.py:396
  28.3 0.7 copy-done.2
  29.0 0.7 copy-done.4
  29.7 1.9 %collective-permute-start.1 = (f32[16,128]{1,0:T(8,128)S(1)}, f32[16,128]{1,0:T(8,128)S(1)}, u32[]{:S(2)}, u32[]{:S(2)}) collective-permute-start(f32[16,128]{1,0:T(8,128)S(1)} %get-tuple-element.25), channel_id=1, source_target_pairs={{0,2},{2,0},{1,3},{3,1},{4,6},{6,4},{5,7},{7,5},{8,10},{10,8},{9,1... | collective-permute-start | bytes 24584 | tf_op jit(solution)/shard_map/ppermute | solution.py:397
  31.6 2.3 %all-to-all-done = f32[128,1,896]{2,1,0:T(1,128)S(1)} async-done(((f32[128,1,896]{2,1,0:T(1,128)}), f32[128,1,896]{2,1,0:T(1,128)S(1)}, u32[]{:S(2)}, u32[]{:S(2)}) %all-to-all-start) | async-done | bytes 458784 | tf_op jit(solution)/shard_map/all_to_all | solution.py:383
  33.9 1.7 %route_kernel.1 = f32[1664,128]{1,0:T(8,128)} custom-call(f32[896,128]{1,0:T(8,128)S(1)} %bitcast.23, s32[2,128]{1,0:T(2,128)S(1)} %get-tuple-element.24.matching_ref), custom_call_target="tpu_custom_call" | custom-call | tf_op jit(solution)/shard_map/route_kernel/pallas_call | solution.py:351
  35.6 3.0 %collective-permute-done.1.theirs_ref = f32[16,128]{1,0:T(8,128)S(1)} collective-permute-done((f32[16,128]{1,0:T(8,128)S(1)}, f32[16,128]{1,0:T(8,128)S(1)}, u32[]{:S(2)}, u32[]{:S(2)}) %collective-permute-start.1) | collective-permute-done | bytes 8224 | tf_op jit(solution)/shard_map/ppermute | solution.py:397
  38.5 0.0 collective-permute-done
  38.5 14.4 %all-to-all-start.1 = ((f32[128,1,1664]{2,1,0:T(1,128)}), f32[128,1,1664]{2,1,0:T(1,128)S(1)}, u32[]{:S(2)}, u32[]{:S(2)}) async-start(f32[128,1,1664]{2,1,0:T(1,128)} %bitcast.5), calls=%async_computation.1 | async-start | bytes 1703936 | tf_op jit(solution)/shard_map/all_to_all | solution.py:407
  53.0 17.0 %all-gather = f32[448,512]{1,0:T(8,128)} all-gather(f32[112,512]{1,0:T(8,128)S(1)} %collective-permute-done), channel_id=2, replica_groups=mesh['x'=4,'yz'=32,'zh'=2,'core'=2] {'x'}, dimensions={0}, use_global_device_ids=true | all-gather | bytes 1146880 | tf_op jit(solution)/shard_map/all_gather | solution.py:408
  69.9 4.8 %collective-permute-start.5 = (f32[4,112,512]{2,1,0:T(8,128)}, f32[4,112,512]{2,1,0:T(8,128)}, u32[]{:S(2)}, u32[]{:S(2)}) collective-permute-start(f32[4,112,512]{2,1,0:T(8,128)} %bitcast.7.far_hbm), channel_id=1, source_target_pairs={{0,1},{1,0},{2,3},{3,2},{4,5},{5,4},{6,7},{7,6},{8,9},{9,8},{10,11... | collective-permute-start | bytes 2752520 | tf_op jit(solution)/shard_map/ppermute | solution.py:409
  74.7 1.9 %collective-permute-start.4 = (f32[400,528]{1,0:T(8,128)S(1)}, f32[400,528]{1,0:T(8,128)}, u32[]{:S(2)}, u32[]{:S(2)}) collective-permute-start(f32[400,528]{1,0:T(8,128)S(1)} %bitcast.25), channel_id=1, source_target_pairs={{0,1},{1,0},{2,3},{3,2},{4,5},{5,4},{6,7},{7,6},{8,9},{9,8},{10,11... | collective-permute-start | bytes 2534408 | tf_op jit(solution)/shard_map/ppermute | solution.py:398
  76.7 4.2 %collective-permute-start.2 = (f32[1664,128]{1,0:T(8,128)S(1)}, f32[1664,128]{1,0:T(8,128)S(1)}, u32[]{:S(2)}, u32[]{:S(2)}) collective-permute-start(f32[1664,128]{1,0:T(8,128)S(1)} %bitcast.13), channel_id=1, source_target_pairs={{0,1},{1,0},{2,3},{3,2},{4,5},{5,4},{6,7},{7,6},{8,9},{9,8},{10,11... | collective-permute-start | bytes 2555912 | tf_op jit(solution)/shard_map/ppermute | solution.py:410
  80.9 4.2 %collective-permute-start.3 = (f32[16,128]{1,0:T(8,128)S(1)}, f32[16,128]{1,0:T(8,128)S(1)}, u32[]{:S(2)}, u32[]{:S(2)}) collective-permute-start(f32[16,128]{1,0:T(8,128)S(1)} %given_kernel.1), channel_id=1, source_target_pairs={{0,2},{2,0},{1,3},{3,1},{4,6},{6,4},{5,7},{7,5},{8,10},{10,8},{9,1... | collective-permute-start | bytes 24584 | tf_op jit(solution)/shard_map/ppermute | solution.py:411
  85.1 0.0 collective-permute-done.4.near2_hbm
  85.1 0.0 collective-permute-done.5.far2_hbm
  85.1 6.8 %relations_kernel.1 = (f32[1024,400]{1,0:T(8,128)S(1)}, bf16[1024,400]{1,0:T(8,128)(2,1)S(1)}, bf16[1024,400]{1,0:T(8,128)(2,1)S(1)}, f32[512,400]{1,0:T(8,128)S...) custom-call(f32[400,512]{1,0:T(8,128)S(1)} %bitcast.19, ...), custom_call_target="tpu_custom_call" | custom-call | flops 8000000000 | bytes 4000000 | tf_op jit(solution)/shard_map/relations_kernel/pallas_call | solution.py:351
  91.9 0.0 collective-permute-done.2.theirs_ref
  91.9 5.6 %head_kernel.1.head_grad = f32[512,400]{1,0:T(8,128)S(1)} custom-call(f32[1664,128]{1,0:T(8,128)S(1)} %bitcast.16, f32[1664,128]{1,0:T(8,128)S(1)} %collective-permute-done.2.theirs_ref, f32[128,128]{1,0:T(8,128)S(1)} %copy-done.5, f32[128,128]{1,0:T(8,128)S(1)} %get-tuple-element.34.lists_theirs, f32[1024,400]{1,0:T(8,128)S(1)} %get-tuple-element.35.rel_ref, ...), custom_call_target="tpu_custom_call" | custom-call | flops 6000000000 | bytes 4000000 | tf_op jit(solution)/shard_map/head_kernel/pallas_call | solution.py:351
  97.5 0.0 collective-permute-done.3.given_ref
  97.6 7.3 %tail_kernel.1 = (f32[400,256]{1,0:T(8,128)S(1)}, f32[400,256]{1,0:T(8,128)S(1)}) custom-call(f32[1664,128]{1,0:T(8,128)S(1)} %bitcast.17, f32[1664,128]{1,0:T(8,128)S(1)} %collective-permute-done.2.theirs_ref, f32[16,128]{1,0:T(8,128)S(1)} %collective-permute-done.3.given_ref, f32[512,400]{1,0:T(8,128)S(1)} %get-tuple-element.30.rel_ref, ...), custom_call_target="tpu_custom_call" | custom-call | flops 8999999488 | bytes 4000000 | tf_op jit(solution)/shard_map/tail_kernel/pallas_call | solution.py:351
  104.9 0.0 copy-start.3
  104.9 2.4 %all-gather.1 = f32[800,256]{1,0:T(8,128)S(1)} all-gather(f32[400,256]{1,0:T(8,128)S(1)} %get-tuple-element.39), channel_id=3, replica_groups=mesh['x'=4,'yz'=32,'zh'=2,'core'=2] {'core'}, dimensions={0}, use_global_device_ids=true | all-gather | bytes 1228800 | tf_op jit(solution)/shard_map/all_gather | solution.py:457
  107.3 0.1 combine_kernel.1
  107.4 24.1 %all-gather.2 = f32[800,256]{1,0:T(8,128)S(1)} all-gather(f32[400,256]{1,0:T(8,128)S(1)} %combine_kernel.1), channel_id=4, replica_groups=mesh['x'=4,'yz'=32,'zh'=2,'core'=2] {'zh'}, dimensions={0}, use_global_device_ids=true | all-gather | bytes 1228800 | tf_op jit(solution)/shard_map/all_gather | solution.py:459
  131.5 0.1 slice_add_fusion
  131.6 3.1 %all-gather.3 = f32[800,256]{1,0:T(8,128)S(1)} all-gather(f32[400,256]{1,0:T(8,128)S(1)} %slice_add_fusion), channel_id=5, replica_groups=mesh['x'=4,'yz'=32,'zh'=2,'core'=2] {'core'}, dimensions={0}, use_global_device_ids=true | all-gather | bytes 1228800 | tf_op jit(solution)/shard_map/all_gather | solution.py:460
  134.7 1.1 update_kernel.1
  (11 shorter events, 0.1 us)
Async XLA Ops:
  0.6 84.5 %copy-start = (f32[512,400]{0,1:T(8,128)S(1)}, f32[512,400]{0,1:T(8,128)}, u32[]{:S(2)}) copy-start(f32[512,400]{0,1:T(8,128)} %param.9) | copy-start | bytes 2457604
  0.6 74.1 %copy-start.1 = (f32[528,400]{0,1:T(8,128)S(1)}, f32[528,400]{0,1:T(8,128)}, u32[]{:S(2)}) copy-start(f32[528,400]{0,1:T(8,128)} %param.11) | copy-start | bytes 2534404
  3.2 82.0 %copy-start.5 = (f32[128,128]{1,0:T(8,128)S(1)}, f32[128,128]{1,0:T(8,128)}, u32[]{:S(2)}) copy-start(f32[128,128]{1,0:T(8,128)} %get-tuple-element.27.cols_ref.lists_mine) | copy-start | bytes 196612
  3.2 30.8 %all-to-all-start = ((f32[128,1,896]{2,1,0:T(1,128)}), f32[128,1,896]{2,1,0:T(1,128)S(1)}, u32[]{:S(2)}, u32[]{:S(2)}) async-start(f32[128,1,896]{2,1,0:T(1,128)} %bitcast.28), calls=%async_computation | async-start | bytes 917504 | tf_op jit(solution)/shard_map/all_to_all | solution.py:383
  20.4 18.2 %collective-permute-start = (f32[112,512]{1,0:T(8,128)}, f32[112,512]{1,0:T(8,128)S(1)}, u32[]{:S(2)}, u32[]{:S(2)}) collective-permute-start(f32[112,512]{1,0:T(8,128)} %bundle_kernel.1), channel_id=1, source_target_pairs={{0,14},{2,12},{4,10},{6,8},{8,6},{10,4},{12,2},{14,0},{16,30},{18,... | collective-permute-start | bytes 688136 | tf_op jit(solution)/shard_map/ppermute | solution.py:396
  28.3 0.7 copy-start.2
  29.0 0.7 copy-start.4
  29.7 8.8 %collective-permute-start.1 = (f32[16,128]{1,0:T(8,128)S(1)}, f32[16,128]{1,0:T(8,128)S(1)}, u32[]{:S(2)}, u32[]{:S(2)}) collective-permute-start(f32[16,128]{1,0:T(8,128)S(1)} %get-tuple-element.25), channel_id=1, source_target_pairs={{0,2},{2,0},{1,3},{3,1},{4,6},{6,4},{5,7},{7,5},{8,10},{10,8},{9,1... | collective-permute-start | bytes 24584 | tf_op jit(solution)/shard_map/ppermute | solution.py:397
  38.5 38.1 %all-to-all-start.1 = ((f32[128,1,1664]{2,1,0:T(1,128)}), f32[128,1,1664]{2,1,0:T(1,128)S(1)}, u32[]{:S(2)}, u32[]{:S(2)}) async-start(f32[128,1,1664]{2,1,0:T(1,128)} %bitcast.5), calls=%async_computation.1 | async-start | bytes 1703936 | tf_op jit(solution)/shard_map/all_to_all | solution.py:407
  69.9 15.2 %collective-permute-start.5 = (f32[4,112,512]{2,1,0:T(8,128)}, f32[4,112,512]{2,1,0:T(8,128)}, u32[]{:S(2)}, u32[]{:S(2)}) collective-permute-start(f32[4,112,512]{2,1,0:T(8,128)} %bitcast.7.far_hbm), channel_id=1, source_target_pairs={{0,1},{1,0},{2,3},{3,2},{4,5},{5,4},{6,7},{7,6},{8,9},{9,8},{10,11... | collective-permute-start | bytes 2752520 | tf_op jit(solution)/shard_map/ppermute | solution.py:409
  74.7 10.4 %collective-permute-start.4 = (f32[400,528]{1,0:T(8,128)S(1)}, f32[400,528]{1,0:T(8,128)}, u32[]{:S(2)}, u32[]{:S(2)}) collective-permute-start(f32[400,528]{1,0:T(8,128)S(1)} %bitcast.25), channel_id=1, source_target_pairs={{0,1},{1,0},{2,3},{3,2},{4,5},{5,4},{6,7},{7,6},{8,9},{9,8},{10,11... | collective-permute-start | bytes 2534408 | tf_op jit(solution)/shard_map/ppermute | solution.py:398
  76.7 15.2 %collective-permute-start.2 = (f32[1664,128]{1,0:T(8,128)S(1)}, f32[1664,128]{1,0:T(8,128)S(1)}, u32[]{:S(2)}, u32[]{:S(2)}) collective-permute-start(f32[1664,128]{1,0:T(8,128)S(1)} %bitcast.13), channel_id=1, source_target_pairs={{0,1},{1,0},{2,3},{3,2},{4,5},{5,4},{6,7},{7,6},{8,9},{9,8},{10,11... | collective-permute-start | bytes 2555912 | tf_op jit(solution)/shard_map/ppermute | solution.py:410
  80.9 16.7 %collective-permute-start.3 = (f32[16,128]{1,0:T(8,128)S(1)}, f32[16,128]{1,0:T(8,128)S(1)}, u32[]{:S(2)}, u32[]{:S(2)}) collective-permute-start(f32[16,128]{1,0:T(8,128)S(1)} %given_kernel.1), channel_id=1, source_target_pairs={{0,2},{2,0},{1,3},{3,1},{4,6},{6,4},{5,7},{7,5},{8,10},{10,8},{9,1... | collective-permute-start | bytes 24584 | tf_op jit(solution)/shard_map/ppermute | solution.py:411
  104.9 29.8 %copy-start.3 = (f32[512]{0:T(512)S(1)}, f32[512]{0:T(512)}, u32[]{:S(2)}) copy-start(f32[512]{0:T(512)} %param.10) | copy-start | bytes 6148

commit v13 on v12

--- a/solution.py
+++ b/solution.py
@@ -54,6 +54,10 @@
     return dot_nt(jnp.concatenate([a_hi, a_lo, a_hi], axis=1), jnp.concatenate([b_lo, b_hi, b_hi], axis=1))
 
 
+def dot3_nn(a_hi, a_lo, b_hi, b_lo):
+    return dot_nn(jnp.concatenate([a_hi, a_lo, a_hi], axis=1), jnp.concatenate([b_lo, b_hi, b_hi], axis=0))
+
+
 def iota(shape, dim):
     return lax.broadcasted_iota(jnp.int32, shape, dim)
 
@@ -83,7 +87,7 @@
     zh, core = place()
     pairs = (
         (head_hbm, head_ref), (rel_hbm, rel_ref), (tail_hbm, tail_ref), (neg_hbm, neg_ref), (count_hbm, count_ref),
-        (entity_hbm, entity_ref),
+        (entity_hbm.at[:, pl.ds(pl.multiple_of(core * HALF, HALF), HALF)], entity_ref),
     )
     copies = [pltpu.make_async_copy(a, b, sems.at[i]) for i, (a, b) in enumerate(pairs)]
     for copy in copies:
@@ -111,7 +115,7 @@
     cols_ref[...] = both
     give_ref[...] = give
     copies[-1].wait()
-    half = jnp.where(core == 0, entity_ref[:, 0:HALF], entity_ref[:, HALF:ROWS]).T
+    half = entity_ref[...].T
     payload = jnp.concatenate([half[0:128, :], half[128:HALF, :], both[:, 0 : 128 * CHUNK1 - 2 * D]], axis=1)
     write_rows(out_ref, payload, CHUNK1)
 
@@ -123,11 +127,9 @@
     marks = [jnp.where(matching_ref[b : b + 1, :] == rows, 1.0, 0.0) for b in range(2)]
     back_keep = jnp.where(zh == 0, marks[0], marks[1])
     back_give = jnp.where(zh == 0, marks[1], marks[0])
-    fore = back_keep.T.astype(BF16)
-    back_keep, back_give = back_keep.astype(BF16), back_give.astype(BF16)
-    partner = sum(dot_nn(fore, p) for p in reversed(parts))
-    source = sum(dot_nn(back_keep, p) for p in reversed(parts))
-    given = sum(dot_nn(back_give, p[:, 768 : 128 * CHUNK1]) for p in reversed(parts))
+    marks = jnp.concatenate([back_keep.T, back_keep, back_give], axis=0).astype(BF16)
+    picked = dot_nn(jnp.concatenate([marks] * 3, axis=1), jnp.concatenate(parts[::-1], axis=0))
+    partner, source, given = picked[0:128], picked[128:256], picked[256:384, 768 : 128 * CHUNK1]
     fill = jnp.zeros((128, 128 * CHUNK2 - 4 * D - 2 * LIST), F32)
     routed = jnp.concatenate([partner[:, 0 : 2 * D], source[:, 0 : 2 * D + LIST], given[:, 48:64], fill], axis=1)
     write_rows(out_ref, routed, CHUNK2)
@@ -277,7 +279,7 @@
         weights = times * jnp.exp(scores - jnp.max(scores, axis=1, keepdims=True))
         weights = weights / jnp.sum(weights, axis=1, keepdims=True) - tails
         w_hi, w_lo = split2(weights)
-        grad_left = dot_nn(w_hi, b_lo) + dot_nn(w_lo, b_hi) + dot_nn(w_hi, b_hi)
+        grad_left = dot3_nn(w_hi, w_lo, b_hi, b_lo)
         g_hi, g_lo = split2(grad_left * rel_ref[span, :])
         rows = lists_rows(lists)
         marks = jnp.concatenate(
@@ -326,7 +328,7 @@
         weights = times * jnp.exp(scores - jnp.max(scores, axis=0, keepdims=True))
         weights = weights / jnp.sum(weights, axis=0, keepdims=True) - tails
         w_hi, w_lo = split2(weights)
-        total = total + (dot_nn(w_lo, l_hi) + dot_nn(w_hi, l_lo) + dot_nn(w_hi, l_hi))
+        total = total + dot3_nn(w_hi, w_lo, l_hi, l_lo)
     first, second = total[0:HALF, :].T, total[HALF:ROWS, :].T
     keep_ref[...] = jnp.where(core == 0, first, second)
     send_ref[...] = jnp.where(core == 0, second, first)
@@ -375,7 +377,7 @@
         [((128 * CHUNK1, 128), F32), ((128, 128), F32), ((LIST, 128), F32)],
         (entity_t, edge_head, edge_rel, edge_tail, negatives, counts.transpose(1, 2, 0)),
         vmem=60,
-        scratch=[pltpu.VMEM((128, 128), F32), pltpu.VMEM((D, ROWS), F32)]
+        scratch=[pltpu.VMEM((128, 128), F32), pltpu.VMEM((D, HALF), F32)]
         + [pltpu.VMEM((2, 1, 1, n), jnp.int32) for n in (SLOTS, SLOTS, SLOTS, NEGS)]
         + [pltpu.VMEM((1, 1, 2), jnp.int32), pltpu.SemaphoreType.DMA((6,))],
         space=pltpu.HBM,

time: 136 us -> 136 us (level)
  no operation moved by 1% of the time
where the time goes in v13:
time: 136 us
  starting transfers between devices  54.6 us (40%)
  blocking collectives  46.6 us (34%)
  Pallas kernels  26.7 us (20%)
  waiting for transfers between devices  5.35 us (4%)
  local copies, waits for them, and re-layouts  1.39 us (1%)
    pallas_call x10, Pallas kernels, call(): pl.pallas_call(kernel, out_shape=out_shape, in_specs=[pl.BlockSpec(memory...  26.7 us
    all_gather x1, blocking collectives, shards(): chips = lax.all_gather(half, 'zh', axis=0)  24.1 us
    all_gather x1, blocking collectives, shards(): far = lax.all_gather(bundle, 'x', axis=0)  17 us
    all_to_all x1, starting transfers between devices, shards(): exchange(payload.reshape(128, 1, 128 * CHUNK1)).reshape(128 * CHUNK1, 128)  15.5 us
    all_to_all x1, starting transfers between devices, shards(): exchange(routed.reshape(128, 1, 128 * CHUNK2)).reshape(128 * CHUNK2, 128)  14.4 us
    ppermute x1, starting transfers between devices, shards(): bundle = lax.ppermute(bundle, ('yz', 'zh'), perm=mirror)  7.95 us
    ppermute x1, starting transfers between devices, shards(): far2 = swap_core(far)  4.81 us
    ppermute x1, starting transfers between devices, shards(): fetched_other = swap_core(fetched)  4.16 us
  transfers between devices with their start and end apart: 8, of which 2 were waited for; matrix products, arithmetic and copies ran while one was open for 0% of the time, Pallas kernels for 12%

profile of v13, /device:TPU:83, one launch (start us, length us, event | category | flops | bytes accessed | tf_op | source)
XLA Modules:
  0.0 135.6 jit_solution(12234624594257002826)
XLA Ops:
  0.6 0.0 copy-start.1
  0.7 2.4 %pack_kernel.1 = (f32[896,128]{1,0:T(8,128)}, f32[128,128]{1,0:T(8,128)}, f32[16,128]{1,0:T(8,128)}) custom-call(f32[400,512]{1,0:T(8,128)} %bitcast.18, s32[2,1,1,512]{3,2,1,0:T(1,128)} %head_hbm.1, s32[2,1,1,512]{3,2,1,0:T(1,128)} %rel_hbm.1, s32[2,1,1,512]{3,2,1,0:T(1,128)} %tail_hbm.1, s32[2,1,1,320]{3,2,1,0:T(1,128)} %neg_hbm.1, s32[1,1,2]{2,1,0:T(1,128)} %bitcast.29), custom_call_target="tpu_custom_call" | custom-call | tf_op jit(solution)/shard_map/pack_kernel/pallas_call | solution.py:353
  3.0 15.5 %all-to-all-start = ((f32[128,1,896]{2,1,0:T(1,128)}), f32[128,1,896]{2,1,0:T(1,128)S(1)}, u32[]{:S(2)}, u32[]{:S(2)}) async-start(f32[128,1,896]{2,1,0:T(1,128)} %bitcast.28), calls=%async_computation | async-start | bytes 917504 | tf_op jit(solution)/shard_map/all_to_all | solution.py:385
  18.5 1.7 %bundle_kernel.1 = f32[112,512]{1,0:T(8,128)} custom-call(f32[400,528]{1,0:T(8,128)} %bitcast.24), custom_call_target="tpu_custom_call" | custom-call | tf_op jit(solution)/shard_map/bundle_kernel/pallas_call | solution.py:353
  20.2 7.9 %collective-permute-start = (f32[112,512]{1,0:T(8,128)}, f32[112,512]{1,0:T(8,128)S(1)}, u32[]{:S(2)}, u32[]{:S(2)}) collective-permute-start(f32[112,512]{1,0:T(8,128)} %bundle_kernel.1), channel_id=1, source_target_pairs={{0,14},{2,12},{4,10},{6,8},{8,6},{10,4},{12,2},{14,0},{16,30},{18,... | collective-permute-start | bytes 688136 | tf_op jit(solution)/shard_map/ppermute | solution.py:398
  28.2 0.7 copy-done.2
  28.9 0.7 copy-done.4
  29.6 1.9 %collective-permute-start.1 = (f32[16,128]{1,0:T(8,128)S(1)}, f32[16,128]{1,0:T(8,128)S(1)}, u32[]{:S(2)}, u32[]{:S(2)}) collective-permute-start(f32[16,128]{1,0:T(8,128)S(1)} %get-tuple-element.25), channel_id=1, source_target_pairs={{0,2},{2,0},{1,3},{3,1},{4,6},{6,4},{5,7},{7,5},{8,10},{10,8},{9,1... | collective-permute-start | bytes 24584 | tf_op jit(solution)/shard_map/ppermute | solution.py:399
  31.5 2.3 %all-to-all-done = f32[128,1,896]{2,1,0:T(1,128)S(1)} async-done(((f32[128,1,896]{2,1,0:T(1,128)}), f32[128,1,896]{2,1,0:T(1,128)S(1)}, u32[]{:S(2)}, u32[]{:S(2)}) %all-to-all-start) | async-done | bytes 458784 | tf_op jit(solution)/shard_map/all_to_all | solution.py:385
  33.8 1.6 %route_kernel.1 = f32[1664,128]{1,0:T(8,128)} custom-call(f32[896,128]{1,0:T(8,128)S(1)} %bitcast.23, s32[2,128]{1,0:T(2,128)S(1)} %get-tuple-element.24.matching_ref), custom_call_target="tpu_custom_call" | custom-call | tf_op jit(solution)/shard_map/route_kernel/pallas_call | solution.py:353
  35.4 3.0 %collective-permute-done.1.theirs_ref = f32[16,128]{1,0:T(8,128)S(1)} collective-permute-done((f32[16,128]{1,0:T(8,128)S(1)}, f32[16,128]{1,0:T(8,128)S(1)}, u32[]{:S(2)}, u32[]{:S(2)}) %collective-permute-start.1) | collective-permute-done | bytes 8224 | tf_op jit(solution)/shard_map/ppermute | solution.py:399
  38.4 0.0 collective-permute-done
  38.4 14.4 %all-to-all-start.1 = ((f32[128,1,1664]{2,1,0:T(1,128)}), f32[128,1,1664]{2,1,0:T(1,128)S(1)}, u32[]{:S(2)}, u32[]{:S(2)}) async-start(f32[128,1,1664]{2,1,0:T(1,128)} %bitcast.5), calls=%async_computation.1 | async-start | bytes 1703936 | tf_op jit(solution)/shard_map/all_to_all | solution.py:409
  52.8 17.0 %all-gather = f32[448,512]{1,0:T(8,128)} all-gather(f32[112,512]{1,0:T(8,128)S(1)} %collective-permute-done), channel_id=2, replica_groups=mesh['x'=4,'yz'=32,'zh'=2,'core'=2] {'x'}, dimensions={0}, use_global_device_ids=true | all-gather | bytes 1146880 | tf_op jit(solution)/shard_map/all_gather | solution.py:410
  69.8 4.8 %collective-permute-start.5 = (f32[4,112,512]{2,1,0:T(8,128)}, f32[4,112,512]{2,1,0:T(8,128)}, u32[]{:S(2)}, u32[]{:S(2)}) collective-permute-start(f32[4,112,512]{2,1,0:T(8,128)} %bitcast.7.far_hbm), channel_id=1, source_target_pairs={{0,1},{1,0},{2,3},{3,2},{4,5},{5,4},{6,7},{7,6},{8,9},{9,8},{10,11... | collective-permute-start | bytes 2752520 | tf_op jit(solution)/shard_map/ppermute | solution.py:411
  74.6 1.9 %collective-permute-start.4 = (f32[400,528]{1,0:T(8,128)S(1)}, f32[400,528]{1,0:T(8,128)}, u32[]{:S(2)}, u32[]{:S(2)}) collective-permute-start(f32[400,528]{1,0:T(8,128)S(1)} %bitcast.25), channel_id=1, source_target_pairs={{0,1},{1,0},{2,3},{3,2},{4,5},{5,4},{6,7},{7,6},{8,9},{9,8},{10,11... | collective-permute-start | bytes 2534408 | tf_op jit(solution)/shard_map/ppermute | solution.py:400
  76.5 0.0 all-to-all-done.1
  76.5 4.2 %collective-permute-start.2 = (f32[1664,128]{1,0:T(8,128)S(1)}, f32[1664,128]{1,0:T(8,128)S(1)}, u32[]{:S(2)}, u32[]{:S(2)}) collective-permute-start(f32[1664,128]{1,0:T(8,128)S(1)} %bitcast.13), channel_id=1, source_target_pairs={{0,1},{1,0},{2,3},{3,2},{4,5},{5,4},{6,7},{7,6},{8,9},{9,8},{10,11... | collective-permute-start | bytes 2555912 | tf_op jit(solution)/shard_map/ppermute | solution.py:412
  80.7 4.0 %collective-permute-start.3 = (f32[16,128]{1,0:T(8,128)S(1)}, f32[16,128]{1,0:T(8,128)S(1)}, u32[]{:S(2)}, u32[]{:S(2)}) collective-permute-start(f32[16,128]{1,0:T(8,128)S(1)} %given_kernel.1), channel_id=1, source_target_pairs={{0,2},{2,0},{1,3},{3,1},{4,6},{6,4},{5,7},{7,5},{8,10},{10,8},{9,1... | collective-permute-start | bytes 24584 | tf_op jit(solution)/shard_map/ppermute | solution.py:413
  84.8 0.0 collective-permute-done.4.near2_hbm
  84.8 0.0 collective-permute-done.5.far2_hbm
  84.8 7.0 %relations_kernel.1 = (f32[1024,400]{1,0:T(8,128)S(1)}, bf16[1024,400]{1,0:T(8,128)(2,1)S(1)}, bf16[1024,400]{1,0:T(8,128)(2,1)S(1)}, f32[512,400]{1,0:T(8,128)S...) custom-call(f32[400,512]{1,0:T(8,128)S(1)} %bitcast.19, ...), custom_call_target="tpu_custom_call" | custom-call | flops 8000000000 | bytes 4000000 | tf_op jit(solution)/shard_map/relations_kernel/pallas_call | solution.py:353
  91.8 5.6 %head_kernel.1.head_grad = f32[512,400]{1,0:T(8,128)S(1)} custom-call(f32[1664,128]{1,0:T(8,128)S(1)} %bitcast.16, f32[1664,128]{1,0:T(8,128)S(1)} %collective-permute-done.2.theirs_ref, f32[128,128]{1,0:T(8,128)S(1)} %copy-done.5, f32[128,128]{1,0:T(8,128)S(1)} %get-tuple-element.34.lists_theirs, f32[1024,400]{1,0:T(8,128)S(1)} %get-tuple-element.35.rel_ref, ...), custom_call_target="tpu_custom_call" | custom-call | flops 6000000000 | bytes 4000000 | tf_op jit(solution)/shard_map/head_kernel/pallas_call | solution.py:353
  97.4 0.0 collective-permute-done.3.given_ref
  97.4 7.3 %tail_kernel.1 = (f32[400,256]{1,0:T(8,128)S(1)}, f32[400,256]{1,0:T(8,128)S(1)}) custom-call(f32[1664,128]{1,0:T(8,128)S(1)} %bitcast.17, f32[1664,128]{1,0:T(8,128)S(1)} %collective-permute-done.2.theirs_ref, f32[16,128]{1,0:T(8,128)S(1)} %collective-permute-done.3.given_ref, f32[512,400]{1,0:T(8,128)S(1)} %get-tuple-element.30.rel_ref, ...), custom_call_target="tpu_custom_call" | custom-call | flops 8999999488 | bytes 4000000 | tf_op jit(solution)/shard_map/tail_kernel/pallas_call | solution.py:353
  104.7 0.0 copy-start.3
  104.7 2.4 %all-gather.1 = f32[800,256]{1,0:T(8,128)S(1)} all-gather(f32[400,256]{1,0:T(8,128)S(1)} %get-tuple-element.39), channel_id=3, replica_groups=mesh['x'=4,'yz'=32,'zh'=2,'core'=2] {'core'}, dimensions={0}, use_global_device_ids=true | all-gather | bytes 1228800 | tf_op jit(solution)/shard_map/all_gather | solution.py:459
  107.1 0.1 combine_kernel.1
  107.2 24.1 %all-gather.2 = f32[800,256]{1,0:T(8,128)S(1)} all-gather(f32[400,256]{1,0:T(8,128)S(1)} %combine_kernel.1), channel_id=4, replica_groups=mesh['x'=4,'yz'=32,'zh'=2,'core'=2] {'zh'}, dimensions={0}, use_global_device_ids=true | all-gather | bytes 1228800 | tf_op jit(solution)/shard_map/all_gather | solution.py:461
  131.3 0.1 slice_add_fusion
  131.4 3.1 %all-gather.3 = f32[800,256]{1,0:T(8,128)S(1)} all-gather(f32[400,256]{1,0:T(8,128)S(1)} %slice_add_fusion), channel_id=5, replica_groups=mesh['x'=4,'yz'=32,'zh'=2,'core'=2] {'core'}, dimensions={0}, use_global_device_ids=true | all-gather | bytes 1228800 | tf_op jit(solution)/shard_map/all_gather | solution.py:462
  134.5 1.1 update_kernel.1
  (11 shorter events, 0.1 us)
Async XLA Ops:
  0.6 84.2 %copy-start = (f32[512,400]{0,1:T(8,128)S(1)}, f32[512,400]{0,1:T(8,128)}, u32[]{:S(2)}) copy-start(f32[512,400]{0,1:T(8,128)} %param.9) | copy-start | bytes 2457604
  0.6 73.9 %copy-start.1 = (f32[528,400]{0,1:T(8,128)S(1)}, f32[528,400]{0,1:T(8,128)}, u32[]{:S(2)}) copy-start(f32[528,400]{0,1:T(8,128)} %param.11) | copy-start | bytes 2534404
  3.0 81.8 %copy-start.5 = (f32[128,128]{1,0:T(8,128)S(1)}, f32[128,128]{1,0:T(8,128)}, u32[]{:S(2)}) copy-start(f32[128,128]{1,0:T(8,128)} %get-tuple-element.27.cols_ref.lists_mine) | copy-start | bytes 196612
  3.0 30.8 %all-to-all-start = ((f32[128,1,896]{2,1,0:T(1,128)}), f32[128,1,896]{2,1,0:T(1,128)S(1)}, u32[]{:S(2)}, u32[]{:S(2)}) async-start(f32[128,1,896]{2,1,0:T(1,128)} %bitcast.28), calls=%async_computation | async-start | bytes 917504 | tf_op jit(solution)/shard_map/all_to_all | solution.py:385
  20.2 18.2 %collective-permute-start = (f32[112,512]{1,0:T(8,128)}, f32[112,512]{1,0:T(8,128)S(1)}, u32[]{:S(2)}, u32[]{:S(2)}) collective-permute-start(f32[112,512]{1,0:T(8,128)} %bundle_kernel.1), channel_id=1, source_target_pairs={{0,14},{2,12},{4,10},{6,8},{8,6},{10,4},{12,2},{14,0},{16,30},{18,... | collective-permute-start | bytes 688136 | tf_op jit(solution)/shard_map/ppermute | solution.py:398
  28.2 0.7 copy-start.2
  28.9 0.7 copy-start.4
  29.6 8.8 %collective-permute-start.1 = (f32[16,128]{1,0:T(8,128)S(1)}, f32[16,128]{1,0:T(8,128)S(1)}, u32[]{:S(2)}, u32[]{:S(2)}) collective-permute-start(f32[16,128]{1,0:T(8,128)S(1)} %get-tuple-element.25), channel_id=1, source_target_pairs={{0,2},{2,0},{1,3},{3,1},{4,6},{6,4},{5,7},{7,5},{8,10},{10,8},{9,1... | collective-permute-start | bytes 24584 | tf_op jit(solution)/shard_map/ppermute | solution.py:399
  38.4 38.1 %all-to-all-start.1 = ((f32[128,1,1664]{2,1,0:T(1,128)}), f32[128,1,1664]{2,1,0:T(1,128)S(1)}, u32[]{:S(2)}, u32[]{:S(2)}) async-start(f32[128,1,1664]{2,1,0:T(1,128)} %bitcast.5), calls=%async_computation.1 | async-start | bytes 1703936 | tf_op jit(solution)/shard_map/all_to_all | solution.py:409
  69.8 15.0 %collective-permute-start.5 = (f32[4,112,512]{2,1,0:T(8,128)}, f32[4,112,512]{2,1,0:T(8,128)}, u32[]{:S(2)}, u32[]{:S(2)}) collective-permute-start(f32[4,112,512]{2,1,0:T(8,128)} %bitcast.7.far_hbm), channel_id=1, source_target_pairs={{0,1},{1,0},{2,3},{3,2},{4,5},{5,4},{6,7},{7,6},{8,9},{9,8},{10,11... | collective-permute-start | bytes 2752520 | tf_op jit(solution)/shard_map/ppermute | solution.py:411
  74.6 10.2 %collective-permute-start.4 = (f32[400,528]{1,0:T(8,128)S(1)}, f32[400,528]{1,0:T(8,128)}, u32[]{:S(2)}, u32[]{:S(2)}) collective-permute-start(f32[400,528]{1,0:T(8,128)S(1)} %bitcast.25), channel_id=1, source_target_pairs={{0,1},{1,0},{2,3},{3,2},{4,5},{5,4},{6,7},{7,6},{8,9},{9,8},{10,11... | collective-permute-start | bytes 2534408 | tf_op jit(solution)/shard_map/ppermute | solution.py:400
  76.5 15.3 %collective-permute-start.2 = (f32[1664,128]{1,0:T(8,128)S(1)}, f32[1664,128]{1,0:T(8,128)S(1)}, u32[]{:S(2)}, u32[]{:S(2)}) collective-permute-start(f32[1664,128]{1,0:T(8,128)S(1)} %bitcast.13), channel_id=1, source_target_pairs={{0,1},{1,0},{2,3},{3,2},{4,5},{5,4},{6,7},{7,6},{8,9},{9,8},{10,11... | collective-permute-start | bytes 2555912 | tf_op jit(solution)/shard_map/ppermute | solution.py:412
  80.7 16.6 %collective-permute-start.3 = (f32[16,128]{1,0:T(8,128)S(1)}, f32[16,128]{1,0:T(8,128)S(1)}, u32[]{:S(2)}, u32[]{:S(2)}) collective-permute-start(f32[16,128]{1,0:T(8,128)S(1)} %given_kernel.1), channel_id=1, source_target_pairs={{0,2},{2,0},{1,3},{3,1},{4,6},{6,4},{5,7},{7,5},{8,10},{10,8},{9,1... | collective-permute-start | bytes 24584 | tf_op jit(solution)/shard_map/ppermute | solution.py:413
  104.7 29.8 %copy-start.3 = (f32[512]{0:T(512)S(1)}, f32[512]{0:T(512)}, u32[]{:S(2)}) copy-start(f32[512]{0:T(512)} %param.10) | copy-start | bytes 6148
